TPU v7x, 512 devices: a whole 4x4x16 slice. The times are simulated.
512 devices in a mesh: section: 4 (over x_lo, core), seq: 32 (over z, x_hi), tp: 4 (over y).
Axes of the slice: x: 4 (x_hi: 2, x_lo: 2; x = x_hi * 2 + x_lo), y: 4, z: 16, core: 2. Of those that a mesh axis runs over, the one named last changes fastest.
Arguments:
- first_stream: bfloat16 [4, 4096, 4096], P('section', 'seq', 'tp'), may hold values from -6 to 6
- gate_stream: bfloat16 [4, 4096, 4096], P('section', 'seq', 'tp'), may hold values from -6 to 6
- value_stream: bfloat16 [4, 4096, 4096], P('section', 'seq', 'tp'), may hold values from -6 to 6
- short_taps: float32 [4, 3, 3, 4096], P('section', None, None, 'tp'), may hold values from -3 to 3
- long_filter: float32 [4, 4, 32, 32, 4096], P('section', 'tp', 'seq'), may hold values from -2 to 2, as said below
- skip_gain: float32 [4, 4096], P('section', 'tp'), may hold values from -4 to 4
- queries: bfloat16 [4, 4096, 2048], P('section', 'seq', 'tp'), may hold values from -5 to 5
- attn_keys: bfloat16 [4, 4096, 2048], P('section', 'seq', 'tp'), may hold values from -5 to 5
- attn_values: bfloat16 [4, 4096, 2048], P('section', 'seq', 'tp'), may hold values from -6 to 6
- out_weight: bfloat16 [4, 2048, 4, 1024], P('section', 'tp', None, 'seq'), may hold values from -0.125 to 0.125
Outputs:
- handed: bfloat16 [4, 4096, 4096], P('section', 'seq', 'tp')
- attended: bfloat16 [4, 4096, 4096], P('section', 'seq', 'tp')
Inputs may be any that keep to these rules, and one draw needn't show every extreme that they name: `long_filter`: a causal filter for each channel over lags 0 to 4095.
All inputs are finite; a program needn't handle non-finite values.
Results may differ from a plain program's by a relative error of at most 0.015.
Values may be sent and summed in bfloat16 or wider, within the bound.
No kernel may reach another device: no remote copies, remote signals or barrier semaphores. Data moves between devices by JAX's collectives and lax.ppermute only.
A program may use at most 64 MiB of HBM per device.

v0:
```python
import math

import jax
import jax.numpy as jnp
from jax import lax
from jax.sharding import PartitionSpec as P

HD = 128


HIGHEST = lax.Precision.HIGHEST


def from_behind(x, axis, by):
    length = lax.axis_size(axis)
    return lax.ppermute(x, axis, [(i, (i + by) % length) for i in range(length)])


def phase_table(height, breadth, period, direction):
    row_ids = lax.broadcasted_iota(jnp.int32, (height, breadth), 0)
    col_ids = lax.broadcasted_iota(jnp.int32, (height, breadth), 1)
    angles = direction * 2.0 * math.pi / period * (row_ids * col_ids % period).astype(jnp.float32)
    return (jnp.cos(angles), jnp.sin(angles))


def forward_transform(signal, half_depth):
    channels, length = signal.shape
    breadth = length // half_depth
    full_depth = 2 * half_depth
    blocks = signal.reshape(channels, half_depth, breadth)
    cos_one, sin_one = phase_table(full_depth, half_depth, full_depth, -1.0)
    real_part = jnp.einsum("ka,nab->nkb", cos_one, blocks, precision=HIGHEST)
    imag_part = jnp.einsum("ka,nab->nkb", sin_one, blocks, precision=HIGHEST)
    cos_mid, sin_mid = phase_table(full_depth, breadth, full_depth * breadth, -1.0)
    real_part, imag_part = (
        real_part * cos_mid - imag_part * sin_mid,
        real_part * sin_mid + imag_part * cos_mid,
    )
    cos_two, sin_two = phase_table(breadth, breadth, breadth, -1.0)
    out_real = jnp.einsum("nkb,bd->nkd", real_part, cos_two, precision=HIGHEST) - jnp.einsum(
        "nkb,bd->nkd", imag_part, sin_two, precision=HIGHEST
    )
    out_imag = jnp.einsum("nkb,bd->nkd", real_part, sin_two, precision=HIGHEST) + jnp.einsum(
        "nkb,bd->nkd", imag_part, cos_two, precision=HIGHEST
    )
    return (out_real, out_imag)


def inverse_transform(spec_real, spec_imag, half_depth):
    channels, full_depth, breadth = spec_real.shape
    cos_two, sin_two = phase_table(breadth, breadth, breadth, 1.0)
    mid_real = jnp.einsum("nkd,db->nkb", spec_real, cos_two, precision=HIGHEST) - jnp.einsum(
        "nkd,db->nkb", spec_imag, sin_two, precision=HIGHEST
    )
    mid_imag = jnp.einsum("nkd,db->nkb", spec_real, sin_two, precision=HIGHEST) + jnp.einsum(
        "nkd,db->nkb", spec_imag, cos_two, precision=HIGHEST
    )
    cos_mid, sin_mid = phase_table(full_depth, breadth, full_depth * breadth, 1.0)
    mid_real, mid_imag = (
        mid_real * cos_mid - mid_imag * sin_mid,
        mid_real * sin_mid + mid_imag * cos_mid,
    )
    cos_one, sin_one = phase_table(half_depth, full_depth, full_depth, 1.0)
    result = jnp.einsum("ak,nkb->nab", cos_one, mid_real, precision=HIGHEST) - jnp.einsum(
        "ak,nkb->nab", sin_one, mid_imag, precision=HIGHEST
    )
    return result.reshape(channels, half_depth * breadth) / (full_depth * breadth)


def long_convolution(product, kernel, skip_gains, half_depth):
    signal = product.astype(jnp.float32)
    sig_real, sig_imag = forward_transform(signal, half_depth)
    ker_real, ker_imag = forward_transform(kernel, half_depth)
    convolved = inverse_transform(
        sig_real * ker_real - sig_imag * ker_imag,
        sig_real * ker_imag + sig_imag * ker_real,
        half_depth,
    )
    return (convolved + skip_gains[:, None] * signal).astype(jnp.bfloat16)


def lagged_tokens(signal, amount):
    return jnp.pad(signal[:, : signal.shape[1] - amount], ((0, 0), (amount, 0)))


def short_by_channel(stream, weights):
    signal = stream.astype(jnp.float32)
    return (
        weights[0][:, None] * signal
        + weights[1][:, None] * lagged_tokens(signal, 1)
        + weights[2][:, None] * lagged_tokens(signal, 2)
    )


def body(
    first_stream,
    gate_stream,
    value_stream,
    short_taps,
    long_filter,
    skip_gain,
    queries,
    attn_keys,
    attn_values,
    out_weight,
):
    seq_count = lax.axis_size("seq")
    channels = long_filter.shape[3]
    offset = lax.axis_index("seq") * channels
    kernel = long_filter[0, 0, 0]
    local_gain = lax.dynamic_slice_in_dim(skip_gain[0], offset, channels, 0)
    local_taps = lax.dynamic_slice_in_dim(short_taps[0], offset, channels, 2)
    regrouped = (
        lax.all_to_all(first_stream[0].T, "seq", split_axis=0, concat_axis=1, tiled=True),
        lax.all_to_all(gate_stream[0].T, "seq", split_axis=0, concat_axis=1, tiled=True),
        lax.all_to_all(value_stream[0].T, "seq", split_axis=0, concat_axis=1, tiled=True),
    )
    first_short = short_by_channel(regrouped[0], local_taps[0])
    gate_short = short_by_channel(regrouped[1], local_taps[1])
    value_short = short_by_channel(regrouped[2], local_taps[2])
    product = (first_short * value_short).astype(jnp.bfloat16)
    convolved = long_convolution(product, kernel, local_gain, seq_count)
    gated = (gate_short * convolved.astype(jnp.float32)).astype(jnp.bfloat16)
    mixed_rows = lax.all_to_all(gated, "seq", split_axis=1, concat_axis=0, tiled=True).T
    handed = from_behind(mixed_rows, "section", 1)
    rows_local = queries.shape[1]
    heads_local = queries.shape[2] // HD
    score_scale = 1.0 / math.sqrt(HD)
    query_heads = queries[0].reshape(rows_local, heads_local, HD)
    query_first = lax.axis_index("seq") * rows_local
    query_pos = query_first + lax.broadcasted_iota(jnp.int32, (rows_local, 1), 0)
    start_state = (
        jnp.full((heads_local, rows_local), -1e30, jnp.float32),
        jnp.zeros((heads_local, rows_local), jnp.float32),
        jnp.zeros((rows_local, heads_local, HD), jnp.float32),
    )
    key_piece = lax.all_gather(attn_keys[0], "seq", axis=0, tiled=True)
    value_piece = lax.all_gather(attn_values[0], "seq", axis=0, tiled=True)
    piece_rows = key_piece.shape[0]

    def update(running):
        highest, totals, weighted = running
        key_heads = key_piece.reshape(piece_rows, heads_local, HD)
        value_heads = value_piece.reshape(piece_rows, heads_local, HD)
        scores = (
            jnp.einsum("rhd,nhd->hrn", query_heads, key_heads, preferred_element_type=jnp.float32)
            * score_scale
        )
        allowed = lax.broadcasted_iota(jnp.int32, (1, piece_rows), 1) <= query_pos
        masked = jnp.where(allowed[None], scores, -1e30)
        new_high = jnp.maximum(highest, jnp.max(masked, axis=2))
        probs = jnp.where(allowed[None], jnp.exp(masked - new_high[:, :, None]), 0.0)
        rescale = jnp.exp(highest - new_high)
        totals = jnp.sum(probs, axis=2)
        weighted = weighted * rescale.T[:, :, None] + jnp.einsum(
            "hrn,nhd->rhd",
            probs.astype(jnp.bfloat16),
            value_heads,
            preferred_element_type=jnp.float32,
        )
        return (new_high, totals, weighted)

    highest, totals, weighted = lax.cond(
        jnp.int32(0) > query_first + rows_local - 1, lambda running: running, update, start_state
    )
    heads_out = (
        (weighted / totals.T[:, :, None]).astype(jnp.bfloat16).reshape(rows_local, heads_local * HD)
    )
    partials = jnp.einsum(
        "rk,ktc->rtc",
        heads_out,
        lax.all_gather(out_weight[0], "seq", axis=2, tiled=True),
        preferred_element_type=jnp.float32,
    )
    attended = lax.psum_scatter(
        partials.reshape(rows_local, -1).astype(jnp.bfloat16), "tp", scatter_dimension=1, tiled=True
    )
    return (handed[None], attended[None])


def solution(mesh):
    placed = (
        P("section", "seq", "tp"),
        P("section", "seq", "tp"),
        P("section", "seq", "tp"),
        P("section", None, None, "tp"),
        P("section", "tp", "seq", None, None),
        P("section", "tp"),
        P("section", "seq", "tp"),
        P("section", "seq", "tp"),
        P("section", "seq", "tp"),
        P("section", "tp", None, "seq"),
    )
    return jax.shard_map(
        body,
        mesh=mesh,
        in_specs=placed,
        out_specs=(P("section", "seq", "tp"), P("section", "seq", "tp")),
        check_vma=False,
    )
```

profile of v0, /device:TPU:6, one launch (start us, length us, event | category | flops | bytes accessed | tf_op | source)
XLA Modules:
  0.0 557.3 jit_solution(16158469175858641583)
XLA Ops:
  8.7 1.8 copy.47
  10.5 18.2 %all-to-all-start.2 = ((bf16[32,32,128]{2,1,0:T(8,128)(2,1)}), bf16[32,32,128]{2,1,0:T(8,128)(2,1)S(1)}, u32[]{:S(2)}, u32[]{:S(2)}) async-start(bf16[32,32,128]{2,1,0:T(8,128)(2,1)} %bitcast.20), calls=%async_computation.2 | async-start | bytes 524288 | tf_op jit(solution)/shard_map/all_to_all | solution.py:116
  33.1 1.2 fusion.33
  34.3 1.5 fusion.148
  35.8 1.8 copy.43
  37.6 1.8 copy.45
  40.6 2.3 convolution_subtract_fusion.1
  42.9 1.2 convolution_add_fusion.1
  44.2 7.7 %all-to-all-done.2 = bf16[32,32,128]{2,1,0:T(8,128)(2,1)S(1)} async-done(((bf16[32,32,128]{2,1,0:T(8,128)(2,1)}), bf16[32,32,128]{2,1,0:T(8,128)(2,1)S(1)}, u32[]{:S(2)}, u32[]{:S(2)}) %all-to-all-start.2) | async-done | bytes 262176 | tf_op jit(solution)/shard_map/all_to_all | solution.py:116
  51.9 6.9 %all-to-all-start.1 = ((bf16[32,32,128]{2,1,0:T(8,128)(2,1)}), bf16[32,32,128]{2,1,0:T(8,128)(2,1)S(1)}, u32[]{:S(2)}, u32[]{:S(2)}) async-start(bf16[32,32,128]{2,1,0:T(8,128)(2,1)} %bitcast.219), calls=%async_computation.1 | async-start | bytes 524288 | tf_op jit(solution)/shard_map/all_to_all | solution.py:114
  58.9 22.2 %all-to-all-done.1 = bf16[32,32,128]{2,1,0:T(8,128)(2,1)S(1)} async-done(((bf16[32,32,128]{2,1,0:T(8,128)(2,1)}), bf16[32,32,128]{2,1,0:T(8,128)(2,1)S(1)}, u32[]{:S(2)}, u32[]{:S(2)}) %all-to-all-start.1) | async-done | bytes 262176 | tf_op jit(solution)/shard_map/all_to_all | solution.py:114
  81.1 6.4 %all-to-all-start = ((bf16[32,32,128]{2,1,0:T(8,128)(2,1)}), bf16[32,32,128]{2,1,0:T(8,128)(2,1)}, u32[]{:S(2)}, u32[]{:S(2)}) async-start(bf16[32,32,128]{2,1,0:T(8,128)(2,1)} %bitcast.218), calls=%async_computation | async-start | bytes 524288 | tf_op jit(solution)/shard_map/all_to_all | solution.py:115
  87.7 1.4 multiply_convert_fusion.1
  90.6 1.2 fusion.48
  91.9 1.2 fusion.47
  93.1 1.2 convolution_subtract_fusion.2
  94.4 1.5 multiply_add_fusion
  98.4 1.3 convolution_add_fusion
  99.6 1.5 convolution_subtract_fusion
  101.1 6.9 %all-to-all-done = bf16[32,32,128]{2,1,0:T(8,128)(2,1)} async-done(((bf16[32,32,128]{2,1,0:T(8,128)(2,1)}), bf16[32,32,128]{2,1,0:T(8,128)(2,1)}, u32[]{:S(2)}, u32[]{:S(2)}) %all-to-all-start) | async-done | bytes 262176 | tf_op jit(solution)/shard_map/all_to_all | solution.py:115
  109.1 73.8 %all-gather.7.cloned.1.call-done = bf16[1,4096,512]{2,1,0:T(8,128)(2,1)} async-done(((bf16[1,128,512]{2,1,0:T(8,128)(2,1)}), bf16[1,4096,512]{2,1,0:T(8,128)(2,1)}) %all-gather.7.cloned.1.call-update) | async-done | bytes 4194320 | tf_op jit(solution)/shard_map/all_gather | solution.py:137
  182.8 161.8 %all-gather.9.cloned.1.call-done = bf16[1,4096,512]{2,1,0:T(8,128)(2,1)} async-done(((bf16[1,128,512]{2,1,0:T(8,128)(2,1)}), bf16[1,4096,512]{2,1,0:T(8,128)(2,1)}) %all-gather.9.cloned.1.call-update) | async-done | bytes 4194320 | tf_op jit(solution)/shard_map/all_gather | solution.py:138
  344.7 9.8 %conditional.1 = (f32[4,128]{1,0:T(4,128)S(1)}, f32[128,4,128]{0,2,1:T(8,128)S(1)}) conditional(s32[]{:T(128)} %convert_element_type.162, (s32[]{:T(128)}, s32[128,1]{0,1:T(1,128)S(1)}, bf16[1,128,512]{2,1,0:T(8,128)(2,1)S(1)}, bf16[4096,512]{1,0:T(8,128)(2,1)}, bf16[4096,512]{1,0:T(8,128)(2,1)}) %tuple.49, () %tuple.17), branch_computations={%region_0.3_spmd, %region_3.4_spmd} | conditional | flops 1101595264 | bytes 53626416 | solution.py:163
  345.1 4.0 fusion
  349.2 2.5 fusion.2
  351.7 2.7 fusion.19
  354.6 152.0 %all-gather.11.cloned.1.call-done = bf16[1,512,4,1024]{1,3,2,0:T(8,128)(2,1)} async-done(((bf16[1,512,4,32]{1,3,2,0:T(8,128)(2,1)}), bf16[1,512,4,1024]{1,3,2,0:T(8,128)(2,1)}) %all-gather.11.cloned.1.call-update) | async-done | bytes 4194320 | tf_op jit(solution)/shard_map/all_gather | solution.py:172
  506.6 4.7 convolution_convert_fusion
  513.2 1.4 copy_bitcast_fusion.3
  514.6 27.7 %all_to_all.58 = bf16[32,32,128]{2,0,1:T(8,128)(2,1)S(1)} all-to-all(bf16[32,32,128]{2,0,1:T(8,128)(2,1)S(1)} %copy_bitcast_fusion.3), channel_id=1, replica_groups=mesh['section'=4,'seq'=32,'tp'=4] {'seq'}, dimensions={1} | all-to-all | bytes 524288 | tf_op jit(solution)/shard_map/all_to_all | solution.py:124
  542.3 1.9 collective-permute-start
  544.2 5.8 %collective-permute-done = bf16[128,1024]{0,1:T(8,128)(2,1)S(1)} collective-permute-done((bf16[128,1024]{0,1:T(8,128)(2,1)S(1)}, bf16[128,1024]{0,1:T(8,128)(2,1)S(1)}, u32[]{:S(2)}, u32[]{:S(2)}) %collective-permute-start) | collective-permute-done | bytes 262176 | tf_op jit(solution)/shard_map/ppermute | solution.py:16
  (52 shorter events, 15.6 us)
Async XLA Ops:
  7.2 51.6 %copy-start = (f32[1,1024]{1,0:T(1,128)S(1)}, f32[1,1024]{1,0:T(1,128)}, u32[]{:S(2)}) copy-start(f32[1,1024]{1,0:T(1,128)} %param.17) | copy-start | bytes 12292
  7.2 175.7 %all-gather.7.cloned.1.call-start = ((), (), s32[]{:S(2)}) async-start(), calls=%async_computation.6 | async-start | bytes 4325376 | tf_op jit(solution)/shard_map/all_gather | solution.py:137
  7.9 336.7 %all-gather.9.cloned.1.call-start = ((), (), s32[]{:S(2)}) async-start(), calls=%async_computation.7 | async-start | bytes 4325376 | tf_op jit(solution)/shard_map/all_gather | solution.py:138
  10.5 41.5 %all-to-all-start.2 = ((bf16[32,32,128]{2,1,0:T(8,128)(2,1)}), bf16[32,32,128]{2,1,0:T(8,128)(2,1)S(1)}, u32[]{:S(2)}, u32[]{:S(2)}) async-start(bf16[32,32,128]{2,1,0:T(8,128)(2,1)} %bitcast.20), calls=%async_computation.2 | async-start | bytes 524288 | tf_op jit(solution)/shard_map/all_to_all | solution.py:116
  28.7 477.9 %all-gather.11.cloned.1.call-start = ((), (), s32[]{:S(2)}) async-start(), calls=%async_computation.8 | async-start | bytes 4325376 | tf_op jit(solution)/shard_map/all_gather | solution.py:172
  51.9 29.2 %all-to-all-start.1 = ((bf16[32,32,128]{2,1,0:T(8,128)(2,1)}), bf16[32,32,128]{2,1,0:T(8,128)(2,1)S(1)}, u32[]{:S(2)}, u32[]{:S(2)}) async-start(bf16[32,32,128]{2,1,0:T(8,128)(2,1)} %bitcast.219), calls=%async_computation.1 | async-start | bytes 524288 | tf_op jit(solution)/shard_map/all_to_all | solution.py:114
  81.1 27.0 %all-to-all-start = ((bf16[32,32,128]{2,1,0:T(8,128)(2,1)}), bf16[32,32,128]{2,1,0:T(8,128)(2,1)}, u32[]{:S(2)}, u32[]{:S(2)}) async-start(bf16[32,32,128]{2,1,0:T(8,128)(2,1)} %bitcast.218), calls=%async_computation | async-start | bytes 524288 | tf_op jit(solution)/shard_map/all_to_all | solution.py:115
  87.4 463.4 %reduce-scatter.2.cloned.1.call-start = ((), (), s32[]{:S(2)}) async-start(), calls=%async_computation.5 | async-start | bytes 1310720 | tf_op jit(solution)/shard_map/reduce_scatter | solution.py:175
  87.7 6.7 %copy-start.1 = (f32[32,64,128]{2,1,0:T(8,128)S(1)}, f32[32,64,128]{2,1,0:T(8,128)}, u32[]{:S(2)}) copy-start(f32[32,64,128]{2,1,0:T(8,128)} %convolution_subtract_fusion.1) | copy-start | bytes 3145732
  89.2 6.7 %copy-start.2 = (bf16[32,4096]{1,0:T(8,128)(2,1)}, bf16[32,4096]{1,0:T(8,128)(2,1)S(1)}, u32[]{:S(2)}) copy-start(bf16[32,4096]{1,0:T(8,128)(2,1)S(1)} %multiply_convert_fusion.1) | copy-start | bytes 786436
  94.4 250.3 %copy-start.4 = (bf16[1,128,512]{2,1,0:T(8,128)(2,1)S(1)}, bf16[1,128,512]{2,1,0:T(8,128)(2,1)}, u32[]{:S(2)}) copy-start(bf16[1,128,512]{2,1,0:T(8,128)(2,1)} %param.18) | copy-start | bytes 393220
  345.1 6.6 %copy-start.8 = (bf16[4096,512]{1,0:T(8,128)(2,1)S(1)}, bf16[4096,512]{1,0:T(8,128)(2,1)}, u32[]{:S(2)}) copy-start(bf16[4096,512]{1,0:T(8,128)(2,1)} %get-tuple-element.17) | copy-start | bytes 12582916 | tf_op jit(solution)/shard_map/cond
  354.5 158.6 %copy-start.3 = (bf16[32,4096]{1,0:T(8,128)(2,1)S(1)}, bf16[32,4096]{1,0:T(8,128)(2,1)}, u32[]{:S(2)}) copy-start(bf16[32,4096]{1,0:T(8,128)(2,1)} %copy-done.2) | copy-start | bytes 786436
  354.5 158.6 %copy-start.5 = (f32[32]{0:T(128)S(1)}, f32[32]{0:T(128)}, u32[]{:S(2)}) copy-start(f32[32]{0:T(128)} %get-tuple-element.39) | copy-start | bytes 388
  354.5 158.6 %copy-start.6 = (f32[32]{0:T(128)S(1)}, f32[32]{0:T(128)}, u32[]{:S(2)}) copy-start(f32[32]{0:T(128)} %get-tuple-element.45) | copy-start | bytes 388
  354.5 158.6 %copy-start.7 = (f32[32]{0:T(128)S(1)}, f32[32]{0:T(128)}, u32[]{:S(2)}) copy-start(f32[32]{0:T(128)} %get-tuple-element.46) | copy-start | bytes 388
  542.3 7.7 %collective-permute-start = (bf16[128,1024]{0,1:T(8,128)(2,1)S(1)}, bf16[128,1024]{0,1:T(8,128)(2,1)S(1)}, u32[]{:S(2)}, u32[]{:S(2)}) collective-permute-start(bf16[128,1024]{0,1:T(8,128)(2,1)S(1)} %bitcast.222), channel_id=1, source_target_pairs={{0,128},{128,256},{256,384},{384,0},{1,129},{129,257},{257,385},{3... | collective-permute-start | bytes 786440 | tf_op jit(solution)/shard_map/ppermute | solution.py:16
Sparse Core Ops, SparseCore 0:
  11.1 171.6 all-gather.6
  185.9 158.6 all-gather.8
  347.8 158.7 all-gather.10
  511.4 27.5 reduce-scatter.1
where the time goes:
time: 558 us; the launch traced here: 557 us
  waiting for transfers between devices  432 us (77%)
  starting transfers between devices  33.7 us (6%)
  matrix products  33.2 us (6%)
  blocking collectives  27.7 us (5%)
  between operations  14.1 us (3%)
  local copies, waits for them, and re-layouts  9.19 us (2%)
  other arithmetic  7.1 us (1%)
    all_gather x1, waiting for transfers between devices, body(): value_piece = lax.all_gather(attn_values[0], 'seq', axis=0, tiled=True)  162 us
    all_gather x1, waiting for transfers between devices, body(): lax.all_gather(out_weight[0], 'seq', axis=2, tiled=True)  152 us
    all_gather x1, waiting for transfers between devices, body(): key_piece = lax.all_gather(attn_keys[0], 'seq', axis=0, tiled=True)  73.8 us
    all_to_all x1, blocking collectives, body(): lax.all_to_all(gated, 'seq', split_axis=1, concat_axis=0, tiled=True)  27.7 us
    all_to_all x1, waiting for transfers between devices, body(): lax.all_to_all(first_stream[0].T, 'seq', split_axis=0, concat_axis=1, til...  22.2 us
    all_to_all x1, starting transfers between devices, body(): lax.all_to_all(value_stream[0].T, 'seq', split_axis=0, concat_axis=1, til...  18.2 us
  transfers between devices with their start and end apart: 8, of which 7 were waited for; matrix products, arithmetic and copies ran while one was open for 8% of the time, Pallas kernels for 0%

commit v1 on v0

v1 whole, which is shorter than its diff:
```python
import math

import jax
import jax.numpy as jnp
import numpy as np
from jax import lax
from jax.sharding import Mesh, PartitionSpec as P

HD = 128
BF16 = jnp.bfloat16
F32 = jnp.float32
HIGH = lax.Precision.HIGH


def dot(left, right, contract, precision=None):
    return lax.dot_general(
        left, right, (contract, ((), ())), precision=precision, preferred_element_type=F32
    )


def transform_tables(depth, breadth):
    full = 2 * depth
    half = depth + 1
    k = np.arange(half)
    a = np.arange(depth)
    b = np.arange(breadth)
    one = -2.0 * np.pi * np.outer(k, a) / full
    first = np.stack([np.cos(one), np.sin(one)])
    mid = -2.0 * np.pi * np.outer(k, b) / (full * breadth)
    two = -2.0 * np.pi * (np.outer(b, b) % breadth) / breadth
    cos_two, sin_two = np.cos(two), np.sin(two)
    forward = np.block([[cos_two, sin_two], [-sin_two, cos_two]])
    backward = np.block([[cos_two, -sin_two], [sin_two, cos_two]])
    weight = np.where((k == 0) | (k == depth), 1.0, 2.0) / (full * breadth)
    last = np.concatenate([np.cos(one).T * weight, np.sin(one).T * weight], axis=1)
    as32 = lambda x: np.asarray(x, np.float32)
    return as32(first), as32(np.cos(mid)), as32(np.sin(mid)), as32(forward), as32(backward), as32(last)


def forward_transform(blocks, tables):
    first, cos_mid, sin_mid, forward, _, _ = tables
    depth, channels, breadth = blocks.shape
    flat = blocks.reshape(depth, channels * breadth)
    real = dot(first[0], flat, ((1,), (0,)), HIGH).reshape(-1, channels, breadth)
    imag = dot(first[1], flat, ((1,), (0,)), HIGH).reshape(-1, channels, breadth)
    cos_mid, sin_mid = cos_mid[:, None], sin_mid[:, None]
    turned = jnp.concatenate(
        [real * cos_mid - imag * sin_mid, real * sin_mid + imag * cos_mid], axis=2
    )
    return dot(turned, forward, ((2,), (0,)), HIGH)


def inverse_transform(spectrum, tables):
    _, cos_mid, sin_mid, _, backward, last = tables
    half, channels, twice = spectrum.shape
    breadth = twice // 2
    mid = dot(spectrum, backward, ((2,), (0,)), HIGH)
    real, imag = mid[:, :, :breadth], mid[:, :, breadth:]
    cos_mid, sin_mid = cos_mid[:, None], sin_mid[:, None]
    turned = jnp.concatenate(
        [real * cos_mid + imag * sin_mid, imag * cos_mid - real * sin_mid], axis=0
    )
    out = dot(last, turned.reshape(2 * half, channels * breadth), ((1,), (0,)), HIGH)
    return out.reshape(-1, channels, breadth)


def short_by_token(stream, before, taps):
    rows = stream.shape[0]
    whole = jnp.concatenate([before, stream], axis=0).astype(F32)
    return taps[0] * whole[2:] + taps[1] * whole[1 : rows + 1] + taps[2] * whole[:rows]


def body(
    first_stream,
    gate_stream,
    value_stream,
    short_taps,
    long_filter,
    skip_gain,
    queries,
    attn_keys,
    attn_values,
    out_weight,
):
    n_z, n_x, n_tp = lax.axis_size("z"), lax.axis_size("xh"), lax.axis_size("tp")
    n_seq = n_z * n_x
    n_plane = n_x * n_tp
    seq_at = lax.axis_index(("z", "xh"))
    tp_at = lax.axis_index("tp")
    x_at = lax.axis_index("xh")
    rows = queries.shape[1]
    wide = queries.shape[2]
    channels = long_filter.shape[3]
    heads = wide // HD
    quarter = rows // n_tp
    eighth = quarter // n_x

    streams = jnp.stack([first_stream[0], gate_stream[0], value_stream[0]])
    tails = lax.ppermute(
        streams[:, -2:], ("z", "xh"), [(i, i + 1) for i in range(n_seq - 1)]
    )

    weight = out_weight[0].transpose(1, 2, 0)
    packed = jnp.concatenate(
        [
            queries[0].reshape(n_tp, quarter, wide),
            attn_keys[0].reshape(n_tp, quarter, wide),
            attn_values[0].reshape(n_tp, quarter, wide),
            weight,
        ],
        axis=1,
    )
    packed = lax.all_to_all(packed, "tp", 0, 0)
    weight = packed[:, 3 * quarter :].transpose(1, 0, 2).reshape(channels, n_tp * wide)
    weight = lax.all_gather(weight, "z", axis=0, tiled=True)

    taps = short_taps[0]
    first_short = short_by_token(first_stream[0], tails[0], taps[0])
    value_short = short_by_token(value_stream[0], tails[2], taps[2])
    product = (first_short * value_short).astype(BF16)
    product = product.T.reshape(n_seq, channels, rows)
    attn_in = packed[:, : 3 * quarter].reshape(n_tp, 3, n_x, eighth, heads, HD)
    attn_in = attn_in.transpose(0, 4, 2, 1, 3, 5).reshape(n_seq, 3 * eighth, HD)
    mixed = lax.all_to_all(jnp.concatenate([attn_in, product], axis=1), ("z", "xh"), 0, 0)

    tables = transform_tables(n_seq, rows)
    kernel = long_filter[0, 0, 0].reshape(channels, n_seq, rows).transpose(1, 0, 2)
    kernel_spec = forward_transform(kernel, tables)

    own = mixed[:, : 3 * eighth].reshape(n_seq, 3, eighth, HD).transpose(1, 0, 2, 3)
    query = own[0].reshape(n_seq * eighth, HD)
    pairs = lax.all_to_all(
        jnp.broadcast_to(own[None, 1:], (n_plane, 2, n_seq, eighth, HD)), ("xh", "tp"), 0, 0
    )

    product = mixed[:, 3 * eighth :].astype(F32)
    spec = forward_transform(product, tables)
    real, imag = spec[:, :, :rows], spec[:, :, rows:]
    kernel_real, kernel_imag = kernel_spec[:, :, :rows], kernel_spec[:, :, rows:]
    joined = jnp.concatenate(
        [real * kernel_real - imag * kernel_imag, real * kernel_imag + imag * kernel_real], axis=2
    )
    convolved = inverse_transform(joined, tables)
    gain = lax.dynamic_slice_in_dim(skip_gain[0], seq_at * channels, channels, 0)
    long_out = (convolved + gain[None, :, None] * product).astype(BF16)

    keys = pairs[:, 0].reshape(-1, HD)
    values = pairs[:, 1].reshape(-1, HD)
    scores = dot(query, keys, ((1,), (1,))) * (1.0 / math.sqrt(HD))
    q_ids = lax.broadcasted_iota(jnp.int32, (n_seq * eighth, 1), 0)
    q_pos = q_ids // eighth * rows + q_ids % eighth + tp_at * quarter + x_at * eighth
    k_ids = lax.broadcasted_iota(jnp.int32, (1, n_seq * rows), 1)
    k_from = k_ids // (n_seq * eighth)
    k_in = k_ids % (n_seq * eighth)
    k_pos = (
        k_in // eighth * rows + k_in % eighth + k_from % n_tp * quarter + k_from // n_tp * eighth
    )
    allowed = k_pos <= q_pos
    masked = jnp.where(allowed, scores, -1e30)
    highest = jnp.max(masked, axis=1, keepdims=True)
    probs = jnp.exp(masked - highest)
    totals = jnp.sum(probs, axis=1, keepdims=True)
    heads_out = (dot(probs.astype(BF16), values, ((1,), (0,))) / totals).astype(BF16)

    back = lax.all_to_all(
        jnp.concatenate([heads_out.reshape(n_seq, eighth, HD), long_out], axis=1),
        ("z", "xh"),
        0,
        0,
    )
    heads_rows = back[:, :eighth].reshape(n_z, n_x, eighth, HD).transpose(1, 2, 0, 3)
    heads_rows = heads_rows.reshape(quarter, n_z * HD)
    plane_rows = lax.all_to_all(
        jnp.broadcast_to(heads_rows[None], (n_plane, quarter, n_z * HD)), ("xh", "tp"), 0, 0
    ).reshape(n_x * rows, n_z * HD)

    gate_short = short_by_token(gate_stream[0], tails[1], taps[1])
    long_rows = back[:, eighth:].reshape(n_seq * channels, rows).T
    hyena = (gate_short * long_rows.astype(F32)).astype(BF16)
    n_sec = lax.axis_size("section")
    handed = lax.ppermute(hyena, "section", [(i, (i + 1) % n_sec) for i in range(n_sec)])

    out = dot(plane_rows, weight, ((1,), (1,))).astype(BF16)
    out = lax.all_to_all(out.reshape(n_x, rows, n_z * channels), "xh", 0, 0)
    attended = out.reshape(n_x, rows, n_z, channels).transpose(1, 2, 0, 3).reshape(rows, -1)
    return (handed[None], attended[None])


def solution(mesh):
    n_sec, n_seq, n_tp = (mesh.shape[name] for name in ("section", "seq", "tp"))
    finer = Mesh(mesh.devices.reshape(n_sec, n_seq // 2, 2, n_tp), ("section", "z", "xh", "tp"))
    seq = ("z", "xh")
    placed = (
        P("section", seq, "tp"),
        P("section", seq, "tp"),
        P("section", seq, "tp"),
        P("section", None, None, "tp"),
        P("section", "tp", seq, None, None),
        P("section", "tp"),
        P("section", seq, "tp"),
        P("section", seq, "tp"),
        P("section", seq, "tp"),
        P("section", "tp", None, seq),
    )
    return jax.shard_map(
        body,
        mesh=finer,
        in_specs=placed,
        out_specs=(P("section", seq, "tp"), P("section", seq, "tp")),
        check_vma=False,
    )
```

time: 558 us -> 197 us (0.35)
  the two profiles are of different devices: /device:TPU:6 before, /device:TPU:2 now
where the time goes in v1:
time: 197 us; the launch traced here: 196 us
  waiting for transfers between devices  70.7 us (36%)
  starting transfers between devices  41 us (21%)
  blocking collectives  36 us (18%)
  between operations  14.6 us (7%)
  local copies, waits for them, and re-layouts  12.8 us (6%)
  matrix products  11.2 us (6%)
  other arithmetic  10.1 us (5%)
    all_to_all x1, blocking collectives, body(): lax.all_to_all(jnp.concatenate([heads_out.reshape(n_seq, eighth, HD), lon...  36 us
    all_to_all x1, waiting for transfers between devices, body(): lax.all_to_all(jnp.concatenate([attn_in, product], axis=1), ('z', 'xh'),...  32.7 us
    all_to_all x1, starting transfers between devices, body(): lax.all_to_all(jnp.concatenate([attn_in, product], axis=1), ('z', 'xh'),...  16.8 us
    all_to_all x1, waiting for transfers between devices, body(): lax.all_to_all(jnp.broadcast_to(heads_rows[None], (n_plane, quarter, n_z...  13.2 us
    all_to_all x1, waiting for transfers between devices, body(): lax.all_to_all(jnp.broadcast_to(own[None, 1:], (n_plane, 2, n_seq, eighth...  13.1 us
    dot_general x11, matrix products, dot(): lax.dot_general(left, right, (contract, ((), ())), precision=precision, p...  11.2 us
    unnamed x54, local copies, waits for them, and re-layouts  6.17 us
    all_to_all x1, waiting for transfers between devices, body(): packed = lax.all_to_all(packed, 'tp', 0, 0)  5.81 us
  transfers between devices with their start and end apart: 8, of which 5 were waited for; matrix products, arithmetic and copies ran while one was open for 15% of the time, Pallas kernels for 0%

profile of v1, /device:TPU:2, one launch (start us, length us, event | category | flops | bytes accessed | tf_op | source)
XLA Modules:
  0.0 196.4 jit_solution(9264037655178319686)
XLA Ops:
  7.2 0.8 pad_maximum_fusion.4
  8.0 4.0 %collective-permute-start = (bf16[3,2,1024]{2,1,0:T(2,128)(2,1)S(1)}, bf16[3,2,1024]{2,1,0:T(2,128)(2,1)S(1)}, u32[]{:S(2)}, u32[]{:S(2)}) collective-permute-start(bf16[3,2,1024]{2,1,0:T(2,128)(2,1)S(1)} %pad_maximum_fusion.4), channel_id=1, source_target_pairs={{0,4},{4,8},{8,12},{12,16},{16,20},{20,24},{24,28},{28,32},{32,36}... | collective-permute-start | bytes 36872 | tf_op jit(solution)/shard_map/ppermute | solution.py:99
  12.1 2.0 %pad_maximum_fusion.2 = bf16[4,128,512]{2,1,0:T(8,128)(2,1)} fusion(bf16[4,32,512]{2,1,0:T(8,128)(2,1)} %bitcast.159, bf16[4,32,512]{2,1,0:T(8,128)(2,1)} %bitcast.160, bf16[4,32,512]{2,1,0:T(8,128)(2,1)} %bitcast.161, bf16[4,32,512]{2,1,0:T(8,128)(2,1)} %bitcast.162), kind=kLoop, calls=%fused_computation.59 | loop fusion | flops 2097152 | bytes 1048576 | tf_op jit(solution)/shard_map/concatenate | solution.py:104
  14.0 4.5 %all-to-all-start = ((bf16[4,128,512]{2,1,0:T(8,128)(2,1)}), bf16[4,128,512]{2,1,0:T(8,128)(2,1)S(1)}, u32[]{:S(2)}, u32[]{:S(2)}) async-start(bf16[4,128,512]{2,1,0:T(8,128)(2,1)} %pad_maximum_fusion.2), calls=%async_computation | async-start | bytes 1048576 | tf_op jit(solution)/shard_map/all_to_all | solution.py:113
  20.3 1.5 fusion.30
  21.9 5.8 %all-to-all-done = bf16[4,128,512]{2,1,0:T(8,128)(2,1)S(1)} async-done(((bf16[4,128,512]{2,1,0:T(8,128)(2,1)}), bf16[4,128,512]{2,1,0:T(8,128)(2,1)S(1)}, u32[]{:S(2)}, u32[]{:S(2)}) %all-to-all-start) | async-done | bytes 524320 | tf_op jit(solution)/shard_map/all_to_all | solution.py:113
  27.9 0.9 pad_maximum_fusion.1
  28.8 16.8 %all-to-all-start.1 = ((bf16[32,80,128]{2,1,0:T(8,128)(2,1)}), bf16[32,80,128]{2,1,0:T(8,128)(2,1)S(1)}, u32[]{:S(2)}, u32[]{:S(2)}) async-start(bf16[32,80,128]{2,1,0:T(8,128)(2,1)} %pad_maximum_fusion.1), calls=%async_computation.1 | async-start | bytes 1310720 | tf_op jit(solution)/shard_map/all_to_all | solution.py:124
  47.9 0.7 fusion.24
  48.7 1.6 fusion.26
  50.9 32.7 %all-to-all-done.1 = bf16[32,80,128]{2,1,0:T(8,128)(2,1)S(1)} async-done(((bf16[32,80,128]{2,1,0:T(8,128)(2,1)}), bf16[32,80,128]{2,1,0:T(8,128)(2,1)S(1)}, u32[]{:S(2)}, u32[]{:S(2)}) %all-to-all-start.1) | async-done | bytes 655392 | tf_op jit(solution)/shard_map/all_to_all | solution.py:124
  83.7 1.7 broadcast_in_dim.12
  85.5 4.7 %all-to-all-start.2 = ((bf16[8,2,32,16,128]{4,3,2,1,0:T(8,128)(2,1)}), bf16[8,2,32,16,128]{4,3,2,1,0:T(8,128)(2,1)S(1)}, u32[]{:S(2)}, u32[]{:S(2)}) async-start(bf16[8,2,32,16,128]{4,3,2,1,0:T(8,128)(2,1)} %broadcast_in_dim.12), calls=%async_computation.2 | async-start | bytes 4194304 | tf_op jit(solution)/shard_map/all_to_all | solution.py:132
  90.2 1.1 fusion.42
  94.9 0.8 copy-done.7
  96.7 0.7 copy.86
  98.2 13.1 %all-to-all-done.2 = bf16[8,2,32,16,128]{4,3,2,1,0:T(8,128)(2,1)S(1)} async-done(((bf16[8,2,32,16,128]{4,3,2,1,0:T(8,128)(2,1)}), bf16[8,2,32,16,128]{4,3,2,1,0:T(8,128)(2,1)S(1)}, u32[]{:S(2)}, u32[]{:S(2)}) %all-to-all-start.2) | async-done | bytes 2097184 | tf_op jit(solution)/shard_map/all_to_all | solution.py:132
  111.6 1.6 fusion.90
  113.2 1.3 fusion
  114.5 1.3 fusion.8
  115.9 36.0 %all_to_all.30 = bf16[32,48,128]{2,1,0:T(8,128)(2,1)S(1)} all-to-all(bf16[32,48,128]{2,1,0:T(8,128)(2,1)S(1)} %pad_maximum_fusion.3), channel_id=1, replica_groups=mesh['section'=4,'z'=16,'xh'=2,'tp'=4] {'z','xh'}, dimensions={0} | all-to-all | bytes 786432 | tf_op jit(solution)/shard_map/all_to_all | solution.py:165
  152.0 1.1 broadcast_in_dim.27
  153.1 5.6 %all-to-all-start.4 = ((bf16[8,32,2048]{2,1,0:T(8,128)(2,1)}), bf16[8,32,2048]{2,1,0:T(8,128)(2,1)S(1)}, u32[]{:S(2)}, u32[]{:S(2)}) async-start(bf16[8,32,2048]{2,1,0:T(8,128)(2,1)} %broadcast_in_dim.27), calls=%async_computation.4 | async-start | bytes 2097152 | tf_op jit(solution)/shard_map/all_to_all | solution.py:173
  159.4 0.7 fusion.36
  160.2 1.9 collective-permute-start.1
  162.1 13.2 %all-to-all-done.4 = bf16[8,32,2048]{2,1,0:T(8,128)(2,1)S(1)} async-done(((bf16[8,32,2048]{2,1,0:T(8,128)(2,1)}), bf16[8,32,2048]{2,1,0:T(8,128)(2,1)S(1)}, u32[]{:S(2)}, u32[]{:S(2)}) %all-to-all-start.4) | async-done | bytes 1048608 | tf_op jit(solution)/shard_map/all_to_all | solution.py:173
  175.3 2.3 %convolution_convert_fusion = bf16[256,512]{1,0:T(8,128)(2,1)S(1)} fusion(bf16[256,2048]{1,0:T(8,128)(2,1)S(1)} %bitcast.143, bf16[512,2048]{1,0:T(8,128)(2,1)} %all-gather.2.cloned.1.call-done), kind=kOutput, calls=%fused_computation.7 | convolution fusion | flops 537001984 | bytes 3407872 | tf_op jit(solution)/shard_map/dot_general | solution.py:16
  177.7 0.8 copy.72
  178.5 3.4 %all-to-all-start.5 = ((bf16[2,128,512]{1,2,0:T(8,128)(2,1)}), bf16[2,128,512]{1,2,0:T(8,128)(2,1)S(1)}, u32[]{:S(2)}, u32[]{:S(2)}) async-start(bf16[2,128,512]{1,2,0:T(8,128)(2,1)} %copy.72), calls=%async_computation.5 | async-start | bytes 524288 | tf_op jit(solution)/shard_map/all_to_all | solution.py:184
  182.0 0.9 copy.74
  182.8 5.8 %all-to-all-done.5 = bf16[2,128,512]{1,2,0:T(8,128)(2,1)S(1)} async-done(((bf16[2,128,512]{1,2,0:T(8,128)(2,1)}), bf16[2,128,512]{1,2,0:T(8,128)(2,1)S(1)}, u32[]{:S(2)}, u32[]{:S(2)}) %all-to-all-start.5) | async-done | bytes 262176 | tf_op jit(solution)/shard_map/all_to_all | solution.py:184
  188.7 0.9 copy.75
  (88 shorter events, 11.4 us)
Async XLA Ops:
  7.2 39.0 %copy-start = (f32[1,1024]{1,0:T(1,128)S(1)}, f32[1,1024]{1,0:T(1,128)}, u32[]{:S(2)}) copy-start(f32[1,1024]{1,0:T(1,128)} %param.28) | copy-start | bytes 12292
  7.2 11.3 %copy-start.3 = (bf16[1,128,1024]{2,1,0:T(8,128)(2,1)S(1)}, bf16[1,128,1024]{2,1,0:T(8,128)(2,1)}, u32[]{:S(2)}) copy-start(bf16[1,128,1024]{2,1,0:T(8,128)(2,1)} %param.23) | copy-start | bytes 786436
  7.2 11.3 %copy-start.10 = (f32[1,3,3,1024]{3,0,2,1:T(1,128)S(1)}, f32[1,3,3,1024]{3,0,2,1:T(1,128)}, u32[]{:S(2)}) copy-start(f32[1,3,3,1024]{3,0,2,1:T(1,128)} %param.26) | copy-start | bytes 110596
  8.0 10.9 %collective-permute-start = (bf16[3,2,1024]{2,1,0:T(2,128)(2,1)S(1)}, bf16[3,2,1024]{2,1,0:T(2,128)(2,1)S(1)}, u32[]{:S(2)}, u32[]{:S(2)}) collective-permute-start(bf16[3,2,1024]{2,1,0:T(2,128)(2,1)S(1)} %pad_maximum_fusion.4), channel_id=1, source_target_pairs={{0,4},{4,8},{8,12},{12,16},{16,20},{20,24},{24,28},{28,32},{32,36}... | collective-permute-start | bytes 36872 | tf_op jit(solution)/shard_map/ppermute | solution.py:99
  12.1 6.6 %copy-start.4 = (bf16[1,128,1024]{2,1,0:T(8,128)(2,1)S(1)}, bf16[1,128,1024]{2,1,0:T(8,128)(2,1)}, u32[]{:S(2)}) copy-start(bf16[1,128,1024]{2,1,0:T(8,128)(2,1)} %param.25) | copy-start | bytes 786436
  14.0 13.7 %all-to-all-start = ((bf16[4,128,512]{2,1,0:T(8,128)(2,1)}), bf16[4,128,512]{2,1,0:T(8,128)(2,1)S(1)}, u32[]{:S(2)}, u32[]{:S(2)}) async-start(bf16[4,128,512]{2,1,0:T(8,128)(2,1)} %pad_maximum_fusion.2), calls=%async_computation | async-start | bytes 1048576 | tf_op jit(solution)/shard_map/all_to_all | solution.py:113
  27.9 17.8 %copy-start.6 = (f32[1,1,1,32,4096]{4,3,2,1,0:T(8,128)S(1)}, f32[1,1,1,32,4096]{4,3,2,1,0:T(8,128)}, u32[]{:S(2)}) copy-start(f32[1,1,1,32,4096]{4,3,2,1,0:T(8,128)} %param.27) | copy-start | bytes 1572868
  28.8 54.8 %all-to-all-start.1 = ((bf16[32,80,128]{2,1,0:T(8,128)(2,1)}), bf16[32,80,128]{2,1,0:T(8,128)(2,1)S(1)}, u32[]{:S(2)}, u32[]{:S(2)}) async-start(bf16[32,80,128]{2,1,0:T(8,128)(2,1)} %pad_maximum_fusion.1), calls=%async_computation.1 | async-start | bytes 1310720 | tf_op jit(solution)/shard_map/all_to_all | solution.py:124
  45.6 2.3 %copy-start.14 = (f32[33,32,1]{0,1,2:T(8,128)S(1)}, f32[33,32,1]{0,1,2:T(8,128)}, u32[]{:S(2)}) copy-start(f32[33,32,1]{0,1,2:T(8,128)} %constant.159) | copy-start | bytes 12676
  45.6 116.5 %all-gather.2.cloned.1.call-start = ((), (), s32[]{:S(2)}) async-start(), calls=%async_computation.6 | async-start | bytes 2228224 | tf_op jit(solution)/shard_map/all_gather | solution.py:115
  45.8 2.9 %copy-start.13 = (f32[33,32,1]{0,1,2:T(8,128)S(1)}, f32[33,32,1]{0,1,2:T(8,128)}, u32[]{:S(2)}) copy-start(f32[33,32,1]{0,1,2:T(8,128)} %constant.158) | copy-start | bytes 12676
  85.5 25.7 %all-to-all-start.2 = ((bf16[8,2,32,16,128]{4,3,2,1,0:T(8,128)(2,1)}), bf16[8,2,32,16,128]{4,3,2,1,0:T(8,128)(2,1)S(1)}, u32[]{:S(2)}, u32[]{:S(2)}) async-start(bf16[8,2,32,16,128]{4,3,2,1,0:T(8,128)(2,1)} %broadcast_in_dim.12), calls=%async_computation.2 | async-start | bytes 4194304 | tf_op jit(solution)/shard_map/all_to_all | solution.py:132
  90.2 1.3 copy-start.12
  91.5 1.1 copy-start.1
  91.5 1.1 copy-start.8
  91.5 1.1 copy-start.9
  92.6 1.0 copy-start.2
  94.7 1.0 copy-start.7
  96.6 0.7 copy-start.11
  97.4 0.6 copy-start.18
  98.1 13.4 %copy-start.16 = (s32[4096]{0:T(1024)S(1)}, s32[4096]{0:T(1024)}, u32[]{:S(2)}) copy-start(s32[4096]{0:T(1024)} %fusion.55) | copy-start | bytes 49156
  98.2 13.4 %copy-start.17 = (s32[512]{0:T(512)S(1)}, s32[512]{0:T(512)}, u32[]{:S(2)}) copy-start(s32[512]{0:T(512)} %fusion.80) | copy-start | bytes 6148
  153.1 5.6 %copy-start.5 = (bf16[1,128,1024]{2,1,0:T(8,128)(2,1)S(1)}, bf16[1,128,1024]{2,1,0:T(8,128)(2,1)}, u32[]{:S(2)}) copy-start(bf16[1,128,1024]{2,1,0:T(8,128)(2,1)} %param.24) | copy-start | bytes 786436
  153.1 5.8 %copy-start.15 = (bf16[1,2,1024]{2,1,0:T(2,128)(2,1)S(1)}, bf16[1,2,1024]{2,1,0:T(2,128)(2,1)}, u32[]{:S(2)}) copy-start(bf16[1,2,1024]{2,1,0:T(2,128)(2,1)} %get-tuple-element.28) | copy-start | bytes 12292
  153.1 22.2 %all-to-all-start.4 = ((bf16[8,32,2048]{2,1,0:T(8,128)(2,1)}), bf16[8,32,2048]{2,1,0:T(8,128)(2,1)S(1)}, u32[]{:S(2)}, u32[]{:S(2)}) async-start(bf16[8,32,2048]{2,1,0:T(8,128)(2,1)} %broadcast_in_dim.27), calls=%async_computation.4 | async-start | bytes 2097152 | tf_op jit(solution)/shard_map/all_to_all | solution.py:173
  160.2 21.8 %collective-permute-start.1 = (bf16[128,1024]{0,1:T(8,128)(2,1)S(1)}, bf16[128,1024]{0,1:T(8,128)(2,1)S(1)}, u32[]{:S(2)}, u32[]{:S(2)}) collective-permute-start(bf16[128,1024]{0,1:T(8,128)(2,1)S(1)} %fusion.36), channel_id=1, source_target_pairs={{0,128},{128,256},{256,384},{384,0},{1,129},{129,257},{257,385},{3... | collective-permute-start | bytes 786440 | tf_op jit(solution)/shard_map/ppermute | solution.py:181
  178.5 10.1 %all-to-all-start.5 = ((bf16[2,128,512]{1,2,0:T(8,128)(2,1)}), bf16[2,128,512]{1,2,0:T(8,128)(2,1)S(1)}, u32[]{:S(2)}, u32[]{:S(2)}) async-start(bf16[2,128,512]{1,2,0:T(8,128)(2,1)} %copy.72), calls=%async_computation.5 | async-start | bytes 524288 | tf_op jit(solution)/shard_map/all_to_all | solution.py:184
Sparse Core Ops, SparseCore 0:
  51.0 75.7 all-gather.1

commit v2 on v1

--- a/solution.py
+++ b/solution.py
@@ -101,27 +101,28 @@
     )
 
     weight = out_weight[0].transpose(1, 2, 0)
+    early, late = weight[: n_tp // 2], weight[n_tp // 2 :]
+    early = lax.all_gather(early.reshape(-1, wide), "z")
     packed = jnp.concatenate(
         [
             queries[0].reshape(n_tp, quarter, wide),
             attn_keys[0].reshape(n_tp, quarter, wide),
             attn_values[0].reshape(n_tp, quarter, wide),
-            weight,
         ],
         axis=1,
     )
     packed = lax.all_to_all(packed, "tp", 0, 0)
-    weight = packed[:, 3 * quarter :].transpose(1, 0, 2).reshape(channels, n_tp * wide)
-    weight = lax.all_gather(weight, "z", axis=0, tiled=True)
 
     taps = short_taps[0]
     first_short = short_by_token(first_stream[0], tails[0], taps[0])
     value_short = short_by_token(value_stream[0], tails[2], taps[2])
     product = (first_short * value_short).astype(BF16)
     product = product.T.reshape(n_seq, channels, rows)
-    attn_in = packed[:, : 3 * quarter].reshape(n_tp, 3, n_x, eighth, heads, HD)
+    attn_in = packed.reshape(n_tp, 3, n_x, eighth, heads, HD)
     attn_in = attn_in.transpose(0, 4, 2, 1, 3, 5).reshape(n_seq, 3 * eighth, HD)
     mixed = lax.all_to_all(jnp.concatenate([attn_in, product], axis=1), ("z", "xh"), 0, 0)
+    mixed, late = lax.optimization_barrier((mixed, late))
+    late = lax.all_gather(late.reshape(-1, wide), "z")
 
     tables = transform_tables(n_seq, rows)
     kernel = long_filter[0, 0, 0].reshape(channels, n_seq, rows).transpose(1, 0, 2)
@@ -168,11 +169,13 @@
         0,
         0,
     )
-    heads_rows = back[:, :eighth].reshape(n_z, n_x, eighth, HD).transpose(1, 2, 0, 3)
-    heads_rows = heads_rows.reshape(quarter, n_z * HD)
+    heads_rows = back[:, :eighth].reshape(n_tp, heads, n_x, eighth, HD).transpose(0, 2, 3, 1, 4)
+    heads_rows = jnp.broadcast_to(
+        heads_rows.reshape(1, n_tp, quarter, wide), (n_x, n_tp, quarter, wide)
+    )
     plane_rows = lax.all_to_all(
-        jnp.broadcast_to(heads_rows[None], (n_plane, quarter, n_z * HD)), ("xh", "tp"), 0, 0
-    ).reshape(n_x * rows, n_z * HD)
+        heads_rows.reshape(n_plane, quarter, wide), ("xh", "tp"), 0, 0
+    ).reshape(n_x * rows, wide)
 
     gate_short = short_by_token(gate_stream[0], tails[1], taps[1])
     long_rows = back[:, eighth:].reshape(n_seq * channels, rows).T
@@ -180,8 +183,16 @@
     n_sec = lax.axis_size("section")
     handed = lax.ppermute(hyena, "section", [(i, (i + 1) % n_sec) for i in range(n_sec)])
 
-    out = dot(plane_rows, weight, ((1,), (1,))).astype(BF16)
-    out = lax.all_to_all(out.reshape(n_x, rows, n_z * channels), "xh", 0, 0)
+    partials = []
+    for weight in (early, late):
+        weight = weight.reshape(n_z, n_tp // 2, channels, wide)
+        for at in range(n_tp // 2):
+            part = weight[:, at].reshape(n_z * channels, wide)
+            part = dot(plane_rows, part, ((1,), (1,))).astype(BF16)
+            partials.append(part.reshape(n_x, rows, n_z * channels))
+    partials = jnp.stack(partials, axis=1).reshape(n_plane, rows, n_z * channels)
+    partials = lax.all_to_all(partials, ("xh", "tp"), 0, 0)
+    out = jnp.sum(partials.reshape(n_x, n_tp, rows, n_z * channels).astype(F32), axis=1).astype(BF16)
     attended = out.reshape(n_x, rows, n_z, channels).transpose(1, 2, 0, 3).reshape(rows, -1)
     return (handed[None], attended[None])
 

time: 197 us -> 224 us (1.14)
  waiting for transfers between devices: 70.7 us -> 116 us
  blocking collectives: 36 us -> 0 us
  starting transfers between devices: 41 us -> 52.8 us
  local copies, waits for them, and re-layouts: 12.8 us -> 15.8 us
  other arithmetic: 10.1 us -> 12.5 us
    all_to_all x1 -> x0, blocking collectives: 36 us -> none  [body(): lax.all_to_all(jnp.concatenate([heads_out.reshape(n_seq, eighth, HD), lon...]
    all_gather x1 -> x2, waiting for transfers between devices: 0.02 us -> 29.9 us  [the longest x1 29.9 us: body(): late = lax.all_gather(late.reshape(-1, wide), 'z')]
    all_to_all x2 -> x3, waiting for transfers between devices: 19 us -> 30.4 us  [the longest x1 27.9 us: body(): lax.all_to_all(jnp.concatenate([heads_out.reshape(n_seq, eighth, HD), lon...]
    all_to_all x2 -> x3, starting transfers between devices: 9.07 us -> 20.1 us  [the longest x1 8.37 us: body(): lax.all_to_all(jnp.concatenate([heads_out.reshape(n_seq, eighth, HD), lon...]
    ppermute x1, waiting for transfers between devices: 0.01 us -> 7.28 us  [body(): lax.ppermute(hyena, 'section', [(i, (i + 1) % n_sec) for i in range(n_sec)])]
    slice x2 -> x4, local copies, waits for them, and re-layouts: 0.04 us -> 3.23 us  [the longest x2 2.56 us: body(): part = weight[:, at].reshape(n_z * channels, wide)]
    dot_general x11 -> x14, matrix products: 11.2 us -> 11.4 us  [dot(): lax.dot_general(left, right, (contract, ((), ())), precision=precision, p...]
    unnamed x54 -> x56, local copies, waits for them, and re-layouts: 6.17 us -> 6.31 us
  transfers between devices with their start and end apart: 8 -> 10, of which waited for: 5 -> 7; matrix products, arithmetic and copies ran while one was open for 15% -> 14% of each run, Pallas kernels for 0% -> 0%
where the time goes in v2:
time: 224 us
  waiting for transfers between devices  116 us (52%)
  starting transfers between devices  52.8 us (24%)
  local copies, waits for them, and re-layouts  15.8 us (7%)
  between operations  14.7 us (7%)
  other arithmetic  12.5 us (6%)
  matrix products  11.4 us (5%)
    all_to_all x1, waiting for transfers between devices, body(): lax.all_to_all(jnp.concatenate([attn_in, product], axis=1), ('z', 'xh'),...  33.2 us
    all_gather x1, waiting for transfers between devices, body(): late = lax.all_gather(late.reshape(-1, wide), 'z')  29.9 us
    all_to_all x1, waiting for transfers between devices, body(): lax.all_to_all(jnp.concatenate([heads_out.reshape(n_seq, eighth, HD), lon...  27.9 us
    all_to_all x1, starting transfers between devices, body(): lax.all_to_all(jnp.concatenate([attn_in, product], axis=1), ('z', 'xh'),...  16.8 us
    dot_general x14, matrix products, dot(): lax.dot_general(left, right, (contract, ((), ())), precision=precision, p...  11.4 us
    all_to_all x1, waiting for transfers between devices, body(): lax.all_to_all(jnp.broadcast_to(own[None, 1:], (n_plane, 2, n_seq, eighth...  11.1 us
    all_to_all x1, starting transfers between devices, body(): lax.all_to_all(jnp.concatenate([heads_out.reshape(n_seq, eighth, HD), lon...  8.37 us
    ppermute x1, waiting for transfers between devices, body(): lax.ppermute(hyena, 'section', [(i, (i + 1) % n_sec) for i in range(n_sec)])  7.28 us
  transfers between devices with their start and end apart: 10, of which 7 were waited for; matrix products, arithmetic and copies ran while one was open for 14% of the time, Pallas kernels for 0%

profile of v2, /device:TPU:2, one launch (start us, length us, event | category | flops | bytes accessed | tf_op | source)
XLA Modules:
  0.0 223.5 jit_solution(8578151601505947936)
XLA Ops:
  7.2 0.8 pad_maximum_fusion.5
  8.0 4.2 %collective-permute-start = (bf16[3,2,1024]{2,1,0:T(2,128)(2,1)S(1)}, bf16[3,2,1024]{2,1,0:T(2,128)(2,1)S(1)}, u32[]{:S(2)}, u32[]{:S(2)}) collective-permute-start(bf16[3,2,1024]{2,1,0:T(2,128)(2,1)S(1)} %pad_maximum_fusion.5), channel_id=1, source_target_pairs={{0,4},{4,8},{8,12},{12,16},{16,20},{20,24},{24,28},{28,32},{32,36}... | collective-permute-start | bytes 36872 | tf_op jit(solution)/shard_map/ppermute | solution.py:99
  12.2 1.8 pad_maximum_fusion.3
  14.0 4.5 %all-to-all-start = ((bf16[4,96,512]{2,1,0:T(8,128)(2,1)}), bf16[4,96,512]{2,1,0:T(8,128)(2,1)S(1)}, u32[]{:S(2)}, u32[]{:S(2)}) async-start(bf16[4,96,512]{2,1,0:T(8,128)(2,1)} %pad_maximum_fusion.3), calls=%async_computation | async-start | bytes 786432 | tf_op jit(solution)/shard_map/all_to_all | solution.py:114
  20.3 1.5 fusion.30
  21.8 4.4 %all-to-all-done = bf16[4,96,512]{2,1,0:T(8,128)(2,1)S(1)} async-done(((bf16[4,96,512]{2,1,0:T(8,128)(2,1)}), bf16[4,96,512]{2,1,0:T(8,128)(2,1)S(1)}, u32[]{:S(2)}, u32[]{:S(2)}) %all-to-all-start) | async-done | bytes 393248 | tf_op jit(solution)/shard_map/all_to_all | solution.py:114
  26.5 0.9 pad_maximum_fusion.2
  27.3 16.8 %all-to-all-start.1 = ((bf16[32,80,128]{2,1,0:T(8,128)(2,1)}), bf16[32,80,128]{2,1,0:T(8,128)(2,1)S(1)}, u32[]{:S(2)}, u32[]{:S(2)}) async-start(bf16[32,80,128]{2,1,0:T(8,128)(2,1)} %pad_maximum_fusion.2), calls=%async_computation.1 | async-start | bytes 1310720 | tf_op jit(solution)/shard_map/all_to_all | solution.py:123
  47.9 1.5 fusion.26
  49.4 33.2 %all-to-all-done.1 = bf16[32,80,128]{2,1,0:T(8,128)(2,1)S(1)} async-done(((bf16[32,80,128]{2,1,0:T(8,128)(2,1)}), bf16[32,80,128]{2,1,0:T(8,128)(2,1)S(1)}, u32[]{:S(2)}, u32[]{:S(2)}) %all-to-all-start.1) | async-done | bytes 655392 | tf_op jit(solution)/shard_map/all_to_all | solution.py:123
  84.0 1.8 broadcast_in_dim.12
  85.8 5.1 %all-to-all-start.2 = ((bf16[8,2,32,16,128]{4,3,2,1,0:T(8,128)(2,1)}), bf16[8,2,32,16,128]{4,3,2,1,0:T(8,128)(2,1)S(1)}, u32[]{:S(2)}, u32[]{:S(2)}) async-start(bf16[8,2,32,16,128]{4,3,2,1,0:T(8,128)(2,1)} %broadcast_in_dim.12), calls=%async_computation.2 | async-start | bytes 4194304 | tf_op jit(solution)/shard_map/all_to_all | solution.py:133
  91.2 1.3 fusion.42
  92.5 1.3 fusion.40
  94.1 0.8 copy-done.1
  101.1 11.1 %all-to-all-done.2 = bf16[8,2,32,16,128]{4,3,2,1,0:T(8,128)(2,1)S(1)} async-done(((bf16[8,2,32,16,128]{4,3,2,1,0:T(8,128)(2,1)}), bf16[8,2,32,16,128]{4,3,2,1,0:T(8,128)(2,1)S(1)}, u32[]{:S(2)}, u32[]{:S(2)}) %all-to-all-start.2) | async-done | bytes 2097184 | tf_op jit(solution)/shard_map/all_to_all | solution.py:133
  112.6 1.6 fusion.93
  114.2 1.3 fusion
  115.5 1.3 fusion.8
  117.6 8.4 %all-to-all-start.3 = ((bf16[32,48,128]{2,1,0:T(8,128)(2,1)}), bf16[32,48,128]{2,1,0:T(8,128)(2,1)S(1)}, u32[]{:S(2)}, u32[]{:S(2)}) async-start(bf16[32,48,128]{2,1,0:T(8,128)(2,1)} %pad_maximum_fusion.4), calls=%async_computation.3 | async-start | bytes 786432 | tf_op jit(solution)/shard_map/all_to_all | solution.py:166
  126.0 1.3 fusion.88
  127.3 27.9 %all-to-all-done.3 = bf16[32,48,128]{2,1,0:T(8,128)(2,1)S(1)} async-done(((bf16[32,48,128]{2,1,0:T(8,128)(2,1)}), bf16[32,48,128]{2,1,0:T(8,128)(2,1)S(1)}, u32[]{:S(2)}, u32[]{:S(2)}) %all-to-all-start.3) | async-done | bytes 393248 | tf_op jit(solution)/shard_map/all_to_all | solution.py:166
  156.1 5.4 %all-to-all-start.4 = ((bf16[8,32,512]{2,1,0:T(8,128)(2,1)}), bf16[8,32,512]{2,1,0:T(8,128)(2,1)S(1)}, u32[]{:S(2)}, u32[]{:S(2)}) async-start(bf16[8,32,512]{2,1,0:T(8,128)(2,1)} %bitcast.43), calls=%async_computation.4 | async-start | bytes 524288 | tf_op jit(solution)/shard_map/all_to_all | solution.py:176
  161.5 29.9 %all-gather.5.cloned.1.call-done = bf16[16,64,512]{2,1,0:T(8,128)(2,1)} async-done(((bf16[1,64,512]{2,1,0:T(8,128)(2,1)}), bf16[16,64,512]{2,1,0:T(8,128)(2,1)}) %all-gather.5.cloned.1.call-update) | async-done | bytes 1048592 | tf_op jit(solution)/shard_map/all_gather | solution.py:125
  191.5 1.3 fusion.89
  194.1 1.1 pad_maximum_fusion.1
  195.2 6.3 %all-to-all-start.5 = ((bf16[8,128,512]{2,1,0:T(8,128)(2,1)}), bf16[8,128,512]{2,1,0:T(8,128)(2,1)S(1)}, u32[]{:S(2)}, u32[]{:S(2)}) async-start(bf16[8,128,512]{2,1,0:T(8,128)(2,1)} %bitcast.62), calls=%async_computation.5 | async-start | bytes 2097152 | tf_op jit(solution)/shard_map/all_to_all | solution.py:194
  203.0 1.9 collective-permute-start.1
  204.9 7.3 %collective-permute-done.1 = bf16[128,1024]{0,1:T(8,128)(2,1)S(1)} collective-permute-done((bf16[128,1024]{0,1:T(8,128)(2,1)S(1)}, bf16[128,1024]{0,1:T(8,128)(2,1)S(1)}, u32[]{:S(2)}, u32[]{:S(2)}) %collective-permute-start.1) | collective-permute-done | bytes 262176 | tf_op jit(solution)/shard_map/ppermute | solution.py:184
  212.2 0.8 copy.122
  213.0 2.5 %all-to-all-done.5 = bf16[8,128,512]{2,1,0:T(8,128)(2,1)S(1)} async-done(((bf16[8,128,512]{2,1,0:T(8,128)(2,1)}), bf16[8,128,512]{2,1,0:T(8,128)(2,1)S(1)}, u32[]{:S(2)}, u32[]{:S(2)}) %all-to-all-start.5) | async-done | bytes 1048608 | tf_op jit(solution)/shard_map/all_to_all | solution.py:194
  215.8 0.9 copy.123
  (101 shorter events, 18.6 us)
Async XLA Ops:
  7.2 38.2 %copy-start = (f32[1,1024]{1,0:T(1,128)S(1)}, f32[1,1024]{1,0:T(1,128)}, u32[]{:S(2)}) copy-start(f32[1,1024]{1,0:T(1,128)} %param.28) | copy-start | bytes 12292
  7.2 11.3 %copy-start.3 = (bf16[1,128,1024]{2,1,0:T(8,128)(2,1)S(1)}, bf16[1,128,1024]{2,1,0:T(8,128)(2,1)}, u32[]{:S(2)}) copy-start(bf16[1,128,1024]{2,1,0:T(8,128)(2,1)} %param.23) | copy-start | bytes 786436
  7.2 11.3 %copy-start.12 = (f32[1,3,3,1024]{3,0,2,1:T(1,128)S(1)}, f32[1,3,3,1024]{3,0,2,1:T(1,128)}, u32[]{:S(2)}) copy-start(f32[1,3,3,1024]{3,0,2,1:T(1,128)} %param.26) | copy-start | bytes 110596
  8.0 10.6 %copy-start.4 = (bf16[1,128,1024]{2,1,0:T(8,128)(2,1)S(1)}, bf16[1,128,1024]{2,1,0:T(8,128)(2,1)}, u32[]{:S(2)}) copy-start(bf16[1,128,1024]{2,1,0:T(8,128)(2,1)} %param.25) | copy-start | bytes 786436
  8.0 10.8 %collective-permute-start = (bf16[3,2,1024]{2,1,0:T(2,128)(2,1)S(1)}, bf16[3,2,1024]{2,1,0:T(2,128)(2,1)S(1)}, u32[]{:S(2)}, u32[]{:S(2)}) collective-permute-start(bf16[3,2,1024]{2,1,0:T(2,128)(2,1)S(1)} %pad_maximum_fusion.5), channel_id=1, source_target_pairs={{0,4},{4,8},{8,12},{12,16},{16,20},{20,24},{24,28},{28,32},{32,36}... | collective-permute-start | bytes 36872 | tf_op jit(solution)/shard_map/ppermute | solution.py:99
  14.0 12.3 %all-to-all-start = ((bf16[4,96,512]{2,1,0:T(8,128)(2,1)}), bf16[4,96,512]{2,1,0:T(8,128)(2,1)S(1)}, u32[]{:S(2)}, u32[]{:S(2)}) async-start(bf16[4,96,512]{2,1,0:T(8,128)(2,1)} %pad_maximum_fusion.3), calls=%async_computation | async-start | bytes 786432 | tf_op jit(solution)/shard_map/all_to_all | solution.py:114
  26.4 17.7 %copy-start.8 = (bf16[1,512,4,32]{1,3,2,0:T(8,128)(2,1)S(1)}, bf16[1,512,4,32]{1,3,2,0:T(8,128)(2,1)}, u32[]{:S(2)}) copy-start(bf16[1,512,4,32]{1,3,2,0:T(8,128)(2,1)} %param.32) | copy-start | bytes 393220
  26.4 18.4 %copy-start.6 = (f32[1,1,1,32,4096]{4,3,2,1,0:T(8,128)S(1)}, f32[1,1,1,32,4096]{4,3,2,1,0:T(8,128)}, u32[]{:S(2)}) copy-start(f32[1,1,1,32,4096]{4,3,2,1,0:T(8,128)} %param.27) | copy-start | bytes 1572868
  27.3 55.2 %all-to-all-start.1 = ((bf16[32,80,128]{2,1,0:T(8,128)(2,1)}), bf16[32,80,128]{2,1,0:T(8,128)(2,1)S(1)}, u32[]{:S(2)}, u32[]{:S(2)}) async-start(bf16[32,80,128]{2,1,0:T(8,128)(2,1)} %pad_maximum_fusion.2), calls=%async_computation.1 | async-start | bytes 1310720 | tf_op jit(solution)/shard_map/all_to_all | solution.py:123
  44.1 81.9 %all-gather.3.cloned.1.call-start = ((), (), s32[]{:S(2)}) async-start(), calls=%async_computation.6 | async-start | bytes 1114112 | tf_op jit(solution)/shard_map/all_gather | solution.py:105
  44.8 2.3 %copy-start.17 = (f32[33,32,1]{0,1,2:T(8,128)S(1)}, f32[33,32,1]{0,1,2:T(8,128)}, u32[]{:S(2)}) copy-start(f32[33,32,1]{0,1,2:T(8,128)} %constant.161) | copy-start | bytes 12676
  45.0 2.9 %copy-start.16 = (f32[33,32,1]{0,1,2:T(8,128)S(1)}, f32[33,32,1]{0,1,2:T(8,128)}, u32[]{:S(2)}) copy-start(f32[33,32,1]{0,1,2:T(8,128)} %constant.160) | copy-start | bytes 12676
  85.8 5.4 %copy-start.15 = (f32[33,32]{0,1:T(8,128)S(1)}, f32[33,32]{0,1:T(8,128)}, u32[]{:S(2)}) copy-start(f32[33,32]{0,1:T(8,128)} %constant.140.clone) | copy-start | bytes 12676
  85.8 6.7 %copy-start.14 = (f32[33,32]{0,1:T(8,128)S(1)}, f32[33,32]{0,1:T(8,128)}, u32[]{:S(2)}) copy-start(f32[33,32]{0,1:T(8,128)} %constant.141.clone) | copy-start | bytes 12676
  85.8 26.4 %all-to-all-start.2 = ((bf16[8,2,32,16,128]{4,3,2,1,0:T(8,128)(2,1)}), bf16[8,2,32,16,128]{4,3,2,1,0:T(8,128)(2,1)S(1)}, u32[]{:S(2)}, u32[]{:S(2)}) async-start(bf16[8,2,32,16,128]{4,3,2,1,0:T(8,128)(2,1)} %broadcast_in_dim.12), calls=%async_computation.2 | async-start | bytes 4194304 | tf_op jit(solution)/shard_map/all_to_all | solution.py:133
  90.9 100.5 %all-gather.5.cloned.1.call-start = ((), (), s32[]{:S(2)}) async-start(), calls=%async_computation.7 | async-start | bytes 1114112 | tf_op jit(solution)/shard_map/all_gather | solution.py:125
  93.9 1.1 copy-start.1
  93.9 1.1 copy-start.10
  93.9 1.1 copy-start.11
  95.0 1.0 copy-start.2
  97.1 1.0 copy-start.7
  99.0 0.7 copy-start.13
  101.1 11.5 %copy-start.9 = (bf16[1,32,16,128]{3,2,0,1:T(8,128)(2,1)S(1)}, bf16[1,32,16,128]{3,2,0,1:T(8,128)(2,1)}, u32[]{:S(2)}) copy-start(bf16[1,32,16,128]{3,2,0,1:T(8,128)(2,1)} %slice.205) | copy-start | bytes 393220
  101.1 11.5 %copy-start.19 = (s32[4096]{0:T(1024)S(1)}, s32[4096]{0:T(1024)}, u32[]{:S(2)}) copy-start(s32[4096]{0:T(1024)} %fusion.55) | copy-start | bytes 49156
  101.1 11.5 %copy-start.20 = (s32[512]{0:T(512)S(1)}, s32[512]{0:T(512)}, u32[]{:S(2)}) copy-start(s32[512]{0:T(512)} %fusion.80) | copy-start | bytes 6148
  117.6 37.6 %all-to-all-start.3 = ((bf16[32,48,128]{2,1,0:T(8,128)(2,1)}), bf16[32,48,128]{2,1,0:T(8,128)(2,1)S(1)}, u32[]{:S(2)}, u32[]{:S(2)}) async-start(bf16[32,48,128]{2,1,0:T(8,128)(2,1)} %pad_maximum_fusion.4), calls=%async_computation.3 | async-start | bytes 786432 | tf_op jit(solution)/shard_map/all_to_all | solution.py:166
  156.1 36.6 %all-to-all-start.4 = ((bf16[8,32,512]{2,1,0:T(8,128)(2,1)}), bf16[8,32,512]{2,1,0:T(8,128)(2,1)S(1)}, u32[]{:S(2)}, u32[]{:S(2)}) async-start(bf16[8,32,512]{2,1,0:T(8,128)(2,1)} %bitcast.43), calls=%async_computation.4 | async-start | bytes 524288 | tf_op jit(solution)/shard_map/all_to_all | solution.py:176
  195.2 6.3 %copy-start.5 = (bf16[1,128,1024]{2,1,0:T(8,128)(2,1)S(1)}, bf16[1,128,1024]{2,1,0:T(8,128)(2,1)}, u32[]{:S(2)}) copy-start(bf16[1,128,1024]{2,1,0:T(8,128)(2,1)} %param.24) | copy-start | bytes 786436
  195.2 6.5 %copy-start.18 = (bf16[1,2,1024]{2,1,0:T(2,128)(2,1)S(1)}, bf16[1,2,1024]{2,1,0:T(2,128)(2,1)}, u32[]{:S(2)}) copy-start(bf16[1,2,1024]{2,1,0:T(2,128)(2,1)} %get-tuple-element.42) | copy-start | bytes 12292
  195.2 20.2 %all-to-all-start.5 = ((bf16[8,128,512]{2,1,0:T(8,128)(2,1)}), bf16[8,128,512]{2,1,0:T(8,128)(2,1)S(1)}, u32[]{:S(2)}, u32[]{:S(2)}) async-start(bf16[8,128,512]{2,1,0:T(8,128)(2,1)} %bitcast.62), calls=%async_computation.5 | async-start | bytes 2097152 | tf_op jit(solution)/shard_map/all_to_all | solution.py:194
  203.0 9.2 %collective-permute-start.1 = (bf16[128,1024]{0,1:T(8,128)(2,1)S(1)}, bf16[128,1024]{0,1:T(8,128)(2,1)S(1)}, u32[]{:S(2)}, u32[]{:S(2)}) collective-permute-start(bf16[128,1024]{0,1:T(8,128)(2,1)S(1)} %fusion.36), channel_id=1, source_target_pairs={{0,128},{128,256},{256,384},{384,0},{1,129},{129,257},{257,385},{3... | collective-permute-start | bytes 786440 | tf_op jit(solution)/shard_map/ppermute | solution.py:184
Sparse Core Ops, SparseCore 0:
  47.0 72.5 all-gather.2
  121.7 69.7 all-gather.4

commit v3 on v1

v3 whole, which is shorter than its diff:
```python
import math

import jax
import jax.numpy as jnp
import numpy as np
from jax import lax
from jax.sharding import Mesh, PartitionSpec as P

HD = 128
BF16 = jnp.bfloat16
F32 = jnp.float32
HIGH = lax.Precision.HIGH


def dot(left, right, contract, precision=None):
    return lax.dot_general(
        left, right, (contract, ((), ())), precision=precision, preferred_element_type=F32
    )


def transform_tables(depth, breadth):
    full = 2 * depth
    half = depth + 1
    k = np.arange(half)
    a = np.arange(depth)
    b = np.arange(breadth)
    one = -2.0 * np.pi * np.outer(k, a) / full
    first = np.stack([np.cos(one), np.sin(one)])
    mid = -2.0 * np.pi * np.outer(k, b) / (full * breadth)
    two = -2.0 * np.pi * (np.outer(b, b) % breadth) / breadth
    cos_two, sin_two = np.cos(two), np.sin(two)
    forward = np.block([[cos_two, sin_two], [-sin_two, cos_two]])
    backward = np.block([[cos_two, -sin_two], [sin_two, cos_two]])
    weight = np.where((k == 0) | (k == depth), 1.0, 2.0) / (full * breadth)
    last = np.concatenate([np.cos(one).T * weight, np.sin(one).T * weight], axis=1)
    as32 = lambda x: np.asarray(x, np.float32)
    return as32(first), as32(np.cos(mid)), as32(np.sin(mid)), as32(forward), as32(backward), as32(last)


def forward_transform(blocks, tables):
    first, cos_mid, sin_mid, forward, _, _ = tables
    depth, channels, breadth = blocks.shape
    flat = blocks.reshape(depth, channels * breadth)
    real = dot(first[0], flat, ((1,), (0,)), HIGH).reshape(-1, channels, breadth)
    imag = dot(first[1], flat, ((1,), (0,)), HIGH).reshape(-1, channels, breadth)
    cos_mid, sin_mid = cos_mid[:, None], sin_mid[:, None]
    turned = jnp.concatenate(
        [real * cos_mid - imag * sin_mid, real * sin_mid + imag * cos_mid], axis=2
    )
    return dot(turned, forward, ((2,), (0,)), HIGH)


def inverse_transform(spectrum, tables):
    _, cos_mid, sin_mid, _, backward, last = tables
    half, channels, twice = spectrum.shape
    breadth = twice // 2
    mid = dot(spectrum, backward, ((2,), (0,)), HIGH)
    real, imag = mid[:, :, :breadth], mid[:, :, breadth:]
    cos_mid, sin_mid = cos_mid[:, None], sin_mid[:, None]
    turned = jnp.concatenate(
        [real * cos_mid + imag * sin_mid, imag * cos_mid - real * sin_mid], axis=0
    )
    out = dot(last, turned.reshape(2 * half, channels * breadth), ((1,), (0,)), HIGH)
    return out.reshape(-1, channels, breadth)


def short_by_token(stream, before, taps):
    rows = stream.shape[0]
    whole = jnp.concatenate([before, stream], axis=0).astype(F32)
    return taps[0] * whole[2:] + taps[1] * whole[1 : rows + 1] + taps[2] * whole[:rows]


def edge_short(edges, taps):
    edges = edges.astype(F32)
    before = jnp.pad(edges[:-1, 2:], ((1, 0), (0, 0), (0, 0)))
    zero = taps[0] * edges[:, 0] + taps[1] * before[:, 1] + taps[2] * before[:, 0]
    one = taps[0] * edges[:, 1] + taps[1] * edges[:, 0] + taps[2] * before[:, 1]
    return zero, one


def part_of_attention(query, keys, values, q_pos, k_pos):
    scores = dot(query, keys, ((1,), (1,))) * (1.0 / math.sqrt(HD))
    allowed = k_pos <= q_pos
    masked = jnp.where(allowed, scores, -1e30)
    highest = jnp.max(masked, axis=1, keepdims=True)
    probs = jnp.where(allowed, jnp.exp(masked - highest), 0.0)
    totals = jnp.sum(probs, axis=1, keepdims=True)
    out = dot(probs.astype(BF16), values, ((1,), (0,))) / jnp.maximum(totals, 1e-30)
    return out, jnp.where(totals > 0.0, highest + jnp.log(jnp.maximum(totals, 1e-30)), -1e30)


def in_three(x):
    first = x.astype(BF16)
    rest = x - first.astype(F32)
    second = rest.astype(BF16)
    return [first, second, (rest - second.astype(F32)).astype(BF16)]


def body(
    first_stream,
    gate_stream,
    value_stream,
    short_taps,
    long_filter,
    skip_gain,
    queries,
    attn_keys,
    attn_values,
    out_weight,
):
    seq = ("zi", "zp", "zq", "xh")
    n_seq, n_x, n_tp = lax.axis_size(seq), lax.axis_size("xh"), lax.axis_size("tp")
    n_pair = lax.axis_size("zq") * n_x
    n_z = n_seq // n_x
    n_plane = n_x * n_tp
    seq_at = lax.axis_index(seq)
    half_at = lax.axis_index("zp")
    pair_at = lax.axis_index(("zq", "xh"))
    rows = queries.shape[1]
    wide = queries.shape[2]
    channels = long_filter.shape[3]
    heads = wide // HD
    chunks = n_seq // heads
    few = rows // chunks
    own_rows = n_seq * few
    taps = short_taps[0]

    weight = out_weight[0].transpose(1, 2, 0).reshape(-1, wide)
    weight = lax.all_gather(weight, ("zi", "zp", "zq"))

    nothing = jnp.zeros_like(first_stream[0, :2])
    first_short = short_by_token(first_stream[0], nothing, taps[0])
    value_short = short_by_token(value_stream[0], nothing, taps[2])
    product = (first_short * value_short).astype(BF16)
    product = product.T.reshape(n_seq, channels, rows)
    edges = jnp.concatenate(
        [x[0, at : at + 2] for x in (first_stream, value_stream) for at in (0, rows - 2)]
    )
    edges = edges.reshape(8, n_seq, channels).transpose(1, 0, 2).reshape(n_seq, -1, rows)
    attn_in = jnp.stack([queries[0], attn_keys[0], attn_values[0]])
    attn_in = attn_in.reshape(3, chunks, few, heads, HD).transpose(3, 1, 0, 2, 4)
    attn_in = attn_in.reshape(n_seq, 3 * few, HD)
    mixed = lax.all_to_all(jnp.concatenate([attn_in, product, edges], axis=1), seq, 0, 0)

    tail = lax.ppermute(gate_stream[0, -2:], seq, [(i, i + 1) for i in range(n_seq - 1)])
    tables = transform_tables(n_seq, rows)
    kernel = long_filter[0, 0, 0].reshape(channels, n_seq, rows).transpose(1, 0, 2)
    kernel_spec = forward_transform(kernel, tables)

    own = mixed[:, : 3 * few].reshape(n_seq, 3, few, HD).transpose(1, 0, 2, 3)
    query = own[0].reshape(own_rows, HD)
    swap = [(0, 1), (1, 0)]
    other_query = lax.ppermute(query, "zp", swap)
    pairs = lax.all_to_all(
        jnp.broadcast_to(own[None, 1:], (n_pair, 2, n_seq, few, HD)), ("zq", "xh"), 0, 0
    )

    local_taps = lax.dynamic_slice_in_dim(taps, seq_at * channels, channels, 2)
    edges = mixed[:, 3 * few + channels :].reshape(n_seq, 8, channels)
    first_zero, first_one = edge_short(edges[:, :4], local_taps[0])
    value_zero, value_one = edge_short(edges[:, 4:], local_taps[2])
    token = lax.broadcasted_iota(jnp.int32, (1, 1, rows), 2)
    product = mixed[:, 3 * few : 3 * few + channels]
    product = jnp.where(token == 0, (first_zero * value_zero).astype(BF16)[:, :, None], product)
    product = jnp.where(token == 1, (first_one * value_one).astype(BF16)[:, :, None], product)
    product = product.astype(F32)
    spec = forward_transform(product, tables)
    real, imag = spec[:, :, :rows], spec[:, :, rows:]
    kernel_real, kernel_imag = kernel_spec[:, :, :rows], kernel_spec[:, :, rows:]
    joined = jnp.concatenate(
        [real * kernel_real - imag * kernel_imag, real * kernel_imag + imag * kernel_real], axis=2
    )
    convolved = inverse_transform(joined, tables)
    gain = lax.dynamic_slice_in_dim(skip_gain[0], seq_at * channels, channels, 0)
    long_out = (convolved + gain[None, :, None] * product).astype(BF16)

    keys = pairs[:, 0].reshape(-1, HD)
    values = pairs[:, 1].reshape(-1, HD)
    q_ids = lax.broadcasted_iota(jnp.int32, (own_rows, 1), 0)
    q_base = q_ids // few * rows + q_ids % few + pair_at * few
    k_ids = lax.broadcasted_iota(jnp.int32, (1, n_pair * own_rows), 1)
    k_in = k_ids % own_rows
    k_pos = k_in // few * rows + k_in % few + (half_at * n_pair + k_ids // own_rows) * few
    other_out, other_log = part_of_attention(
        other_query, keys, values, q_base + (1 - half_at) * (n_pair * few), k_pos
    )
    sent = jnp.concatenate(
        [other_out.astype(BF16), jnp.concatenate(in_three(other_log.reshape(-1, HD)))]
    )
    got = lax.ppermute(sent, "zp", swap)
    own_out, own_log = part_of_attention(
        query, keys, values, q_base + half_at * (n_pair * few), k_pos
    )
    got_log = got[own_rows:].astype(F32).reshape(3, -1, HD)
    got_log = (got_log[0] + got_log[1] + got_log[2]).reshape(own_rows, 1)
    highest = jnp.maximum(own_log, got_log)
    own_share, got_share = jnp.exp(own_log - highest), jnp.exp(got_log - highest)
    heads_out = own_out * own_share + got[:own_rows].astype(F32) * got_share
    heads_out = (heads_out / (own_share + got_share)).astype(BF16)

    back = lax.all_to_all(
        jnp.concatenate([heads_out.reshape(n_seq, few, HD), long_out], axis=1), seq, 0, 0
    )
    natural = back[:, :few].reshape(heads, chunks, few, HD).transpose(1, 2, 0, 3)
    plane_rows = lax.all_to_all(
        jnp.broadcast_to(natural.reshape(1, rows, wide), (n_x, rows, wide)), "xh", 0, 0
    ).reshape(n_x * rows, wide)

    gate_short = short_by_token(gate_stream[0], tail, taps[1])
    long_rows = back[:, few:].reshape(n_seq * channels, rows).T
    hyena = (gate_short * long_rows.astype(F32)).astype(BF16)
    plane_rows, hyena = lax.optimization_barrier((plane_rows, hyena))
    n_sec = lax.axis_size("section")
    handed = lax.ppermute(hyena, "section", [(i, (i + 1) % n_sec) for i in range(n_sec)])

    partials = []
    weight = weight.reshape(n_z, n_tp, channels, wide)
    for at in range(n_tp):
        part = weight[:, at].reshape(n_z * channels, wide)
        part = dot(plane_rows, part, ((1,), (1,))).astype(BF16)
        partials.append(part.reshape(n_x, rows, n_z * channels))
    partials = jnp.stack(partials, axis=1).reshape(n_plane, rows, n_z * channels)
    partials = lax.all_to_all(partials, ("xh", "tp"), 0, 0)
    out = jnp.sum(partials.reshape(n_x, n_tp, rows, n_z * channels).astype(F32), axis=1).astype(BF16)
    attended = out.reshape(n_x, rows, n_z, channels).transpose(1, 2, 0, 3).reshape(rows, -1)
    return (handed[None], attended[None])


def solution(mesh):
    n_sec, n_seq, n_tp = (mesh.shape[name] for name in ("section", "seq", "tp"))
    finer = Mesh(
        mesh.devices.reshape(n_sec, n_seq // 8, 2, 2, 2, n_tp),
        ("section", "zi", "zp", "zq", "xh", "tp"),
    )
    seq = ("zi", "zp", "zq", "xh")
    placed = (
        P("section", seq, "tp"),
        P("section", seq, "tp"),
        P("section", seq, "tp"),
        P("section", None, None, "tp"),
        P("section", "tp", seq, None, None),
        P("section", "tp"),
        P("section", seq, "tp"),
        P("section", seq, "tp"),
        P("section", seq, "tp"),
        P("section", "tp", None, seq),
    )
    return jax.shard_map(
        body,
        mesh=finer,
        in_specs=placed,
        out_specs=(P("section", seq, "tp"), P("section", seq, "tp")),
        check_vma=False,
    )
```

time: 197 us -> 205 us (1.041)
  the two profiles are of different devices: /device:TPU:2 before, /device:TPU:64 now
where the time goes in v3:
time: 205 us; the launch traced here: 204 us
  waiting for transfers between devices  84.4 us (41%)
  starting transfers between devices  59.6 us (29%)
  local copies, waits for them, and re-layouts  18.2 us (9%)
  between operations  14.8 us (7%)
  matrix products  13.9 us (7%)
  other arithmetic  13 us (6%)
    all_to_all x1, waiting for transfers between devices, body(): lax.all_to_all(jnp.concatenate([attn_in, product, edges], axis=1), seq, 0...  35.2 us
    ppermute x1, waiting for transfers between devices, body(): lax.ppermute(gate_stream[0, -2:], seq, [(i, i + 1) for i in range(n_seq -...  19.8 us
    all_to_all x1, starting transfers between devices, body(): lax.all_to_all(jnp.concatenate([attn_in, product, edges], axis=1), seq, 0...  17.4 us
    dot_general x16, matrix products, dot(): lax.dot_general(left, right, (contract, ((), ())), precision=precision, p...  13.9 us
    all_to_all x1, starting transfers between devices, body(): lax.all_to_all(jnp.concatenate([heads_out.reshape(n_seq, few, HD), long_o...  11.5 us
    ppermute x1, waiting for transfers between devices, body(): lax.ppermute(hyena, 'section', [(i, (i + 1) % n_sec) for i in range(n_sec)])  11.2 us
    ppermute x1, starting transfers between devices, body(): got = lax.ppermute(sent, 'zp', swap)  5.49 us
    unnamed x48, local copies, waits for them, and re-layouts  5.47 us
  transfers between devices with their start and end apart: 10, of which 8 were waited for; matrix products, arithmetic and copies ran while one was open for 15% of the time, Pallas kernels for 0%

profile of v3, /device:TPU:64, one launch (start us, length us, event | category | flops | bytes accessed | tf_op | source)
XLA Modules:
  0.0 203.9 jit_solution(5431008008249491061)
XLA Ops:
  7.9 1.1 copy.125
  9.8 1.1 copy.124
  11.6 1.4 fusion.127
  14.6 1.5 fusion.39
  17.1 17.4 %all-to-all-start = ((bf16[32,82,128]{2,1,0:T(8,128)(2,1)}), bf16[32,82,128]{2,1,0:T(8,128)(2,1)S(1)}, u32[]{:S(2)}, u32[]{:S(2)}) async-start(bf16[32,82,128]{2,1,0:T(8,128)(2,1)} %pad_maximum_fusion.2), calls=%async_computation | async-start | bytes 1441792 | tf_op jit(solution)/shard_map/all_to_all | solution.py:143
  36.8 1.4 fusion.103
  40.2 35.2 %all-to-all-done = bf16[32,82,128]{2,1,0:T(8,128)(2,1)S(1)} async-done(((bf16[32,82,128]{2,1,0:T(8,128)(2,1)}), bf16[32,82,128]{2,1,0:T(8,128)(2,1)S(1)}, u32[]{:S(2)}, u32[]{:S(2)}) %all-to-all-start) | async-done | bytes 671776 | tf_op jit(solution)/shard_map/all_to_all | solution.py:143
  75.6 1.1 broadcast_in_dim.64
  76.8 5.4 %all-to-all-start.1 = ((bf16[4,2,32,16,128]{4,3,2,1,0:T(8,128)(2,1)}), bf16[4,2,32,16,128]{4,3,2,1,0:T(8,128)(2,1)S(1)}, u32[]{:S(2)}, u32[]{:S(2)}) async-start(bf16[4,2,32,16,128]{4,3,2,1,0:T(8,128)(2,1)} %broadcast_in_dim.64), calls=%async_computation.1 | async-start | bytes 2097152 | tf_op jit(solution)/shard_map/all_to_all | solution.py:154
  85.8 1.1 fusion.47
  91.1 4.5 %collective-permute-start = (bf16[512,128]{1,0:T(8,128)(2,1)}, bf16[512,128]{1,0:T(8,128)(2,1)S(1)}, u32[]{:S(2)}, u32[]{:S(2)}) collective-permute-start(bf16[512,128]{1,0:T(8,128)(2,1)} %bitcast.15), channel_id=1, source_target_pairs={{0,16},{16,0},{1,17},{17,1},{2,18},{18,2},{3,19},{19,3},{4,20},{20... | collective-permute-start | bytes 393224 | tf_op jit(solution)/shard_map/ppermute | solution.py:153
  95.7 5.2 %all-to-all-done.1 = bf16[4,2,32,16,128]{4,3,2,1,0:T(8,128)(2,1)S(1)} async-done(((bf16[4,2,32,16,128]{4,3,2,1,0:T(8,128)(2,1)}), bf16[4,2,32,16,128]{4,3,2,1,0:T(8,128)(2,1)S(1)}, u32[]{:S(2)}, u32[]{:S(2)}) %all-to-all-start.1) | async-done | bytes 1048608 | tf_op jit(solution)/shard_map/all_to_all | solution.py:154
  101.1 1.9 fusion
  102.9 2.0 collective-permute-done
  105.0 2.1 %fusion.2 = (f32[512]{0:T(512)S(1)}, f32[512]{0:T(512)S(1)}, f32[512,2048]{1,0:T(8,128)S(1)}) fusion(f32[512,2048]{1,0:T(8,128)S(1)} %get-tuple-element.64, f32[512]{0:T(512)S(1)} %get-tuple-element.63, s32[2048]{0:T(1024)S(1)} %fusion.74, s32[512]{0:T(512)S(1)} %copy-done.14, s32[512]{0:T(512)S(1)} %copy-done.13, ...), kind=kOutput, calls=%fused_computation.6 | convolution fusion | flops 278920192 | bytes 9062400 | tf_op jit(solution)/shard_map/dot_general | solution.py:16
  107.1 1.3 fusion.4
  108.4 1.1 divide_convert_fusion.1
  109.6 5.5 %collective-permute-start.1 = (bf16[524,128]{1,0:T(8,128)(2,1)S(1)}, bf16[524,128]{1,0:T(8,128)(2,1)S(1)}, u32[]{:S(2)}, u32[]{:S(2)}) collective-permute-start(bf16[524,128]{1,0:T(8,128)(2,1)S(1)} %pad_maximum_fusion.5), channel_id=1, source_target_pairs={{0,16},{16,0},{1,17},{17,1},{2,18},{18,2},{3,19},{19,3},{4,20},{20... | collective-permute-start | bytes 402440 | tf_op jit(solution)/shard_map/ppermute | solution.py:190
  115.4 3.2 %collective-permute-done.1 = bf16[524,128]{1,0:T(8,128)(2,1)S(1)} collective-permute-done((bf16[524,128]{1,0:T(8,128)(2,1)S(1)}, bf16[524,128]{1,0:T(8,128)(2,1)S(1)}, u32[]{:S(2)}, u32[]{:S(2)}) %collective-permute-start.1) | collective-permute-done | bytes 134176 | tf_op jit(solution)/shard_map/ppermute | solution.py:190
  118.7 1.7 divide_convert_fusion
  121.1 11.5 %all-to-all-start.2 = ((bf16[32,48,128]{2,1,0:T(8,128)(2,1)}), bf16[32,48,128]{2,1,0:T(8,128)(2,1)}, u32[]{:S(2)}, u32[]{:S(2)}) async-start(bf16[32,48,128]{2,1,0:T(8,128)(2,1)} %pad_maximum_fusion.4), calls=%async_computation.2 | async-start | bytes 786432 | tf_op jit(solution)/shard_map/all_to_all | solution.py:201
  133.0 4.9 %collective-permute-start.2 = (bf16[2,1024]{0,1:T(8,128)(2,1)S(1)}, bf16[2,1024]{0,1:T(8,128)(2,1)S(1)}, u32[]{:S(2)}, u32[]{:S(2)}) collective-permute-start(bf16[2,1024]{0,1:T(8,128)(2,1)S(1)} %slice_bitcast_fusion), channel_id=1, source_target_pairs={{0,4},{4,8},{8,12},{12,16},{16,20},{20,24},{24,28},{28,32},{32,36}... | collective-permute-start | bytes 12296 | tf_op jit(solution)/shard_map/ppermute | solution.py:145
  137.8 19.8 %collective-permute-done.2 = bf16[2,1024]{0,1:T(8,128)(2,1)S(1)} collective-permute-done((bf16[2,1024]{0,1:T(8,128)(2,1)S(1)}, bf16[2,1024]{0,1:T(8,128)(2,1)S(1)}, u32[]{:S(2)}, u32[]{:S(2)}) %collective-permute-start.2) | collective-permute-done | bytes 4128 | tf_op jit(solution)/shard_map/ppermute | solution.py:145
  157.9 1.7 fusion.122
  161.4 3.4 %all-to-all-start.3 = ((bf16[2,128,512]{2,1,0:T(8,128)(2,1)}), bf16[2,128,512]{2,1,0:T(8,128)(2,1)S(1)}, u32[]{:S(2)}, u32[]{:S(2)}) async-start(bf16[2,128,512]{2,1,0:T(8,128)(2,1)} %broadcast_in_dim.73), calls=%async_computation.3 | async-start | bytes 524288 | tf_op jit(solution)/shard_map/all_to_all | solution.py:205
  165.8 1.5 fusion.35
  167.3 4.5 %all-to-all-done.3 = bf16[2,128,512]{2,1,0:T(8,128)(2,1)S(1)} async-done(((bf16[2,128,512]{2,1,0:T(8,128)(2,1)}), bf16[2,128,512]{2,1,0:T(8,128)(2,1)S(1)}, u32[]{:S(2)}, u32[]{:S(2)}) %all-to-all-start.3) | async-done | bytes 262176 | tf_op jit(solution)/shard_map/all_to_all | solution.py:205
  173.2 1.1 pad_maximum_fusion.1
  174.3 5.0 %all-to-all-start.4 = ((bf16[8,128,512]{2,1,0:T(8,128)(2,1)}), bf16[8,128,512]{2,1,0:T(8,128)(2,1)S(1)}, u32[]{:S(2)}, u32[]{:S(2)}) async-start(bf16[8,128,512]{2,1,0:T(8,128)(2,1)} %bitcast.70), calls=%async_computation.4 | async-start | bytes 2097152 | tf_op jit(solution)/shard_map/all_to_all | solution.py:223
  179.3 1.9 collective-permute-start.3
  181.2 11.2 %collective-permute-done.3 = bf16[128,1024]{0,1:T(8,128)(2,1)S(1)} collective-permute-done((bf16[128,1024]{0,1:T(8,128)(2,1)S(1)}, bf16[128,1024]{0,1:T(8,128)(2,1)S(1)}, u32[]{:S(2)}, u32[]{:S(2)}) %collective-permute-start.3) | collective-permute-done | bytes 262176 | tf_op jit(solution)/shard_map/ppermute | solution.py:214
  193.2 2.6 %all-to-all-done.4 = bf16[8,128,512]{2,1,0:T(8,128)(2,1)S(1)} async-done(((bf16[8,128,512]{2,1,0:T(8,128)(2,1)}), bf16[8,128,512]{2,1,0:T(8,128)(2,1)S(1)}, u32[]{:S(2)}, u32[]{:S(2)}) %all-to-all-start.4) | async-done | bytes 1048608 | tf_op jit(solution)/shard_map/all_to_all | solution.py:223
  (117 shorter events, 24.8 us)
Async XLA Ops:
  7.2 28.5 %copy-start = (f32[1,1024]{1,0:T(1,128)S(1)}, f32[1,1024]{1,0:T(1,128)}, u32[]{:S(2)}) copy-start(f32[1,1024]{1,0:T(1,128)} %param.28) | copy-start | bytes 12292
  14.3 21.0 %copy-start.2 = (f32[1,1,1,32,4096]{4,3,2,1,0:T(8,128)S(1)}, f32[1,1,1,32,4096]{4,3,2,1,0:T(8,128)}, u32[]{:S(2)}) copy-start(f32[1,1,1,32,4096]{4,3,2,1,0:T(8,128)} %param.27) | copy-start | bytes 1572868
  14.6 24.2 %copy-start.10 = (f32[33,32,1]{0,1,2:T(8,128)S(1)}, f32[33,32,1]{0,1,2:T(8,128)}, u32[]{:S(2)}) copy-start(f32[33,32,1]{0,1,2:T(8,128)} %constant.170) | copy-start | bytes 12676
  14.6 24.9 %copy-start.9 = (f32[33,32,1]{0,1,2:T(8,128)S(1)}, f32[33,32,1]{0,1,2:T(8,128)}, u32[]{:S(2)}) copy-start(f32[33,32,1]{0,1,2:T(8,128)} %constant.169) | copy-start | bytes 12676
  17.1 58.3 %all-to-all-start = ((bf16[32,82,128]{2,1,0:T(8,128)(2,1)}), bf16[32,82,128]{2,1,0:T(8,128)(2,1)S(1)}, u32[]{:S(2)}, u32[]{:S(2)}) async-start(bf16[32,82,128]{2,1,0:T(8,128)(2,1)} %pad_maximum_fusion.2), calls=%async_computation | async-start | bytes 1441792 | tf_op jit(solution)/shard_map/all_to_all | solution.py:143
  34.5 123.4 %all-gather.2.cloned.1.call-start = ((), (), s32[]{:S(2)}) async-start(), calls=%async_computation.5 | async-start | bytes 2228224 | tf_op jit(solution)/shard_map/all_gather | solution.py:129
  76.8 24.1 %all-to-all-start.1 = ((bf16[4,2,32,16,128]{4,3,2,1,0:T(8,128)(2,1)}), bf16[4,2,32,16,128]{4,3,2,1,0:T(8,128)(2,1)S(1)}, u32[]{:S(2)}, u32[]{:S(2)}) async-start(bf16[4,2,32,16,128]{4,3,2,1,0:T(8,128)(2,1)} %broadcast_in_dim.64), calls=%async_computation.1 | async-start | bytes 2097152 | tf_op jit(solution)/shard_map/all_to_all | solution.py:154
  82.2 4.9 %copy-start.6 = (f32[33,128]{1,0:T(8,128)S(1)}, f32[33,128]{1,0:T(8,128)}, u32[]{:S(2)}) copy-start(f32[33,128]{1,0:T(8,128)} %constant.167) | copy-start | bytes 50692
  82.2 4.9 %copy-start.7 = (f32[33,128]{1,0:T(8,128)S(1)}, f32[33,128]{1,0:T(8,128)}, u32[]{:S(2)}) copy-start(f32[33,128]{1,0:T(8,128)} %constant.166) | copy-start | bytes 50692
  85.7 1.8 copy-start.1
  87.4 1.4 copy-start.3
  89.4 1.1 copy-start.8
  89.7 11.4 %copy-start.14 = (s32[512]{0:T(512)S(1)}, s32[512]{0:T(512)}, u32[]{:S(2)}) copy-start(s32[512]{0:T(512)} %get-tuple-element.69) | copy-start | bytes 6148
  91.0 14.0 %copy-start.13 = (s32[512]{0:T(512)S(1)}, s32[512]{0:T(512)}, u32[]{:S(2)}) copy-start(s32[512]{0:T(512)} %get-tuple-element.68) | copy-start | bytes 6148
  91.1 13.9 %collective-permute-start = (bf16[512,128]{1,0:T(8,128)(2,1)}, bf16[512,128]{1,0:T(8,128)(2,1)S(1)}, u32[]{:S(2)}, u32[]{:S(2)}) collective-permute-start(bf16[512,128]{1,0:T(8,128)(2,1)} %bitcast.15), channel_id=1, source_target_pairs={{0,16},{16,0},{1,17},{17,1},{2,18},{18,2},{3,19},{19,3},{4,20},{20... | collective-permute-start | bytes 393224 | tf_op jit(solution)/shard_map/ppermute | solution.py:153
  108.4 6.7 %copy-start.15 = (pred[128]{0:T(512)(128)(4,1)S(1)}, pred[128]{0:T(512)(128)(4,1)}, u32[]{:S(2)}) copy-start(pred[128]{0:T(512)(128)(4,1)} %get-tuple-element.70) | copy-start | bytes 388
  108.4 6.7 %copy-start.16 = (pred[128]{0:T(512)(128)(4,1)S(1)}, pred[128]{0:T(512)(128)(4,1)}, u32[]{:S(2)}) copy-start(pred[128]{0:T(512)(128)(4,1)} %get-tuple-element.71) | copy-start | bytes 388
  108.4 6.7 %copy-start.17 = (f32[32]{0:T(128)S(1)}, f32[32]{0:T(128)}, u32[]{:S(2)}) copy-start(f32[32]{0:T(128)} %fusion.102) | copy-start | bytes 388
  109.6 9.1 %collective-permute-start.1 = (bf16[524,128]{1,0:T(8,128)(2,1)S(1)}, bf16[524,128]{1,0:T(8,128)(2,1)S(1)}, u32[]{:S(2)}, u32[]{:S(2)}) collective-permute-start(bf16[524,128]{1,0:T(8,128)(2,1)S(1)} %pad_maximum_fusion.5), channel_id=1, source_target_pairs={{0,16},{16,0},{1,17},{17,1},{2,18},{18,2},{3,19},{19,3},{4,20},{20... | collective-permute-start | bytes 402440 | tf_op jit(solution)/shard_map/ppermute | solution.py:190
  118.7 13.9 %copy-start.4 = (bf16[1,128,1024]{2,1,0:T(8,128)(2,1)S(1)}, bf16[1,128,1024]{2,1,0:T(8,128)(2,1)}, u32[]{:S(2)}) copy-start(bf16[1,128,1024]{2,1,0:T(8,128)(2,1)} %param.24) | copy-start | bytes 786436
  121.1 38.4 %all-to-all-start.2 = ((bf16[32,48,128]{2,1,0:T(8,128)(2,1)}), bf16[32,48,128]{2,1,0:T(8,128)(2,1)}, u32[]{:S(2)}, u32[]{:S(2)}) async-start(bf16[32,48,128]{2,1,0:T(8,128)(2,1)} %pad_maximum_fusion.4), calls=%async_computation.2 | async-start | bytes 786432 | tf_op jit(solution)/shard_map/all_to_all | solution.py:201
  132.8 33.0 %copy-start.11 = (f32[1,1,1,1024]{3,0,2,1:T(1,128)S(1)}, f32[1,1,1,1024]{3,0,2,1:T(1,128)}, u32[]{:S(2)}) copy-start(f32[1,1,1,1024]{3,0,2,1:T(1,128)} %get-tuple-element.50) | copy-start | bytes 12292
  132.8 33.0 %copy-start.12 = (f32[1,1,1,1024]{3,0,2,1:T(1,128)S(1)}, f32[1,1,1,1024]{3,0,2,1:T(1,128)}, u32[]{:S(2)}) copy-start(f32[1,1,1,1024]{3,0,2,1:T(1,128)} %get-tuple-element.51) | copy-start | bytes 12292
  133.0 24.7 %collective-permute-start.2 = (bf16[2,1024]{0,1:T(8,128)(2,1)S(1)}, bf16[2,1024]{0,1:T(8,128)(2,1)S(1)}, u32[]{:S(2)}, u32[]{:S(2)}) collective-permute-start(bf16[2,1024]{0,1:T(8,128)(2,1)S(1)} %slice_bitcast_fusion), channel_id=1, source_target_pairs={{0,4},{4,8},{8,12},{12,16},{16,20},{20,24},{24,28},{28,32},{32,36}... | collective-permute-start | bytes 12296 | tf_op jit(solution)/shard_map/ppermute | solution.py:145
  161.4 10.4 %all-to-all-start.3 = ((bf16[2,128,512]{2,1,0:T(8,128)(2,1)}), bf16[2,128,512]{2,1,0:T(8,128)(2,1)S(1)}, u32[]{:S(2)}, u32[]{:S(2)}) async-start(bf16[2,128,512]{2,1,0:T(8,128)(2,1)} %broadcast_in_dim.73), calls=%async_computation.3 | async-start | bytes 524288 | tf_op jit(solution)/shard_map/all_to_all | solution.py:205
  171.8 7.5 %copy-start.5 = (bf16[128,1024]{0,1:T(8,128)(2,1)S(1)}, bf16[128,1024]{0,1:T(8,128)(2,1)}, u32[]{:S(2)}) copy-start(bf16[128,1024]{0,1:T(8,128)(2,1)} %fusion.35) | copy-start | bytes 786436
  174.3 21.6 %all-to-all-start.4 = ((bf16[8,128,512]{2,1,0:T(8,128)(2,1)}), bf16[8,128,512]{2,1,0:T(8,128)(2,1)S(1)}, u32[]{:S(2)}, u32[]{:S(2)}) async-start(bf16[8,128,512]{2,1,0:T(8,128)(2,1)} %bitcast.70), calls=%async_computation.4 | async-start | bytes 2097152 | tf_op jit(solution)/shard_map/all_to_all | solution.py:223
  179.3 13.1 %collective-permute-start.3 = (bf16[128,1024]{0,1:T(8,128)(2,1)S(1)}, bf16[128,1024]{0,1:T(8,128)(2,1)S(1)}, u32[]{:S(2)}, u32[]{:S(2)}) collective-permute-start(bf16[128,1024]{0,1:T(8,128)(2,1)S(1)} %copy-done.5), channel_id=1, source_target_pairs={{0,128},{128,256},{256,384},{384,0},{1,129},{129,257},{257,385},{3... | collective-permute-start | bytes 786440 | tf_op jit(solution)/shard_map/ppermute | solution.py:214
Sparse Core Ops, SparseCore 0:
  37.4 82.5 all-gather.1

commit v4 on v3

v4 whole, which is shorter than its diff:
```python
import functools
import math

import jax
import jax.numpy as jnp
import numpy as np
from jax import lax
from jax.experimental import pallas as pl
from jax.experimental.pallas import tpu as pltpu
from jax.sharding import Mesh, PartitionSpec as P

HD = 128
BF16 = jnp.bfloat16
F32 = jnp.float32
HIGH = lax.Precision.HIGH


def dot(left, right, contract, precision=None):
    return lax.dot_general(
        left, right, (contract, ((), ())), precision=precision, preferred_element_type=F32
    )


def transform_tables(depth, breadth):
    full = 2 * depth
    half = depth + 1
    k = np.arange(half)
    a = np.arange(depth)
    b = np.arange(breadth)
    one = -2.0 * np.pi * np.outer(k, a) / full
    first = np.stack([np.cos(one), np.sin(one)])
    mid = -2.0 * np.pi * np.outer(k, b) / (full * breadth)
    two = -2.0 * np.pi * (np.outer(b, b) % breadth) / breadth
    cos_two, sin_two = np.cos(two), np.sin(two)
    forward = np.block([[cos_two, sin_two], [-sin_two, cos_two]])
    backward = np.block([[cos_two, -sin_two], [sin_two, cos_two]])
    weight = np.where((k == 0) | (k == depth), 1.0, 2.0) / (full * breadth)
    last = np.concatenate([np.cos(one).T * weight, np.sin(one).T * weight], axis=1)
    as32 = lambda x: np.asarray(x, np.float32)
    return as32(first), as32(np.cos(mid)), as32(np.sin(mid)), as32(forward), as32(backward), as32(last)


def forward_transform(blocks, tables):
    first, cos_mid, sin_mid, forward, _, _ = tables
    depth, channels, breadth = blocks.shape
    flat = blocks.reshape(depth, channels * breadth)
    real = dot(first[0], flat, ((1,), (0,)), HIGH).reshape(-1, channels, breadth)
    imag = dot(first[1], flat, ((1,), (0,)), HIGH).reshape(-1, channels, breadth)
    cos_mid, sin_mid = cos_mid[:, None], sin_mid[:, None]
    turned = jnp.concatenate(
        [real * cos_mid - imag * sin_mid, real * sin_mid + imag * cos_mid], axis=2
    )
    return dot(turned, forward, ((2,), (0,)), HIGH)


def inverse_transform(spectrum, tables):
    _, cos_mid, sin_mid, _, backward, last = tables
    half, channels, twice = spectrum.shape
    breadth = twice // 2
    mid = dot(spectrum, backward, ((2,), (0,)), HIGH)
    real, imag = mid[:, :, :breadth], mid[:, :, breadth:]
    cos_mid, sin_mid = cos_mid[:, None], sin_mid[:, None]
    turned = jnp.concatenate(
        [real * cos_mid + imag * sin_mid, imag * cos_mid - real * sin_mid], axis=0
    )
    out = dot(last, turned.reshape(2 * half, channels * breadth), ((1,), (0,)), HIGH)
    return out.reshape(-1, channels, breadth)


def edge_short(edges, taps):
    edges = edges.astype(F32)
    before = jnp.pad(edges[:-1, 2:], ((1, 0), (0, 0), (0, 0)))
    zero = taps[0] * edges[:, 0] + taps[1] * before[:, 1] + taps[2] * before[:, 0]
    one = taps[0] * edges[:, 1] + taps[1] * edges[:, 0] + taps[2] * before[:, 1]
    return zero, one


def kernel_call(kernel, out_shape, scalars, arrays, scratch=(), flops=0):
    in_specs = [pl.BlockSpec(memory_space=pltpu.SMEM)] * len(scalars)
    in_specs += [pl.BlockSpec(memory_space=pltpu.VMEM)] * len(arrays)
    outs = out_shape if isinstance(out_shape, tuple) else (out_shape,)
    moved = sum(x.size * x.dtype.itemsize for x in (*arrays, *outs))
    return pl.pallas_call(
        kernel,
        out_shape=out_shape,
        in_specs=in_specs,
        out_specs=jax.tree.map(lambda _: pl.BlockSpec(memory_space=pltpu.VMEM), out_shape),
        scratch_shapes=list(scratch),
        compiler_params=pltpu.CompilerParams(vmem_limit_bytes=32 * 1024 * 1024),
        cost_estimate=pl.CostEstimate(flops=flops, bytes_accessed=moved, transcendentals=0),
    )(*scalars, *arrays)


def pack_kernel(first_ref, value_ref, taps_ref, query_ref, key_ref, value_head_ref, out_ref):
    n_seq, _, lanes = out_ref.shape
    rows, wide = query_ref.shape
    heads = wide // HD
    chunks = n_seq // heads
    few = rows // chunks
    per = n_seq * lanes // first_ref.shape[1]
    channels = lanes // per
    for at, ref in enumerate((query_ref, key_ref, value_head_ref)):
        for head in range(heads):
            block = ref[:, head * HD : (head + 1) * HD].reshape(chunks, few, HD)
            out_ref[head * chunks : (head + 1) * chunks, at * few : (at + 1) * few, :] = block
    for group in range(n_seq // per):
        span = slice(group * lanes, (group + 1) * lanes)
        shorts, edges = [], []
        for ref, which in ((first_ref, 0), (value_ref, 2)):
            x = ref[:, span].astype(F32)
            shorts.append(
                taps_ref[which, 0:1, span] * x
                + taps_ref[which, 1:2, span] * pltpu.roll(x, 1, 0)
                + taps_ref[which, 2:3, span] * pltpu.roll(x, 2, 0)
            )
            edges += [x[:2], x[rows - 2 :]]
        turned = (shorts[0] * shorts[1]).T.astype(BF16).reshape(per, channels, rows)
        out_ref[group * per : (group + 1) * per, 3 * few : 3 * few + channels, :] = turned
        edges = jnp.concatenate(edges, axis=0)
        for at in range(per):
            edge = pltpu.roll(edges, lanes - at * channels, 1) if at else edges
            out_ref[group * per + at, 3 * few + channels :, :] = edge.astype(BF16)


def attend(delta, query_ref, pairs_ref, tile, few, rows):
    size = 128
    query = query_ref[tile * size : (tile + 1) * size, :]
    row = lax.broadcasted_iota(jnp.int32, (size, size), 0)
    column = lax.broadcasted_iota(jnp.int32, (size, size), 1)
    q_pos = row // few * rows + row % few
    k_pos = column // few * rows + column % few
    parts = []
    for at in range(pairs_ref.shape[0]):
        allowed = k_pos + (at * few + delta) <= q_pos
        for start, stop in ((0, tile * size), (tile * size, (tile + 1) * size)):
            if start == stop:
                continue
            keys = pairs_ref[at, 0, start:stop, :]
            scores = dot(query, keys, ((1,), (1,))) * (1.0 / math.sqrt(HD))
            if start == tile * size:
                parts.append((jnp.where(allowed, scores, -1e30), allowed, at, start, stop))
            else:
                parts.append((scores, None, at, start, stop))
    highest = parts[0][0].max(axis=1, keepdims=True)
    for part in parts[1:]:
        highest = jnp.maximum(highest, part[0].max(axis=1, keepdims=True))
    totals = jnp.zeros((size, 1), F32)
    weighted = jnp.zeros((size, HD), F32)
    for scores, allowed, at, start, stop in parts:
        probs = jnp.exp(scores - highest)
        if allowed is not None:
            probs = jnp.where(allowed, probs, 0.0)
        totals = totals + probs.sum(axis=1, keepdims=True)
        values = pairs_ref[at, 1, start:stop, :]
        weighted = weighted + dot(probs.astype(BF16), values, ((1,), (0,)))
    some = totals > 0.0
    totals = jnp.maximum(totals, 1e-30)
    return weighted / totals, jnp.where(some, highest + jnp.log(totals), -1e30)


def other_kernel(rows, few, delta_ref, query_ref, pairs_ref, out_ref, log_ref):
    own_rows = query_ref.shape[0]
    log_ref[...] = jnp.zeros_like(log_ref)
    for tile in range(own_rows // 128):
        out, log = attend(delta_ref[0], query_ref, pairs_ref, tile, few, rows)
        out_ref[tile * 128 : (tile + 1) * 128, :] = out.astype(BF16)
        line = jnp.broadcast_to(log, (128, 128)).T[:8]
        first = line.astype(BF16).astype(F32)
        second = (line - first).astype(BF16).astype(F32)
        third = line - first - second
        for at, term in enumerate((first, second, third)):
            log_ref[at * 8 + tile : at * 8 + tile + 1, :] = term[:1]
    out_ref[own_rows:, :] = log_ref[...].astype(BF16)


def own_kernel(rows, few, delta_ref, query_ref, pairs_ref, out_ref, log_ref):
    for tile in range(query_ref.shape[0] // 128):
        span = slice(tile * 128, (tile + 1) * 128)
        out, log = attend(delta_ref[0], query_ref, pairs_ref, tile, few, rows)
        out_ref[span, :] = out
        log_ref[span, :] = jnp.broadcast_to(log, (128, 128))


def merge_kernel(few, own_ref, log_ref, got_ref, long_ref, out_ref):
    own_rows = own_ref.shape[0]
    per = 128 // (2 * few)
    logs = got_ref[own_rows:, :].astype(F32)
    for tile in range(own_rows // 128):
        span = slice(tile * 128, (tile + 1) * 128)
        log = log_ref[span, :]
        line = logs[tile : tile + 1] + logs[8 + tile : 9 + tile] + logs[16 + tile : 17 + tile]
        got_log = jnp.broadcast_to(line, (128, 128)).T
        highest = jnp.maximum(log, got_log)
        own_share, got_share = jnp.exp(log - highest), jnp.exp(got_log - highest)
        merged = own_ref[span, :] * own_share + got_ref[span, :].astype(F32) * got_share
        merged = (merged / (own_share + got_share)).astype(BF16).reshape(per, 2 * few, HD)
        for x_at in range(2):
            out_ref[tile * per : (tile + 1) * per, x_at, : 2 * few, :] = merged
    out_ref[:, :, 2 * few :, :] = long_ref[...]


def project_kernel(heads, few, back_ref, weight_ref, out_ref):
    n_seq = back_ref.shape[0]
    chunks = n_seq // heads
    n_z, n_tp, channels, wide = weight_ref.shape
    blocks = []
    for x_at in range(2):
        columns = [
            back_ref[head * chunks : (head + 1) * chunks, x_at * few : (x_at + 1) * few, :].reshape(
                chunks * few, HD
            )
            for head in range(heads)
        ]
        blocks.append(jnp.concatenate(columns, axis=1))
    whole = jnp.concatenate(blocks, axis=0)
    for at in range(n_tp):
        part = weight_ref[:, at].reshape(n_z * channels, wide)
        out = dot(whole, part, ((1,), (1,))).astype(BF16)
        for x_at in range(2):
            out_ref[x_at, at] = out[x_at * chunks * few : (x_at + 1) * chunks * few]


def split_kernel(few, mixed_ref, pairs_ref, query_ref):
    n_seq = mixed_ref.shape[0]
    query_ref[...] = mixed_ref[:, :few, :].reshape(n_seq * few, HD)
    for at in range(2):
        block = mixed_ref[:, (at + 1) * few : (at + 2) * few, :].reshape(n_seq * few, HD)
        for to in range(pairs_ref.shape[0]):
            pairs_ref[to, at] = block


def gate_kernel(start, back_ref, gate_ref, tail_ref, taps_ref, out_ref):
    rows = gate_ref.shape[0]
    lanes = 128
    per = lanes // (back_ref.shape[1] - start)
    row = lax.broadcasted_iota(jnp.int32, (rows, lanes), 0)
    for group in range(gate_ref.shape[1] // lanes):
        span = slice(group * lanes, (group + 1) * lanes)
        x = gate_ref[:, span].astype(F32)
        tail = tail_ref[:, span].astype(F32)
        one = jnp.where(row == 0, tail[1:2], pltpu.roll(x, 1, 0))
        two = jnp.where(row == 0, tail[0:1], jnp.where(row == 1, tail[1:2], pltpu.roll(x, 2, 0)))
        short = (
            taps_ref[1, 0:1, span] * x + taps_ref[1, 1:2, span] * one + taps_ref[1, 2:3, span] * two
        )
        rows_long = back_ref[group * per : (group + 1) * per, start:, :].astype(F32)
        out_ref[:, span] = (short * rows_long.reshape(lanes, rows).T).astype(BF16)


def unite_kernel(channels, parts_ref, out_ref):
    n_tp = parts_ref.shape[0] // 2
    rows, lanes = parts_ref.shape[1], 128
    sums = []
    for x_at in range(2):
        total = parts_ref[x_at * n_tp].astype(F32)
        for at in range(1, n_tp):
            total = total + parts_ref[x_at * n_tp + at].astype(F32)
        sums.append(total)
    lane = lax.broadcasted_iota(jnp.int32, (rows, lanes), 1)
    for group in range(out_ref.shape[1] // lanes):
        span = slice(group // 2 * lanes, (group // 2 + 1) * lanes)
        start = group % 2 * 2 * channels
        even, odd = sums[0][:, span], sums[1][:, span]

        def moved(x, by):
            by = by % lanes
            return pltpu.roll(x, by, 1) if by else x

        low = jnp.where(lane < channels, moved(even, -start), moved(odd, channels - start))
        high = jnp.where(
            lane < 3 * channels, moved(even, channels - start), moved(odd, 2 * channels - start)
        )
        out_ref[:, group * lanes : (group + 1) * lanes] = jnp.where(
            lane < 2 * channels, low, high
        ).astype(BF16)


def body(
    first_stream,
    gate_stream,
    value_stream,
    short_taps,
    long_filter,
    skip_gain,
    queries,
    attn_keys,
    attn_values,
    out_weight,
):
    seq = ("zi", "zp", "zq", "xh")
    n_seq, n_x, n_tp = lax.axis_size(seq), lax.axis_size("xh"), lax.axis_size("tp")
    n_pair = lax.axis_size("zq") * n_x
    n_z = n_seq // n_x
    n_plane = n_x * n_tp
    seq_at = lax.axis_index(seq)
    half_at = lax.axis_index("zp")
    pair_at = lax.axis_index(("zq", "xh"))
    rows = queries.shape[1]
    wide = queries.shape[2]
    channels = long_filter.shape[3]
    heads = wide // HD
    chunks = n_seq // heads
    few = rows // chunks
    own_rows = n_seq * few
    taps = short_taps[0]

    weight = out_weight[0].transpose(1, 2, 0).reshape(-1, wide)
    weight = lax.all_gather(weight, ("zi", "zp", "zq"))

    packed = kernel_call(
        pack_kernel,
        jax.ShapeDtypeStruct((n_seq, 3 * few + channels + 8, rows), BF16),
        (),
        (first_stream[0], value_stream[0], taps, queries[0], attn_keys[0], attn_values[0]),
    )
    mixed = lax.all_to_all(packed, seq, 0, 0)

    tail = lax.ppermute(gate_stream[0, -2:], seq, [(i, i + 1) for i in range(n_seq - 1)])
    mixed, tail = lax.optimization_barrier((mixed, tail))
    tables = transform_tables(n_seq, rows)
    kernel = long_filter[0, 0, 0].reshape(channels, n_seq, rows).transpose(1, 0, 2)
    kernel_spec = forward_transform(kernel, tables)

    sent_pairs, query = kernel_call(
        functools.partial(split_kernel, few),
        (
            jax.ShapeDtypeStruct((n_pair, 2, own_rows, HD), BF16),
            jax.ShapeDtypeStruct((own_rows, HD), BF16),
        ),
        (),
        (mixed,),
    )
    swap = [(0, 1), (1, 0)]
    other_query = lax.ppermute(query, "zp", swap)
    pairs = lax.all_to_all(sent_pairs, ("zq", "xh"), 0, 0)

    local_taps = lax.dynamic_slice_in_dim(taps, seq_at * channels, channels, 2)
    edges = mixed[:, 3 * few + channels :, :channels]
    first_zero, first_one = edge_short(edges[:, :4], local_taps[0])
    value_zero, value_one = edge_short(edges[:, 4:], local_taps[2])
    token = lax.broadcasted_iota(jnp.int32, (1, 1, rows), 2)
    product = mixed[:, 3 * few : 3 * few + channels]
    product = jnp.where(token == 0, (first_zero * value_zero).astype(BF16)[:, :, None], product)
    product = jnp.where(token == 1, (first_one * value_one).astype(BF16)[:, :, None], product)
    product = product.astype(F32)
    spec = forward_transform(product, tables)
    real, imag = spec[:, :, :rows], spec[:, :, rows:]
    kernel_real, kernel_imag = kernel_spec[:, :, :rows], kernel_spec[:, :, rows:]
    joined = jnp.concatenate(
        [real * kernel_real - imag * kernel_imag, real * kernel_imag + imag * kernel_real], axis=2
    )
    convolved = inverse_transform(joined, tables)
    gain = lax.dynamic_slice_in_dim(skip_gain[0], seq_at * channels, channels, 0)
    long_out = (convolved + gain[None, :, None] * product).astype(BF16)

    work = 2 * own_rows * n_pair * own_rows * HD
    own_delta = -pair_at * few
    other_delta = (2 * half_at - 1) * (n_pair * few) + own_delta
    sent = kernel_call(
        functools.partial(other_kernel, rows, few),
        jax.ShapeDtypeStruct((own_rows + 32, HD), BF16),
        (other_delta.astype(jnp.int32).reshape(1),),
        (other_query, pairs),
        (pltpu.VMEM((32, HD), F32),),
        work,
    )
    got = lax.ppermute(sent, "zp", swap)
    query, sent = lax.optimization_barrier((query, sent))
    own_out, own_log = kernel_call(
        functools.partial(own_kernel, rows, few),
        (jax.ShapeDtypeStruct((own_rows, HD), F32),) * 2,
        (own_delta.astype(jnp.int32).reshape(1),),
        (query, pairs),
        (),
        work,
    )
    returned = kernel_call(
        functools.partial(merge_kernel, few),
        jax.ShapeDtypeStruct((n_z, n_x, n_x * few + channels, HD), BF16),
        (),
        (own_out, own_log, got, long_out.reshape(n_z, n_x, channels, rows)),
    )
    back = lax.all_to_all(returned.reshape(n_seq, -1, HD), seq, 0, 0)

    hyena = kernel_call(
        functools.partial(gate_kernel, n_x * few),
        jax.ShapeDtypeStruct(gate_stream.shape[1:], BF16),
        (),
        (back, gate_stream[0], tail, taps),
    )
    n_sec = lax.axis_size("section")
    handed = lax.ppermute(hyena, "section", [(i, (i + 1) % n_sec) for i in range(n_sec)])

    partials = kernel_call(
        functools.partial(project_kernel, heads, few),
        jax.ShapeDtypeStruct((n_x, n_tp, rows, n_z * channels), BF16),
        (),
        (back, weight.reshape(n_z, n_tp, channels, wide)),
        (),
        2 * n_x * rows * wide * n_seq * channels * n_tp // n_x,
    ).reshape(n_plane, rows, n_z * channels)
    partials = lax.all_to_all(partials, ("xh", "tp"), 0, 0)
    attended = kernel_call(
        functools.partial(unite_kernel, channels),
        jax.ShapeDtypeStruct(handed.shape, BF16),
        (),
        (partials,),
    )
    return (handed[None], attended[None])


def solution(mesh):
    n_sec, n_seq, n_tp = (mesh.shape[name] for name in ("section", "seq", "tp"))
    finer = Mesh(
        mesh.devices.reshape(n_sec, n_seq // 8, 2, 2, 2, n_tp),
        ("section", "zi", "zp", "zq", "xh", "tp"),
    )
    seq = ("zi", "zp", "zq", "xh")
    placed = (
        P("section", seq, "tp"),
        P("section", seq, "tp"),
        P("section", seq, "tp"),
        P("section", None, None, "tp"),
        P("section", "tp", seq, None, None),
        P("section", "tp"),
        P("section", seq, "tp"),
        P("section", seq, "tp"),
        P("section", seq, "tp"),
        P("section", "tp", None, seq),
    )
    return jax.shard_map(
        body,
        mesh=finer,
        in_specs=placed,
        out_specs=(P("section", seq, "tp"), P("section", seq, "tp")),
        check_vma=False,
    )
```

time: 205 us -> 192 us (0.937)
  the two profiles are of different devices: /device:TPU:64 before, /device:TPU:2 now
where the time goes in v4:
time: 192 us; the launch traced here: 191 us
  waiting for transfers between devices  95 us (49%)
  starting transfers between devices  51.9 us (27%)
  between operations  14.5 us (8%)
  local copies, waits for them, and re-layouts  12.5 us (7%)
  Pallas kernels  10.9 us (6%)
  matrix products  5.19 us (3%)
    all_to_all x1, waiting for transfers between devices, body(): mixed = lax.all_to_all(packed, seq, 0, 0)  35.5 us
    all_to_all x1, waiting for transfers between devices, body(): back = lax.all_to_all(returned.reshape(n_seq, -1, HD), seq, 0, 0)  31.5 us
    all_to_all x1, starting transfers between devices, body(): mixed = lax.all_to_all(packed, seq, 0, 0)  17.2 us
    unnamed x46, local copies, waits for them, and re-layouts  11.1 us
    pallas_call x8, Pallas kernels, kernel_call(): pl.pallas_call(kernel, out_shape=out_shape, in_specs=in_specs, out_specs=...  10.9 us
    all_to_all x1, starting transfers between devices, body(): back = lax.all_to_all(returned.reshape(n_seq, -1, HD), seq, 0, 0)  10.8 us
    ppermute x1, waiting for transfers between devices, body(): other_query = lax.ppermute(query, 'zp', swap)  9.24 us
    ppermute x1, waiting for transfers between devices, body(): lax.ppermute(hyena, 'section', [(i, (i + 1) % n_sec) for i in range(n_sec)])  8.7 us
  transfers between devices with their start and end apart: 9, of which 7 were waited for; matrix products, arithmetic and copies ran while one was open for 5% of the time, Pallas kernels for 4%

profile of v4, /device:TPU:2, one launch (start us, length us, event | category | flops | bytes accessed | tf_op | source)
XLA Modules:
  0.0 191.4 jit_solution(7214955613427935011)
XLA Ops:
  7.2 0.8 copy.104
  8.0 0.9 copy-done.3
  8.9 0.9 copy-done.4
  9.9 0.9 copy-done.5
  10.8 0.9 copy-done.6
  11.7 0.9 copy-done.7
  12.6 1.4 shard_map.230
  14.0 17.2 %all-to-all-start = ((bf16[32,88,128]{2,1,0:T(8,128)(2,1)}), bf16[32,88,128]{2,1,0:T(8,128)(2,1)S(1)}, u32[]{:S(2)}, u32[]{:S(2)}) async-start(bf16[32,88,128]{2,1,0:T(8,128)(2,1)} %shard_map.230), calls=%async_computation | async-start | bytes 1441792 | tf_op jit(solution)/shard_map/all_to_all | solution.py:316
  31.2 5.2 %collective-permute-start = (bf16[2,1024]{1,0:T(2,128)(2,1)S(1)}, bf16[2,1024]{1,0:T(2,128)(2,1)S(1)}, u32[]{:S(2)}, u32[]{:S(2)}) collective-permute-start(bf16[2,1024]{1,0:T(2,128)(2,1)S(1)} %slice_bitcast_fusion.2), channel_id=1, source_target_pairs={{0,4},{4,8},{8,12},{12,16},{16,20},{20,24},{24,28},{28,32},{32,36}... | collective-permute-start | bytes 12296 | tf_op jit(solution)/shard_map/ppermute | solution.py:318
  36.9 0.8 fusion.38
  38.5 1.5 fusion.15
  40.1 35.5 %all-to-all-done.mixed_ref = bf16[32,88,128]{2,1,0:T(8,128)(2,1)S(1)} async-done(((bf16[32,88,128]{2,1,0:T(8,128)(2,1)}), bf16[32,88,128]{2,1,0:T(8,128)(2,1)S(1)}, u32[]{:S(2)}, u32[]{:S(2)}) %all-to-all-start) | async-done | bytes 720928 | tf_op jit(solution)/shard_map/all_to_all | solution.py:316
  75.7 1.1 shard_map.231
  76.9 4.1 %all-to-all-start.1 = ((bf16[4,2,512,128]{3,2,1,0:T(8,128)(2,1)}), bf16[4,2,512,128]{3,2,1,0:T(8,128)(2,1)S(1)}, u32[]{:S(2)}, u32[]{:S(2)}) async-start(bf16[4,2,512,128]{3,2,1,0:T(8,128)(2,1)} %get-tuple-element.11), calls=%async_computation.1 | async-start | bytes 2097152 | tf_op jit(solution)/shard_map/all_to_all | solution.py:335
  85.7 0.8 copy-done.11
  88.1 2.4 %collective-permute-start.1 = (bf16[512,128]{1,0:T(8,128)(2,1)S(1)}, bf16[512,128]{1,0:T(8,128)(2,1)S(1)}, u32[]{:S(2)}, u32[]{:S(2)}) collective-permute-start(bf16[512,128]{1,0:T(8,128)(2,1)S(1)} %get-tuple-element.12.query_ref), channel_id=1, source_target_pairs={{0,16},{16,0},{1,17},{17,1},{2,18},{18,2},{3,19},{19,3},{4,20},{20... | collective-permute-start | bytes 393224 | tf_op jit(solution)/shard_map/ppermute | solution.py:334
  91.0 9.2 %collective-permute-done.1.query_ref = bf16[512,128]{1,0:T(8,128)(2,1)S(1)} collective-permute-done((bf16[512,128]{1,0:T(8,128)(2,1)S(1)}, bf16[512,128]{1,0:T(8,128)(2,1)S(1)}, u32[]{:S(2)}, u32[]{:S(2)}) %collective-permute-start.1) | collective-permute-done | bytes 131104 | tf_op jit(solution)/shard_map/ppermute | solution.py:334
  100.3 2.3 %all-to-all-done.1.pairs_ref = bf16[4,2,512,128]{3,2,1,0:T(8,128)(2,1)S(1)} async-done(((bf16[4,2,512,128]{3,2,1,0:T(8,128)(2,1)}), bf16[4,2,512,128]{3,2,1,0:T(8,128)(2,1)S(1)}, u32[]{:S(2)}, u32[]{:S(2)}) %all-to-all-start.1) | async-done | bytes 1048608 | tf_op jit(solution)/shard_map/all_to_all | solution.py:335
  102.6 2.1 %shard_map.232 = bf16[544,128]{1,0:T(8,128)(2,1)S(1)} custom-call(s32[1]{0:T(128)} %bitcast.7.delta_ref, bf16[512,128]{1,0:T(8,128)(2,1)S(1)} %collective-permute-done.1.query_ref, bf16[4,2,512,128]{3,2,1,0:T(8,128)(2,1)S(1)} %all-to-all-done.1.pairs_ref), custom_call_target="tpu_custom_call" | custom-call | flops 268435456 | bytes 1318912 | tf_op jit(solution)/shard_map/pallas_call | solution.py:83
  104.7 3.2 %collective-permute-start.2 = (bf16[544,128]{1,0:T(8,128)(2,1)S(1)}, bf16[544,128]{1,0:T(8,128)(2,1)S(1)}, u32[]{:S(2)}, u32[]{:S(2)}) collective-permute-start(bf16[544,128]{1,0:T(8,128)(2,1)S(1)} %shard_map.232), channel_id=1, source_target_pairs={{0,16},{16,0},{1,17},{17,1},{2,18},{18,2},{3,19},{19,3},{4,20},{20... | collective-permute-start | bytes 417800 | tf_op jit(solution)/shard_map/ppermute | solution.py:367
  108.3 2.2 %shard_map.233 = (f32[512,128]{1,0:T(8,128)S(1)}, f32[512,128]{1,0:T(8,128)S(1)}) custom-call(s32[1]{0:T(128)} %bitcast.delta_ref, bf16[512,128]{1,0:T(8,128)(2,1)S(1)} %get-tuple-element.12.query_ref, bf16[4,2,512,128]{3,2,1,0:T(8,128)(2,1)S(1)} %all-to-all-done.1.pairs_ref), custom_call_target="tpu_custom_call" | custom-call | flops 268435456 | bytes 1703936 | tf_op jit(solution)/shard_map/pallas_call | solution.py:83
  110.5 3.6 %collective-permute-done.2.got_ref = bf16[544,128]{1,0:T(8,128)(2,1)S(1)} collective-permute-done((bf16[544,128]{1,0:T(8,128)(2,1)S(1)}, bf16[544,128]{1,0:T(8,128)(2,1)S(1)}, u32[]{:S(2)}, u32[]{:S(2)}) %collective-permute-start.2) | collective-permute-done | bytes 139296 | tf_op jit(solution)/shard_map/ppermute | solution.py:367
  114.1 1.0 shard_map.234
  115.1 10.8 %all-to-all-start.2 = ((bf16[32,64,128]{2,1,0:T(8,128)(2,1)}), bf16[32,64,128]{2,1,0:T(8,128)(2,1)S(1)}, u32[]{:S(2)}, u32[]{:S(2)}) async-start(bf16[32,64,128]{2,1,0:T(8,128)(2,1)} %bitcast.30), calls=%async_computation.2 | async-start | bytes 1048576 | tf_op jit(solution)/shard_map/all_to_all | solution.py:383
  126.0 31.5 %all-to-all-done.2.back_ref = bf16[32,64,128]{2,1,0:T(8,128)(2,1)S(1)} async-done(((bf16[32,64,128]{2,1,0:T(8,128)(2,1)}), bf16[32,64,128]{2,1,0:T(8,128)(2,1)S(1)}, u32[]{:S(2)}, u32[]{:S(2)}) %all-to-all-start.2) | async-done | bytes 524320 | tf_op jit(solution)/shard_map/all_to_all | solution.py:383
  157.5 1.6 copy-done.1
  159.1 1.8 shard_map.236
  160.9 7.1 %all-to-all-start.3 = ((bf16[8,128,512]{2,1,0:T(8,128)(2,1)}), bf16[8,128,512]{2,1,0:T(8,128)(2,1)S(1)}, u32[]{:S(2)}, u32[]{:S(2)}) async-start(bf16[8,128,512]{2,1,0:T(8,128)(2,1)} %bitcast.37), calls=%async_computation.3 | async-start | bytes 2097152 | tf_op jit(solution)/shard_map/all_to_all | solution.py:402
  168.2 1.9 %collective-permute-start.3 = (bf16[128,1024]{1,0:T(8,128)(2,1)S(1)}, bf16[128,1024]{1,0:T(8,128)(2,1)S(1)}, u32[]{:S(2)}, u32[]{:S(2)}) collective-permute-start(bf16[128,1024]{1,0:T(8,128)(2,1)S(1)} %shard_map.235), channel_id=1, source_target_pairs={{0,128},{128,256},{256,384},{384,0},{1,129},{129,257},{257,385},{3... | collective-permute-start | bytes 786440 | tf_op jit(solution)/shard_map/ppermute | solution.py:392
  170.2 8.7 %collective-permute-done.3 = bf16[128,1024]{1,0:T(8,128)(2,1)S(1)} collective-permute-done((bf16[128,1024]{1,0:T(8,128)(2,1)S(1)}, bf16[128,1024]{1,0:T(8,128)(2,1)S(1)}, u32[]{:S(2)}, u32[]{:S(2)}) %collective-permute-start.3) | collective-permute-done | bytes 262176 | tf_op jit(solution)/shard_map/ppermute | solution.py:392
  178.9 4.0 %all-to-all-done.3.parts_ref = bf16[8,128,512]{2,1,0:T(8,128)(2,1)S(1)} async-done(((bf16[8,128,512]{2,1,0:T(8,128)(2,1)}), bf16[8,128,512]{2,1,0:T(8,128)(2,1)S(1)}, u32[]{:S(2)}, u32[]{:S(2)}) %all-to-all-start.3) | async-done | bytes 1048608 | tf_op jit(solution)/shard_map/all_to_all | solution.py:402
  182.9 1.0 shard_map.237
  (68 shorter events, 9.4 us)
Async XLA Ops:
  7.2 32.8 %copy-start = (f32[1,1024]{1,0:T(1,128)S(1)}, f32[1,1024]{1,0:T(1,128)}, u32[]{:S(2)}) copy-start(f32[1,1024]{1,0:T(1,128)} %param.28) | copy-start | bytes 12292
  8.0 1.0 copy-start.3
  8.9 0.9 copy-start.4
  9.9 0.9 copy-start.5
  10.8 0.9 copy-start.6
  11.7 0.9 copy-start.7
  14.0 17.2 %copy-start.2 = (bf16[1,128,1024]{2,1,0:T(8,128)(2,1)S(1)}, bf16[1,128,1024]{2,1,0:T(8,128)(2,1)}, u32[]{:S(2)}) copy-start(bf16[1,128,1024]{2,1,0:T(8,128)(2,1)} %param.24) | copy-start | bytes 786436
  14.0 22.5 %copy-start.10 = (f32[1,1,1,32,4096]{4,3,2,1,0:T(8,128)S(1)}, f32[1,1,1,32,4096]{4,3,2,1,0:T(8,128)}, u32[]{:S(2)}) copy-start(f32[1,1,1,32,4096]{4,3,2,1,0:T(8,128)} %param.27) | copy-start | bytes 1572868
  14.0 61.6 %all-to-all-start = ((bf16[32,88,128]{2,1,0:T(8,128)(2,1)}), bf16[32,88,128]{2,1,0:T(8,128)(2,1)S(1)}, u32[]{:S(2)}, u32[]{:S(2)}) async-start(bf16[32,88,128]{2,1,0:T(8,128)(2,1)} %shard_map.230), calls=%async_computation | async-start | bytes 1441792 | tf_op jit(solution)/shard_map/all_to_all | solution.py:316
  31.1 94.8 %all-gather.2.cloned.1.call-start = ((), (), s32[]{:S(2)}) async-start(), calls=%async_computation.4 | async-start | bytes 2228224 | tf_op jit(solution)/shard_map/all_gather | solution.py:308
  31.2 8.9 %collective-permute-start = (bf16[2,1024]{1,0:T(2,128)(2,1)S(1)}, bf16[2,1024]{1,0:T(2,128)(2,1)S(1)}, u32[]{:S(2)}, u32[]{:S(2)}) collective-permute-start(bf16[2,1024]{1,0:T(2,128)(2,1)S(1)} %slice_bitcast_fusion.2), channel_id=1, source_target_pairs={{0,4},{4,8},{8,12},{12,16},{16,20},{20,24},{24,28},{28,32},{32,36}... | collective-permute-start | bytes 12296 | tf_op jit(solution)/shard_map/ppermute | solution.py:318
  36.5 1.3 copy-start.18
  36.6 1.9 copy-start.17
  76.9 4.6 %copy-start.16 = (f32[33,32]{0,1:T(8,128)S(1)}, f32[33,32]{0,1:T(8,128)}, u32[]{:S(2)}) copy-start(f32[33,32]{0,1:T(8,128)} %constant.58.clone) | copy-start | bytes 12676
  76.9 25.6 %all-to-all-start.1 = ((bf16[4,2,512,128]{3,2,1,0:T(8,128)(2,1)}), bf16[4,2,512,128]{3,2,1,0:T(8,128)(2,1)S(1)}, u32[]{:S(2)}, u32[]{:S(2)}) async-start(bf16[4,2,512,128]{3,2,1,0:T(8,128)(2,1)} %get-tuple-element.11), calls=%async_computation.1 | async-start | bytes 2097152 | tf_op jit(solution)/shard_map/all_to_all | solution.py:335
  81.5 0.7 copy-start.15
  82.3 1.1 copy-start.8
  82.3 1.1 copy-start.12
  82.3 1.1 copy-start.13
  83.3 1.0 copy-start.9
  85.5 1.0 copy-start.11
  87.4 3.1 %copy-start.14 = (f32[32,66]{1,0:T(8,128)S(1)}, f32[32,66]{1,0:T(8,128)}, u32[]{:S(2)}) copy-start(f32[32,66]{1,0:T(8,128)} %constant.64.clone) | copy-start | bytes 25348
  88.1 12.1 %collective-permute-start.1 = (bf16[512,128]{1,0:T(8,128)(2,1)S(1)}, bf16[512,128]{1,0:T(8,128)(2,1)S(1)}, u32[]{:S(2)}, u32[]{:S(2)}) collective-permute-start(bf16[512,128]{1,0:T(8,128)(2,1)S(1)} %get-tuple-element.12.query_ref), channel_id=1, source_target_pairs={{0,16},{16,0},{1,17},{17,1},{2,18},{18,2},{3,19},{19,3},{4,20},{20... | collective-permute-start | bytes 393224 | tf_op jit(solution)/shard_map/ppermute | solution.py:334
  104.7 9.4 %collective-permute-start.2 = (bf16[544,128]{1,0:T(8,128)(2,1)S(1)}, bf16[544,128]{1,0:T(8,128)(2,1)S(1)}, u32[]{:S(2)}, u32[]{:S(2)}) collective-permute-start(bf16[544,128]{1,0:T(8,128)(2,1)S(1)} %shard_map.232), channel_id=1, source_target_pairs={{0,16},{16,0},{1,17},{17,1},{2,18},{18,2},{3,19},{19,3},{4,20},{20... | collective-permute-start | bytes 417800 | tf_op jit(solution)/shard_map/ppermute | solution.py:367
  115.1 42.4 %all-to-all-start.2 = ((bf16[32,64,128]{2,1,0:T(8,128)(2,1)}), bf16[32,64,128]{2,1,0:T(8,128)(2,1)S(1)}, u32[]{:S(2)}, u32[]{:S(2)}) async-start(bf16[32,64,128]{2,1,0:T(8,128)(2,1)} %bitcast.30), calls=%async_computation.2 | async-start | bytes 1048576 | tf_op jit(solution)/shard_map/all_to_all | solution.py:383
  157.5 1.6 copy-start.1
  160.9 22.0 %all-to-all-start.3 = ((bf16[8,128,512]{2,1,0:T(8,128)(2,1)}), bf16[8,128,512]{2,1,0:T(8,128)(2,1)S(1)}, u32[]{:S(2)}, u32[]{:S(2)}) async-start(bf16[8,128,512]{2,1,0:T(8,128)(2,1)} %bitcast.37), calls=%async_computation.3 | async-start | bytes 2097152 | tf_op jit(solution)/shard_map/all_to_all | solution.py:402
  168.2 10.6 %collective-permute-start.3 = (bf16[128,1024]{1,0:T(8,128)(2,1)S(1)}, bf16[128,1024]{1,0:T(8,128)(2,1)S(1)}, u32[]{:S(2)}, u32[]{:S(2)}) collective-permute-start(bf16[128,1024]{1,0:T(8,128)(2,1)S(1)} %shard_map.235), channel_id=1, source_target_pairs={{0,128},{128,256},{256,384},{384,0},{1,129},{129,257},{257,385},{3... | collective-permute-start | bytes 786440 | tf_op jit(solution)/shard_map/ppermute | solution.py:392
Sparse Core Ops, SparseCore 0:
  36.6 81.6 all-gather.1

commit v5 on v4

--- a/solution.py
+++ b/solution.py
@@ -67,15 +67,7 @@
     return out.reshape(-1, channels, breadth)
 
 
-def edge_short(edges, taps):
-    edges = edges.astype(F32)
-    before = jnp.pad(edges[:-1, 2:], ((1, 0), (0, 0), (0, 0)))
-    zero = taps[0] * edges[:, 0] + taps[1] * before[:, 1] + taps[2] * before[:, 0]
-    one = taps[0] * edges[:, 1] + taps[1] * edges[:, 0] + taps[2] * before[:, 1]
-    return zero, one
-
-
-def kernel_call(kernel, out_shape, scalars, arrays, scratch=(), flops=0):
+def kernel_call(kernel, out_shape, scalars, arrays, scratch=(), flops=0, grant=32):
     in_specs = [pl.BlockSpec(memory_space=pltpu.SMEM)] * len(scalars)
     in_specs += [pl.BlockSpec(memory_space=pltpu.VMEM)] * len(arrays)
     outs = out_shape if isinstance(out_shape, tuple) else (out_shape,)
@@ -86,7 +78,7 @@
         in_specs=in_specs,
         out_specs=jax.tree.map(lambda _: pl.BlockSpec(memory_space=pltpu.VMEM), out_shape),
         scratch_shapes=list(scratch),
-        compiler_params=pltpu.CompilerParams(vmem_limit_bytes=32 * 1024 * 1024),
+        compiler_params=pltpu.CompilerParams(vmem_limit_bytes=grant * 1024 * 1024),
         cost_estimate=pl.CostEstimate(flops=flops, bytes_accessed=moved, transcendentals=0),
     )(*scalars, *arrays)
 
@@ -109,9 +101,9 @@
         for ref, which in ((first_ref, 0), (value_ref, 2)):
             x = ref[:, span].astype(F32)
             shorts.append(
-                taps_ref[which, 0:1, span] * x
-                + taps_ref[which, 1:2, span] * pltpu.roll(x, 1, 0)
-                + taps_ref[which, 2:3, span] * pltpu.roll(x, 2, 0)
+                taps_ref[0, which, 0:1, span] * x
+                + taps_ref[0, which, 1:2, span] * pltpu.roll(x, 1, 0)
+                + taps_ref[0, which, 2:3, span] * pltpu.roll(x, 2, 0)
             )
             edges += [x[:2], x[rows - 2 :]]
         turned = (shorts[0] * shorts[1]).T.astype(BF16).reshape(per, channels, rows)
@@ -229,6 +221,25 @@
             pairs_ref[to, at] = block
 
 
+def product_kernel(start, mixed_ref, taps_ref, out_ref):
+    n_seq, channels, rows = out_ref.shape
+    count = n_seq * 8
+    edges = mixed_ref[:, start + channels :, :].astype(F32).reshape(count, rows).T[:channels]
+    lane = lax.broadcasted_iota(jnp.int32, (channels, count), 1)
+    kind = lane % 8
+    before = jnp.where(lane >= 8, 1.0, 0.0)
+    ahead = jnp.where(kind % 4 == 0, pltpu.roll(edges, 5, 1) * before, pltpu.roll(edges, 1, 1))
+    further = pltpu.roll(edges, 6, 1) * before
+    tap = [jnp.where(kind < 4, taps_ref[:, i : i + 1], taps_ref[:, 6 + i : 7 + i]) for i in range(3)]
+    short = tap[0] * edges + tap[1] * ahead + tap[2] * further
+    made = (short * pltpu.roll(short, count - 4, 1)).astype(BF16).astype(F32)
+    column = lax.broadcasted_iota(jnp.int32, (channels, rows), 1)
+    for at in range(n_seq):
+        turned = pltpu.roll(made, count - 8 * at, 1) if at else made
+        block = mixed_ref[at, start : start + channels, :].astype(F32)
+        out_ref[at] = jnp.where(column < 2, turned[:, :rows], block)
+
+
 def gate_kernel(start, back_ref, gate_ref, tail_ref, taps_ref, out_ref):
     rows = gate_ref.shape[0]
     lanes = 128
@@ -241,7 +252,7 @@
         one = jnp.where(row == 0, tail[1:2], pltpu.roll(x, 1, 0))
         two = jnp.where(row == 0, tail[0:1], jnp.where(row == 1, tail[1:2], pltpu.roll(x, 2, 0)))
         short = (
-            taps_ref[1, 0:1, span] * x + taps_ref[1, 1:2, span] * one + taps_ref[1, 2:3, span] * two
+            taps_ref[0:1, span] * x + taps_ref[1:2, span] * one + taps_ref[2:3, span] * two
         )
         rows_long = back_ref[group * per : (group + 1) * per, start:, :].astype(F32)
         out_ref[:, span] = (short * rows_long.reshape(lanes, rows).T).astype(BF16)
@@ -311,12 +322,23 @@
         pack_kernel,
         jax.ShapeDtypeStruct((n_seq, 3 * few + channels + 8, rows), BF16),
         (),
-        (first_stream[0], value_stream[0], taps, queries[0], attn_keys[0], attn_values[0]),
+        (first_stream[0], value_stream[0], short_taps, queries[0], attn_keys[0], attn_values[0]),
+        grant=56,
     )
     mixed = lax.all_to_all(packed, seq, 0, 0)
 
-    tail = lax.ppermute(gate_stream[0, -2:], seq, [(i, i + 1) for i in range(n_seq - 1)])
-    mixed, tail = lax.optimization_barrier((mixed, tail))
+    n_sec = lax.axis_size("section")
+    onward = [(i, (i + 1) % n_sec) for i in range(n_sec)]
+    gate = lax.ppermute(gate_stream[0], "section", onward)
+    gate_taps = lax.ppermute(taps[1], "section", onward)
+    tail = lax.ppermute(
+        gate_stream[0, -2:],
+        ("section",) + seq,
+        [(s * n_seq + i, t * n_seq + i + 1) for s, t in onward for i in range(n_seq - 1)],
+    )
+    local_taps = lax.dynamic_slice_in_dim(taps, seq_at * channels, channels, 2)
+    local_taps = local_taps.reshape(9, channels).T
+    mixed, gate, gate_taps, tail = lax.optimization_barrier((mixed, gate, gate_taps, tail))
     tables = transform_tables(n_seq, rows)
     kernel = long_filter[0, 0, 0].reshape(channels, n_seq, rows).transpose(1, 0, 2)
     kernel_spec = forward_transform(kernel, tables)
@@ -334,16 +356,14 @@
     other_query = lax.ppermute(query, "zp", swap)
     pairs = lax.all_to_all(sent_pairs, ("zq", "xh"), 0, 0)
 
-    local_taps = lax.dynamic_slice_in_dim(taps, seq_at * channels, channels, 2)
-    edges = mixed[:, 3 * few + channels :, :channels]
-    first_zero, first_one = edge_short(edges[:, :4], local_taps[0])
-    value_zero, value_one = edge_short(edges[:, 4:], local_taps[2])
-    token = lax.broadcasted_iota(jnp.int32, (1, 1, rows), 2)
-    product = mixed[:, 3 * few : 3 * few + channels]
-    product = jnp.where(token == 0, (first_zero * value_zero).astype(BF16)[:, :, None], product)
-    product = jnp.where(token == 1, (first_one * value_one).astype(BF16)[:, :, None], product)
-    product = product.astype(F32)
+    product = kernel_call(
+        functools.partial(product_kernel, 3 * few),
+        jax.ShapeDtypeStruct((n_seq, channels, rows), F32),
+        (),
+        (mixed, local_taps),
+    )
     spec = forward_transform(product, tables)
+    spec, other_query = lax.optimization_barrier((spec, other_query))
     real, imag = spec[:, :, :rows], spec[:, :, rows:]
     kernel_real, kernel_imag = kernel_spec[:, :, :rows], kernel_spec[:, :, rows:]
     joined = jnp.concatenate(
@@ -352,6 +372,7 @@
     convolved = inverse_transform(joined, tables)
     gain = lax.dynamic_slice_in_dim(skip_gain[0], seq_at * channels, channels, 0)
     long_out = (convolved + gain[None, :, None] * product).astype(BF16)
+    long_out = lax.ppermute(long_out, "section", onward)
 
     work = 2 * own_rows * n_pair * own_rows * HD
     own_delta = -pair_at * few
@@ -382,14 +403,12 @@
     )
     back = lax.all_to_all(returned.reshape(n_seq, -1, HD), seq, 0, 0)
 
-    hyena = kernel_call(
+    handed = kernel_call(
         functools.partial(gate_kernel, n_x * few),
         jax.ShapeDtypeStruct(gate_stream.shape[1:], BF16),
         (),
-        (back, gate_stream[0], tail, taps),
-    )
-    n_sec = lax.axis_size("section")
-    handed = lax.ppermute(hyena, "section", [(i, (i + 1) % n_sec) for i in range(n_sec)])
+        (back, gate, tail, gate_taps),
+    )
 
     partials = kernel_call(
         functools.partial(project_kernel, heads, few),
@@ -398,6 +417,7 @@
         (back, weight.reshape(n_z, n_tp, channels, wide)),
         (),
         2 * n_x * rows * wide * n_seq * channels * n_tp // n_x,
+        56,
     ).reshape(n_plane, rows, n_z * channels)
     partials = lax.all_to_all(partials, ("xh", "tp"), 0, 0)
     attended = kernel_call(

time: 192 us -> 196 us (1.021)
  the two profiles are of different devices: /device:TPU:2 before, /device:TPU:8 now
where the time goes in v5:
time: 196 us; the launch traced here: 195 us
  waiting for transfers between devices  93.2 us (48%)
  starting transfers between devices  59.6 us (30%)
  Pallas kernels  14.9 us (8%)
  between operations  14.5 us (7%)
  local copies, waits for them, and re-layouts  7.09 us (4%)
  matrix products  5.05 us (3%)
    all_to_all x1, waiting for transfers between devices, body(): back = lax.all_to_all(returned.reshape(n_seq, -1, HD), seq, 0, 0)  33.3 us
    all_to_all x1, waiting for transfers between devices, body(): mixed = lax.all_to_all(packed, seq, 0, 0)  28.7 us
    all_to_all x1, starting transfers between devices, body(): mixed = lax.all_to_all(packed, seq, 0, 0)  18.1 us
    pallas_call x9, Pallas kernels, kernel_call(): pl.pallas_call(kernel, out_shape=out_shape, in_specs=in_specs, out_specs=...  14.9 us
    all_to_all x1, waiting for transfers between devices, body(): partials = lax.all_to_all(partials, ('xh', 'tp'), 0, 0)  13.5 us
    ppermute x1, waiting for transfers between devices, body(): other_query = lax.ppermute(query, 'zp', swap)  11.9 us
    all_to_all x1, starting transfers between devices, body(): back = lax.all_to_all(returned.reshape(n_seq, -1, HD), seq, 0, 0)  11.3 us
    all_to_all x1, starting transfers between devices, body(): partials = lax.all_to_all(partials, ('xh', 'tp'), 0, 0)  6.38 us
  transfers between devices with their start and end apart: 11, of which 5 were waited for; matrix products, arithmetic and copies ran while one was open for 5% of the time, Pallas kernels for 4%

profile of v5, /device:TPU:8, one launch (start us, length us, event | category | flops | bytes accessed | tf_op | source)
XLA Modules:
  0.0 195.2 jit_solution(1953848825942027060)
XLA Ops:
  7.2 1.4 copy.42.taps_ref
  8.6 2.5 %shard_map.230 = bf16[32,88,128]{2,1,0:T(8,128)(2,1)} custom-call(bf16[128,1024]{1,0:T(8,128)(2,1)} %bitcast.100, bf16[128,1024]{1,0:T(8,128)(2,1)} %bitcast.101, f32[1,3,3,1024]{3,2,1,0:T(4,128)} %copy.42.taps_ref, bf16[128,512]{1,0:T(8,128)(2,1)} %bitcast.104, bf16[128,512]{1,0:T(8,128)(2,1)} %bitcast.105, bf16[128,512]{1,0:T(8,128)(2,1)} %bitcast.106), custom_call_target="tpu_custom_call" | custom-call | bytes 1675264 | tf_op jit(solution)/shard_map/pallas_call | solution.py:75
  11.1 18.1 %all-to-all-start = ((bf16[32,88,128]{2,1,0:T(8,128)(2,1)}), bf16[32,88,128]{2,1,0:T(8,128)(2,1)S(1)}, u32[]{:S(2)}, u32[]{:S(2)}) async-start(bf16[32,88,128]{2,1,0:T(8,128)(2,1)} %shard_map.230), calls=%async_computation | async-start | bytes 1441792 | tf_op jit(solution)/shard_map/all_to_all | solution.py:328
  29.3 0.7 slice_bitcast_fusion
  30.0 1.9 collective-permute-start.1
  31.9 2.6 %collective-permute-start = (bf16[128,1024]{1,0:T(8,128)(2,1)}, bf16[128,1024]{1,0:T(8,128)(2,1)S(1)}, u32[]{:S(2)}, u32[]{:S(2)}) collective-permute-start(bf16[128,1024]{1,0:T(8,128)(2,1)} %bitcast.6), channel_id=1, source_target_pairs={{0,128},{128,256},{256,384},{384,0},{1,129},{129,257},{257,385},{3... | collective-permute-start | bytes 786440 | tf_op jit(solution)/shard_map/ppermute | solution.py:332
  34.5 0.7 slice_bitcast_fusion.1
  35.2 5.4 %collective-permute-start.2 = (bf16[2,1024]{1,0:T(2,128)(2,1)S(1)}, bf16[2,1024]{1,0:T(2,128)(2,1)S(1)}, u32[]{:S(2)}, u32[]{:S(2)}) collective-permute-start(bf16[2,1024]{1,0:T(2,128)(2,1)S(1)} %slice_bitcast_fusion.1), channel_id=1, source_target_pairs={{0,132},{4,136},{8,140},{12,144},{16,148},{20,152},{24,156},{28,16... | collective-permute-start | bytes 12296 | tf_op jit(solution)/shard_map/ppermute | solution.py:334
  42.1 0.8 dynamic-slice_reduce_fusion
  43.0 28.7 %all-to-all-done.mixed_ref = bf16[32,88,128]{2,1,0:T(8,128)(2,1)S(1)} async-done(((bf16[32,88,128]{2,1,0:T(8,128)(2,1)}), bf16[32,88,128]{2,1,0:T(8,128)(2,1)S(1)}, u32[]{:S(2)}, u32[]{:S(2)}) %all-to-all-start) | async-done | bytes 720928 | tf_op jit(solution)/shard_map/all_to_all | solution.py:328
  71.7 1.1 shard_map.231
  72.8 4.3 %all-to-all-start.1 = ((bf16[4,2,512,128]{3,2,1,0:T(8,128)(2,1)}), bf16[4,2,512,128]{3,2,1,0:T(8,128)(2,1)S(1)}, u32[]{:S(2)}, u32[]{:S(2)}) async-start(bf16[4,2,512,128]{3,2,1,0:T(8,128)(2,1)} %get-tuple-element.16), calls=%async_computation.1 | async-start | bytes 2097152 | tf_op jit(solution)/shard_map/all_to_all | solution.py:357
  77.2 0.7 fusion.19
  78.3 0.7 fusion.15
  79.2 0.7 fusion.13
  80.0 2.3 %collective-permute-start.3 = (bf16[512,128]{1,0:T(8,128)(2,1)S(1)}, bf16[512,128]{1,0:T(8,128)(2,1)S(1)}, u32[]{:S(2)}, u32[]{:S(2)}) collective-permute-start(bf16[512,128]{1,0:T(8,128)(2,1)S(1)} %get-tuple-element.17.query_ref), channel_id=1, source_target_pairs={{0,16},{16,0},{1,17},{17,1},{2,18},{18,2},{3,19},{19,3},{4,20},{20... | collective-permute-start | bytes 393224 | tf_op jit(solution)/shard_map/ppermute | solution.py:356
  84.5 11.9 %collective-permute-done.3.query_ref = bf16[512,128]{1,0:T(8,128)(2,1)S(1)} collective-permute-done((bf16[512,128]{1,0:T(8,128)(2,1)S(1)}, bf16[512,128]{1,0:T(8,128)(2,1)S(1)}, u32[]{:S(2)}, u32[]{:S(2)}) %collective-permute-start.3) | collective-permute-done | bytes 131104 | tf_op jit(solution)/shard_map/ppermute | solution.py:356
  97.5 0.7 copy.59
  98.9 1.9 collective-permute-start.5
  100.9 2.1 %shard_map.233 = bf16[544,128]{1,0:T(8,128)(2,1)S(1)} custom-call(s32[1]{0:T(128)} %bitcast.9.delta_ref, bf16[512,128]{1,0:T(8,128)(2,1)S(1)} %collective-permute-done.3.query_ref, bf16[4,2,512,128]{3,2,1,0:T(8,128)(2,1)S(1)} %all-to-all-done.1.pairs_ref), custom_call_target="tpu_custom_call" | custom-call | flops 268435456 | bytes 1318912 | tf_op jit(solution)/shard_map/pallas_call | solution.py:75
  103.0 5.5 %collective-permute-start.4 = (bf16[544,128]{1,0:T(8,128)(2,1)S(1)}, bf16[544,128]{1,0:T(8,128)(2,1)S(1)}, u32[]{:S(2)}, u32[]{:S(2)}) collective-permute-start(bf16[544,128]{1,0:T(8,128)(2,1)S(1)} %shard_map.233), channel_id=1, source_target_pairs={{0,16},{16,0},{1,17},{17,1},{2,18},{18,2},{3,19},{19,3},{4,20},{20... | collective-permute-start | bytes 417800 | tf_op jit(solution)/shard_map/ppermute | solution.py:388
  108.5 2.2 %shard_map.234 = (f32[512,128]{1,0:T(8,128)S(1)}, f32[512,128]{1,0:T(8,128)S(1)}) custom-call(s32[1]{0:T(128)} %bitcast.delta_ref, bf16[512,128]{1,0:T(8,128)(2,1)S(1)} %get-tuple-element.17.query_ref, bf16[4,2,512,128]{3,2,1,0:T(8,128)(2,1)S(1)} %all-to-all-done.1.pairs_ref), custom_call_target="tpu_custom_call" | custom-call | flops 268435456 | bytes 1703936 | tf_op jit(solution)/shard_map/pallas_call | solution.py:75
  110.7 5.8 %collective-permute-done.4.got_ref = bf16[544,128]{1,0:T(8,128)(2,1)S(1)} collective-permute-done((bf16[544,128]{1,0:T(8,128)(2,1)S(1)}, bf16[544,128]{1,0:T(8,128)(2,1)S(1)}, u32[]{:S(2)}, u32[]{:S(2)}) %collective-permute-start.4) | collective-permute-done | bytes 139296 | tf_op jit(solution)/shard_map/ppermute | solution.py:388
  116.5 1.0 shard_map.235
  117.5 11.3 %all-to-all-start.2 = ((bf16[32,64,128]{2,1,0:T(8,128)(2,1)}), bf16[32,64,128]{2,1,0:T(8,128)(2,1)S(1)}, u32[]{:S(2)}, u32[]{:S(2)}) async-start(bf16[32,64,128]{2,1,0:T(8,128)(2,1)} %bitcast.19), calls=%async_computation.2 | async-start | bytes 1048576 | tf_op jit(solution)/shard_map/all_to_all | solution.py:404
  128.9 33.3 %all-to-all-done.2.back_ref = bf16[32,64,128]{2,1,0:T(8,128)(2,1)S(1)} async-done(((bf16[32,64,128]{2,1,0:T(8,128)(2,1)}), bf16[32,64,128]{2,1,0:T(8,128)(2,1)S(1)}, u32[]{:S(2)}, u32[]{:S(2)}) %all-to-all-start.2) | async-done | bytes 524320 | tf_op jit(solution)/shard_map/all_to_all | solution.py:404
  162.2 0.8 copy-done.1
  163.0 3.5 %shard_map.237 = bf16[2,4,128,512]{3,2,1,0:T(8,128)(2,1)} custom-call(bf16[32,64,128]{2,1,0:T(8,128)(2,1)} %copy-done.1, bf16[16,4,32,512]{3,2,1,0:T(8,128)(2,1)} %bitcast.97), custom_call_target="tpu_custom_call" | custom-call | flops 536870912 | bytes 3670016 | tf_op jit(solution)/shard_map/pallas_call | solution.py:75
  166.5 6.4 %all-to-all-start.3 = ((bf16[8,128,512]{2,1,0:T(8,128)(2,1)}), bf16[8,128,512]{2,1,0:T(8,128)(2,1)S(1)}, u32[]{:S(2)}, u32[]{:S(2)}) async-start(bf16[8,128,512]{2,1,0:T(8,128)(2,1)} %bitcast.92), calls=%async_computation.3 | async-start | bytes 2097152 | tf_op jit(solution)/shard_map/all_to_all | solution.py:422
  172.9 1.0 shard_map.236
  173.8 13.5 %all-to-all-done.3.parts_ref = bf16[8,128,512]{2,1,0:T(8,128)(2,1)S(1)} async-done(((bf16[8,128,512]{2,1,0:T(8,128)(2,1)}), bf16[8,128,512]{2,1,0:T(8,128)(2,1)S(1)}, u32[]{:S(2)}, u32[]{:S(2)}) %all-to-all-start.3) | async-done | bytes 1048608 | tf_op jit(solution)/shard_map/all_to_all | solution.py:422
  187.3 1.0 shard_map.238
  (53 shorter events, 6.2 us)
Async XLA Ops:
  7.2 69.9 %copy-start = (f32[1,1024]{1,0:T(1,128)S(1)}, f32[1,1024]{1,0:T(1,128)}, u32[]{:S(2)}) copy-start(f32[1,1024]{1,0:T(1,128)} %param.28) | copy-start | bytes 12292
  11.1 29.6 %copy-start.4 = (f32[1,1,1,32,4096]{4,3,2,1,0:T(8,128)S(1)}, f32[1,1,1,32,4096]{4,3,2,1,0:T(8,128)}, u32[]{:S(2)}) copy-start(f32[1,1,1,32,4096]{4,3,2,1,0:T(8,128)} %param.27) | copy-start | bytes 1572868
  11.1 60.6 %all-to-all-start = ((bf16[32,88,128]{2,1,0:T(8,128)(2,1)}), bf16[32,88,128]{2,1,0:T(8,128)(2,1)S(1)}, u32[]{:S(2)}, u32[]{:S(2)}) async-start(bf16[32,88,128]{2,1,0:T(8,128)(2,1)} %shard_map.230), calls=%async_computation | async-start | bytes 1441792 | tf_op jit(solution)/shard_map/all_to_all | solution.py:328
  29.2 99.7 %all-gather.2.cloned.1.call-start = ((), (), s32[]{:S(2)}) async-start(), calls=%async_computation.4 | async-start | bytes 2228224 | tf_op jit(solution)/shard_map/all_gather | solution.py:319
  30.0 13.0 %collective-permute-start.1 = (f32[3,1024]{1,0:T(4,128)S(1)}, f32[3,1024]{1,0:T(4,128)S(1)}, u32[]{:S(2)}, u32[]{:S(2)}) collective-permute-start(f32[3,1024]{1,0:T(4,128)S(1)} %slice_bitcast_fusion), channel_id=1, source_target_pairs={{0,128},{128,256},{256,384},{384,0},{1,129},{129,257},{257,385},{3... | collective-permute-start | bytes 36872 | tf_op jit(solution)/shard_map/ppermute | solution.py:333
  31.9 11.1 %collective-permute-start = (bf16[128,1024]{1,0:T(8,128)(2,1)}, bf16[128,1024]{1,0:T(8,128)(2,1)S(1)}, u32[]{:S(2)}, u32[]{:S(2)}) collective-permute-start(bf16[128,1024]{1,0:T(8,128)(2,1)} %bitcast.6), channel_id=1, source_target_pairs={{0,128},{128,256},{256,384},{384,0},{1,129},{129,257},{257,385},{3... | collective-permute-start | bytes 786440 | tf_op jit(solution)/shard_map/ppermute | solution.py:332
  35.2 7.8 %collective-permute-start.2 = (bf16[2,1024]{1,0:T(2,128)(2,1)S(1)}, bf16[2,1024]{1,0:T(2,128)(2,1)S(1)}, u32[]{:S(2)}, u32[]{:S(2)}) collective-permute-start(bf16[2,1024]{1,0:T(2,128)(2,1)S(1)} %slice_bitcast_fusion.1), channel_id=1, source_target_pairs={{0,132},{4,136},{8,140},{12,144},{16,148},{20,152},{24,156},{28,16... | collective-permute-start | bytes 12296 | tf_op jit(solution)/shard_map/ppermute | solution.py:334
  40.7 0.7 copy-start.12
  72.8 4.3 %copy-start.11 = (f32[33,32,1]{0,1,2:T(8,128)S(1)}, f32[33,32,1]{0,1,2:T(8,128)}, u32[]{:S(2)}) copy-start(f32[33,32,1]{0,1,2:T(8,128)} %constant.73) | copy-start | bytes 12676
  72.8 28.0 %all-to-all-start.1 = ((bf16[4,2,512,128]{3,2,1,0:T(8,128)(2,1)}), bf16[4,2,512,128]{3,2,1,0:T(8,128)(2,1)S(1)}, u32[]{:S(2)}, u32[]{:S(2)}) async-start(bf16[4,2,512,128]{3,2,1,0:T(8,128)(2,1)} %get-tuple-element.16), calls=%async_computation.1 | async-start | bytes 2097152 | tf_op jit(solution)/shard_map/all_to_all | solution.py:357
  77.2 1.1 copy-start.10
  78.3 0.9 copy-start.9
  79.1 3.1 %copy-start.6 = (f32[33,128]{1,0:T(8,128)S(1)}, f32[33,128]{1,0:T(8,128)}, u32[]{:S(2)}) copy-start(f32[33,128]{1,0:T(8,128)} %constant.70) | copy-start | bytes 50692
  79.2 3.1 %copy-start.7 = (f32[33,128]{1,0:T(8,128)S(1)}, f32[33,128]{1,0:T(8,128)}, u32[]{:S(2)}) copy-start(f32[33,128]{1,0:T(8,128)} %constant.71) | copy-start | bytes 50692
  80.0 16.3 %collective-permute-start.3 = (bf16[512,128]{1,0:T(8,128)(2,1)S(1)}, bf16[512,128]{1,0:T(8,128)(2,1)S(1)}, u32[]{:S(2)}, u32[]{:S(2)}) collective-permute-start(bf16[512,128]{1,0:T(8,128)(2,1)S(1)} %get-tuple-element.17.query_ref), channel_id=1, source_target_pairs={{0,16},{16,0},{1,17},{17,1},{2,18},{18,2},{3,19},{19,3},{4,20},{20... | collective-permute-start | bytes 393224 | tf_op jit(solution)/shard_map/ppermute | solution.py:356
  82.3 1.0 copy-start.3
  84.5 12.0 %copy-start.5 = (f32[256,256,1]{1,0,2:T(8,128)S(1)}, f32[256,256,1]{1,0,2:T(8,128)}, u32[]{:S(2)}) copy-start(f32[256,256,1]{1,0,2:T(8,128)} %constant.75) | copy-start | bytes 786436
  97.5 0.7 copy-start.8
  98.9 11.8 %collective-permute-start.5 = (bf16[32,32,128]{2,1,0:T(8,128)(2,1)S(1)}, bf16[32,32,128]{2,1,0:T(8,128)(2,1)S(1)}, u32[]{:S(2)}, u32[]{:S(2)}) collective-permute-start(bf16[32,32,128]{2,1,0:T(8,128)(2,1)S(1)} %fusion.12), channel_id=1, source_target_pairs={{0,128},{128,256},{256,384},{384,0},{1,129},{129,257},{257,385},{3... | collective-permute-start | bytes 786440 | tf_op jit(solution)/shard_map/ppermute | solution.py:375
  103.0 13.5 %collective-permute-start.4 = (bf16[544,128]{1,0:T(8,128)(2,1)S(1)}, bf16[544,128]{1,0:T(8,128)(2,1)S(1)}, u32[]{:S(2)}, u32[]{:S(2)}) collective-permute-start(bf16[544,128]{1,0:T(8,128)(2,1)S(1)} %shard_map.233), channel_id=1, source_target_pairs={{0,16},{16,0},{1,17},{17,1},{2,18},{18,2},{3,19},{19,3},{4,20},{20... | collective-permute-start | bytes 417800 | tf_op jit(solution)/shard_map/ppermute | solution.py:388
  117.5 44.6 %all-to-all-start.2 = ((bf16[32,64,128]{2,1,0:T(8,128)(2,1)}), bf16[32,64,128]{2,1,0:T(8,128)(2,1)S(1)}, u32[]{:S(2)}, u32[]{:S(2)}) async-start(bf16[32,64,128]{2,1,0:T(8,128)(2,1)} %bitcast.19), calls=%async_computation.2 | async-start | bytes 1048576 | tf_op jit(solution)/shard_map/all_to_all | solution.py:404
  162.2 0.8 copy-start.1
  166.5 6.4 %copy-start.2 = (bf16[32,64,128]{2,1,0:T(8,128)(2,1)S(1)}, bf16[32,64,128]{2,1,0:T(8,128)(2,1)}, u32[]{:S(2)}) copy-start(bf16[32,64,128]{2,1,0:T(8,128)(2,1)} %copy-done.1) | copy-start | bytes 1572868
  166.5 20.8 %all-to-all-start.3 = ((bf16[8,128,512]{2,1,0:T(8,128)(2,1)}), bf16[8,128,512]{2,1,0:T(8,128)(2,1)S(1)}, u32[]{:S(2)}, u32[]{:S(2)}) async-start(bf16[8,128,512]{2,1,0:T(8,128)(2,1)} %bitcast.92), calls=%async_computation.3 | async-start | bytes 2097152 | tf_op jit(solution)/shard_map/all_to_all | solution.py:422
Sparse Core Ops, SparseCore 0:
  40.8 79.3 all-gather.1

commit v6 on v1

v6 whole, which is shorter than its diff:
```python
import functools
import math

import jax
import jax.numpy as jnp
import numpy as np
from jax import lax
from jax.experimental import pallas as pl
from jax.experimental.pallas import tpu as pltpu
from jax.sharding import Mesh, PartitionSpec as P

HD = 128
BF16 = jnp.bfloat16
F32 = jnp.float32
HIGH = lax.Precision.HIGH


def dot(left, right, contract, precision=None):
    return lax.dot_general(
        left, right, (contract, ((), ())), precision=precision, preferred_element_type=F32
    )


def transform_tables(depth, breadth):
    full = 2 * depth
    half = depth + 1
    k = np.arange(half)
    a = np.arange(depth)
    b = np.arange(breadth)
    one = -2.0 * np.pi * np.outer(k, a) / full
    first = np.stack([np.cos(one), np.sin(one)])
    mid = -2.0 * np.pi * np.outer(k, b) / (full * breadth)
    two = -2.0 * np.pi * (np.outer(b, b) % breadth) / breadth
    cos_two, sin_two = np.cos(two), np.sin(two)
    forward = np.block([[cos_two, sin_two], [-sin_two, cos_two]])
    backward = np.block([[cos_two, -sin_two], [sin_two, cos_two]])
    weight = np.where((k == 0) | (k == depth), 1.0, 2.0) / (full * breadth)
    last = np.concatenate([np.cos(one).T * weight, np.sin(one).T * weight], axis=1)
    as32 = lambda x: np.asarray(x, np.float32)
    return as32(first), as32(np.cos(mid)), as32(np.sin(mid)), as32(forward), as32(backward), as32(last)


def forward_transform(blocks, tables):
    first, cos_mid, sin_mid, forward, _, _ = tables
    depth, channels, breadth = blocks.shape
    flat = blocks.reshape(depth, channels * breadth)
    real = dot(first[0], flat, ((1,), (0,)), HIGH).reshape(-1, channels, breadth)
    imag = dot(first[1], flat, ((1,), (0,)), HIGH).reshape(-1, channels, breadth)
    cos_mid, sin_mid = cos_mid[:, None], sin_mid[:, None]
    turned = jnp.concatenate(
        [real * cos_mid - imag * sin_mid, real * sin_mid + imag * cos_mid], axis=2
    )
    return dot(turned, forward, ((2,), (0,)), HIGH)


def inverse_transform(spectrum, tables):
    _, cos_mid, sin_mid, _, backward, last = tables
    half, channels, twice = spectrum.shape
    breadth = twice // 2
    mid = dot(spectrum, backward, ((2,), (0,)), HIGH)
    real, imag = mid[:, :, :breadth], mid[:, :, breadth:]
    cos_mid, sin_mid = cos_mid[:, None], sin_mid[:, None]
    turned = jnp.concatenate(
        [real * cos_mid + imag * sin_mid, imag * cos_mid - real * sin_mid], axis=0
    )
    out = dot(last, turned.reshape(2 * half, channels * breadth), ((1,), (0,)), HIGH)
    return out.reshape(-1, channels, breadth)


def kernel_call(kernel, out_shape, scalars, arrays, scratch=(), flops=0, grant=32):
    in_specs = [pl.BlockSpec(memory_space=pltpu.SMEM)] * len(scalars)
    in_specs += [pl.BlockSpec(memory_space=pltpu.VMEM)] * len(arrays)
    outs = out_shape if isinstance(out_shape, tuple) else (out_shape,)
    moved = sum(x.size * x.dtype.itemsize for x in (*arrays, *outs))
    return pl.pallas_call(
        kernel,
        out_shape=out_shape,
        in_specs=in_specs,
        out_specs=jax.tree.map(lambda _: pl.BlockSpec(memory_space=pltpu.VMEM), out_shape),
        scratch_shapes=list(scratch),
        compiler_params=pltpu.CompilerParams(vmem_limit_bytes=grant * 1024 * 1024),
        cost_estimate=pl.CostEstimate(flops=flops, bytes_accessed=moved, transcendentals=0),
    )(*scalars, *arrays)


def pack_kernel(x_ref, first_ref, value_ref, taps_ref, query_ref, key_ref, value_head_ref, weight_ref, rows_ref, own_ref, other_ref):
    n_tp = rows_ref.shape[0]
    rows = query_ref.shape[0]
    part = rows // n_tp
    for at, ref in enumerate((query_ref, key_ref, value_head_ref)):
        rows_ref[:, at * part : (at + 1) * part, :] = ref[...].reshape(n_tp, part, -1)
    rows_ref[:, 3 * part :, :] = weight_ref[...]
    n_z, _, lanes = own_ref.shape
    per = 2 * n_z * lanes // first_ref.shape[1]
    channels = lanes // per
    low = x_ref[0] == 0
    for group in range(2 * n_z // per):
        span = slice(group * lanes, (group + 1) * lanes)
        shorts, edges = [], []
        for ref, which in ((first_ref, 0), (value_ref, 2)):
            x = ref[:, span].astype(F32)
            shorts.append(
                taps_ref[0, which, 0:1, span] * x
                + taps_ref[0, which, 1:2, span] * pltpu.roll(x, 1, 0)
                + taps_ref[0, which, 2:3, span] * pltpu.roll(x, 2, 0)
            )
            edges += [x[:2], x[rows - 2 :]]
        turned = (shorts[0] * shorts[1]).T
        edges = jnp.concatenate(edges, axis=0)
        for at in range(per // 2):
            z_at = group * per // 2 + at
            blocks = []
            for x_at in range(2):
                j = 2 * at + x_at
                edge = pltpu.roll(edges, lanes - j * channels, 1) if j else edges
                blocks.append(jnp.concatenate([turned[j * channels : (j + 1) * channels], edge], axis=0))
            own_ref[z_at] = jnp.where(low, blocks[0], blocks[1]).astype(BF16)
            other_ref[z_at] = jnp.where(low, blocks[1], blocks[0]).astype(BF16)


def repack_kernel(x_ref, rows_ref, own_ref, got_ref, out_ref, weight_ref):
    n_tp, height, wide = rows_ref.shape
    channels = weight_ref.shape[1]
    size = height - channels
    heads = wide // HD
    for at in range(n_tp):
        for head in range(heads):
            block = rows_ref[at, :size, head * HD : (head + 1) * HD]
            out_ref[at * heads + head, :size, :] = block
    weight_ref[...] = rows_ref[:, size:, :]
    low = x_ref[0] == 0
    own, got = own_ref[...].astype(F32), got_ref[...].astype(F32)
    even = jnp.where(low, own, got).astype(BF16)
    odd = jnp.where(low, got, own).astype(BF16)
    out_ref[:, size : size + channels, :] = even[:, :channels]
    out_ref[:, size + channels : size + 2 * channels, :] = odd[:, :channels]
    out_ref[:, size + 2 * channels : size + 2 * channels + 8, :] = even[:, channels:]
    out_ref[:, size + 2 * channels + 8 :, :] = odd[:, channels:]


def split_kernel(part, mixed_ref, pairs_ref, query_ref):
    n_z = mixed_ref.shape[0]
    query_ref[...] = mixed_ref[:, :part, :].reshape(n_z * part, HD)
    for at in range(2):
        block = mixed_ref[:, (at + 1) * part : (at + 2) * part, :].reshape(n_z * part, HD)
        for to in range(pairs_ref.shape[0]):
            pairs_ref[to, at] = block


def product_kernel(start, mixed_ref, taps_ref, out_ref):
    n_seq, channels, rows = out_ref.shape
    count = n_seq * 8
    edges = mixed_ref[:, start + 2 * channels :, :].astype(F32).reshape(count, rows).T[:channels]
    lane = lax.broadcasted_iota(jnp.int32, (channels, count), 1)
    kind = lane % 8
    before = jnp.where(lane >= 8, 1.0, 0.0)
    ahead = jnp.where(kind % 4 == 0, pltpu.roll(edges, 5, 1) * before, pltpu.roll(edges, 1, 1))
    further = pltpu.roll(edges, 6, 1) * before
    tap = [jnp.where(kind < 4, taps_ref[:, i : i + 1], taps_ref[:, 6 + i : 7 + i]) for i in range(3)]
    short = tap[0] * edges + tap[1] * ahead + tap[2] * further
    made = (short * pltpu.roll(short, count - 4, 1)).astype(BF16).astype(F32)
    column = lax.broadcasted_iota(jnp.int32, (channels, rows), 1)
    for at in range(n_seq):
        turned = pltpu.roll(made, count - 8 * at, 1) if at else made
        begin = start + at % 2 * channels
        block = mixed_ref[at // 2, begin : begin + channels, :].astype(F32)
        out_ref[at] = jnp.where(column < 2, turned[:, :rows], block)


def attend_kernel(rows, delta_ref, query_ref, pairs_ref, long_ref, out_ref):
    size = 128
    n_z, height, _ = out_ref.shape
    own_rows = query_ref.shape[0]
    part = own_rows // n_z
    per = size // part
    row = lax.broadcasted_iota(jnp.int32, (size, size), 0)
    column = lax.broadcasted_iota(jnp.int32, (size, size), 1)
    q_pos = row // part * (2 * rows) + row % part
    k_pos = column // part * (2 * rows) + column % part + delta_ref[0]
    out_ref[:, part:, :] = long_ref[...]
    for tile in range(own_rows // size):
        query = query_ref[tile * size : (tile + 1) * size, :]
        parts = []
        for at in range(pairs_ref.shape[0]):
            n_tp = pairs_ref.shape[0] // 2
            allowed = k_pos + (at // n_tp * rows + at % n_tp * part) <= q_pos
            for start, stop in ((0, tile * size), (tile * size, (tile + 1) * size)):
                if start == stop:
                    continue
                keys = pairs_ref[at, 0, start:stop, :]
                scores = dot(query, keys, ((1,), (1,))) * (1.0 / math.sqrt(HD))
                if start == tile * size:
                    parts.append((jnp.where(allowed, scores, -1e30), allowed, at, start, stop))
                else:
                    parts.append((scores, None, at, start, stop))
        highest = parts[0][0].max(axis=1, keepdims=True)
        for piece in parts[1:]:
            highest = jnp.maximum(highest, piece[0].max(axis=1, keepdims=True))
        totals = jnp.zeros((size, 1), F32)
        weighted = jnp.zeros((size, HD), F32)
        for scores, allowed, at, start, stop in parts:
            probs = jnp.exp(scores - highest)
            if allowed is not None:
                probs = jnp.where(allowed, probs, 0.0)
            totals = totals + probs.sum(axis=1, keepdims=True)
            values = pairs_ref[at, 1, start:stop, :]
            weighted = weighted + dot(probs.astype(BF16), values, ((1,), (0,)))
        out = (weighted / totals).astype(BF16).reshape(per, part, HD)
        out_ref[tile * per : (tile + 1) * per, :part, :] = out


def rows_kernel(x_ref, back_ref, rows_ref, own_ref, other_ref):
    part = rows_ref.shape[1]
    channels = own_ref.shape[1]
    for head in range(back_ref.shape[0]):
        block = back_ref[head, :part, :]
        for to in range(rows_ref.shape[0]):
            rows_ref[to, :, head * HD : (head + 1) * HD] = block
    low = x_ref[0] == 0
    even = back_ref[:, part : part + channels, :].astype(F32)
    odd = back_ref[:, part + channels :, :].astype(F32)
    own_ref[...] = jnp.where(low, even, odd).astype(BF16)
    other_ref[...] = jnp.where(low, odd, even).astype(BF16)


def gate_kernel(x_ref, own_ref, got_ref, gate_ref, tail_ref, taps_ref, out_ref):
    rows = gate_ref.shape[0]
    lanes = 128
    channels = own_ref.shape[1]
    per = lanes // channels
    row = lax.broadcasted_iota(jnp.int32, (rows, lanes), 0)
    low = x_ref[0] == 0
    for group in range(gate_ref.shape[1] // lanes):
        span = slice(group * lanes, (group + 1) * lanes)
        x = gate_ref[:, span].astype(F32)
        tail = tail_ref[:, span].astype(F32)
        one = jnp.where(row == 0, tail[1:2], pltpu.roll(x, 1, 0))
        two = jnp.where(row == 0, tail[0:1], jnp.where(row == 1, tail[1:2], pltpu.roll(x, 2, 0)))
        short = taps_ref[0:1, span] * x + taps_ref[1:2, span] * one + taps_ref[2:3, span] * two
        blocks = []
        for at in range(per // 2):
            own = own_ref[group * per // 2 + at].astype(F32)
            got = got_ref[group * per // 2 + at].astype(F32)
            blocks += [jnp.where(low, own, got), jnp.where(low, got, own)]
        out_ref[:, span] = (short * jnp.concatenate(blocks, axis=0).T).astype(BF16)


def project_kernel(x_ref, rows_ref, weight_ref, own_ref, other_ref):
    half = own_ref.shape[0]
    n_z, n_tp, channels, wide = weight_ref.shape
    part = rows_ref.shape[1]
    whole = rows_ref[...].reshape(2 * half, n_tp * wide)
    out = jnp.zeros((2 * half, n_z * channels), F32)
    for at in range(n_tp):
        block = weight_ref[:, at].reshape(n_z * channels, wide)
        out = out + dot(whole[:, at * wide : (at + 1) * wide], block, ((1,), (1,)))
    low = x_ref[0] == 0
    own_ref[...] = jnp.where(low, out[:half], out[half:]).astype(BF16)
    other_ref[...] = jnp.where(low, out[half:], out[:half]).astype(BF16)


def unite_kernel(channels, x_ref, own_ref, got_ref, out_ref):
    rows, lanes = own_ref.shape[0], 128
    low = x_ref[0] == 0
    lane = lax.broadcasted_iota(jnp.int32, (rows, lanes), 1)
    for group in range(out_ref.shape[1] // lanes):
        span = slice(group // 2 * lanes, (group // 2 + 1) * lanes)
        start = group % 2 * 2 * channels
        own, got = own_ref[:, span].astype(F32), got_ref[:, span].astype(F32)
        even, odd = jnp.where(low, own, got), jnp.where(low, got, own)

        def moved(x, by):
            by = by % lanes
            return pltpu.roll(x, by, 1) if by else x

        left = jnp.where(lane < channels, moved(even, -start), moved(odd, channels - start))
        right = jnp.where(
            lane < 3 * channels, moved(even, channels - start), moved(odd, 2 * channels - start)
        )
        out_ref[:, group * lanes : (group + 1) * lanes] = jnp.where(
            lane < 2 * channels, left, right
        ).astype(BF16)


def body(
    first_stream,
    gate_stream,
    value_stream,
    short_taps,
    long_filter,
    skip_gain,
    queries,
    attn_keys,
    attn_values,
    out_weight,
):
    seq = ("z", "xh")
    n_z, n_x, n_tp = lax.axis_size("z"), lax.axis_size("xh"), lax.axis_size("tp")
    n_seq, n_plane = n_z * n_x, n_x * n_tp
    seq_at = lax.axis_index(seq)
    x_at = lax.axis_index("xh")
    x_scalar = x_at.astype(jnp.int32).reshape(1)
    rows = queries.shape[1]
    wide = queries.shape[2]
    channels = long_filter.shape[3]
    part = rows // n_tp
    own_rows = n_z * part
    taps = short_taps[0]
    swap = [(0, 1), (1, 0)]
    shape = jax.ShapeDtypeStruct

    sent_rows, own, other = kernel_call(
        pack_kernel,
        (
            shape((n_tp, 3 * part + channels, wide), BF16),
            shape((n_z, channels + 8, rows), BF16),
            shape((n_z, channels + 8, rows), BF16),
        ),
        (x_scalar,),
        (
            first_stream[0],
            value_stream[0],
            short_taps,
            queries[0],
            attn_keys[0],
            attn_values[0],
            out_weight[0].transpose(1, 2, 0),
        ),
        grant=56,
    )
    got = lax.ppermute(other, "xh", swap)
    got_rows = lax.all_to_all(sent_rows, "tp", 0, 0)
    packed, weight = kernel_call(
        repack_kernel,
        (
            shape((n_z, 3 * part + 2 * channels + 16, HD), BF16),
            shape((n_tp, channels, wide), BF16),
        ),
        (x_scalar,),
        (got_rows, own, got),
    )
    mixed = lax.all_to_all(packed, "z", 0, 0)
    weight = lax.all_gather(weight, "z")

    n_sec = lax.axis_size("section")
    onward = [(i, (i + 1) % n_sec) for i in range(n_sec)]
    gate = lax.ppermute(gate_stream[0], "section", onward)
    gate_taps = lax.ppermute(taps[1], "section", onward)
    tail = lax.ppermute(
        gate_stream[0, -2:],
        ("section",) + seq,
        [(s * n_seq + i, t * n_seq + i + 1) for s, t in onward for i in range(n_seq - 1)],
    )
    local_taps = lax.dynamic_slice_in_dim(taps, seq_at * channels, channels, 2)
    local_taps = local_taps.reshape(9, channels).T
    tables = transform_tables(n_seq, rows)
    kernel = long_filter[0, 0, 0].reshape(channels, n_seq, rows).transpose(1, 0, 2)
    kernel_spec = forward_transform(kernel, tables)
    mixed, gate, gate_taps, tail, local_taps, kernel_spec = lax.optimization_barrier(
        (mixed, gate, gate_taps, tail, local_taps, kernel_spec)
    )

    sent_pairs, query = kernel_call(
        functools.partial(split_kernel, part),
        (shape((n_plane, 2, own_rows, HD), BF16), shape((own_rows, HD), BF16)),
        (),
        (mixed,),
    )
    pairs = lax.all_to_all(sent_pairs, ("xh", "tp"), 0, 0)

    product = kernel_call(
        functools.partial(product_kernel, 3 * part),
        shape((n_seq, channels, rows), F32),
        (),
        (mixed, local_taps),
    )
    spec = forward_transform(product, tables)
    real, imag = spec[:, :, :rows], spec[:, :, rows:]
    kernel_real, kernel_imag = kernel_spec[:, :, :rows], kernel_spec[:, :, rows:]
    joined = jnp.concatenate(
        [real * kernel_real - imag * kernel_imag, real * kernel_imag + imag * kernel_real], axis=2
    )
    convolved = inverse_transform(joined, tables)
    gain = lax.dynamic_slice_in_dim(skip_gain[0], seq_at * channels, channels, 0)
    long_out = (convolved + gain[None, :, None] * product).astype(BF16)

    delta = -(x_at * rows + lax.axis_index("tp") * part)
    returned = kernel_call(
        functools.partial(attend_kernel, rows),
        shape((n_z, part + n_x * channels, HD), BF16),
        (delta.astype(jnp.int32).reshape(1),),
        (query, pairs, long_out.reshape(n_z, n_x * channels, rows)),
        (),
        4 * own_rows * n_plane * own_rows * HD,
    )
    back = lax.all_to_all(returned, "z", 0, 0)
    back, weight = lax.optimization_barrier((back, weight))

    plane_rows, own_long, other_long = kernel_call(
        rows_kernel,
        (
            shape((n_plane, part, n_z * HD), BF16),
            shape((n_z, channels, rows), BF16),
            shape((n_z, channels, rows), BF16),
        ),
        (x_scalar,),
        (back,),
    )
    plane_rows = lax.all_to_all(plane_rows, ("xh", "tp"), 0, 0)
    own_long = lax.ppermute(own_long, "section", onward)
    got_long = lax.ppermute(
        other_long, ("section", "xh"), [(2 * s + x, 2 * t + 1 - x) for s, t in onward for x in range(2)]
    )
    handed = kernel_call(
        gate_kernel,
        shape(gate_stream.shape[1:], BF16),
        (x_scalar,),
        (own_long, got_long, gate, tail, gate_taps),
    )
    own_out, other_out = kernel_call(
        project_kernel,
        (shape((rows, n_z * channels), BF16),) * 2,
        (x_scalar,),
        (plane_rows, weight),
        (),
        4 * rows * n_tp * wide * n_z * channels,
    )
    got_out = lax.ppermute(other_out, "xh", swap)
    attended = kernel_call(
        functools.partial(unite_kernel, channels),
        shape(handed.shape, BF16),
        (x_scalar,),
        (own_out, got_out),
    )
    return (handed[None], attended[None])


def solution(mesh):
    n_sec, n_seq, n_tp = (mesh.shape[name] for name in ("section", "seq", "tp"))
    finer = Mesh(mesh.devices.reshape(n_sec, n_seq // 2, 2, n_tp), ("section", "z", "xh", "tp"))
    seq = ("z", "xh")
    placed = (
        P("section", seq, "tp"),
        P("section", seq, "tp"),
        P("section", seq, "tp"),
        P("section", None, None, "tp"),
        P("section", "tp", seq, None, None),
        P("section", "tp"),
        P("section", seq, "tp"),
        P("section", seq, "tp"),
        P("section", seq, "tp"),
        P("section", "tp", None, seq),
    )
    return jax.shard_map(
        body,
        mesh=finer,
        in_specs=placed,
        out_specs=(P("section", seq, "tp"), P("section", seq, "tp")),
        check_vma=False,
    )
```

time: 197 us -> 191 us (0.970)
  the two profiles are of different devices: /device:TPU:2 before, /device:TPU:32 now
where the time goes in v6:
time: 191 us; the launch traced here: 190 us
  starting transfers between devices  72.9 us (38%)
  waiting for transfers between devices  65.7 us (34%)
  Pallas kernels  14.5 us (8%)
  between operations  14.5 us (8%)
  local copies, waits for them, and re-layouts  12.6 us (7%)
  matrix products  7.27 us (4%)
  other arithmetic  2.63 us (1%)
    all_to_all x1, waiting for transfers between devices, body(): back = lax.all_to_all(returned, 'z', 0, 0)  19.6 us
    all_to_all x1, starting transfers between devices, body(): back = lax.all_to_all(returned, 'z', 0, 0)  15.7 us
    all_to_all x1, waiting for transfers between devices, body(): mixed = lax.all_to_all(packed, 'z', 0, 0)  15.5 us
    all_to_all x1, starting transfers between devices, body(): mixed = lax.all_to_all(packed, 'z', 0, 0)  15.2 us
    pallas_call x9, Pallas kernels, kernel_call(): pl.pallas_call(kernel, out_shape=out_shape, in_specs=in_specs, out_specs=...  14.5 us
    all_to_all x1, waiting for transfers between devices, body(): pairs = lax.all_to_all(sent_pairs, ('xh', 'tp'), 0, 0)  11 us
    unnamed x51, local copies, waits for them, and re-layouts  9.5 us
    all_to_all x1, waiting for transfers between devices, body(): plane_rows = lax.all_to_all(plane_rows, ('xh', 'tp'), 0, 0)  7.46 us
  transfers between devices with their start and end apart: 13, of which 9 were waited for; matrix products, arithmetic and copies ran while one was open for 7% of the time, Pallas kernels for 5%

profile of v6, /device:TPU:32, one launch (start us, length us, event | category | flops | bytes accessed | tf_op | source)
XLA Modules:
  0.0 190.0 jit_solution(5634679754436403117)
XLA Ops:
  7.2 1.4 copy.47.taps_ref
  8.6 2.6 %shard_map.230 = (bf16[4,128,512]{2,1,0:T(8,128)(2,1)}, bf16[16,40,128]{2,1,0:T(8,128)(2,1)}, bf16[16,40,128]{2,1,0:T(8,128)(2,1)}) custom-call(s32[1]{0:T(128)} %bitcast.x_ref, bf16[128,1024]{1,0:T(8,128)(2,1)} %bitcast.98, bf16[128,1024]{1,0:T(8,128)(2,1)} %bitcast.99, f32[1,3,3,1024]{3,2,1,0:T(4,128)} %copy.47.taps_ref, bf16[128,512]{1,0:T(8,128)(2,1)} %bitcast.101, ...), custom_call_target="tpu_custom_call" | custom-call | bytes 1937408 | tf_op jit(solution)/shard_map/pallas_call | solution.py:75
  11.2 4.6 %all-to-all-start = ((bf16[4,128,512]{2,1,0:T(8,128)(2,1)}), bf16[4,128,512]{2,1,0:T(8,128)(2,1)S(1)}, u32[]{:S(2)}, u32[]{:S(2)}) async-start(bf16[4,128,512]{2,1,0:T(8,128)(2,1)} %get-tuple-element.22), calls=%async_computation | async-start | bytes 1048576 | tf_op jit(solution)/shard_map/all_to_all | solution.py:332
  15.8 4.9 %collective-permute-start = (bf16[16,40,128]{2,1,0:T(8,128)(2,1)}, bf16[16,40,128]{2,1,0:T(8,128)(2,1)S(1)}, u32[]{:S(2)}, u32[]{:S(2)}) collective-permute-start(bf16[16,40,128]{2,1,0:T(8,128)(2,1)} %get-tuple-element.24), channel_id=1, source_target_pairs={{0,4},{4,0},{1,5},{5,1},{2,6},{6,2},{3,7},{7,3},{8,12},{12,8},{9,1... | collective-permute-start | bytes 491528 | tf_op jit(solution)/shard_map/ppermute | solution.py:331
  20.7 4.3 %collective-permute-done.got_ref = bf16[16,40,128]{2,1,0:T(8,128)(2,1)S(1)} collective-permute-done((bf16[16,40,128]{2,1,0:T(8,128)(2,1)}, bf16[16,40,128]{2,1,0:T(8,128)(2,1)S(1)}, u32[]{:S(2)}, u32[]{:S(2)}) %collective-permute-start) | collective-permute-done | bytes 163872 | tf_op jit(solution)/shard_map/ppermute | solution.py:331
  26.2 1.0 shard_map.231
  27.2 15.2 %all-to-all-start.1 = ((bf16[16,176,128]{2,1,0:T(8,128)(2,1)}), bf16[16,176,128]{2,1,0:T(8,128)(2,1)S(1)}, u32[]{:S(2)}, u32[]{:S(2)}) async-start(bf16[16,176,128]{2,1,0:T(8,128)(2,1)} %get-tuple-element.25), calls=%async_computation.1 | async-start | bytes 1441792 | tf_op jit(solution)/shard_map/all_to_all | solution.py:342
  43.2 1.9 %collective-permute-start.2 = (f32[3,1024]{1,0:T(4,128)S(1)}, f32[3,1024]{1,0:T(4,128)S(1)}, u32[]{:S(2)}, u32[]{:S(2)}) collective-permute-start(f32[3,1024]{1,0:T(4,128)S(1)} %slice_bitcast_fusion), channel_id=1, source_target_pairs={{0,128},{128,256},{256,384},{384,0},{1,129},{129,257},{257,385},{3... | collective-permute-start | bytes 36872 | tf_op jit(solution)/shard_map/ppermute | solution.py:348
  45.1 3.5 %collective-permute-start.1 = (bf16[128,1024]{1,0:T(8,128)(2,1)S(1)}, bf16[128,1024]{1,0:T(8,128)(2,1)S(1)}, u32[]{:S(2)}, u32[]{:S(2)}) collective-permute-start(bf16[128,1024]{1,0:T(8,128)(2,1)S(1)} %bitcast.105), channel_id=1, source_target_pairs={{0,128},{128,256},{256,384},{384,0},{1,129},{129,257},{257,385},{3... | collective-permute-start | bytes 786440 | tf_op jit(solution)/shard_map/ppermute | solution.py:347
  48.6 4.3 %collective-permute-start.3 = (bf16[2,1024]{1,0:T(2,128)(2,1)S(1)}, bf16[2,1024]{1,0:T(2,128)(2,1)S(1)}, u32[]{:S(2)}, u32[]{:S(2)}) collective-permute-start(bf16[2,1024]{1,0:T(2,128)(2,1)S(1)} %slice_bitcast_fusion.1), channel_id=1, source_target_pairs={{0,132},{4,136},{8,140},{12,144},{16,148},{20,152},{24,156},{28,16... | collective-permute-start | bytes 12296 | tf_op jit(solution)/shard_map/ppermute | solution.py:349
  55.9 1.8 fusion.4
  58.7 1.6 collective-permute-done.3.tail_ref
  61.6 15.5 %all-to-all-done.1.mixed_ref = bf16[16,176,128]{2,1,0:T(8,128)(2,1)S(1)} async-done(((bf16[16,176,128]{2,1,0:T(8,128)(2,1)}), bf16[16,176,128]{2,1,0:T(8,128)(2,1)S(1)}, u32[]{:S(2)}, u32[]{:S(2)}) %all-to-all-start.1) | async-done | bytes 720928 | tf_op jit(solution)/shard_map/all_to_all | solution.py:342
  79.0 1.6 shard_map.232
  81.7 6.8 %all-to-all-start.2 = ((bf16[8,2,512,128]{3,2,1,0:T(8,128)(2,1)}), bf16[8,2,512,128]{3,2,1,0:T(8,128)(2,1)S(1)}, u32[]{:S(2)}, u32[]{:S(2)}) async-start(bf16[8,2,512,128]{3,2,1,0:T(8,128)(2,1)} %get-tuple-element.28), calls=%async_computation.2 | async-start | bytes 4194304 | tf_op jit(solution)/shard_map/all_to_all | solution.py:369
  88.5 1.8 fusion.6
  93.6 1.2 fusion
  96.9 11.0 %all-to-all-done.2.pairs_ref = bf16[8,2,512,128]{3,2,1,0:T(8,128)(2,1)S(1)} async-done(((bf16[8,2,512,128]{3,2,1,0:T(8,128)(2,1)}), bf16[8,2,512,128]{3,2,1,0:T(8,128)(2,1)S(1)}, u32[]{:S(2)}, u32[]{:S(2)}) %all-to-all-start.2) | async-done | bytes 2097184 | tf_op jit(solution)/shard_map/all_to_all | solution.py:369
  107.9 4.3 %shard_map.234 = bf16[16,96,128]{2,1,0:T(8,128)(2,1)} custom-call(s32[1]{0:T(128)} %bitcast.1.delta_ref, bf16[512,128]{1,0:T(8,128)(2,1)S(1)} %get-tuple-element.27.query_ref, bf16[8,2,512,128]{3,2,1,0:T(8,128)(2,1)S(1)} %all-to-all-done.2.pairs_ref, bf16[16,64,128]{2,1,0:T(8,128)(2,1)S(1)} %bitcast.85), custom_call_target="tpu_custom_call" | custom-call | flops 1073741824 | bytes 2883584 | tf_op jit(solution)/shard_map/pallas_call | solution.py:75
  112.2 15.7 %all-to-all-start.3 = ((bf16[16,96,128]{2,1,0:T(8,128)(2,1)}), bf16[16,96,128]{2,1,0:T(8,128)(2,1)S(1)}, u32[]{:S(2)}, u32[]{:S(2)}) async-start(bf16[16,96,128]{2,1,0:T(8,128)(2,1)} %shard_map.234), calls=%async_computation.3 | async-start | bytes 786432 | tf_op jit(solution)/shard_map/all_to_all | solution.py:396
  127.9 2.7 %all-gather.3.cloned.1.call-done = bf16[64,32,512]{2,1,0:T(8,128)(2,1)} async-done(((bf16[4,32,512]{2,1,0:T(8,128)(2,1)}), bf16[64,32,512]{2,1,0:T(8,128)(2,1)}) %all-gather.3.cloned.1.call-update) | async-done | bytes 2097168 | tf_op jit(solution)/shard_map/all_gather | solution.py:343
  130.6 19.6 %all-to-all-done.3.back_ref = bf16[16,96,128]{2,1,0:T(8,128)(2,1)S(1)} async-done(((bf16[16,96,128]{2,1,0:T(8,128)(2,1)}), bf16[16,96,128]{2,1,0:T(8,128)(2,1)S(1)}, u32[]{:S(2)}, u32[]{:S(2)}) %all-to-all-start.3) | async-done | bytes 393248 | tf_op jit(solution)/shard_map/all_to_all | solution.py:396
  150.2 0.9 shard_map.235
  151.1 1.0 copy-done.2
  152.7 4.3 %all-to-all-start.4 = ((bf16[8,32,2048]{2,1,0:T(8,128)(2,1)}), bf16[8,32,2048]{2,1,0:T(8,128)(2,1)S(1)}, u32[]{:S(2)}, u32[]{:S(2)}) async-start(bf16[8,32,2048]{2,1,0:T(8,128)(2,1)} %copy-done.2), calls=%async_computation.4 | async-start | bytes 2097152 | tf_op jit(solution)/shard_map/all_to_all | solution.py:409
  157.1 1.9 %collective-permute-start.4 = (bf16[16,32,128]{2,1,0:T(8,128)(2,1)}, bf16[16,32,128]{2,1,0:T(8,128)(2,1)S(1)}, u32[]{:S(2)}, u32[]{:S(2)}) collective-permute-start(bf16[16,32,128]{2,1,0:T(8,128)(2,1)} %get-tuple-element.33), channel_id=1, source_target_pairs={{0,128},{128,256},{256,384},{384,0},{1,129},{129,257},{257,385},{3... | collective-permute-start | bytes 393224 | tf_op jit(solution)/shard_map/ppermute | solution.py:410
  159.0 6.6 %collective-permute-start.5 = (bf16[16,32,128]{2,1,0:T(8,128)(2,1)}, bf16[16,32,128]{2,1,0:T(8,128)(2,1)}, u32[]{:S(2)}, u32[]{:S(2)}) collective-permute-start(bf16[16,32,128]{2,1,0:T(8,128)(2,1)} %copy-done.8), channel_id=1, source_target_pairs={{0,132},{4,128},{128,260},{132,256},{256,388},{260,384},{384,4},{3... | collective-permute-start | bytes 393224 | tf_op jit(solution)/shard_map/ppermute | solution.py:411
  165.6 7.5 %all-to-all-done.4.rows_ref = bf16[8,32,2048]{2,1,0:T(8,128)(2,1)S(1)} async-done(((bf16[8,32,2048]{2,1,0:T(8,128)(2,1)}), bf16[8,32,2048]{2,1,0:T(8,128)(2,1)S(1)}, u32[]{:S(2)}, u32[]{:S(2)}) %all-to-all-start.4) | async-done | bytes 1048608 | tf_op jit(solution)/shard_map/all_to_all | solution.py:409
  173.8 3.1 %collective-permute-start.6 = (bf16[128,512]{1,0:T(8,128)(2,1)S(1)}, bf16[128,512]{1,0:T(8,128)(2,1)S(1)}, u32[]{:S(2)}, u32[]{:S(2)}) collective-permute-start(bf16[128,512]{1,0:T(8,128)(2,1)S(1)} %get-tuple-element.41), channel_id=1, source_target_pairs={{0,4},{4,0},{1,5},{5,1},{2,6},{6,2},{3,7},{7,3},{8,12},{12,8},{9,1... | collective-permute-start | bytes 393224 | tf_op jit(solution)/shard_map/ppermute | solution.py:428
  177.0 1.9 shard_map.236
  178.9 3.3 %collective-permute-done.6.got_ref = bf16[128,512]{1,0:T(8,128)(2,1)S(1)} collective-permute-done((bf16[128,512]{1,0:T(8,128)(2,1)S(1)}, bf16[128,512]{1,0:T(8,128)(2,1)S(1)}, u32[]{:S(2)}, u32[]{:S(2)}) %collective-permute-start.6) | collective-permute-done | bytes 131104 | tf_op jit(solution)/shard_map/ppermute | solution.py:428
  182.2 1.0 shard_map.238
  (81 shorter events, 16.7 us)
Async XLA Ops:
  7.2 50.6 %copy-start = (f32[1,1024]{1,0:T(1,128)S(1)}, f32[1,1024]{1,0:T(1,128)}, u32[]{:S(2)}) copy-start(f32[1,1024]{1,0:T(1,128)} %param.28) | copy-start | bytes 12292
  11.2 33.9 %copy-start.21 = (bf16[1,128,1024]{2,1,0:T(8,128)(2,1)S(1)}, bf16[1,128,1024]{2,1,0:T(8,128)(2,1)}, u32[]{:S(2)}) copy-start(bf16[1,128,1024]{2,1,0:T(8,128)(2,1)} %param.24) | copy-start | bytes 786436
  11.2 41.7 %copy-start.12 = (f32[1,1,1,32,4096]{4,3,2,1,0:T(8,128)S(1)}, f32[1,1,1,32,4096]{4,3,2,1,0:T(8,128)}, u32[]{:S(2)}) copy-start(f32[1,1,1,32,4096]{4,3,2,1,0:T(8,128)} %param.27) | copy-start | bytes 1572868
  11.2 14.1 %all-to-all-start = ((bf16[4,128,512]{2,1,0:T(8,128)(2,1)}), bf16[4,128,512]{2,1,0:T(8,128)(2,1)S(1)}, u32[]{:S(2)}, u32[]{:S(2)}) async-start(bf16[4,128,512]{2,1,0:T(8,128)(2,1)} %get-tuple-element.22), calls=%async_computation | async-start | bytes 1048576 | tf_op jit(solution)/shard_map/all_to_all | solution.py:332
  15.8 9.3 %collective-permute-start = (bf16[16,40,128]{2,1,0:T(8,128)(2,1)}, bf16[16,40,128]{2,1,0:T(8,128)(2,1)S(1)}, u32[]{:S(2)}, u32[]{:S(2)}) collective-permute-start(bf16[16,40,128]{2,1,0:T(8,128)(2,1)} %get-tuple-element.24), channel_id=1, source_target_pairs={{0,4},{4,0},{1,5},{5,1},{2,6},{6,2},{3,7},{7,3},{8,12},{12,8},{9,1... | collective-permute-start | bytes 491528 | tf_op jit(solution)/shard_map/ppermute | solution.py:331
  25.2 0.9 copy-start.5
  27.2 50.0 %all-to-all-start.1 = ((bf16[16,176,128]{2,1,0:T(8,128)(2,1)}), bf16[16,176,128]{2,1,0:T(8,128)(2,1)S(1)}, u32[]{:S(2)}, u32[]{:S(2)}) async-start(bf16[16,176,128]{2,1,0:T(8,128)(2,1)} %get-tuple-element.25), calls=%async_computation.1 | async-start | bytes 1441792 | tf_op jit(solution)/shard_map/all_to_all | solution.py:342
  42.4 11.0 %copy-start.20 = (f32[33,32,1]{0,1,2:T(8,128)S(1)}, f32[33,32,1]{0,1,2:T(8,128)}, u32[]{:S(2)}) copy-start(f32[33,32,1]{0,1,2:T(8,128)} %constant.59) | copy-start | bytes 12676
  42.4 88.2 %all-gather.3.cloned.1.call-start = ((), (), s32[]{:S(2)}) async-start(), calls=%async_computation.5 | async-start | bytes 2228224 | tf_op jit(solution)/shard_map/all_gather | solution.py:343
  43.2 17.2 %collective-permute-start.2 = (f32[3,1024]{1,0:T(4,128)S(1)}, f32[3,1024]{1,0:T(4,128)S(1)}, u32[]{:S(2)}, u32[]{:S(2)}) collective-permute-start(f32[3,1024]{1,0:T(4,128)S(1)} %slice_bitcast_fusion), channel_id=1, source_target_pairs={{0,128},{128,256},{256,384},{384,0},{1,129},{129,257},{257,385},{3... | collective-permute-start | bytes 36872 | tf_op jit(solution)/shard_map/ppermute | solution.py:348
  45.1 15.8 %collective-permute-start.1 = (bf16[128,1024]{1,0:T(8,128)(2,1)S(1)}, bf16[128,1024]{1,0:T(8,128)(2,1)S(1)}, u32[]{:S(2)}, u32[]{:S(2)}) collective-permute-start(bf16[128,1024]{1,0:T(8,128)(2,1)S(1)} %bitcast.105), channel_id=1, source_target_pairs={{0,128},{128,256},{256,384},{384,0},{1,129},{129,257},{257,385},{3... | collective-permute-start | bytes 786440 | tf_op jit(solution)/shard_map/ppermute | solution.py:347
  48.6 11.7 %collective-permute-start.3 = (bf16[2,1024]{1,0:T(2,128)(2,1)S(1)}, bf16[2,1024]{1,0:T(2,128)(2,1)S(1)}, u32[]{:S(2)}, u32[]{:S(2)}) collective-permute-start(bf16[2,1024]{1,0:T(2,128)(2,1)S(1)} %slice_bitcast_fusion.1), channel_id=1, source_target_pairs={{0,132},{4,136},{8,140},{12,144},{16,148},{20,152},{24,156},{28,16... | collective-permute-start | bytes 12296 | tf_op jit(solution)/shard_map/ppermute | solution.py:349
  53.0 1.1 copy-start.14
  53.0 1.1 copy-start.15
  53.0 1.1 copy-start.19
  55.0 1.0 copy-start.10
  57.7 19.8 %copy-start.18 = (f32[33,32]{0,1:T(8,128)S(1)}, f32[33,32]{0,1:T(8,128)}, u32[]{:S(2)}) copy-start(f32[33,32]{0,1:T(8,128)} %constant.40.clone) | copy-start | bytes 12676
  77.1 1.1 copy-start.17
  81.7 26.2 %all-to-all-start.2 = ((bf16[8,2,512,128]{3,2,1,0:T(8,128)(2,1)}), bf16[8,2,512,128]{3,2,1,0:T(8,128)(2,1)S(1)}, u32[]{:S(2)}, u32[]{:S(2)}) async-start(bf16[8,2,512,128]{3,2,1,0:T(8,128)(2,1)} %get-tuple-element.28), calls=%async_computation.2 | async-start | bytes 4194304 | tf_op jit(solution)/shard_map/all_to_all | solution.py:369
  90.3 1.0 copy-start.11
  91.3 1.2 copy-start.9
  92.7 1.0 copy-start.13
  95.4 0.7 copy-start.16
  112.2 38.0 %all-to-all-start.3 = ((bf16[16,96,128]{2,1,0:T(8,128)(2,1)}), bf16[16,96,128]{2,1,0:T(8,128)(2,1)S(1)}, u32[]{:S(2)}, u32[]{:S(2)}) async-start(bf16[16,96,128]{2,1,0:T(8,128)(2,1)} %shard_map.234), calls=%async_computation.3 | async-start | bytes 786432 | tf_op jit(solution)/shard_map/all_to_all | solution.py:396
  150.2 22.9 %copy-start.1 = (bf16[64,32,512]{2,1,0:T(8,128)(2,1)S(1)}, bf16[64,32,512]{2,1,0:T(8,128)(2,1)}, u32[]{:S(2)}) copy-start(bf16[64,32,512]{2,1,0:T(8,128)(2,1)} %all-gather.3.cloned.1.call-done) | copy-start | bytes 6291460
  151.1 1.0 copy-start.2
  152.7 20.3 %all-to-all-start.4 = ((bf16[8,32,2048]{2,1,0:T(8,128)(2,1)}), bf16[8,32,2048]{2,1,0:T(8,128)(2,1)S(1)}, u32[]{:S(2)}, u32[]{:S(2)}) async-start(bf16[8,32,2048]{2,1,0:T(8,128)(2,1)} %copy-done.2), calls=%async_computation.4 | async-start | bytes 2097152 | tf_op jit(solution)/shard_map/all_to_all | solution.py:409
  157.1 19.9 %collective-permute-start.4 = (bf16[16,32,128]{2,1,0:T(8,128)(2,1)}, bf16[16,32,128]{2,1,0:T(8,128)(2,1)S(1)}, u32[]{:S(2)}, u32[]{:S(2)}) collective-permute-start(bf16[16,32,128]{2,1,0:T(8,128)(2,1)} %get-tuple-element.33), channel_id=1, source_target_pairs={{0,128},{128,256},{256,384},{384,0},{1,129},{129,257},{257,385},{3... | collective-permute-start | bytes 393224 | tf_op jit(solution)/shard_map/ppermute | solution.py:410
  159.0 18.0 %copy-start.4 = (bf16[128,1024]{1,0:T(8,128)(2,1)S(1)}, bf16[128,1024]{1,0:T(8,128)(2,1)}, u32[]{:S(2)}) copy-start(bf16[128,1024]{1,0:T(8,128)(2,1)} %copy-done.3) | copy-start | bytes 786436
  159.0 18.0 %collective-permute-start.5 = (bf16[16,32,128]{2,1,0:T(8,128)(2,1)}, bf16[16,32,128]{2,1,0:T(8,128)(2,1)}, u32[]{:S(2)}, u32[]{:S(2)}) collective-permute-start(bf16[16,32,128]{2,1,0:T(8,128)(2,1)} %copy-done.8), channel_id=1, source_target_pairs={{0,132},{4,128},{128,260},{132,256},{256,388},{260,384},{384,4},{3... | collective-permute-start | bytes 393224 | tf_op jit(solution)/shard_map/ppermute | solution.py:411
  173.1 3.9 %copy-start.7 = (f32[3,1024]{1,0:T(4,128)S(1)}, f32[3,1024]{1,0:T(4,128)}, u32[]{:S(2)}) copy-start(f32[3,1024]{1,0:T(4,128)} %copy-done.6) | copy-start | bytes 36868
  173.8 8.4 %collective-permute-start.6 = (bf16[128,512]{1,0:T(8,128)(2,1)S(1)}, bf16[128,512]{1,0:T(8,128)(2,1)S(1)}, u32[]{:S(2)}, u32[]{:S(2)}) collective-permute-start(bf16[128,512]{1,0:T(8,128)(2,1)S(1)} %get-tuple-element.41), channel_id=1, source_target_pairs={{0,4},{4,0},{1,5},{5,1},{2,6},{6,2},{3,7},{7,3},{8,12},{12,8},{9,1... | collective-permute-start | bytes 393224 | tf_op jit(solution)/shard_map/ppermute | solution.py:428
  (3 other events, 2.0 us)
Sparse Core Ops, SparseCore 0:
  58.9 71.7 all-gather.2

commit v7 on v6

--- a/solution.py
+++ b/solution.py
@@ -12,71 +12,71 @@
 HD = 128
 BF16 = jnp.bfloat16
 F32 = jnp.float32
-HIGH = lax.Precision.HIGH
-
-
-def dot(left, right, contract, precision=None):
-    return lax.dot_general(
-        left, right, (contract, ((), ())), precision=precision, preferred_element_type=F32
-    )
+
+
+def dot(left, right, contract):
+    return lax.dot_general(left, right, (contract, ((), ())), preferred_element_type=F32)
 
 
 def transform_tables(depth, breadth):
     full = 2 * depth
-    half = depth + 1
-    k = np.arange(half)
-    a = np.arange(depth)
+    half = -(-(depth + 1) // 8) * 8
+    k = np.arange(depth + 1)
     b = np.arange(breadth)
-    one = -2.0 * np.pi * np.outer(k, a) / full
-    first = np.stack([np.cos(one), np.sin(one)])
-    mid = -2.0 * np.pi * np.outer(k, b) / (full * breadth)
+    one = -2.0 * np.pi * np.outer(k, np.arange(depth)) / full
+    first = np.zeros((2 * half, depth))
+    first[: depth + 1], first[half : half + depth + 1] = np.cos(one), np.sin(one)
+    angle = -2.0 * np.pi * np.outer(k, b) / (full * breadth)
+    mid = np.zeros((2, half, breadth))
+    mid[0, : depth + 1], mid[1, : depth + 1] = np.cos(angle), np.sin(angle)
     two = -2.0 * np.pi * (np.outer(b, b) % breadth) / breadth
     cos_two, sin_two = np.cos(two), np.sin(two)
-    forward = np.block([[cos_two, sin_two], [-sin_two, cos_two]])
-    backward = np.block([[cos_two, -sin_two], [sin_two, cos_two]])
     weight = np.where((k == 0) | (k == depth), 1.0, 2.0) / (full * breadth)
-    last = np.concatenate([np.cos(one).T * weight, np.sin(one).T * weight], axis=1)
-    as32 = lambda x: np.asarray(x, np.float32)
-    return as32(first), as32(np.cos(mid)), as32(np.sin(mid)), as32(forward), as32(backward), as32(last)
-
-
-def forward_transform(blocks, tables):
-    first, cos_mid, sin_mid, forward, _, _ = tables
-    depth, channels, breadth = blocks.shape
-    flat = blocks.reshape(depth, channels * breadth)
-    real = dot(first[0], flat, ((1,), (0,)), HIGH).reshape(-1, channels, breadth)
-    imag = dot(first[1], flat, ((1,), (0,)), HIGH).reshape(-1, channels, breadth)
-    cos_mid, sin_mid = cos_mid[:, None], sin_mid[:, None]
-    turned = jnp.concatenate(
-        [real * cos_mid - imag * sin_mid, real * sin_mid + imag * cos_mid], axis=2
-    )
-    return dot(turned, forward, ((2,), (0,)), HIGH)
-
-
-def inverse_transform(spectrum, tables):
-    _, cos_mid, sin_mid, _, backward, last = tables
-    half, channels, twice = spectrum.shape
-    breadth = twice // 2
-    mid = dot(spectrum, backward, ((2,), (0,)), HIGH)
-    real, imag = mid[:, :, :breadth], mid[:, :, breadth:]
-    cos_mid, sin_mid = cos_mid[:, None], sin_mid[:, None]
-    turned = jnp.concatenate(
-        [real * cos_mid + imag * sin_mid, imag * cos_mid - real * sin_mid], axis=0
-    )
-    out = dot(last, turned.reshape(2 * half, channels * breadth), ((1,), (0,)), HIGH)
-    return out.reshape(-1, channels, breadth)
-
-
-def kernel_call(kernel, out_shape, scalars, arrays, scratch=(), flops=0, grant=32):
+    last = np.zeros((depth, 2 * half))
+    last[:, : depth + 1] = np.cos(one).T * weight
+    last[:, half : half + depth + 1] = np.sin(one).T * weight
+
+    def halves(x):
+        high = x.astype(BF16)
+        return high, (x - high.astype(np.float64)).astype(BF16)
+
+    first_high, first_low = halves(first)
+    last_high, last_low = halves(last)
+    return {
+        "first_two": np.concatenate([first_high, first_low], axis=1),
+        "first_three": np.concatenate([first_high, first_high, first_low], axis=1),
+        "mid": mid.astype(np.float32),
+        "forward": np.stack(halves(np.block([[cos_two, sin_two], [-sin_two, cos_two]]))),
+        "backward": np.stack(halves(np.block([[cos_two, -sin_two], [sin_two, cos_two]]))),
+        "last": np.concatenate([last_high, last_high, last_low], axis=1),
+    }
+
+
+def kernel_call(
+    kernel, out_shape, scalars, arrays, scratch=(), flops=0, grant=32, hbm_in=(), hbm_out=()
+):
+    single = not isinstance(out_shape, tuple)
+    outs = (out_shape,) if single else out_shape
+
+    def spec(at, hbm):
+        return pl.BlockSpec(memory_space=pltpu.HBM if at in hbm else pltpu.VMEM)
+
+    arrays = [
+        pltpu.with_memory_space_constraint(x, pltpu.HBM) if at in hbm_in else x
+        for at, x in enumerate(arrays)
+    ]
     in_specs = [pl.BlockSpec(memory_space=pltpu.SMEM)] * len(scalars)
-    in_specs += [pl.BlockSpec(memory_space=pltpu.VMEM)] * len(arrays)
-    outs = out_shape if isinstance(out_shape, tuple) else (out_shape,)
+    in_specs += [spec(at, hbm_in) for at in range(len(arrays))]
+    out_specs = tuple(spec(at, hbm_out) for at in range(len(outs)))
     moved = sum(x.size * x.dtype.itemsize for x in (*arrays, *outs))
+    placed = tuple(
+        pltpu.HBM(x.shape, x.dtype) if at in hbm_out else x for at, x in enumerate(outs)
+    )
     return pl.pallas_call(
         kernel,
-        out_shape=out_shape,
+        out_shape=placed[0] if single else placed,
         in_specs=in_specs,
-        out_specs=jax.tree.map(lambda _: pl.BlockSpec(memory_space=pltpu.VMEM), out_shape),
+        out_specs=out_specs[0] if single else out_specs,
         scratch_shapes=list(scratch),
         compiler_params=pltpu.CompilerParams(vmem_limit_bytes=grant * 1024 * 1024),
         cost_estimate=pl.CostEstimate(flops=flops, bytes_accessed=moved, transcendentals=0),
@@ -100,9 +100,9 @@
         for ref, which in ((first_ref, 0), (value_ref, 2)):
             x = ref[:, span].astype(F32)
             shorts.append(
-                taps_ref[0, which, 0:1, span] * x
-                + taps_ref[0, which, 1:2, span] * pltpu.roll(x, 1, 0)
-                + taps_ref[0, which, 2:3, span] * pltpu.roll(x, 2, 0)
+                taps_ref[3 * which, :, span] * x
+                + taps_ref[3 * which + 1, :, span] * pltpu.roll(x, 1, 0)
+                + taps_ref[3 * which + 2, :, span] * pltpu.roll(x, 2, 0)
             )
             edges += [x[:2], x[rows - 2 :]]
         turned = (shorts[0] * shorts[1]).T
@@ -118,17 +118,23 @@
             other_ref[z_at] = jnp.where(low, blocks[1], blocks[0]).astype(BF16)
 
 
-def repack_kernel(x_ref, rows_ref, own_ref, got_ref, out_ref, weight_ref):
+def repack_kernel(
+    x_ref, rows_ref, own_hbm, got_ref, out_hbm, weight_hbm, own_ref, out_ref, sems
+):
     n_tp, height, wide = rows_ref.shape
-    channels = weight_ref.shape[1]
+    channels = weight_hbm.shape[1]
     size = height - channels
     heads = wide // HD
+    fetch = pltpu.make_async_copy(own_hbm, own_ref, sems.at[0])
+    fetch.start()
+    pass_on = pltpu.make_async_copy(rows_ref.at[:, size:, :], weight_hbm, sems.at[1])
+    pass_on.start()
     for at in range(n_tp):
         for head in range(heads):
             block = rows_ref[at, :size, head * HD : (head + 1) * HD]
             out_ref[at * heads + head, :size, :] = block
-    weight_ref[...] = rows_ref[:, size:, :]
     low = x_ref[0] == 0
+    fetch.wait()
     own, got = own_ref[...].astype(F32), got_ref[...].astype(F32)
     even = jnp.where(low, own, got).astype(BF16)
     odd = jnp.where(low, got, own).astype(BF16)
@@ -136,18 +142,74 @@
     out_ref[:, size + channels : size + 2 * channels, :] = odd[:, :channels]
     out_ref[:, size + 2 * channels : size + 2 * channels + 8, :] = even[:, channels:]
     out_ref[:, size + 2 * channels + 8 :, :] = odd[:, channels:]
-
-
-def split_kernel(part, mixed_ref, pairs_ref, query_ref):
+    store = pltpu.make_async_copy(out_ref, out_hbm, sems.at[2])
+    store.start()
+    store.wait()
+    pass_on.wait()
+
+
+def split_kernel(part, mixed_ref, pairs_hbm, query_ref, block_ref, sems):
     n_z = mixed_ref.shape[0]
+    for at in range(2):
+        block = mixed_ref[:, (at + 1) * part : (at + 2) * part, :]
+        block_ref[at] = block.reshape(n_z * part, HD)
+    stores = [
+        pltpu.make_async_copy(block_ref, pairs_hbm.at[to], sems.at[to])
+        for to in range(pairs_hbm.shape[0])
+    ]
+    for store in stores:
+        store.start()
     query_ref[...] = mixed_ref[:, :part, :].reshape(n_z * part, HD)
-    for at in range(2):
-        block = mixed_ref[:, (at + 1) * part : (at + 2) * part, :].reshape(n_z * part, HD)
-        for to in range(pairs_ref.shape[0]):
-            pairs_ref[to, at] = block
-
-
-def product_kernel(start, mixed_ref, taps_ref, out_ref):
+    for store in stores:
+        store.wait()
+
+
+def split_two(x):
+    high = x.astype(BF16)
+    return high, (x - high.astype(F32)).astype(BF16)
+
+
+def dot_three(x, high, low):
+    x_high, x_low = split_two(x)
+    rows = ((1,), (0,))
+    return dot(x_high, high, rows) + (dot(x_low, high, rows) + dot(x_high, low, rows))
+
+
+def turn(real, imag, cos_mid, sin_mid, turned_ref, span):
+    breadth = cos_mid.shape[1]
+    turned_ref[span, :breadth] = real * cos_mid - imag * sin_mid
+    turned_ref[span, breadth:] = real * sin_mid + imag * cos_mid
+
+
+def spectrum_kernel(filter_ref, first_ref, mid_ref, forward_ref, out_ref, turned_ref):
+    channels = filter_ref.shape[0]
+    half = mid_ref.shape[1]
+    cos_mid, sin_mid = mid_ref[0], mid_ref[1]
+    for at in range(channels):
+        high, low = split_two(filter_ref[at])
+        both = dot(first_ref[...], jnp.concatenate([high, low, high], axis=0), ((1,), (0,)))
+        turn(both[:half], both[half:], cos_mid, sin_mid, turned_ref, slice(at * half, (at + 1) * half))
+    step = 4 * half
+    for at in range(channels // 4):
+        span = slice(at * step, (at + 1) * step)
+        out_ref[span, :] = dot_three(turned_ref[span, :], forward_ref[0], forward_ref[1])
+
+
+def convolve_kernel(
+    start,
+    gain_ref,
+    mixed_ref,
+    taps_ref,
+    spectrum_ref,
+    first_ref,
+    mid_ref,
+    forward_ref,
+    backward_ref,
+    last_ref,
+    out_ref,
+    signal_ref,
+    turned_ref,
+):
     n_seq, channels, rows = out_ref.shape
     count = n_seq * 8
     edges = mixed_ref[:, start + 2 * channels :, :].astype(F32).reshape(count, rows).T[:channels]
@@ -164,7 +226,36 @@
         turned = pltpu.roll(made, count - 8 * at, 1) if at else made
         begin = start + at % 2 * channels
         block = mixed_ref[at // 2, begin : begin + channels, :].astype(F32)
-        out_ref[at] = jnp.where(column < 2, turned[:, :rows], block)
+        signal_ref[at * channels : (at + 1) * channels, :] = jnp.where(
+            column < 2, turned[:, :rows], block
+        )
+    half = mid_ref.shape[1]
+    cos_mid, sin_mid = mid_ref[0], mid_ref[1]
+    for at in range(channels):
+        signal = signal_ref[pl.ds(at, n_seq, stride=channels), :].astype(BF16)
+        both = dot(first_ref[...], jnp.concatenate([signal, signal], axis=0), ((1,), (0,)))
+        turn(both[:half], both[half:], cos_mid, sin_mid, turned_ref, slice(at * half, (at + 1) * half))
+    step = 4 * half
+    for group in range(channels // 4):
+        span = slice(group * step, (group + 1) * step)
+        mine = dot_three(turned_ref[span, :], forward_ref[0], forward_ref[1])
+        real, imag = mine[:, :rows], mine[:, rows:]
+        other_real, other_imag = spectrum_ref[span, :rows], spectrum_ref[span, rows:]
+        joined = jnp.concatenate(
+            [real * other_real - imag * other_imag, real * other_imag + imag * other_real], axis=1
+        )
+        mid = dot_three(joined, backward_ref[0], backward_ref[1])
+        for at in range(4):
+            real, imag = (mid[at * half : (at + 1) * half, c * rows : (c + 1) * rows] for c in (0, 1))
+            back = jnp.concatenate(
+                [real * cos_mid + imag * sin_mid, imag * cos_mid - real * sin_mid], axis=0
+            )
+            high, low = split_two(back)
+            out = dot(last_ref[...], jnp.concatenate([high, low, high], axis=0), ((1,), (0,)))
+            channel = group * 4 + at
+            strided = pl.ds(channel, n_seq, stride=channels)
+            signal_ref[strided, :] = out + gain_ref[channel] * signal_ref[strided, :]
+    out_ref[...] = signal_ref[...].astype(BF16).reshape(n_seq, channels, rows)
 
 
 def attend_kernel(rows, delta_ref, query_ref, pairs_ref, long_ref, out_ref):
@@ -190,18 +281,16 @@
                 keys = pairs_ref[at, 0, start:stop, :]
                 scores = dot(query, keys, ((1,), (1,))) * (1.0 / math.sqrt(HD))
                 if start == tile * size:
-                    parts.append((jnp.where(allowed, scores, -1e30), allowed, at, start, stop))
+                    parts.append((jnp.where(allowed, scores, -1e30), at, start, stop))
                 else:
-                    parts.append((scores, None, at, start, stop))
+                    parts.append((scores, at, start, stop))
         highest = parts[0][0].max(axis=1, keepdims=True)
         for piece in parts[1:]:
             highest = jnp.maximum(highest, piece[0].max(axis=1, keepdims=True))
         totals = jnp.zeros((size, 1), F32)
         weighted = jnp.zeros((size, HD), F32)
-        for scores, allowed, at, start, stop in parts:
+        for scores, at, start, stop in parts:
             probs = jnp.exp(scores - highest)
-            if allowed is not None:
-                probs = jnp.where(allowed, probs, 0.0)
             totals = totals + probs.sum(axis=1, keepdims=True)
             values = pairs_ref[at, 1, start:stop, :]
             weighted = weighted + dot(probs.astype(BF16), values, ((1,), (0,)))
@@ -209,18 +298,30 @@
         out_ref[tile * per : (tile + 1) * per, :part, :] = out
 
 
-def rows_kernel(x_ref, back_ref, rows_ref, own_ref, other_ref):
-    part = rows_ref.shape[1]
+def rows_kernel(
+    x_ref, back_ref, rows_hbm, own_hbm, other_hbm, rows_ref, own_ref, other_ref, sems
+):
+    part = rows_ref.shape[0]
     channels = own_ref.shape[1]
+    count = rows_hbm.shape[0]
     for head in range(back_ref.shape[0]):
-        block = back_ref[head, :part, :]
-        for to in range(rows_ref.shape[0]):
-            rows_ref[to, :, head * HD : (head + 1) * HD] = block
+        rows_ref[:, head * HD : (head + 1) * HD] = back_ref[head, :part, :]
+    stores = [pltpu.make_async_copy(rows_ref, rows_hbm.at[to], sems.at[to]) for to in range(count)]
+    for store in stores:
+        store.start()
     low = x_ref[0] == 0
     even = back_ref[:, part : part + channels, :].astype(F32)
     odd = back_ref[:, part + channels :, :].astype(F32)
     own_ref[...] = jnp.where(low, even, odd).astype(BF16)
     other_ref[...] = jnp.where(low, odd, even).astype(BF16)
+    stores += [
+        pltpu.make_async_copy(own_ref, own_hbm, sems.at[count]),
+        pltpu.make_async_copy(other_ref, other_hbm, sems.at[count + 1]),
+    ]
+    for store in stores[count:]:
+        store.start()
+    for store in stores:
+        store.wait()
 
 
 def gate_kernel(x_ref, own_ref, got_ref, gate_ref, tail_ref, taps_ref, out_ref):
@@ -320,7 +421,7 @@
         (
             first_stream[0],
             value_stream[0],
-            short_taps,
+            short_taps.reshape(9, 1, -1),
             queries[0],
             attn_keys[0],
             attn_values[0],
@@ -338,6 +439,13 @@
         ),
         (x_scalar,),
         (got_rows, own, got),
+        (
+            pltpu.VMEM((n_z, channels + 8, rows), BF16),
+            pltpu.VMEM((n_z, 3 * part + 2 * channels + 16, HD), BF16),
+            pltpu.SemaphoreType.DMA((3,)),
+        ),
+        hbm_in=(1,),
+        hbm_out=(0, 1),
     )
     mixed = lax.all_to_all(packed, "z", 0, 0)
     weight = lax.all_gather(weight, "z")
@@ -354,8 +462,19 @@
     local_taps = lax.dynamic_slice_in_dim(taps, seq_at * channels, channels, 2)
     local_taps = local_taps.reshape(9, channels).T
     tables = transform_tables(n_seq, rows)
-    kernel = long_filter[0, 0, 0].reshape(channels, n_seq, rows).transpose(1, 0, 2)
-    kernel_spec = forward_transform(kernel, tables)
+    half = tables["mid"].shape[1]
+    kernel_spec = kernel_call(
+        spectrum_kernel,
+        shape((channels * half, 2 * rows), F32),
+        (),
+        (
+            long_filter[0, 0, 0].reshape(channels, n_seq, rows),
+            tables["first_three"],
+            tables["mid"],
+            tables["forward"],
+        ),
+        (pltpu.VMEM((channels * half, 2 * rows), F32),),
+    )
     mixed, gate, gate_taps, tail, local_taps, kernel_spec = lax.optimization_barrier(
         (mixed, gate, gate_taps, tail, local_taps, kernel_spec)
     )
@@ -365,24 +484,31 @@
         (shape((n_plane, 2, own_rows, HD), BF16), shape((own_rows, HD), BF16)),
         (),
         (mixed,),
+        (pltpu.VMEM((2, own_rows, HD), BF16), pltpu.SemaphoreType.DMA((n_plane,))),
+        hbm_out=(0,),
     )
     pairs = lax.all_to_all(sent_pairs, ("xh", "tp"), 0, 0)
 
-    product = kernel_call(
-        functools.partial(product_kernel, 3 * part),
-        shape((n_seq, channels, rows), F32),
-        (),
-        (mixed, local_taps),
-    )
-    spec = forward_transform(product, tables)
-    real, imag = spec[:, :, :rows], spec[:, :, rows:]
-    kernel_real, kernel_imag = kernel_spec[:, :, :rows], kernel_spec[:, :, rows:]
-    joined = jnp.concatenate(
-        [real * kernel_real - imag * kernel_imag, real * kernel_imag + imag * kernel_real], axis=2
-    )
-    convolved = inverse_transform(joined, tables)
     gain = lax.dynamic_slice_in_dim(skip_gain[0], seq_at * channels, channels, 0)
-    long_out = (convolved + gain[None, :, None] * product).astype(BF16)
+    long_out = kernel_call(
+        functools.partial(convolve_kernel, 3 * part),
+        shape((n_seq, channels, rows), BF16),
+        (gain,),
+        (
+            mixed,
+            local_taps,
+            kernel_spec,
+            tables["first_two"],
+            tables["mid"],
+            tables["forward"],
+            tables["backward"],
+            tables["last"],
+        ),
+        (
+            pltpu.VMEM((n_seq * channels, rows), F32),
+            pltpu.VMEM((channels * half, 2 * rows), F32),
+        ),
+    )
 
     delta = -(x_at * rows + lax.axis_index("tp") * part)
     returned = kernel_call(
@@ -405,6 +531,13 @@
         ),
         (x_scalar,),
         (back,),
+        (
+            pltpu.VMEM((part, n_z * HD), BF16),
+            pltpu.VMEM((n_z, channels, rows), BF16),
+            pltpu.VMEM((n_z, channels, rows), BF16),
+            pltpu.SemaphoreType.DMA((n_plane + 2,)),
+        ),
+        hbm_out=(0, 1, 2),
     )
     plane_rows = lax.all_to_all(plane_rows, ("xh", "tp"), 0, 0)
     own_long = lax.ppermute(own_long, "section", onward)

time: 191 us -> 189 us (0.990)
  local copies, waits for them, and re-layouts: 12.6 us -> 2.56 us
  Pallas kernels: 14.5 us -> 23.7 us
  waiting for transfers between devices: 65.7 us -> 73.6 us
  matrix products: 7.27 us -> 0 us
  other arithmetic: 2.63 us -> 0 us
    unnamed x51 -> x24, local copies, waits for them, and re-layouts: 9.5 us -> 0.16 us
    pallas_call x9 -> x10, Pallas kernels: 14.5 us -> 23.7 us  [kernel_call(): pl.pallas_call(kernel, out_shape=placed[0] if single else placed, in_spec...]
    dot_general x8 -> x0, matrix products: 7.27 us -> none  [dot(): lax.dot_general(left, right, (contract, ((), ())), precision=precision, p...]
    all_to_all x1, waiting for transfers between devices: 11 us -> 14.8 us  [body(): pairs = lax.all_to_all(sent_pairs, ('xh', 'tp'), 0, 0)]
    all_gather x1, waiting for transfers between devices: 2.71 us -> 0.01 us  [body(): weight = lax.all_gather(weight, 'z')]
    ppermute x1, waiting for transfers between devices: 1.6 us -> 3.98 us  [body(): lax.ppermute(gate_stream[0, -2:], ('section',) + seq, [(s * n_seq + i, t...]
    all_to_all x1, waiting for transfers between devices: 19.6 us -> 21.7 us  [body(): back = lax.all_to_all(returned, 'z', 0, 0)]
    sub x2 -> x0, other arithmetic: 1.98 us -> none  [the longest x1 1.82 us: forward_transform(): real * cos_mid - imag * sin_mid]
  transfers between devices with their start and end apart: 13 -> 13, of which waited for: 9 -> 8; matrix products, arithmetic and copies ran while one was open for 7% -> 1% of each run, Pallas kernels for 5% -> 9%
where the time goes in v7:
time: 189 us; the launch traced here: 188 us
  starting transfers between devices  74 us (39%)
  waiting for transfers between devices  73.6 us (39%)
  Pallas kernels  23.7 us (13%)
  between operations  14.3 us (8%)
  local copies, waits for them, and re-layouts  2.56 us (1%)
    pallas_call x10, Pallas kernels, kernel_call(): pl.pallas_call(kernel, out_shape=placed[0] if single else placed, in_spec...  23.7 us
    all_to_all x1, waiting for transfers between devices, body(): back = lax.all_to_all(returned, 'z', 0, 0)  21.7 us
    all_to_all x1, waiting for transfers between devices, body(): mixed = lax.all_to_all(packed, 'z', 0, 0)  16.6 us
    all_to_all x1, starting transfers between devices, body(): back = lax.all_to_all(returned, 'z', 0, 0)  16.4 us
    all_to_all x1, starting transfers between devices, body(): mixed = lax.all_to_all(packed, 'z', 0, 0)  15.2 us
    all_to_all x1, waiting for transfers between devices, body(): pairs = lax.all_to_all(sent_pairs, ('xh', 'tp'), 0, 0)  14.8 us
    all_to_all x1, waiting for transfers between devices, body(): plane_rows = lax.all_to_all(plane_rows, ('xh', 'tp'), 0, 0)  7.43 us
    all_to_all x1, starting transfers between devices, body(): pairs = lax.all_to_all(sent_pairs, ('xh', 'tp'), 0, 0)  6.77 us
  transfers between devices with their start and end apart: 13, of which 8 were waited for; matrix products, arithmetic and copies ran while one was open for 1% of the time, Pallas kernels for 9%

profile of v7, /device:TPU:32, one launch (start us, length us, event | category | flops | bytes accessed | tf_op | source)
XLA Modules:
  0.0 188.1 jit_solution(15168933561558996786)
XLA Ops:
  7.2 2.7 %shard_map.167 = (bf16[4,128,512]{2,1,0:T(8,128)(2,1)}, bf16[16,40,128]{2,1,0:T(8,128)(2,1)}, bf16[16,40,128]{2,1,0:T(8,128)(2,1)}) custom-call(s32[1]{0:T(128)} %bitcast.x_ref, bf16[128,1024]{1,0:T(8,128)(2,1)} %bitcast.34, bf16[128,1024]{1,0:T(8,128)(2,1)} %bitcast.35, f32[9,1,1024]{2,1,0:T(1,128)} %bitcast.41, bf16[128,512]{1,0:T(8,128)(2,1)} %bitcast.37, ...), custom_call_target="tpu_custom_call" | custom-call | bytes 1937408 | tf_op jit(solution)/shard_map/pallas_call | solution.py:75
  9.9 4.6 %all-to-all-start = ((bf16[4,128,512]{2,1,0:T(8,128)(2,1)}), bf16[4,128,512]{2,1,0:T(8,128)(2,1)S(1)}, u32[]{:S(2)}, u32[]{:S(2)}) async-start(bf16[4,128,512]{2,1,0:T(8,128)(2,1)} %get-tuple-element.22), calls=%async_computation | async-start | bytes 1048576 | tf_op jit(solution)/shard_map/all_to_all | solution.py:433
  14.5 4.9 %collective-permute-start = (bf16[16,40,128]{2,1,0:T(8,128)(2,1)}, bf16[16,40,128]{2,1,0:T(8,128)(2,1)S(1)}, u32[]{:S(2)}, u32[]{:S(2)}) collective-permute-start(bf16[16,40,128]{2,1,0:T(8,128)(2,1)} %get-tuple-element.24), channel_id=1, source_target_pairs={{0,4},{4,0},{1,5},{5,1},{2,6},{6,2},{3,7},{7,3},{8,12},{12,8},{9,1... | collective-permute-start | bytes 491528 | tf_op jit(solution)/shard_map/ppermute | solution.py:432
  19.4 4.3 %collective-permute-done.got_ref = bf16[16,40,128]{2,1,0:T(8,128)(2,1)S(1)} collective-permute-done((bf16[16,40,128]{2,1,0:T(8,128)(2,1)}, bf16[16,40,128]{2,1,0:T(8,128)(2,1)S(1)}, u32[]{:S(2)}, u32[]{:S(2)}) %collective-permute-start) | collective-permute-done | bytes 163872 | tf_op jit(solution)/shard_map/ppermute | solution.py:432
  23.9 1.9 %shard_map.168 = (bf16[16,176,128]{2,1,0:T(8,128)(2,1)}, bf16[4,32,512]{2,1,0:T(8,128)(2,1)}) custom-call(s32[1]{0:T(128)} %bitcast.x_ref, bf16[4,128,512]{2,1,0:T(8,128)(2,1)S(1)} %all-to-all-done.rows_ref, bf16[16,40,128]{2,1,0:T(8,128)(2,1)} %get-tuple-element.23.own_hbm, bf16[16,40,128]{2,1,0:T(8,128)(2,1)S(1)} %collective-permute-done.got_ref), custom_call_target="tpu_custom_call" | custom-call | bytes 1703936 | tf_op jit(solution)/shard_map/pallas_call | solution.py:75
  25.9 15.2 %all-to-all-start.1 = ((bf16[16,176,128]{2,1,0:T(8,128)(2,1)}), bf16[16,176,128]{2,1,0:T(8,128)(2,1)S(1)}, u32[]{:S(2)}, u32[]{:S(2)}) async-start(bf16[16,176,128]{2,1,0:T(8,128)(2,1)} %get-tuple-element.25), calls=%async_computation.1 | async-start | bytes 1441792 | tf_op jit(solution)/shard_map/all_to_all | solution.py:450
  41.8 1.9 %collective-permute-start.1 = (bf16[128,1024]{1,0:T(8,128)(2,1)}, bf16[128,1024]{1,0:T(8,128)(2,1)S(1)}, u32[]{:S(2)}, u32[]{:S(2)}) collective-permute-start(bf16[128,1024]{1,0:T(8,128)(2,1)} %bitcast.10), channel_id=1, source_target_pairs={{0,128},{128,256},{256,384},{384,0},{1,129},{129,257},{257,385},{3... | collective-permute-start | bytes 786440 | tf_op jit(solution)/shard_map/ppermute | solution.py:455
  43.8 0.7 slice.7
  44.5 3.5 %collective-permute-start.2 = (f32[3,1024]{1,0:T(4,128)S(1)}, f32[3,1024]{1,0:T(4,128)S(1)}, u32[]{:S(2)}, u32[]{:S(2)}) collective-permute-start(f32[3,1024]{1,0:T(4,128)S(1)} %bitcast.42), channel_id=1, source_target_pairs={{0,128},{128,256},{256,384},{384,0},{1,129},{129,257},{257,385},{3... | collective-permute-start | bytes 36872 | tf_op jit(solution)/shard_map/ppermute | solution.py:456
  48.0 0.7 slice_bitcast_fusion
  48.7 4.2 %collective-permute-start.3 = (bf16[2,1024]{1,0:T(2,128)(2,1)S(1)}, bf16[2,1024]{1,0:T(2,128)(2,1)S(1)}, u32[]{:S(2)}, u32[]{:S(2)}) collective-permute-start(bf16[2,1024]{1,0:T(2,128)(2,1)S(1)} %slice_bitcast_fusion), channel_id=1, source_target_pairs={{0,132},{4,136},{8,140},{12,144},{16,148},{20,152},{24,156},{28,16... | collective-permute-start | bytes 12296 | tf_op jit(solution)/shard_map/ppermute | solution.py:457
  53.0 0.8 dynamic-slice_reduce_fusion
  54.0 1.1 shard_map.169.spectrum_ref
  55.1 4.0 %collective-permute-done.3.tail_ref = bf16[2,1024]{1,0:T(2,128)(2,1)S(1)} collective-permute-done((bf16[2,1024]{1,0:T(2,128)(2,1)S(1)}, bf16[2,1024]{1,0:T(2,128)(2,1)S(1)}, u32[]{:S(2)}, u32[]{:S(2)}) %collective-permute-start.3) | collective-permute-done | bytes 4128 | tf_op jit(solution)/shard_map/ppermute | solution.py:457
  59.1 16.6 %all-to-all-done.1.mixed_ref = bf16[16,176,128]{2,1,0:T(8,128)(2,1)S(1)} async-done(((bf16[16,176,128]{2,1,0:T(8,128)(2,1)}), bf16[16,176,128]{2,1,0:T(8,128)(2,1)S(1)}, u32[]{:S(2)}, u32[]{:S(2)}) %all-to-all-start.1) | async-done | bytes 720928 | tf_op jit(solution)/shard_map/all_to_all | solution.py:450
  75.7 1.5 shard_map.170
  77.2 6.8 %all-to-all-start.2 = ((bf16[8,2,512,128]{3,2,1,0:T(8,128)(2,1)}), bf16[8,2,512,128]{3,2,1,0:T(8,128)(2,1)}, u32[]{:S(2)}, u32[]{:S(2)}) async-start(bf16[8,2,512,128]{3,2,1,0:T(8,128)(2,1)} %get-tuple-element.28), calls=%async_computation.2 | async-start | bytes 4194304 | tf_op jit(solution)/shard_map/all_to_all | solution.py:490
  84.1 6.0 %shard_map.171 = bf16[32,32,128]{2,1,0:T(8,128)(2,1)S(1)} custom-call(f32[32]{0:T(128)S(1)} %dynamic-slice_bitcast_fusion.gain_ref, bf16[16,176,128]{2,1,0:T(8,128)(2,1)S(1)} %all-to-all-done.1.mixed_ref, f32[32,9]{1,0:T(8,128)S(1)} %bitcast.31, f32[1280,256]{1,0:T(8,128)S(1)} %shard_map.169.spectrum_ref, bf16[80,64]{1,0:T(8,128)(2,1)S(1)} %copy-done.5, ...), custom_call_target="tpu_custom_call" | custom-call | bytes 2885760 | tf_op jit(solution)/shard_map/pallas_call | solution.py:75
  90.1 14.8 %all-to-all-done.2.pairs_ref = bf16[8,2,512,128]{3,2,1,0:T(8,128)(2,1)} async-done(((bf16[8,2,512,128]{3,2,1,0:T(8,128)(2,1)}), bf16[8,2,512,128]{3,2,1,0:T(8,128)(2,1)}, u32[]{:S(2)}, u32[]{:S(2)}) %all-to-all-start.2) | async-done | bytes 2097184 | tf_op jit(solution)/shard_map/all_to_all | solution.py:490
  104.9 5.8 %shard_map.172 = bf16[16,96,128]{2,1,0:T(8,128)(2,1)} custom-call(s32[1]{0:T(128)} %bitcast.1.delta_ref, bf16[512,128]{1,0:T(8,128)(2,1)S(1)} %get-tuple-element.27.query_ref, bf16[8,2,512,128]{3,2,1,0:T(8,128)(2,1)} %all-to-all-done.2.pairs_ref, bf16[16,64,128]{2,1,0:T(8,128)(2,1)S(1)} %bitcast.30), custom_call_target="tpu_custom_call" | custom-call | flops 1073741824 | bytes 2883584 | tf_op jit(solution)/shard_map/pallas_call | solution.py:75
  110.7 16.4 %all-to-all-start.3 = ((bf16[16,96,128]{2,1,0:T(8,128)(2,1)}), bf16[16,96,128]{2,1,0:T(8,128)(2,1)S(1)}, u32[]{:S(2)}, u32[]{:S(2)}) async-start(bf16[16,96,128]{2,1,0:T(8,128)(2,1)} %shard_map.172), calls=%async_computation.3 | async-start | bytes 786432 | tf_op jit(solution)/shard_map/all_to_all | solution.py:522
  127.1 21.7 %all-to-all-done.3.back_ref = bf16[16,96,128]{2,1,0:T(8,128)(2,1)S(1)} async-done(((bf16[16,96,128]{2,1,0:T(8,128)(2,1)}), bf16[16,96,128]{2,1,0:T(8,128)(2,1)S(1)}, u32[]{:S(2)}, u32[]{:S(2)}) %all-to-all-start.3) | async-done | bytes 393248 | tf_op jit(solution)/shard_map/all_to_all | solution.py:522
  148.8 1.1 shard_map.173
  149.9 5.3 %all-to-all-start.4 = ((bf16[8,32,2048]{2,1,0:T(8,128)(2,1)}), bf16[8,32,2048]{2,1,0:T(8,128)(2,1)S(1)}, u32[]{:S(2)}, u32[]{:S(2)}) async-start(bf16[8,32,2048]{2,1,0:T(8,128)(2,1)} %get-tuple-element.38), calls=%async_computation.4 | async-start | bytes 2097152 | tf_op jit(solution)/shard_map/all_to_all | solution.py:542
  155.2 1.9 %collective-permute-start.4 = (bf16[16,32,128]{2,1,0:T(8,128)(2,1)}, bf16[16,32,128]{2,1,0:T(8,128)(2,1)S(1)}, u32[]{:S(2)}, u32[]{:S(2)}) collective-permute-start(bf16[16,32,128]{2,1,0:T(8,128)(2,1)} %get-tuple-element.33), channel_id=1, source_target_pairs={{0,128},{128,256},{256,384},{384,0},{1,129},{129,257},{257,385},{3... | collective-permute-start | bytes 393224 | tf_op jit(solution)/shard_map/ppermute | solution.py:543
  157.2 6.6 %collective-permute-start.5 = (bf16[16,32,128]{2,1,0:T(8,128)(2,1)}, bf16[16,32,128]{2,1,0:T(8,128)(2,1)}, u32[]{:S(2)}, u32[]{:S(2)}) collective-permute-start(bf16[16,32,128]{2,1,0:T(8,128)(2,1)} %get-tuple-element.34), channel_id=1, source_target_pairs={{0,132},{4,128},{128,260},{132,256},{256,388},{260,384},{384,4},{3... | collective-permute-start | bytes 393224 | tf_op jit(solution)/shard_map/ppermute | solution.py:544
  163.8 7.4 %all-to-all-done.4.rows_ref = bf16[8,32,2048]{2,1,0:T(8,128)(2,1)S(1)} async-done(((bf16[8,32,2048]{2,1,0:T(8,128)(2,1)}), bf16[8,32,2048]{2,1,0:T(8,128)(2,1)S(1)}, u32[]{:S(2)}, u32[]{:S(2)}) %all-to-all-start.4) | async-done | bytes 1048608 | tf_op jit(solution)/shard_map/all_to_all | solution.py:542
  171.2 0.7 shard_map.175
  171.9 2.6 %collective-permute-start.6 = (bf16[128,512]{1,0:T(8,128)(2,1)S(1)}, bf16[128,512]{1,0:T(8,128)(2,1)S(1)}, u32[]{:S(2)}, u32[]{:S(2)}) collective-permute-start(bf16[128,512]{1,0:T(8,128)(2,1)S(1)} %get-tuple-element.41), channel_id=1, source_target_pairs={{0,4},{4,0},{1,5},{5,1},{2,6},{6,2},{3,7},{7,3},{8,12},{12,8},{9,1... | collective-permute-start | bytes 393224 | tf_op jit(solution)/shard_map/ppermute | solution.py:561
  174.6 1.9 %shard_map.174 = bf16[128,1024]{1,0:T(8,128)(2,1)} custom-call(s32[1]{0:T(128)} %bitcast.x_ref, bf16[16,32,128]{2,1,0:T(8,128)(2,1)S(1)} %collective-permute-done.4.own_ref, bf16[16,32,128]{2,1,0:T(8,128)(2,1)} %collective-permute-done.5.got_ref, bf16[128,1024]{1,0:T(8,128)(2,1)S(1)} %collective-permute-done.1.gate_ref, ...), custom_call_target="tpu_custom_call" | custom-call | bytes 802816 | tf_op jit(solution)/shard_map/pallas_call | solution.py:75
  176.5 3.8 %collective-permute-done.6.got_ref = bf16[128,512]{1,0:T(8,128)(2,1)S(1)} collective-permute-done((bf16[128,512]{1,0:T(8,128)(2,1)S(1)}, bf16[128,512]{1,0:T(8,128)(2,1)S(1)}, u32[]{:S(2)}, u32[]{:S(2)}) %collective-permute-start.6) | collective-permute-done | bytes 131104 | tf_op jit(solution)/shard_map/ppermute | solution.py:561
  180.3 1.0 shard_map.176
  (35 shorter events, 1.3 us)
Async XLA Ops:
  7.2 76.8 %copy-start = (f32[1,1024]{1,0:T(1,128)S(1)}, f32[1,1024]{1,0:T(1,128)}, u32[]{:S(2)}) copy-start(f32[1,1024]{1,0:T(1,128)} %param.21) | copy-start | bytes 12292
  7.2 46.7 %copy-start.10 = (f32[1,1,1,32,4096]{4,3,2,1,0:T(8,128)S(1)}, f32[1,1,1,32,4096]{4,3,2,1,0:T(8,128)}, u32[]{:S(2)}) copy-start(f32[1,1,1,32,4096]{4,3,2,1,0:T(8,128)} %param.20) | copy-start | bytes 1572868
  9.9 44.1 %copy-start.2 = (bf16[2,256,256]{2,1,0:T(8,128)(2,1)S(1)}, bf16[2,256,256]{2,1,0:T(8,128)(2,1)}, u32[]{:S(2)}) copy-start(bf16[2,256,256]{2,1,0:T(8,128)(2,1)} %constant.40.clone.forward_ref) | copy-start | bytes 786436
  9.9 44.1 %copy-start.4 = (f32[2,40,128]{2,1,0:T(8,128)S(1)}, f32[2,40,128]{2,1,0:T(8,128)}, u32[]{:S(2)}) copy-start(f32[2,40,128]{2,1,0:T(8,128)} %constant.39.clone.mid_ref) | copy-start | bytes 122884
  9.9 44.1 %copy-start.6 = (bf16[80,96]{1,0:T(8,128)(2,1)S(1)}, bf16[80,96]{1,0:T(8,128)(2,1)}, u32[]{:S(2)}) copy-start(bf16[80,96]{1,0:T(8,128)(2,1)} %constant.38.clone.first_ref) | copy-start | bytes 46084
  9.9 14.1 %all-to-all-start = ((bf16[4,128,512]{2,1,0:T(8,128)(2,1)}), bf16[4,128,512]{2,1,0:T(8,128)(2,1)S(1)}, u32[]{:S(2)}, u32[]{:S(2)}) async-start(bf16[4,128,512]{2,1,0:T(8,128)(2,1)} %get-tuple-element.22), calls=%async_computation | async-start | bytes 1048576 | tf_op jit(solution)/shard_map/all_to_all | solution.py:433
  14.5 9.3 %collective-permute-start = (bf16[16,40,128]{2,1,0:T(8,128)(2,1)}, bf16[16,40,128]{2,1,0:T(8,128)(2,1)S(1)}, u32[]{:S(2)}, u32[]{:S(2)}) collective-permute-start(bf16[16,40,128]{2,1,0:T(8,128)(2,1)} %get-tuple-element.24), channel_id=1, source_target_pairs={{0,4},{4,0},{1,5},{5,1},{2,6},{6,2},{3,7},{7,3},{8,12},{12,8},{9,1... | collective-permute-start | bytes 491528 | tf_op jit(solution)/shard_map/ppermute | solution.py:432
  25.9 49.8 %all-to-all-start.1 = ((bf16[16,176,128]{2,1,0:T(8,128)(2,1)}), bf16[16,176,128]{2,1,0:T(8,128)(2,1)S(1)}, u32[]{:S(2)}, u32[]{:S(2)}) async-start(bf16[16,176,128]{2,1,0:T(8,128)(2,1)} %get-tuple-element.25), calls=%async_computation.1 | async-start | bytes 1441792 | tf_op jit(solution)/shard_map/all_to_all | solution.py:450
  41.1 85.9 %all-gather.3.cloned.1.call-start = ((), (), s32[]{:S(2)}) async-start(), calls=%async_computation.5 | async-start | bytes 2228224 | tf_op jit(solution)/shard_map/all_gather | solution.py:451
  41.8 17.2 %collective-permute-start.1 = (bf16[128,1024]{1,0:T(8,128)(2,1)}, bf16[128,1024]{1,0:T(8,128)(2,1)S(1)}, u32[]{:S(2)}, u32[]{:S(2)}) collective-permute-start(bf16[128,1024]{1,0:T(8,128)(2,1)} %bitcast.10), channel_id=1, source_target_pairs={{0,128},{128,256},{256,384},{384,0},{1,129},{129,257},{257,385},{3... | collective-permute-start | bytes 786440 | tf_op jit(solution)/shard_map/ppermute | solution.py:455
  44.5 14.6 %collective-permute-start.2 = (f32[3,1024]{1,0:T(4,128)S(1)}, f32[3,1024]{1,0:T(4,128)S(1)}, u32[]{:S(2)}, u32[]{:S(2)}) collective-permute-start(f32[3,1024]{1,0:T(4,128)S(1)} %bitcast.42), channel_id=1, source_target_pairs={{0,128},{128,256},{256,384},{384,0},{1,129},{129,257},{257,385},{3... | collective-permute-start | bytes 36872 | tf_op jit(solution)/shard_map/ppermute | solution.py:456
  48.7 10.3 %collective-permute-start.3 = (bf16[2,1024]{1,0:T(2,128)(2,1)S(1)}, bf16[2,1024]{1,0:T(2,128)(2,1)S(1)}, u32[]{:S(2)}, u32[]{:S(2)}) collective-permute-start(bf16[2,1024]{1,0:T(2,128)(2,1)S(1)} %slice_bitcast_fusion), channel_id=1, source_target_pairs={{0,132},{4,136},{8,140},{12,144},{16,148},{20,152},{24,156},{28,16... | collective-permute-start | bytes 12296 | tf_op jit(solution)/shard_map/ppermute | solution.py:457
  59.0 18.1 %copy-start.8 = (f32[3,1024]{1,0:T(4,128)}, f32[3,1024]{1,0:T(4,128)S(1)}, u32[]{:S(2)}) copy-start(f32[3,1024]{1,0:T(4,128)S(1)} %collective-permute-done.2.taps_ref) | copy-start | bytes 36868
  77.2 6.9 %copy-start.3 = (bf16[2,256,256]{2,1,0:T(8,128)(2,1)S(1)}, bf16[2,256,256]{2,1,0:T(8,128)(2,1)}, u32[]{:S(2)}) copy-start(bf16[2,256,256]{2,1,0:T(8,128)(2,1)} %constant.42.clone.backward_ref) | copy-start | bytes 786436
  77.2 6.9 %copy-start.5 = (bf16[80,64]{1,0:T(8,128)(2,1)S(1)}, bf16[80,64]{1,0:T(8,128)(2,1)}, u32[]{:S(2)}) copy-start(bf16[80,64]{1,0:T(8,128)(2,1)} %constant.41.clone.first_ref) | copy-start | bytes 30724
  77.2 6.9 %copy-start.7 = (bf16[32,240]{1,0:T(8,128)(2,1)S(1)}, bf16[32,240]{1,0:T(8,128)(2,1)}, u32[]{:S(2)}) copy-start(bf16[32,240]{1,0:T(8,128)(2,1)} %constant.43.clone.last_ref) | copy-start | bytes 46084
  77.2 27.6 %all-to-all-start.2 = ((bf16[8,2,512,128]{3,2,1,0:T(8,128)(2,1)}), bf16[8,2,512,128]{3,2,1,0:T(8,128)(2,1)}, u32[]{:S(2)}, u32[]{:S(2)}) async-start(bf16[8,2,512,128]{3,2,1,0:T(8,128)(2,1)} %get-tuple-element.28), calls=%async_computation.2 | async-start | bytes 4194304 | tf_op jit(solution)/shard_map/all_to_all | solution.py:490
  110.7 38.1 %all-to-all-start.3 = ((bf16[16,96,128]{2,1,0:T(8,128)(2,1)}), bf16[16,96,128]{2,1,0:T(8,128)(2,1)S(1)}, u32[]{:S(2)}, u32[]{:S(2)}) async-start(bf16[16,96,128]{2,1,0:T(8,128)(2,1)} %shard_map.172), calls=%async_computation.3 | async-start | bytes 786432 | tf_op jit(solution)/shard_map/all_to_all | solution.py:522
  127.1 44.1 %copy-start.1 = (bf16[64,32,512]{2,1,0:T(8,128)(2,1)S(1)}, bf16[64,32,512]{2,1,0:T(8,128)(2,1)}, u32[]{:S(2)}) copy-start(bf16[64,32,512]{2,1,0:T(8,128)(2,1)} %all-gather.3.cloned.1.call-done) | copy-start | bytes 6291460
  149.9 21.3 %all-to-all-start.4 = ((bf16[8,32,2048]{2,1,0:T(8,128)(2,1)}), bf16[8,32,2048]{2,1,0:T(8,128)(2,1)S(1)}, u32[]{:S(2)}, u32[]{:S(2)}) async-start(bf16[8,32,2048]{2,1,0:T(8,128)(2,1)} %get-tuple-element.38), calls=%async_computation.4 | async-start | bytes 2097152 | tf_op jit(solution)/shard_map/all_to_all | solution.py:542
  155.2 19.3 %collective-permute-start.4 = (bf16[16,32,128]{2,1,0:T(8,128)(2,1)}, bf16[16,32,128]{2,1,0:T(8,128)(2,1)S(1)}, u32[]{:S(2)}, u32[]{:S(2)}) collective-permute-start(bf16[16,32,128]{2,1,0:T(8,128)(2,1)} %get-tuple-element.33), channel_id=1, source_target_pairs={{0,128},{128,256},{256,384},{384,0},{1,129},{129,257},{257,385},{3... | collective-permute-start | bytes 393224 | tf_op jit(solution)/shard_map/ppermute | solution.py:543
  157.2 17.4 %collective-permute-start.5 = (bf16[16,32,128]{2,1,0:T(8,128)(2,1)}, bf16[16,32,128]{2,1,0:T(8,128)(2,1)}, u32[]{:S(2)}, u32[]{:S(2)}) collective-permute-start(bf16[16,32,128]{2,1,0:T(8,128)(2,1)} %get-tuple-element.34), channel_id=1, source_target_pairs={{0,132},{4,128},{128,260},{132,256},{256,388},{260,384},{384,4},{3... | collective-permute-start | bytes 393224 | tf_op jit(solution)/shard_map/ppermute | solution.py:544
  171.2 3.4 %copy-start.9 = (f32[3,1024]{1,0:T(4,128)S(1)}, f32[3,1024]{1,0:T(4,128)}, u32[]{:S(2)}) copy-start(f32[3,1024]{1,0:T(4,128)} %copy-done.8) | copy-start | bytes 36868
  171.9 8.4 %collective-permute-start.6 = (bf16[128,512]{1,0:T(8,128)(2,1)S(1)}, bf16[128,512]{1,0:T(8,128)(2,1)S(1)}, u32[]{:S(2)}, u32[]{:S(2)}) collective-permute-start(bf16[128,512]{1,0:T(8,128)(2,1)S(1)} %get-tuple-element.41), channel_id=1, source_target_pairs={{0,4},{4,0},{1,5},{5,1},{2,6},{6,2},{3,7},{7,3},{8,12},{12,8},{9,1... | collective-permute-start | bytes 393224 | tf_op jit(solution)/shard_map/ppermute | solution.py:561
Sparse Core Ops, SparseCore 0:
  44.6 79.8 all-gather.2

commit v8 on v7

--- a/solution.py
+++ b/solution.py
@@ -53,7 +53,7 @@
 
 
 def kernel_call(
-    kernel, out_shape, scalars, arrays, scratch=(), flops=0, grant=32, hbm_in=(), hbm_out=()
+    kernel, out_shape, scalars, arrays, scratch=(), flops=0, grant=16, hbm_in=(), hbm_out=()
 ):
     single = not isinstance(out_shape, tuple)
     outs = (out_shape,) if single else out_shape
@@ -258,44 +258,81 @@
     out_ref[...] = signal_ref[...].astype(BF16).reshape(n_seq, channels, rows)
 
 
-def attend_kernel(rows, delta_ref, query_ref, pairs_ref, long_ref, out_ref):
+def attend(delta, query_ref, pairs_ref, tile, few, rows):
     size = 128
-    n_z, height, _ = out_ref.shape
-    own_rows = query_ref.shape[0]
-    part = own_rows // n_z
-    per = size // part
+    query = query_ref[tile * size : (tile + 1) * size, :]
     row = lax.broadcasted_iota(jnp.int32, (size, size), 0)
     column = lax.broadcasted_iota(jnp.int32, (size, size), 1)
-    q_pos = row // part * (2 * rows) + row % part
-    k_pos = column // part * (2 * rows) + column % part + delta_ref[0]
-    out_ref[:, part:, :] = long_ref[...]
-    for tile in range(own_rows // size):
-        query = query_ref[tile * size : (tile + 1) * size, :]
-        parts = []
-        for at in range(pairs_ref.shape[0]):
-            n_tp = pairs_ref.shape[0] // 2
-            allowed = k_pos + (at // n_tp * rows + at % n_tp * part) <= q_pos
-            for start, stop in ((0, tile * size), (tile * size, (tile + 1) * size)):
-                if start == stop:
-                    continue
-                keys = pairs_ref[at, 0, start:stop, :]
-                scores = dot(query, keys, ((1,), (1,))) * (1.0 / math.sqrt(HD))
-                if start == tile * size:
-                    parts.append((jnp.where(allowed, scores, -1e30), at, start, stop))
-                else:
-                    parts.append((scores, at, start, stop))
-        highest = parts[0][0].max(axis=1, keepdims=True)
-        for piece in parts[1:]:
-            highest = jnp.maximum(highest, piece[0].max(axis=1, keepdims=True))
-        totals = jnp.zeros((size, 1), F32)
-        weighted = jnp.zeros((size, HD), F32)
-        for scores, at, start, stop in parts:
-            probs = jnp.exp(scores - highest)
-            totals = totals + probs.sum(axis=1, keepdims=True)
-            values = pairs_ref[at, 1, start:stop, :]
-            weighted = weighted + dot(probs.astype(BF16), values, ((1,), (0,)))
-        out = (weighted / totals).astype(BF16).reshape(per, part, HD)
-        out_ref[tile * per : (tile + 1) * per, :part, :] = out
+    q_pos = row // few * rows + row % few
+    k_pos = column // few * rows + column % few
+    parts = []
+    for at in range(pairs_ref.shape[0]):
+        allowed = k_pos + (at * few + delta) <= q_pos
+        for start, stop in ((0, tile * size), (tile * size, (tile + 1) * size)):
+            if start == stop:
+                continue
+            keys = pairs_ref[at, 0, start:stop, :]
+            scores = dot(query, keys, ((1,), (1,))) * (1.0 / math.sqrt(HD))
+            if start == tile * size:
+                parts.append((jnp.where(allowed, scores, -1e30), allowed, at, start, stop))
+            else:
+                parts.append((scores, None, at, start, stop))
+    highest = parts[0][0].max(axis=1, keepdims=True)
+    for part in parts[1:]:
+        highest = jnp.maximum(highest, part[0].max(axis=1, keepdims=True))
+    totals = jnp.zeros((size, 1), F32)
+    weighted = jnp.zeros((size, HD), F32)
+    for scores, allowed, at, start, stop in parts:
+        probs = jnp.exp(scores - highest)
+        if allowed is not None:
+            probs = jnp.where(allowed, probs, 0.0)
+        totals = totals + probs.sum(axis=1, keepdims=True)
+        values = pairs_ref[at, 1, start:stop, :]
+        weighted = weighted + dot(probs.astype(BF16), values, ((1,), (0,)))
+    some = totals > 0.0
+    totals = jnp.maximum(totals, 1e-30)
+    return weighted / totals, jnp.where(some, highest + jnp.log(totals), -1e30)
+
+
+def other_kernel(rows, few, delta_ref, query_ref, pairs_ref, out_ref, log_ref):
+    own_rows = query_ref.shape[0]
+    log_ref[...] = jnp.zeros_like(log_ref)
+    for tile in range(own_rows // 128):
+        out, log = attend(delta_ref[0], query_ref, pairs_ref, tile, few, rows)
+        out_ref[tile * 128 : (tile + 1) * 128, :] = out.astype(BF16)
+        line = jnp.broadcast_to(log, (128, 128)).T[:8]
+        first = line.astype(BF16).astype(F32)
+        second = (line - first).astype(BF16).astype(F32)
+        third = line - first - second
+        for at, term in enumerate((first, second, third)):
+            log_ref[at * 8 + tile : at * 8 + tile + 1, :] = term[:1]
+    out_ref[own_rows:, :] = log_ref[...].astype(BF16)
+
+
+def own_kernel(rows, few, delta_ref, query_ref, pairs_ref, out_ref, log_ref):
+    for tile in range(query_ref.shape[0] // 128):
+        span = slice(tile * 128, (tile + 1) * 128)
+        out, log = attend(delta_ref[0], query_ref, pairs_ref, tile, few, rows)
+        out_ref[span, :] = out
+        log_ref[span, :] = jnp.broadcast_to(log, (128, 128))
+
+
+def merge_kernel(own_ref, log_ref, got_ref, long_ref, out_ref):
+    own_rows = own_ref.shape[0]
+    few = own_rows // out_ref.shape[0]
+    per = 128 // few
+    logs = got_ref[own_rows:, :].astype(F32)
+    for tile in range(own_rows // 128):
+        span = slice(tile * 128, (tile + 1) * 128)
+        log = log_ref[span, :]
+        line = logs[tile : tile + 1] + logs[8 + tile : 9 + tile] + logs[16 + tile : 17 + tile]
+        got_log = jnp.broadcast_to(line, (128, 128)).T
+        highest = jnp.maximum(log, got_log)
+        own_share, got_share = jnp.exp(log - highest), jnp.exp(got_log - highest)
+        merged = own_ref[span, :] * own_share + got_ref[span, :].astype(F32) * got_share
+        merged = (merged / (own_share + got_share)).astype(BF16).reshape(per, few, HD)
+        out_ref[tile * per : (tile + 1) * per, :few, :] = merged
+    out_ref[:, few:, :] = long_ref[...]
 
 
 def rows_kernel(
@@ -481,13 +518,14 @@
 
     sent_pairs, query = kernel_call(
         functools.partial(split_kernel, part),
-        (shape((n_plane, 2, own_rows, HD), BF16), shape((own_rows, HD), BF16)),
+        (shape((n_tp, 2, own_rows, HD), BF16), shape((own_rows, HD), BF16)),
         (),
         (mixed,),
-        (pltpu.VMEM((2, own_rows, HD), BF16), pltpu.SemaphoreType.DMA((n_plane,))),
+        (pltpu.VMEM((2, own_rows, HD), BF16), pltpu.SemaphoreType.DMA((n_tp,))),
         hbm_out=(0,),
     )
-    pairs = lax.all_to_all(sent_pairs, ("xh", "tp"), 0, 0)
+    other_query = lax.ppermute(query, "xh", swap)
+    pairs = lax.all_to_all(sent_pairs, "tp", 0, 0)
 
     gain = lax.dynamic_slice_in_dim(skip_gain[0], seq_at * channels, channels, 0)
     long_out = kernel_call(
@@ -510,14 +548,33 @@
         ),
     )
 
-    delta = -(x_at * rows + lax.axis_index("tp") * part)
+    pairs, long_out = lax.optimization_barrier((pairs, long_out))
+    work = 2 * own_rows * n_tp * own_rows * HD
+    own_delta = -lax.axis_index("tp") * part
+    other_delta = (2 * x_at - 1) * rows + own_delta
+    sent = kernel_call(
+        functools.partial(other_kernel, n_x * rows, part),
+        shape((own_rows + 32, HD), BF16),
+        (other_delta.astype(jnp.int32).reshape(1),),
+        (other_query, pairs),
+        (pltpu.VMEM((32, HD), F32),),
+        work,
+    )
+    got = lax.ppermute(sent, "xh", swap)
+    query, sent = lax.optimization_barrier((query, sent))
+    own_out, own_log = kernel_call(
+        functools.partial(own_kernel, n_x * rows, part),
+        (shape((own_rows, HD), F32),) * 2,
+        (own_delta.astype(jnp.int32).reshape(1),),
+        (query, pairs),
+        (),
+        work,
+    )
     returned = kernel_call(
-        functools.partial(attend_kernel, rows),
+        merge_kernel,
         shape((n_z, part + n_x * channels, HD), BF16),
-        (delta.astype(jnp.int32).reshape(1),),
-        (query, pairs, long_out.reshape(n_z, n_x * channels, rows)),
         (),
-        4 * own_rows * n_plane * own_rows * HD,
+        (own_out, own_log, got, long_out.reshape(n_z, n_x * channels, rows)),
     )
     back = lax.all_to_all(returned, "z", 0, 0)
     back, weight = lax.optimization_barrier((back, weight))

time: 189 us -> 183 us (0.968)
  waiting for transfers between devices: 73.6 us -> 62.4 us
  local copies, waits for them, and re-layouts: 2.56 us -> 5.39 us
    all_to_all x1, waiting for transfers between devices: 14.8 us -> 0.01 us  [body(): pairs = lax.all_to_all(sent_pairs, 'tp', 0, 0)]
    ppermute x0 -> x2, starting transfers between devices: none -> 7.36 us  [the longest x1 4.93 us: body(): other_query = lax.ppermute(query, 'xh', swap)]
    ppermute x0 -> x2, waiting for transfers between devices: none -> 3.83 us  [the longest x1 3.83 us: body(): got = lax.ppermute(sent, 'xh', swap)]
    unnamed x24 -> x38, local copies, waits for them, and re-layouts: 0.16 us -> 3.72 us
    all_to_all x1, starting transfers between devices: 6.77 us -> 4.2 us  [body(): pairs = lax.all_to_all(sent_pairs, 'tp', 0, 0)]
    all_gather x1, waiting for transfers between devices: 0.01 us -> 1.95 us  [body(): weight = lax.all_gather(weight, 'z')]
    pallas_call x10 -> x12, Pallas kernels: 23.7 us -> 23.7 us  [kernel_call(): pl.pallas_call(kernel, out_shape=placed[0] if single else placed, in_spec...]
  transfers between devices with their start and end apart: 13 -> 15, of which waited for: 8 -> 9; matrix products, arithmetic and copies ran while one was open for 1% -> 1% of each run, Pallas kernels for 9% -> 9%
where the time goes in v8:
time: 183 us; the launch traced here: 182 us
  starting transfers between devices  75.7 us (41%)
  waiting for transfers between devices  62.4 us (34%)
  Pallas kernels  23.7 us (13%)
  between operations  14.4 us (8%)
  local copies, waits for them, and re-layouts  5.39 us (3%)
    pallas_call x12, Pallas kernels, kernel_call(): pl.pallas_call(kernel, out_shape=placed[0] if single else placed, in_spec...  23.7 us
    all_to_all x1, waiting for transfers between devices, body(): back = lax.all_to_all(returned, 'z', 0, 0)  20.3 us
    all_to_all x1, waiting for transfers between devices, body(): mixed = lax.all_to_all(packed, 'z', 0, 0)  15.4 us
    all_to_all x1, starting transfers between devices, body(): mixed = lax.all_to_all(packed, 'z', 0, 0)  15.2 us
    all_to_all x1, starting transfers between devices, body(): back = lax.all_to_all(returned, 'z', 0, 0)  14.9 us
    all_to_all x1, waiting for transfers between devices, body(): plane_rows = lax.all_to_all(plane_rows, ('xh', 'tp'), 0, 0)  7.7 us
    ppermute x1, starting transfers between devices, body(): lax.ppermute(other_long, ('section', 'xh'), [(2 * s + x, 2 * t + 1 - x) f...  6.11 us
    ppermute x1, starting transfers between devices, body(): other_query = lax.ppermute(query, 'xh', swap)  4.93 us
  transfers between devices with their start and end apart: 15, of which 9 were waited for; matrix products, arithmetic and copies ran while one was open for 1% of the time, Pallas kernels for 9%

profile of v8, /device:TPU:32, one launch (start us, length us, event | category | flops | bytes accessed | tf_op | source)
XLA Modules:
  0.0 181.6 jit_solution(12376928617362132253)
XLA Ops:
  7.2 2.7 %shard_map.167 = (bf16[4,128,512]{2,1,0:T(8,128)(2,1)}, bf16[16,40,128]{2,1,0:T(8,128)(2,1)}, bf16[16,40,128]{2,1,0:T(8,128)(2,1)}) custom-call(s32[1]{0:T(128)} %bitcast.x_ref, bf16[128,1024]{1,0:T(8,128)(2,1)} %bitcast.35, bf16[128,1024]{1,0:T(8,128)(2,1)} %bitcast.36, f32[9,1,1024]{2,1,0:T(1,128)} %bitcast.42, bf16[128,512]{1,0:T(8,128)(2,1)} %bitcast.38, ...), custom_call_target="tpu_custom_call" | custom-call | bytes 1937408 | tf_op jit(solution)/shard_map/pallas_call | solution.py:75
  9.9 4.6 %all-to-all-start = ((bf16[4,128,512]{2,1,0:T(8,128)(2,1)}), bf16[4,128,512]{2,1,0:T(8,128)(2,1)S(1)}, u32[]{:S(2)}, u32[]{:S(2)}) async-start(bf16[4,128,512]{2,1,0:T(8,128)(2,1)} %get-tuple-element.27), calls=%async_computation | async-start | bytes 1048576 | tf_op jit(solution)/shard_map/all_to_all | solution.py:470
  14.5 4.9 %collective-permute-start = (bf16[16,40,128]{2,1,0:T(8,128)(2,1)}, bf16[16,40,128]{2,1,0:T(8,128)(2,1)S(1)}, u32[]{:S(2)}, u32[]{:S(2)}) collective-permute-start(bf16[16,40,128]{2,1,0:T(8,128)(2,1)} %get-tuple-element.29), channel_id=1, source_target_pairs={{0,4},{4,0},{1,5},{5,1},{2,6},{6,2},{3,7},{7,3},{8,12},{12,8},{9,1... | collective-permute-start | bytes 491528 | tf_op jit(solution)/shard_map/ppermute | solution.py:469
  19.4 4.3 %collective-permute-done.got_ref = bf16[16,40,128]{2,1,0:T(8,128)(2,1)S(1)} collective-permute-done((bf16[16,40,128]{2,1,0:T(8,128)(2,1)}, bf16[16,40,128]{2,1,0:T(8,128)(2,1)S(1)}, u32[]{:S(2)}, u32[]{:S(2)}) %collective-permute-start) | collective-permute-done | bytes 163872 | tf_op jit(solution)/shard_map/ppermute | solution.py:469
  24.0 1.9 %shard_map.168 = (bf16[16,176,128]{2,1,0:T(8,128)(2,1)}, bf16[4,32,512]{2,1,0:T(8,128)(2,1)}) custom-call(s32[1]{0:T(128)} %bitcast.x_ref, bf16[4,128,512]{2,1,0:T(8,128)(2,1)S(1)} %all-to-all-done.rows_ref, bf16[16,40,128]{2,1,0:T(8,128)(2,1)} %get-tuple-element.28.own_hbm, bf16[16,40,128]{2,1,0:T(8,128)(2,1)S(1)} %collective-permute-done.got_ref), custom_call_target="tpu_custom_call" | custom-call | bytes 1703936 | tf_op jit(solution)/shard_map/pallas_call | solution.py:75
  25.9 15.2 %all-to-all-start.1 = ((bf16[16,176,128]{2,1,0:T(8,128)(2,1)}), bf16[16,176,128]{2,1,0:T(8,128)(2,1)S(1)}, u32[]{:S(2)}, u32[]{:S(2)}) async-start(bf16[16,176,128]{2,1,0:T(8,128)(2,1)} %get-tuple-element.30), calls=%async_computation.1 | async-start | bytes 1441792 | tf_op jit(solution)/shard_map/all_to_all | solution.py:487
  41.9 1.9 %collective-permute-start.1 = (bf16[128,1024]{1,0:T(8,128)(2,1)S(1)}, bf16[128,1024]{1,0:T(8,128)(2,1)S(1)}, u32[]{:S(2)}, u32[]{:S(2)}) collective-permute-start(bf16[128,1024]{1,0:T(8,128)(2,1)S(1)} %bitcast.44), channel_id=1, source_target_pairs={{0,128},{128,256},{256,384},{384,0},{1,129},{129,257},{257,385},{3... | collective-permute-start | bytes 786440 | tf_op jit(solution)/shard_map/ppermute | solution.py:492
  44.5 3.5 %collective-permute-start.2 = (f32[3,1024]{1,0:T(4,128)S(1)}, f32[3,1024]{1,0:T(4,128)S(1)}, u32[]{:S(2)}, u32[]{:S(2)}) collective-permute-start(f32[3,1024]{1,0:T(4,128)S(1)} %bitcast.43), channel_id=1, source_target_pairs={{0,128},{128,256},{256,384},{384,0},{1,129},{129,257},{257,385},{3... | collective-permute-start | bytes 36872 | tf_op jit(solution)/shard_map/ppermute | solution.py:493
  48.0 4.3 %collective-permute-start.3 = (bf16[2,1024]{1,0:T(2,128)(2,1)S(1)}, bf16[2,1024]{1,0:T(2,128)(2,1)S(1)}, u32[]{:S(2)}, u32[]{:S(2)}) collective-permute-start(bf16[2,1024]{1,0:T(2,128)(2,1)S(1)} %slice_bitcast_fusion), channel_id=1, source_target_pairs={{0,132},{4,136},{8,140},{12,144},{16,148},{20,152},{24,156},{28,16... | collective-permute-start | bytes 12296 | tf_op jit(solution)/shard_map/ppermute | solution.py:494
  53.3 1.1 shard_map.169.spectrum_ref
  54.4 4.7 %collective-permute-done.3.tail_ref = bf16[2,1024]{1,0:T(2,128)(2,1)S(1)} collective-permute-done((bf16[2,1024]{1,0:T(2,128)(2,1)S(1)}, bf16[2,1024]{1,0:T(2,128)(2,1)S(1)}, u32[]{:S(2)}, u32[]{:S(2)}) %collective-permute-start.3) | collective-permute-done | bytes 4128 | tf_op jit(solution)/shard_map/ppermute | solution.py:494
  60.3 15.4 %all-to-all-done.1.mixed_ref = bf16[16,176,128]{2,1,0:T(8,128)(2,1)S(1)} async-done(((bf16[16,176,128]{2,1,0:T(8,128)(2,1)}), bf16[16,176,128]{2,1,0:T(8,128)(2,1)S(1)}, u32[]{:S(2)}, u32[]{:S(2)}) %all-to-all-start.1) | async-done | bytes 720928 | tf_op jit(solution)/shard_map/all_to_all | solution.py:487
  75.7 1.1 shard_map.170
  76.7 4.2 %all-to-all-start.2 = ((bf16[4,2,512,128]{3,2,1,0:T(8,128)(2,1)}), bf16[4,2,512,128]{3,2,1,0:T(8,128)(2,1)S(1)}, u32[]{:S(2)}, u32[]{:S(2)}) async-start(bf16[4,2,512,128]{3,2,1,0:T(8,128)(2,1)} %get-tuple-element.33), calls=%async_computation.2 | async-start | bytes 2097152 | tf_op jit(solution)/shard_map/all_to_all | solution.py:528
  80.9 4.9 %collective-permute-start.4 = (bf16[512,128]{1,0:T(8,128)(2,1)S(1)}, bf16[512,128]{1,0:T(8,128)(2,1)}, u32[]{:S(2)}, u32[]{:S(2)}) collective-permute-start(bf16[512,128]{1,0:T(8,128)(2,1)S(1)} %get-tuple-element.37.query_ref), channel_id=1, source_target_pairs={{0,4},{4,0},{1,5},{5,1},{2,6},{6,2},{3,7},{7,3},{8,12},{12,8},{9,1... | collective-permute-start | bytes 393224 | tf_op jit(solution)/shard_map/ppermute | solution.py:527
  87.6 6.0 %shard_map.171 = bf16[32,32,128]{2,1,0:T(8,128)(2,1)S(1)} custom-call(f32[32]{0:T(128)S(1)} %dynamic-slice_bitcast_fusion.gain_ref, bf16[16,176,128]{2,1,0:T(8,128)(2,1)S(1)} %all-to-all-done.1.mixed_ref, f32[32,9]{1,0:T(8,128)S(1)} %bitcast.32, f32[1280,256]{1,0:T(8,128)S(1)} %shard_map.169.spectrum_ref, bf16[80,64]{1,0:T(8,128)(2,1)S(1)} %copy-done.9, ...), custom_call_target="tpu_custom_call" | custom-call | bytes 2885760 | tf_op jit(solution)/shard_map/pallas_call | solution.py:75
  94.3 3.1 %shard_map.172 = bf16[544,128]{1,0:T(8,128)(2,1)S(1)} custom-call(s32[1]{0:T(128)} %bitcast.14.delta_ref, bf16[512,128]{1,0:T(8,128)(2,1)} %collective-permute-done.4.query_ref, bf16[4,2,512,128]{3,2,1,0:T(8,128)(2,1)S(1)} %all-to-all-done.2.pairs_ref), custom_call_target="tpu_custom_call" | custom-call | flops 268435456 | bytes 1318912 | tf_op jit(solution)/shard_map/pallas_call | solution.py:75
  97.4 2.4 %collective-permute-start.5 = (bf16[544,128]{1,0:T(8,128)(2,1)S(1)}, bf16[544,128]{1,0:T(8,128)(2,1)S(1)}, u32[]{:S(2)}, u32[]{:S(2)}) collective-permute-start(bf16[544,128]{1,0:T(8,128)(2,1)S(1)} %shard_map.172), channel_id=1, source_target_pairs={{0,4},{4,0},{1,5},{5,1},{2,6},{6,2},{3,7},{7,3},{8,12},{12,8},{9,1... | collective-permute-start | bytes 417800 | tf_op jit(solution)/shard_map/ppermute | solution.py:563
  99.9 2.2 %shard_map.173 = (f32[512,128]{1,0:T(8,128)S(1)}, f32[512,128]{1,0:T(8,128)S(1)}) custom-call(s32[1]{0:T(128)} %bitcast.1.delta_ref, bf16[512,128]{1,0:T(8,128)(2,1)S(1)} %get-tuple-element.37.query_ref, bf16[4,2,512,128]{3,2,1,0:T(8,128)(2,1)S(1)} %all-to-all-done.2.pairs_ref), custom_call_target="tpu_custom_call" | custom-call | flops 268435456 | bytes 1703936 | tf_op jit(solution)/shard_map/pallas_call | solution.py:75
  102.0 3.8 %collective-permute-done.5.got_ref = bf16[544,128]{1,0:T(8,128)(2,1)S(1)} collective-permute-done((bf16[544,128]{1,0:T(8,128)(2,1)S(1)}, bf16[544,128]{1,0:T(8,128)(2,1)S(1)}, u32[]{:S(2)}, u32[]{:S(2)}) %collective-permute-start.5) | collective-permute-done | bytes 139296 | tf_op jit(solution)/shard_map/ppermute | solution.py:563
  106.9 14.9 %all-to-all-start.3 = ((bf16[16,96,128]{2,1,0:T(8,128)(2,1)}), bf16[16,96,128]{2,1,0:T(8,128)(2,1)S(1)}, u32[]{:S(2)}, u32[]{:S(2)}) async-start(bf16[16,96,128]{2,1,0:T(8,128)(2,1)} %shard_map.174), calls=%async_computation.3 | async-start | bytes 786432 | tf_op jit(solution)/shard_map/all_to_all | solution.py:579
  121.8 2.0 %all-gather.3.cloned.1.call-done = bf16[64,32,512]{2,1,0:T(8,128)(2,1)} async-done(((bf16[4,32,512]{2,1,0:T(8,128)(2,1)}), bf16[64,32,512]{2,1,0:T(8,128)(2,1)}) %all-gather.3.cloned.1.call-update) | async-done | bytes 2097168 | tf_op jit(solution)/shard_map/all_gather | solution.py:488
  123.7 20.3 %all-to-all-done.3.back_ref = bf16[16,96,128]{2,1,0:T(8,128)(2,1)S(1)} async-done(((bf16[16,96,128]{2,1,0:T(8,128)(2,1)}), bf16[16,96,128]{2,1,0:T(8,128)(2,1)S(1)}, u32[]{:S(2)}, u32[]{:S(2)}) %all-to-all-start.3) | async-done | bytes 393248 | tf_op jit(solution)/shard_map/all_to_all | solution.py:579
  144.0 1.1 shard_map.175
  145.2 3.6 %all-to-all-start.4 = ((bf16[8,32,2048]{2,1,0:T(8,128)(2,1)}), bf16[8,32,2048]{2,1,0:T(8,128)(2,1)S(1)}, u32[]{:S(2)}, u32[]{:S(2)}) async-start(bf16[8,32,2048]{2,1,0:T(8,128)(2,1)} %get-tuple-element.48), calls=%async_computation.4 | async-start | bytes 2097152 | tf_op jit(solution)/shard_map/all_to_all | solution.py:599
  148.8 2.1 %collective-permute-start.6 = (bf16[16,32,128]{2,1,0:T(8,128)(2,1)}, bf16[16,32,128]{2,1,0:T(8,128)(2,1)S(1)}, u32[]{:S(2)}, u32[]{:S(2)}) collective-permute-start(bf16[16,32,128]{2,1,0:T(8,128)(2,1)} %get-tuple-element.43), channel_id=1, source_target_pairs={{0,128},{128,256},{256,384},{384,0},{1,129},{129,257},{257,385},{3... | collective-permute-start | bytes 393224 | tf_op jit(solution)/shard_map/ppermute | solution.py:600
  150.9 6.1 %collective-permute-start.7 = (bf16[16,32,128]{2,1,0:T(8,128)(2,1)}, bf16[16,32,128]{2,1,0:T(8,128)(2,1)}, u32[]{:S(2)}, u32[]{:S(2)}) collective-permute-start(bf16[16,32,128]{2,1,0:T(8,128)(2,1)} %get-tuple-element.44), channel_id=1, source_target_pairs={{0,132},{4,128},{128,260},{132,256},{256,388},{260,384},{384,4},{3... | collective-permute-start | bytes 393224 | tf_op jit(solution)/shard_map/ppermute | solution.py:601
  157.0 7.7 %all-to-all-done.4.rows_ref = bf16[8,32,2048]{2,1,0:T(8,128)(2,1)S(1)} async-done(((bf16[8,32,2048]{2,1,0:T(8,128)(2,1)}), bf16[8,32,2048]{2,1,0:T(8,128)(2,1)S(1)}, u32[]{:S(2)}, u32[]{:S(2)}) %all-to-all-start.4) | async-done | bytes 1048608 | tf_op jit(solution)/shard_map/all_to_all | solution.py:599
  165.4 3.1 %collective-permute-start.8 = (bf16[128,512]{1,0:T(8,128)(2,1)S(1)}, bf16[128,512]{1,0:T(8,128)(2,1)S(1)}, u32[]{:S(2)}, u32[]{:S(2)}) collective-permute-start(bf16[128,512]{1,0:T(8,128)(2,1)S(1)} %get-tuple-element.51), channel_id=1, source_target_pairs={{0,4},{4,0},{1,5},{5,1},{2,6},{6,2},{3,7},{7,3},{8,12},{12,8},{9,1... | collective-permute-start | bytes 393224 | tf_op jit(solution)/shard_map/ppermute | solution.py:618
  168.5 1.9 %shard_map.176 = bf16[128,1024]{1,0:T(8,128)(2,1)} custom-call(s32[1]{0:T(128)} %bitcast.x_ref, bf16[16,32,128]{2,1,0:T(8,128)(2,1)S(1)} %collective-permute-done.6.own_ref, bf16[16,32,128]{2,1,0:T(8,128)(2,1)} %collective-permute-done.7.got_ref, bf16[128,1024]{1,0:T(8,128)(2,1)S(1)} %copy-done.7, bf16[2,1024]{1,0:T(2,128)(2,1)S(1)} %copy-done.15, ...), custom_call_target="tpu_custom_call" | custom-call | bytes 802816 | tf_op jit(solution)/shard_map/pallas_call | solution.py:75
  170.4 3.3 %collective-permute-done.8.got_ref = bf16[128,512]{1,0:T(8,128)(2,1)S(1)} collective-permute-done((bf16[128,512]{1,0:T(8,128)(2,1)S(1)}, bf16[128,512]{1,0:T(8,128)(2,1)S(1)}, u32[]{:S(2)}, u32[]{:S(2)}) %collective-permute-start.8) | collective-permute-done | bytes 131104 | tf_op jit(solution)/shard_map/ppermute | solution.py:618
  173.8 1.0 shard_map.178
  (55 shorter events, 8.1 us)
Async XLA Ops:
  7.2 78.7 %copy-start = (f32[1,1024]{1,0:T(1,128)S(1)}, f32[1,1024]{1,0:T(1,128)}, u32[]{:S(2)}) copy-start(f32[1,1024]{1,0:T(1,128)} %param.21) | copy-start | bytes 12292
  7.2 34.7 %copy-start.17 = (bf16[1,128,1024]{2,1,0:T(8,128)(2,1)S(1)}, bf16[1,128,1024]{2,1,0:T(8,128)(2,1)}, u32[]{:S(2)}) copy-start(bf16[1,128,1024]{2,1,0:T(8,128)(2,1)} %param.17) | copy-start | bytes 786436
  7.2 46.0 %copy-start.16 = (f32[1,1,1,32,4096]{4,3,2,1,0:T(8,128)S(1)}, f32[1,1,1,32,4096]{4,3,2,1,0:T(8,128)}, u32[]{:S(2)}) copy-start(f32[1,1,1,32,4096]{4,3,2,1,0:T(8,128)} %param.20) | copy-start | bytes 1572868
  9.9 43.4 %copy-start.2 = (bf16[2,256,256]{2,1,0:T(8,128)(2,1)S(1)}, bf16[2,256,256]{2,1,0:T(8,128)(2,1)}, u32[]{:S(2)}) copy-start(bf16[2,256,256]{2,1,0:T(8,128)(2,1)} %constant.43.clone.forward_ref) | copy-start | bytes 786436
  9.9 43.4 %copy-start.8 = (f32[2,40,128]{2,1,0:T(8,128)S(1)}, f32[2,40,128]{2,1,0:T(8,128)}, u32[]{:S(2)}) copy-start(f32[2,40,128]{2,1,0:T(8,128)} %constant.42.clone.mid_ref) | copy-start | bytes 122884
  9.9 43.4 %copy-start.10 = (bf16[80,96]{1,0:T(8,128)(2,1)S(1)}, bf16[80,96]{1,0:T(8,128)(2,1)}, u32[]{:S(2)}) copy-start(bf16[80,96]{1,0:T(8,128)(2,1)} %constant.41.clone.first_ref) | copy-start | bytes 46084
  9.9 14.1 %all-to-all-start = ((bf16[4,128,512]{2,1,0:T(8,128)(2,1)}), bf16[4,128,512]{2,1,0:T(8,128)(2,1)S(1)}, u32[]{:S(2)}, u32[]{:S(2)}) async-start(bf16[4,128,512]{2,1,0:T(8,128)(2,1)} %get-tuple-element.27), calls=%async_computation | async-start | bytes 1048576 | tf_op jit(solution)/shard_map/all_to_all | solution.py:470
  14.5 9.3 %collective-permute-start = (bf16[16,40,128]{2,1,0:T(8,128)(2,1)}, bf16[16,40,128]{2,1,0:T(8,128)(2,1)S(1)}, u32[]{:S(2)}, u32[]{:S(2)}) collective-permute-start(bf16[16,40,128]{2,1,0:T(8,128)(2,1)} %get-tuple-element.29), channel_id=1, source_target_pairs={{0,4},{4,0},{1,5},{5,1},{2,6},{6,2},{3,7},{7,3},{8,12},{12,8},{9,1... | collective-permute-start | bytes 491528 | tf_op jit(solution)/shard_map/ppermute | solution.py:469
  25.9 49.7 %all-to-all-start.1 = ((bf16[16,176,128]{2,1,0:T(8,128)(2,1)}), bf16[16,176,128]{2,1,0:T(8,128)(2,1)S(1)}, u32[]{:S(2)}, u32[]{:S(2)}) async-start(bf16[16,176,128]{2,1,0:T(8,128)(2,1)} %get-tuple-element.30), calls=%async_computation.1 | async-start | bytes 1441792 | tf_op jit(solution)/shard_map/all_to_all | solution.py:487
  41.1 82.6 %all-gather.3.cloned.1.call-start = ((), (), s32[]{:S(2)}) async-start(), calls=%async_computation.5 | async-start | bytes 2228224 | tf_op jit(solution)/shard_map/all_gather | solution.py:488
  41.9 18.4 %collective-permute-start.1 = (bf16[128,1024]{1,0:T(8,128)(2,1)S(1)}, bf16[128,1024]{1,0:T(8,128)(2,1)S(1)}, u32[]{:S(2)}, u32[]{:S(2)}) collective-permute-start(bf16[128,1024]{1,0:T(8,128)(2,1)S(1)} %bitcast.44), channel_id=1, source_target_pairs={{0,128},{128,256},{256,384},{384,0},{1,129},{129,257},{257,385},{3... | collective-permute-start | bytes 786440 | tf_op jit(solution)/shard_map/ppermute | solution.py:492
  44.5 15.1 %collective-permute-start.2 = (f32[3,1024]{1,0:T(4,128)S(1)}, f32[3,1024]{1,0:T(4,128)S(1)}, u32[]{:S(2)}, u32[]{:S(2)}) collective-permute-start(f32[3,1024]{1,0:T(4,128)S(1)} %bitcast.43), channel_id=1, source_target_pairs={{0,128},{128,256},{256,384},{384,0},{1,129},{129,257},{257,385},{3... | collective-permute-start | bytes 36872 | tf_op jit(solution)/shard_map/ppermute | solution.py:493
  48.0 11.0 %collective-permute-start.3 = (bf16[2,1024]{1,0:T(2,128)(2,1)S(1)}, bf16[2,1024]{1,0:T(2,128)(2,1)S(1)}, u32[]{:S(2)}, u32[]{:S(2)}) collective-permute-start(bf16[2,1024]{1,0:T(2,128)(2,1)S(1)} %slice_bitcast_fusion), channel_id=1, source_target_pairs={{0,132},{4,136},{8,140},{12,144},{16,148},{20,152},{24,156},{28,16... | collective-permute-start | bytes 12296 | tf_op jit(solution)/shard_map/ppermute | solution.py:494
  53.3 32.6 %copy-start.9 = (bf16[80,64]{1,0:T(8,128)(2,1)S(1)}, bf16[80,64]{1,0:T(8,128)(2,1)}, u32[]{:S(2)}) copy-start(bf16[80,64]{1,0:T(8,128)(2,1)} %constant.44.clone.first_ref) | copy-start | bytes 30724
  59.7 0.6 copy-start.12
  60.3 16.5 %copy-start.6 = (bf16[128,1024]{1,0:T(8,128)(2,1)}, bf16[128,1024]{1,0:T(8,128)(2,1)S(1)}, u32[]{:S(2)}) copy-start(bf16[128,1024]{1,0:T(8,128)(2,1)S(1)} %collective-permute-done.1.gate_ref) | copy-start | bytes 786436
  76.7 17.6 %all-to-all-start.2 = ((bf16[4,2,512,128]{3,2,1,0:T(8,128)(2,1)}), bf16[4,2,512,128]{3,2,1,0:T(8,128)(2,1)S(1)}, u32[]{:S(2)}, u32[]{:S(2)}) async-start(bf16[4,2,512,128]{3,2,1,0:T(8,128)(2,1)} %get-tuple-element.33), calls=%async_computation.2 | async-start | bytes 2097152 | tf_op jit(solution)/shard_map/all_to_all | solution.py:528
  80.9 13.4 %collective-permute-start.4 = (bf16[512,128]{1,0:T(8,128)(2,1)S(1)}, bf16[512,128]{1,0:T(8,128)(2,1)}, u32[]{:S(2)}, u32[]{:S(2)}) collective-permute-start(bf16[512,128]{1,0:T(8,128)(2,1)S(1)} %get-tuple-element.37.query_ref), channel_id=1, source_target_pairs={{0,4},{4,0},{1,5},{5,1},{2,6},{6,2},{3,7},{7,3},{8,12},{12,8},{9,1... | collective-permute-start | bytes 393224 | tf_op jit(solution)/shard_map/ppermute | solution.py:527
  86.0 1.0 copy-start.5
  86.9 0.7 copy-start.11
  93.6 0.7 copy-start.3
  94.3 11.6 %copy-start.4 = (bf16[32,32,128]{2,1,0:T(8,128)(2,1)S(1)}, bf16[32,32,128]{2,1,0:T(8,128)(2,1)}, u32[]{:S(2)}) copy-start(bf16[32,32,128]{2,1,0:T(8,128)(2,1)} %copy-done.3) | copy-start | bytes 786436
  97.4 8.5 %collective-permute-start.5 = (bf16[544,128]{1,0:T(8,128)(2,1)S(1)}, bf16[544,128]{1,0:T(8,128)(2,1)S(1)}, u32[]{:S(2)}, u32[]{:S(2)}) collective-permute-start(bf16[544,128]{1,0:T(8,128)(2,1)S(1)} %shard_map.172), channel_id=1, source_target_pairs={{0,4},{4,0},{1,5},{5,1},{2,6},{6,2},{3,7},{7,3},{8,12},{12,8},{9,1... | collective-permute-start | bytes 417800 | tf_op jit(solution)/shard_map/ppermute | solution.py:563
  106.9 37.2 %all-to-all-start.3 = ((bf16[16,96,128]{2,1,0:T(8,128)(2,1)}), bf16[16,96,128]{2,1,0:T(8,128)(2,1)S(1)}, u32[]{:S(2)}, u32[]{:S(2)}) async-start(bf16[16,96,128]{2,1,0:T(8,128)(2,1)} %shard_map.174), calls=%async_computation.3 | async-start | bytes 786432 | tf_op jit(solution)/shard_map/all_to_all | solution.py:579
  123.7 40.9 %copy-start.1 = (bf16[64,32,512]{2,1,0:T(8,128)(2,1)S(1)}, bf16[64,32,512]{2,1,0:T(8,128)(2,1)}, u32[]{:S(2)}) copy-start(bf16[64,32,512]{2,1,0:T(8,128)(2,1)} %all-gather.3.cloned.1.call-done) | copy-start | bytes 6291460
  145.2 19.5 %all-to-all-start.4 = ((bf16[8,32,2048]{2,1,0:T(8,128)(2,1)}), bf16[8,32,2048]{2,1,0:T(8,128)(2,1)S(1)}, u32[]{:S(2)}, u32[]{:S(2)}) async-start(bf16[8,32,2048]{2,1,0:T(8,128)(2,1)} %get-tuple-element.48), calls=%async_computation.4 | async-start | bytes 2097152 | tf_op jit(solution)/shard_map/all_to_all | solution.py:599
  148.8 19.7 %copy-start.7 = (bf16[128,1024]{1,0:T(8,128)(2,1)S(1)}, bf16[128,1024]{1,0:T(8,128)(2,1)}, u32[]{:S(2)}) copy-start(bf16[128,1024]{1,0:T(8,128)(2,1)} %copy-done.6) | copy-start | bytes 786436
  148.8 19.7 %copy-start.15 = (bf16[2,1024]{1,0:T(2,128)(2,1)S(1)}, bf16[2,1024]{1,0:T(2,128)(2,1)}, u32[]{:S(2)}) copy-start(bf16[2,1024]{1,0:T(2,128)(2,1)} %copy-done.14) | copy-start | bytes 12292
  148.8 19.7 %collective-permute-start.6 = (bf16[16,32,128]{2,1,0:T(8,128)(2,1)}, bf16[16,32,128]{2,1,0:T(8,128)(2,1)S(1)}, u32[]{:S(2)}, u32[]{:S(2)}) collective-permute-start(bf16[16,32,128]{2,1,0:T(8,128)(2,1)} %get-tuple-element.43), channel_id=1, source_target_pairs={{0,128},{128,256},{256,384},{384,0},{1,129},{129,257},{257,385},{3... | collective-permute-start | bytes 393224 | tf_op jit(solution)/shard_map/ppermute | solution.py:600
  150.9 17.7 %collective-permute-start.7 = (bf16[16,32,128]{2,1,0:T(8,128)(2,1)}, bf16[16,32,128]{2,1,0:T(8,128)(2,1)}, u32[]{:S(2)}, u32[]{:S(2)}) collective-permute-start(bf16[16,32,128]{2,1,0:T(8,128)(2,1)} %get-tuple-element.44), channel_id=1, source_target_pairs={{0,132},{4,128},{128,260},{132,256},{256,388},{260,384},{384,4},{3... | collective-permute-start | bytes 393224 | tf_op jit(solution)/shard_map/ppermute | solution.py:601
  164.7 3.9 %copy-start.13 = (f32[3,1024]{1,0:T(4,128)S(1)}, f32[3,1024]{1,0:T(4,128)}, u32[]{:S(2)}) copy-start(f32[3,1024]{1,0:T(4,128)} %copy-done.12) | copy-start | bytes 36868
  165.4 8.4 %collective-permute-start.8 = (bf16[128,512]{1,0:T(8,128)(2,1)S(1)}, bf16[128,512]{1,0:T(8,128)(2,1)S(1)}, u32[]{:S(2)}, u32[]{:S(2)}) collective-permute-start(bf16[128,512]{1,0:T(8,128)(2,1)S(1)} %get-tuple-element.51), channel_id=1, source_target_pairs={{0,4},{4,0},{1,5},{5,1},{2,6},{6,2},{3,7},{7,3},{8,12},{12,8},{9,1... | collective-permute-start | bytes 393224 | tf_op jit(solution)/shard_map/ppermute | solution.py:618
  (1 other events, 0.6 us)
Sparse Core Ops, SparseCore 0:
  44.0 79.6 all-gather.2

commit v9 on v8

--- a/solution.py
+++ b/solution.py
@@ -53,7 +53,16 @@
 
 
 def kernel_call(
-    kernel, out_shape, scalars, arrays, scratch=(), flops=0, grant=16, hbm_in=(), hbm_out=()
+    kernel,
+    out_shape,
+    scalars,
+    arrays,
+    scratch=(),
+    flops=0,
+    grant=16,
+    hbm_in=(),
+    hbm_out=(),
+    from_hbm=(),
 ):
     single = not isinstance(out_shape, tuple)
     outs = (out_shape,) if single else out_shape
@@ -62,7 +71,7 @@
         return pl.BlockSpec(memory_space=pltpu.HBM if at in hbm else pltpu.VMEM)
 
     arrays = [
-        pltpu.with_memory_space_constraint(x, pltpu.HBM) if at in hbm_in else x
+        pltpu.with_memory_space_constraint(jnp.asarray(x), pltpu.HBM) if at in hbm_in + from_hbm else x
         for at, x in enumerate(arrays)
     ]
     in_specs = [pl.BlockSpec(memory_space=pltpu.SMEM)] * len(scalars)
@@ -195,22 +204,23 @@
         out_ref[span, :] = dot_three(turned_ref[span, :], forward_ref[0], forward_ref[1])
 
 
-def convolve_kernel(
+def signal_kernel(
     start,
-    gain_ref,
     mixed_ref,
     taps_ref,
     spectrum_ref,
     first_ref,
     mid_ref,
     forward_ref,
-    backward_ref,
-    last_ref,
     out_ref,
     signal_ref,
+    done_ref,
     turned_ref,
 ):
-    n_seq, channels, rows = out_ref.shape
+    done_ref[...] = jnp.zeros_like(done_ref)
+    rows, half = mid_ref.shape[2], mid_ref.shape[1]
+    channels = out_ref.shape[0] // half
+    n_seq = signal_ref.shape[0] // channels
     count = n_seq * 8
     edges = mixed_ref[:, start + 2 * channels :, :].astype(F32).reshape(count, rows).T[:channels]
     lane = lax.broadcasted_iota(jnp.int32, (channels, count), 1)
@@ -229,7 +239,6 @@
         signal_ref[at * channels : (at + 1) * channels, :] = jnp.where(
             column < 2, turned[:, :rows], block
         )
-    half = mid_ref.shape[1]
     cos_mid, sin_mid = mid_ref[0], mid_ref[1]
     for at in range(channels):
         signal = signal_ref[pl.ds(at, n_seq, stride=channels), :].astype(BF16)
@@ -241,10 +250,20 @@
         mine = dot_three(turned_ref[span, :], forward_ref[0], forward_ref[1])
         real, imag = mine[:, :rows], mine[:, rows:]
         other_real, other_imag = spectrum_ref[span, :rows], spectrum_ref[span, rows:]
-        joined = jnp.concatenate(
-            [real * other_real - imag * other_imag, real * other_imag + imag * other_real], axis=1
-        )
-        mid = dot_three(joined, backward_ref[0], backward_ref[1])
+        out_ref[span, :rows] = real * other_real - imag * other_imag
+        out_ref[span, rows:] = real * other_imag + imag * other_real
+
+
+def convolve_kernel(
+    gain_ref, joined_ref, signal_ref, mid_ref, backward_ref, last_ref, out_ref, long_ref
+):
+    n_seq, channels, rows = out_ref.shape
+    half = mid_ref.shape[1]
+    cos_mid, sin_mid = mid_ref[0], mid_ref[1]
+    step = 4 * half
+    for group in range(channels // 4):
+        span = slice(group * step, (group + 1) * step)
+        mid = dot_three(joined_ref[span, :], backward_ref[0], backward_ref[1])
         for at in range(4):
             real, imag = (mid[at * half : (at + 1) * half, c * rows : (c + 1) * rows] for c in (0, 1))
             back = jnp.concatenate(
@@ -254,8 +273,8 @@
             out = dot(last_ref[...], jnp.concatenate([high, low, high], axis=0), ((1,), (0,)))
             channel = group * 4 + at
             strided = pl.ds(channel, n_seq, stride=channels)
-            signal_ref[strided, :] = out + gain_ref[channel] * signal_ref[strided, :]
-    out_ref[...] = signal_ref[...].astype(BF16).reshape(n_seq, channels, rows)
+            long_ref[strided, :] = out + gain_ref[channel] * signal_ref[strided, :]
+    out_ref[...] = long_ref[...].astype(BF16).reshape(n_seq, channels, rows)
 
 
 def attend(delta, query_ref, pairs_ref, tile, few, rows):
@@ -294,7 +313,7 @@
     return weighted / totals, jnp.where(some, highest + jnp.log(totals), -1e30)
 
 
-def other_kernel(rows, few, delta_ref, query_ref, pairs_ref, out_ref, log_ref):
+def other_kernel(rows, few, delta_ref, query_ref, pairs_ref, done_ref, out_ref, log_ref):
     own_rows = query_ref.shape[0]
     log_ref[...] = jnp.zeros_like(log_ref)
     for tile in range(own_rows // 128):
@@ -511,6 +530,7 @@
             tables["forward"],
         ),
         (pltpu.VMEM((channels * half, 2 * rows), F32),),
+        from_hbm=(1, 2, 3),
     )
     mixed, gate, gate_taps, tail, local_taps, kernel_spec = lax.optimization_barrier(
         (mixed, gate, gate_taps, tail, local_taps, kernel_spec)
@@ -528,10 +548,14 @@
     pairs = lax.all_to_all(sent_pairs, "tp", 0, 0)
 
     gain = lax.dynamic_slice_in_dim(skip_gain[0], seq_at * channels, channels, 0)
-    long_out = kernel_call(
-        functools.partial(convolve_kernel, 3 * part),
-        shape((n_seq, channels, rows), BF16),
-        (gain,),
+    joined, signal, done = kernel_call(
+        functools.partial(signal_kernel, 3 * part),
+        (
+            shape((channels * half, 2 * rows), F32),
+            shape((n_seq * channels, rows), F32),
+            shape((8, rows), F32),
+        ),
+        (),
         (
             mixed,
             local_taps,
@@ -539,16 +563,10 @@
             tables["first_two"],
             tables["mid"],
             tables["forward"],
-            tables["backward"],
-            tables["last"],
-        ),
-        (
-            pltpu.VMEM((n_seq * channels, rows), F32),
-            pltpu.VMEM((channels * half, 2 * rows), F32),
-        ),
-    )
-
-    pairs, long_out = lax.optimization_barrier((pairs, long_out))
+        ),
+        (pltpu.VMEM((channels * half, 2 * rows), F32),),
+        from_hbm=(3, 4, 5),
+    )
     work = 2 * own_rows * n_tp * own_rows * HD
     own_delta = -lax.axis_index("tp") * part
     other_delta = (2 * x_at - 1) * rows + own_delta
@@ -556,7 +574,7 @@
         functools.partial(other_kernel, n_x * rows, part),
         shape((own_rows + 32, HD), BF16),
         (other_delta.astype(jnp.int32).reshape(1),),
-        (other_query, pairs),
+        (other_query, pairs, done),
         (pltpu.VMEM((32, HD), F32),),
         work,
     )
@@ -569,6 +587,14 @@
         (query, pairs),
         (),
         work,
+    )
+    long_out = kernel_call(
+        convolve_kernel,
+        shape((n_seq, channels, rows), BF16),
+        (gain,),
+        (joined, signal, tables["mid"], tables["backward"], tables["last"]),
+        (pltpu.VMEM((n_seq * channels, rows), F32),),
+        from_hbm=(2, 3, 4),
     )
     returned = kernel_call(
         merge_kernel,

time: 183 us -> 182 us (level)
  waiting for transfers between devices: 62.4 us -> 59.7 us
  starting transfers between devices: 75.7 us -> 77.8 us
    all_to_all x1, waiting for transfers between devices: 20.3 us -> 15.6 us  [body(): back = lax.all_to_all(returned, 'z', 0, 0)]
    all_gather x1, waiting for transfers between devices: 1.95 us -> 6.26 us  [body(): weight = lax.all_gather(weight, 'z')]
    ppermute x1, waiting for transfers between devices: 3.83 us -> 0.01 us  [body(): got = lax.ppermute(sent, 'xh', swap)]
    all_to_all x1, waiting for transfers between devices: 0.01 us -> 2.02 us  [body(): pairs = lax.all_to_all(sent_pairs, 'tp', 0, 0)]
    ppermute x1, starting transfers between devices: 2.44 us -> 4.4 us  [body(): got = lax.ppermute(sent, 'xh', swap)]
    unnamed x38 -> x20, local copies, waits for them, and re-layouts: 3.72 us -> 3.04 us
    pallas_call x12 -> x13, Pallas kernels: 23.7 us -> 23.9 us  [kernel_call(): pl.pallas_call(kernel, out_shape=placed[0] if single else placed, in_spec...]
  transfers between devices with their start and end apart: 15 -> 15, of which waited for: 9 -> 9; matrix products, arithmetic and copies ran while one was open for 1% -> 1% of each run, Pallas kernels for 9% -> 10%
where the time goes in v9:
time: 182 us; the launch traced here: 181 us
  starting transfers between devices  77.8 us (43%)
  waiting for transfers between devices  59.7 us (33%)
  Pallas kernels  23.9 us (13%)
  between operations  14.3 us (8%)
  local copies, waits for them, and re-layouts  5.43 us (3%)
    pallas_call x13, Pallas kernels, kernel_call(): pl.pallas_call(kernel, out_shape=placed[0] if single else placed, in_spec...  23.9 us
    all_to_all x1, waiting for transfers between devices, body(): mixed = lax.all_to_all(packed, 'z', 0, 0)  16.7 us
    all_to_all x1, waiting for transfers between devices, body(): back = lax.all_to_all(returned, 'z', 0, 0)  15.6 us
    all_to_all x1, starting transfers between devices, body(): mixed = lax.all_to_all(packed, 'z', 0, 0)  15.2 us
    all_to_all x1, starting transfers between devices, body(): back = lax.all_to_all(returned, 'z', 0, 0)  13.9 us
    all_to_all x1, waiting for transfers between devices, body(): plane_rows = lax.all_to_all(plane_rows, ('xh', 'tp'), 0, 0)  7.75 us
    ppermute x1, starting transfers between devices, body(): lax.ppermute(other_long, ('section', 'xh'), [(2 * s + x, 2 * t + 1 - x) f...  6.64 us
    all_gather x1, waiting for transfers between devices, body(): weight = lax.all_gather(weight, 'z')  6.26 us
  transfers between devices with their start and end apart: 15, of which 9 were waited for; matrix products, arithmetic and copies ran while one was open for 1% of the time, Pallas kernels for 10%

profile of v9, /device:TPU:32, one launch (start us, length us, event | category | flops | bytes accessed | tf_op | source)
XLA Modules:
  0.0 181.1 jit_solution(17914096126159701412)
XLA Ops:
  7.2 2.6 %shard_map.167 = (bf16[4,128,512]{2,1,0:T(8,128)(2,1)}, bf16[16,40,128]{2,1,0:T(8,128)(2,1)}, bf16[16,40,128]{2,1,0:T(8,128)(2,1)}) custom-call(s32[1]{0:T(128)} %bitcast.x_ref, bf16[128,1024]{1,0:T(8,128)(2,1)} %bitcast.35, bf16[128,1024]{1,0:T(8,128)(2,1)} %bitcast.36, f32[9,1,1024]{2,1,0:T(1,128)} %bitcast.42, bf16[128,512]{1,0:T(8,128)(2,1)} %bitcast.38, ...), custom_call_target="tpu_custom_call" | custom-call | bytes 1937408 | tf_op jit(solution)/shard_map/pallas_call | solution.py:84
  9.8 4.5 %all-to-all-start = ((bf16[4,128,512]{2,1,0:T(8,128)(2,1)}), bf16[4,128,512]{2,1,0:T(8,128)(2,1)S(1)}, u32[]{:S(2)}, u32[]{:S(2)}) async-start(bf16[4,128,512]{2,1,0:T(8,128)(2,1)} %get-tuple-element.28), calls=%async_computation | async-start | bytes 1048576 | tf_op jit(solution)/shard_map/all_to_all | solution.py:489
  14.3 5.1 %collective-permute-start = (bf16[16,40,128]{2,1,0:T(8,128)(2,1)}, bf16[16,40,128]{2,1,0:T(8,128)(2,1)S(1)}, u32[]{:S(2)}, u32[]{:S(2)}) collective-permute-start(bf16[16,40,128]{2,1,0:T(8,128)(2,1)} %get-tuple-element.30), channel_id=1, source_target_pairs={{0,4},{4,0},{1,5},{5,1},{2,6},{6,2},{3,7},{7,3},{8,12},{12,8},{9,1... | collective-permute-start | bytes 491528 | tf_op jit(solution)/shard_map/ppermute | solution.py:488
  19.3 4.3 %collective-permute-done.got_ref = bf16[16,40,128]{2,1,0:T(8,128)(2,1)S(1)} collective-permute-done((bf16[16,40,128]{2,1,0:T(8,128)(2,1)}, bf16[16,40,128]{2,1,0:T(8,128)(2,1)S(1)}, u32[]{:S(2)}, u32[]{:S(2)}) %collective-permute-start) | collective-permute-done | bytes 163872 | tf_op jit(solution)/shard_map/ppermute | solution.py:488
  23.7 1.9 %shard_map.168 = (bf16[16,176,128]{2,1,0:T(8,128)(2,1)}, bf16[4,32,512]{2,1,0:T(8,128)(2,1)}) custom-call(s32[1]{0:T(128)} %bitcast.x_ref, bf16[4,128,512]{2,1,0:T(8,128)(2,1)S(1)} %all-to-all-done.rows_ref, bf16[16,40,128]{2,1,0:T(8,128)(2,1)} %get-tuple-element.29.own_hbm, bf16[16,40,128]{2,1,0:T(8,128)(2,1)S(1)} %collective-permute-done.got_ref), custom_call_target="tpu_custom_call" | custom-call | bytes 1703936 | tf_op jit(solution)/shard_map/pallas_call | solution.py:84
  25.7 15.2 %all-to-all-start.1 = ((bf16[16,176,128]{2,1,0:T(8,128)(2,1)}), bf16[16,176,128]{2,1,0:T(8,128)(2,1)S(1)}, u32[]{:S(2)}, u32[]{:S(2)}) async-start(bf16[16,176,128]{2,1,0:T(8,128)(2,1)} %get-tuple-element.31), calls=%async_computation.1 | async-start | bytes 1441792 | tf_op jit(solution)/shard_map/all_to_all | solution.py:506
  41.6 1.9 %collective-permute-start.1 = (bf16[128,1024]{1,0:T(8,128)(2,1)}, bf16[128,1024]{1,0:T(8,128)(2,1)S(1)}, u32[]{:S(2)}, u32[]{:S(2)}) collective-permute-start(bf16[128,1024]{1,0:T(8,128)(2,1)} %bitcast.10), channel_id=1, source_target_pairs={{0,128},{128,256},{256,384},{384,0},{1,129},{129,257},{257,385},{3... | collective-permute-start | bytes 786440 | tf_op jit(solution)/shard_map/ppermute | solution.py:511
  44.3 3.5 %collective-permute-start.2 = (f32[3,1024]{1,0:T(4,128)S(1)}, f32[3,1024]{1,0:T(4,128)S(1)}, u32[]{:S(2)}, u32[]{:S(2)}) collective-permute-start(f32[3,1024]{1,0:T(4,128)S(1)} %bitcast.43), channel_id=1, source_target_pairs={{0,128},{128,256},{256,384},{384,0},{1,129},{129,257},{257,385},{3... | collective-permute-start | bytes 36872 | tf_op jit(solution)/shard_map/ppermute | solution.py:512
  48.5 4.2 %collective-permute-start.3 = (bf16[2,1024]{1,0:T(2,128)(2,1)S(1)}, bf16[2,1024]{1,0:T(2,128)(2,1)S(1)}, u32[]{:S(2)}, u32[]{:S(2)}) collective-permute-start(bf16[2,1024]{1,0:T(2,128)(2,1)S(1)} %slice_bitcast_fusion), channel_id=1, source_target_pairs={{0,132},{4,136},{8,140},{12,144},{16,148},{20,152},{24,156},{28,16... | collective-permute-start | bytes 12296 | tf_op jit(solution)/shard_map/ppermute | solution.py:513
  53.8 2.0 %shard_map.169.spectrum_ref = f32[1280,256]{1,0:T(8,128)S(1)} custom-call(f32[32,32,128]{2,1,0:T(8,128)S(1)} %bitcast.30, bf16[80,96]{1,0:T(8,128)(2,1)} %constant.41.clone.first_ref, f32[2,40,128]{2,1,0:T(8,128)} %constant.42.clone.mid_ref, bf16[2,256,256]{2,1,0:T(8,128)(2,1)} %constant.43.clone.forward_ref), custom_call_target="tpu_custom_call" | custom-call | bytes 2153472 | tf_op jit(solution)/shard_map/pallas_call | solution.py:84
  55.8 3.0 %collective-permute-done.3.tail_ref = bf16[2,1024]{1,0:T(2,128)(2,1)S(1)} collective-permute-done((bf16[2,1024]{1,0:T(2,128)(2,1)S(1)}, bf16[2,1024]{1,0:T(2,128)(2,1)S(1)}, u32[]{:S(2)}, u32[]{:S(2)}) %collective-permute-start.3) | collective-permute-done | bytes 4128 | tf_op jit(solution)/shard_map/ppermute | solution.py:513
  58.8 16.7 %all-to-all-done.1.mixed_ref = bf16[16,176,128]{2,1,0:T(8,128)(2,1)S(1)} async-done(((bf16[16,176,128]{2,1,0:T(8,128)(2,1)}), bf16[16,176,128]{2,1,0:T(8,128)(2,1)S(1)}, u32[]{:S(2)}, u32[]{:S(2)}) %all-to-all-start.1) | async-done | bytes 720928 | tf_op jit(solution)/shard_map/all_to_all | solution.py:506
  76.5 3.9 %all-to-all-start.2 = ((bf16[4,2,512,128]{3,2,1,0:T(8,128)(2,1)}), bf16[4,2,512,128]{3,2,1,0:T(8,128)(2,1)S(1)}, u32[]{:S(2)}, u32[]{:S(2)}) async-start(bf16[4,2,512,128]{3,2,1,0:T(8,128)(2,1)} %get-tuple-element.34), calls=%async_computation.2 | async-start | bytes 2097152 | tf_op jit(solution)/shard_map/all_to_all | solution.py:548
  80.5 5.3 %collective-permute-start.4 = (bf16[512,128]{1,0:T(8,128)(2,1)S(1)}, bf16[512,128]{1,0:T(8,128)(2,1)}, u32[]{:S(2)}, u32[]{:S(2)}) collective-permute-start(bf16[512,128]{1,0:T(8,128)(2,1)S(1)} %get-tuple-element.38.query_ref), channel_id=1, source_target_pairs={{0,4},{4,0},{1,5},{5,1},{2,6},{6,2},{3,7},{7,3},{8,12},{12,8},{9,1... | collective-permute-start | bytes 393224 | tf_op jit(solution)/shard_map/ppermute | solution.py:547
  85.8 2.6 %shard_map.171 = (f32[1280,256]{1,0:T(8,128)S(1)}, f32[1024,128]{1,0:T(8,128)S(1)}, f32[8,128]{1,0:T(8,128)S(1)}) custom-call(bf16[16,176,128]{2,1,0:T(8,128)(2,1)S(1)} %all-to-all-done.1.mixed_ref, f32[32,9]{1,0:T(8,128)S(1)} %bitcast.32, f32[1280,256]{1,0:T(8,128)S(1)} %shard_map.169.spectrum_ref, bf16[80,64]{1,0:T(8,128)(2,1)} %constant.44.clone.first_ref, ...), custom_call_target="tpu_custom_call" | custom-call | bytes 4185216 | tf_op jit(solution)/shard_map/pallas_call | solution.py:84
  88.4 1.1 copy-done.2
  90.2 2.0 %all-to-all-done.2.pairs_ref = bf16[4,2,512,128]{3,2,1,0:T(8,128)(2,1)S(1)} async-done(((bf16[4,2,512,128]{3,2,1,0:T(8,128)(2,1)}), bf16[4,2,512,128]{3,2,1,0:T(8,128)(2,1)S(1)}, u32[]{:S(2)}, u32[]{:S(2)}) %all-to-all-start.2) | async-done | bytes 1048608 | tf_op jit(solution)/shard_map/all_to_all | solution.py:548
  92.3 3.0 %shard_map.172 = bf16[544,128]{1,0:T(8,128)(2,1)S(1)} custom-call(s32[1]{0:T(128)} %bitcast.14.delta_ref, bf16[512,128]{1,0:T(8,128)(2,1)} %collective-permute-done.4.query_ref, bf16[4,2,512,128]{3,2,1,0:T(8,128)(2,1)S(1)} %all-to-all-done.2.pairs_ref, f32[8,128]{1,0:T(8,128)S(1)} %get-tuple-element.37.done_ref), custom_call_target="tpu_custom_call" | custom-call | flops 268435456 | bytes 1323008 | tf_op jit(solution)/shard_map/pallas_call | solution.py:84
  95.3 4.4 %collective-permute-start.5 = (bf16[544,128]{1,0:T(8,128)(2,1)S(1)}, bf16[544,128]{1,0:T(8,128)(2,1)S(1)}, u32[]{:S(2)}, u32[]{:S(2)}) collective-permute-start(bf16[544,128]{1,0:T(8,128)(2,1)S(1)} %shard_map.172), channel_id=1, source_target_pairs={{0,4},{4,0},{1,5},{5,1},{2,6},{6,2},{3,7},{7,3},{8,12},{12,8},{9,1... | collective-permute-start | bytes 417800 | tf_op jit(solution)/shard_map/ppermute | solution.py:581
  100.8 2.7 %shard_map.174 = bf16[32,32,128]{2,1,0:T(8,128)(2,1)S(1)} custom-call(f32[32]{0:T(128)S(1)} %dynamic-slice_bitcast_fusion.gain_ref, f32[1280,256]{1,0:T(8,128)S(1)} %copy-done.3, f32[1024,128]{1,0:T(8,128)S(1)} %copy-done.5, f32[2,40,128]{2,1,0:T(8,128)} %constant.42.clone.mid_ref, bf16[2,256,256]{2,1,0:T(8,128)(2,1)} %constant.45.clone.backward_ref, ...), custom_call_target="tpu_custom_call" | custom-call | bytes 2415616 | tf_op jit(solution)/shard_map/pallas_call | solution.py:84
  103.6 2.2 %shard_map.173 = (f32[512,128]{1,0:T(8,128)S(1)}, f32[512,128]{1,0:T(8,128)S(1)}) custom-call(s32[1]{0:T(128)} %bitcast.1.delta_ref, bf16[512,128]{1,0:T(8,128)(2,1)S(1)} %get-tuple-element.38.query_ref, bf16[4,2,512,128]{3,2,1,0:T(8,128)(2,1)S(1)} %all-to-all-done.2.pairs_ref), custom_call_target="tpu_custom_call" | custom-call | flops 268435456 | bytes 1703936 | tf_op jit(solution)/shard_map/pallas_call | solution.py:84
  106.8 13.9 %all-to-all-start.3 = ((bf16[16,96,128]{2,1,0:T(8,128)(2,1)}), bf16[16,96,128]{2,1,0:T(8,128)(2,1)S(1)}, u32[]{:S(2)}, u32[]{:S(2)}) async-start(bf16[16,96,128]{2,1,0:T(8,128)(2,1)} %shard_map.175), calls=%async_computation.3 | async-start | bytes 786432 | tf_op jit(solution)/shard_map/all_to_all | solution.py:605
  120.7 6.3 %all-gather.3.cloned.1.call-done = bf16[64,32,512]{2,1,0:T(8,128)(2,1)} async-done(((bf16[4,32,512]{2,1,0:T(8,128)(2,1)}), bf16[64,32,512]{2,1,0:T(8,128)(2,1)}) %all-gather.3.cloned.1.call-update) | async-done | bytes 2097168 | tf_op jit(solution)/shard_map/all_gather | solution.py:507
  127.0 15.6 %all-to-all-done.3.back_ref = bf16[16,96,128]{2,1,0:T(8,128)(2,1)S(1)} async-done(((bf16[16,96,128]{2,1,0:T(8,128)(2,1)}), bf16[16,96,128]{2,1,0:T(8,128)(2,1)S(1)}, u32[]{:S(2)}, u32[]{:S(2)}) %all-to-all-start.3) | async-done | bytes 393248 | tf_op jit(solution)/shard_map/all_to_all | solution.py:605
  142.6 1.1 shard_map.176
  143.7 4.1 %all-to-all-start.4 = ((bf16[8,32,2048]{2,1,0:T(8,128)(2,1)}), bf16[8,32,2048]{2,1,0:T(8,128)(2,1)S(1)}, u32[]{:S(2)}, u32[]{:S(2)}) async-start(bf16[8,32,2048]{2,1,0:T(8,128)(2,1)} %get-tuple-element.50), calls=%async_computation.4 | async-start | bytes 2097152 | tf_op jit(solution)/shard_map/all_to_all | solution.py:625
  147.9 1.9 %collective-permute-start.6 = (bf16[16,32,128]{2,1,0:T(8,128)(2,1)}, bf16[16,32,128]{2,1,0:T(8,128)(2,1)S(1)}, u32[]{:S(2)}, u32[]{:S(2)}) collective-permute-start(bf16[16,32,128]{2,1,0:T(8,128)(2,1)} %get-tuple-element.45), channel_id=1, source_target_pairs={{0,128},{128,256},{256,384},{384,0},{1,129},{129,257},{257,385},{3... | collective-permute-start | bytes 393224 | tf_op jit(solution)/shard_map/ppermute | solution.py:626
  149.8 6.6 %collective-permute-start.7 = (bf16[16,32,128]{2,1,0:T(8,128)(2,1)}, bf16[16,32,128]{2,1,0:T(8,128)(2,1)}, u32[]{:S(2)}, u32[]{:S(2)}) collective-permute-start(bf16[16,32,128]{2,1,0:T(8,128)(2,1)} %get-tuple-element.46), channel_id=1, source_target_pairs={{0,132},{4,128},{128,260},{132,256},{256,388},{260,384},{384,4},{3... | collective-permute-start | bytes 393224 | tf_op jit(solution)/shard_map/ppermute | solution.py:627
  156.4 7.8 %all-to-all-done.4.rows_ref = bf16[8,32,2048]{2,1,0:T(8,128)(2,1)S(1)} async-done(((bf16[8,32,2048]{2,1,0:T(8,128)(2,1)}), bf16[8,32,2048]{2,1,0:T(8,128)(2,1)S(1)}, u32[]{:S(2)}, u32[]{:S(2)}) %all-to-all-start.4) | async-done | bytes 1048608 | tf_op jit(solution)/shard_map/all_to_all | solution.py:625
  164.9 3.1 %collective-permute-start.8 = (bf16[128,512]{1,0:T(8,128)(2,1)S(1)}, bf16[128,512]{1,0:T(8,128)(2,1)S(1)}, u32[]{:S(2)}, u32[]{:S(2)}) collective-permute-start(bf16[128,512]{1,0:T(8,128)(2,1)S(1)} %get-tuple-element.53), channel_id=1, source_target_pairs={{0,4},{4,0},{1,5},{5,1},{2,6},{6,2},{3,7},{7,3},{8,12},{12,8},{9,1... | collective-permute-start | bytes 393224 | tf_op jit(solution)/shard_map/ppermute | solution.py:644
  168.1 1.9 %shard_map.177 = bf16[128,1024]{1,0:T(8,128)(2,1)} custom-call(s32[1]{0:T(128)} %bitcast.x_ref, bf16[16,32,128]{2,1,0:T(8,128)(2,1)S(1)} %collective-permute-done.6.own_ref, bf16[16,32,128]{2,1,0:T(8,128)(2,1)} %collective-permute-done.7.got_ref, bf16[128,1024]{1,0:T(8,128)(2,1)S(1)} %collective-permute-done.1.gate_ref, ...), custom_call_target="tpu_custom_call" | custom-call | bytes 802816 | tf_op jit(solution)/shard_map/pallas_call | solution.py:84
  170.0 3.3 %collective-permute-done.8.got_ref = bf16[128,512]{1,0:T(8,128)(2,1)S(1)} collective-permute-done((bf16[128,512]{1,0:T(8,128)(2,1)S(1)}, bf16[128,512]{1,0:T(8,128)(2,1)S(1)}, u32[]{:S(2)}, u32[]{:S(2)}) %collective-permute-start.8) | collective-permute-done | bytes 131104 | tf_op jit(solution)/shard_map/ppermute | solution.py:644
  (38 shorter events, 8.9 us)
Async XLA Ops:
  7.2 92.5 %copy-start = (f32[1,1024]{1,0:T(1,128)S(1)}, f32[1,1024]{1,0:T(1,128)}, u32[]{:S(2)}) copy-start(f32[1,1024]{1,0:T(1,128)} %param.21) | copy-start | bytes 12292
  9.8 13.9 %all-to-all-start = ((bf16[4,128,512]{2,1,0:T(8,128)(2,1)}), bf16[4,128,512]{2,1,0:T(8,128)(2,1)S(1)}, u32[]{:S(2)}, u32[]{:S(2)}) async-start(bf16[4,128,512]{2,1,0:T(8,128)(2,1)} %get-tuple-element.28), calls=%async_computation | async-start | bytes 1048576 | tf_op jit(solution)/shard_map/all_to_all | solution.py:489
  14.2 39.4 %copy-start.8 = (f32[1,1,1,32,4096]{4,3,2,1,0:T(8,128)S(1)}, f32[1,1,1,32,4096]{4,3,2,1,0:T(8,128)}, u32[]{:S(2)}) copy-start(f32[1,1,1,32,4096]{4,3,2,1,0:T(8,128)} %param.20) | copy-start | bytes 1572868
  14.3 9.4 %collective-permute-start = (bf16[16,40,128]{2,1,0:T(8,128)(2,1)}, bf16[16,40,128]{2,1,0:T(8,128)(2,1)S(1)}, u32[]{:S(2)}, u32[]{:S(2)}) collective-permute-start(bf16[16,40,128]{2,1,0:T(8,128)(2,1)} %get-tuple-element.30), channel_id=1, source_target_pairs={{0,4},{4,0},{1,5},{5,1},{2,6},{6,2},{3,7},{7,3},{8,12},{12,8},{9,1... | collective-permute-start | bytes 491528 | tf_op jit(solution)/shard_map/ppermute | solution.py:488
  25.7 49.8 %all-to-all-start.1 = ((bf16[16,176,128]{2,1,0:T(8,128)(2,1)}), bf16[16,176,128]{2,1,0:T(8,128)(2,1)S(1)}, u32[]{:S(2)}, u32[]{:S(2)}) async-start(bf16[16,176,128]{2,1,0:T(8,128)(2,1)} %get-tuple-element.31), calls=%async_computation.1 | async-start | bytes 1441792 | tf_op jit(solution)/shard_map/all_to_all | solution.py:506
  40.9 86.1 %all-gather.3.cloned.1.call-start = ((), (), s32[]{:S(2)}) async-start(), calls=%async_computation.5 | async-start | bytes 2228224 | tf_op jit(solution)/shard_map/all_gather | solution.py:507
  41.6 17.2 %collective-permute-start.1 = (bf16[128,1024]{1,0:T(8,128)(2,1)}, bf16[128,1024]{1,0:T(8,128)(2,1)S(1)}, u32[]{:S(2)}, u32[]{:S(2)}) collective-permute-start(bf16[128,1024]{1,0:T(8,128)(2,1)} %bitcast.10), channel_id=1, source_target_pairs={{0,128},{128,256},{256,384},{384,0},{1,129},{129,257},{257,385},{3... | collective-permute-start | bytes 786440 | tf_op jit(solution)/shard_map/ppermute | solution.py:511
  44.3 14.6 %collective-permute-start.2 = (f32[3,1024]{1,0:T(4,128)S(1)}, f32[3,1024]{1,0:T(4,128)S(1)}, u32[]{:S(2)}, u32[]{:S(2)}) collective-permute-start(f32[3,1024]{1,0:T(4,128)S(1)} %bitcast.43), channel_id=1, source_target_pairs={{0,128},{128,256},{256,384},{384,0},{1,129},{129,257},{257,385},{3... | collective-permute-start | bytes 36872 | tf_op jit(solution)/shard_map/ppermute | solution.py:512
  48.5 10.3 %collective-permute-start.3 = (bf16[2,1024]{1,0:T(2,128)(2,1)S(1)}, bf16[2,1024]{1,0:T(2,128)(2,1)S(1)}, u32[]{:S(2)}, u32[]{:S(2)}) collective-permute-start(bf16[2,1024]{1,0:T(2,128)(2,1)S(1)} %slice_bitcast_fusion), channel_id=1, source_target_pairs={{0,132},{4,136},{8,140},{12,144},{16,148},{20,152},{24,156},{28,16... | collective-permute-start | bytes 12296 | tf_op jit(solution)/shard_map/ppermute | solution.py:513
  58.8 17.7 %copy-start.6 = (f32[3,1024]{1,0:T(4,128)}, f32[3,1024]{1,0:T(4,128)S(1)}, u32[]{:S(2)}) copy-start(f32[3,1024]{1,0:T(4,128)S(1)} %collective-permute-done.2.taps_ref) | copy-start | bytes 36868
  76.5 15.7 %all-to-all-start.2 = ((bf16[4,2,512,128]{3,2,1,0:T(8,128)(2,1)}), bf16[4,2,512,128]{3,2,1,0:T(8,128)(2,1)S(1)}, u32[]{:S(2)}, u32[]{:S(2)}) async-start(bf16[4,2,512,128]{3,2,1,0:T(8,128)(2,1)} %get-tuple-element.34), calls=%async_computation.2 | async-start | bytes 2097152 | tf_op jit(solution)/shard_map/all_to_all | solution.py:548
  80.5 9.8 %collective-permute-start.4 = (bf16[512,128]{1,0:T(8,128)(2,1)S(1)}, bf16[512,128]{1,0:T(8,128)(2,1)}, u32[]{:S(2)}, u32[]{:S(2)}) collective-permute-start(bf16[512,128]{1,0:T(8,128)(2,1)S(1)} %get-tuple-element.38.query_ref), channel_id=1, source_target_pairs={{0,4},{4,0},{1,5},{5,1},{2,6},{6,2},{3,7},{7,3},{8,12},{12,8},{9,1... | collective-permute-start | bytes 393224 | tf_op jit(solution)/shard_map/ppermute | solution.py:547
  88.4 1.1 copy-start.2
  89.4 0.8 copy-start.4
  90.2 9.6 %copy-start.3 = (f32[1280,256]{1,0:T(8,128)S(1)}, f32[1280,256]{1,0:T(8,128)}, u32[]{:S(2)}) copy-start(f32[1280,256]{1,0:T(8,128)} %copy-done.2) | copy-start | bytes 3932164
  95.3 10.5 %collective-permute-start.5 = (bf16[544,128]{1,0:T(8,128)(2,1)S(1)}, bf16[544,128]{1,0:T(8,128)(2,1)S(1)}, u32[]{:S(2)}, u32[]{:S(2)}) collective-permute-start(bf16[544,128]{1,0:T(8,128)(2,1)S(1)} %shard_map.172), channel_id=1, source_target_pairs={{0,4},{4,0},{1,5},{5,1},{2,6},{6,2},{3,7},{7,3},{8,12},{12,8},{9,1... | collective-permute-start | bytes 417800 | tf_op jit(solution)/shard_map/ppermute | solution.py:581
  99.8 1.1 copy-start.5
  106.8 35.8 %all-to-all-start.3 = ((bf16[16,96,128]{2,1,0:T(8,128)(2,1)}), bf16[16,96,128]{2,1,0:T(8,128)(2,1)S(1)}, u32[]{:S(2)}, u32[]{:S(2)}) async-start(bf16[16,96,128]{2,1,0:T(8,128)(2,1)} %shard_map.175), calls=%async_computation.3 | async-start | bytes 786432 | tf_op jit(solution)/shard_map/all_to_all | solution.py:605
  127.0 37.2 %copy-start.1 = (bf16[64,32,512]{2,1,0:T(8,128)(2,1)S(1)}, bf16[64,32,512]{2,1,0:T(8,128)(2,1)}, u32[]{:S(2)}) copy-start(bf16[64,32,512]{2,1,0:T(8,128)(2,1)} %all-gather.3.cloned.1.call-done) | copy-start | bytes 6291460
  143.7 20.4 %all-to-all-start.4 = ((bf16[8,32,2048]{2,1,0:T(8,128)(2,1)}), bf16[8,32,2048]{2,1,0:T(8,128)(2,1)S(1)}, u32[]{:S(2)}, u32[]{:S(2)}) async-start(bf16[8,32,2048]{2,1,0:T(8,128)(2,1)} %get-tuple-element.50), calls=%async_computation.4 | async-start | bytes 2097152 | tf_op jit(solution)/shard_map/all_to_all | solution.py:625
  147.9 20.2 %collective-permute-start.6 = (bf16[16,32,128]{2,1,0:T(8,128)(2,1)}, bf16[16,32,128]{2,1,0:T(8,128)(2,1)S(1)}, u32[]{:S(2)}, u32[]{:S(2)}) collective-permute-start(bf16[16,32,128]{2,1,0:T(8,128)(2,1)} %get-tuple-element.45), channel_id=1, source_target_pairs={{0,128},{128,256},{256,384},{384,0},{1,129},{129,257},{257,385},{3... | collective-permute-start | bytes 393224 | tf_op jit(solution)/shard_map/ppermute | solution.py:626
  149.8 18.3 %collective-permute-start.7 = (bf16[16,32,128]{2,1,0:T(8,128)(2,1)}, bf16[16,32,128]{2,1,0:T(8,128)(2,1)}, u32[]{:S(2)}, u32[]{:S(2)}) collective-permute-start(bf16[16,32,128]{2,1,0:T(8,128)(2,1)} %get-tuple-element.46), channel_id=1, source_target_pairs={{0,132},{4,128},{128,260},{132,256},{256,388},{260,384},{384,4},{3... | collective-permute-start | bytes 393224 | tf_op jit(solution)/shard_map/ppermute | solution.py:627
  164.2 3.9 %copy-start.7 = (f32[3,1024]{1,0:T(4,128)S(1)}, f32[3,1024]{1,0:T(4,128)}, u32[]{:S(2)}) copy-start(f32[3,1024]{1,0:T(4,128)} %copy-done.6) | copy-start | bytes 36868
  164.9 8.4 %collective-permute-start.8 = (bf16[128,512]{1,0:T(8,128)(2,1)S(1)}, bf16[128,512]{1,0:T(8,128)(2,1)S(1)}, u32[]{:S(2)}, u32[]{:S(2)}) collective-permute-start(bf16[128,512]{1,0:T(8,128)(2,1)S(1)} %get-tuple-element.53), channel_id=1, source_target_pairs={{0,4},{4,0},{1,5},{5,1},{2,6},{6,2},{3,7},{7,3},{8,12},{12,8},{9,1... | collective-permute-start | bytes 393224 | tf_op jit(solution)/shard_map/ppermute | solution.py:644
Sparse Core Ops, SparseCore 0:
  44.4 82.5 all-gather.2

commit v10 on v9

--- a/solution.py
+++ b/solution.py
@@ -103,6 +103,7 @@
     per = 2 * n_z * lanes // first_ref.shape[1]
     channels = lanes // per
     low = x_ref[0] == 0
+    lane = lax.broadcasted_iota(jnp.int32, (1, lanes), 1)
     for group in range(2 * n_z // per):
         span = slice(group * lanes, (group + 1) * lanes)
         shorts, edges = [], []
@@ -116,13 +117,21 @@
             edges += [x[:2], x[rows - 2 :]]
         turned = (shorts[0] * shorts[1]).T
         edges = jnp.concatenate(edges, axis=0)
+        moved = [pltpu.roll(edges, d * channels, 1) if d else edges for d in range(per)]
         for at in range(per // 2):
             z_at = group * per // 2 + at
             blocks = []
             for x_at in range(2):
                 j = 2 * at + x_at
-                edge = pltpu.roll(edges, lanes - j * channels, 1) if j else edges
-                blocks.append(jnp.concatenate([turned[j * channels : (j + 1) * channels], edge], axis=0))
+                lines = [turned[j * channels : (j + 1) * channels]]
+                for row in range(2):
+                    line = moved[(per - 1 - j) % per][row * per + per - 1 : (row + 1) * per]
+                    for kind in reversed(range(per - 1)):
+                        piece = moved[(kind - j) % per][row * per + kind : row * per + kind + 1]
+                        line = jnp.where(lane < (kind + 1) * channels, piece, line)
+                    lines.append(line)
+                lines.append(jnp.zeros((6, lanes), F32))
+                blocks.append(jnp.concatenate(lines, axis=0))
             own_ref[z_at] = jnp.where(low, blocks[0], blocks[1]).astype(BF16)
             other_ref[z_at] = jnp.where(low, blocks[1], blocks[0]).astype(BF16)
 
@@ -145,12 +154,12 @@
     low = x_ref[0] == 0
     fetch.wait()
     own, got = own_ref[...].astype(F32), got_ref[...].astype(F32)
-    even = jnp.where(low, own, got).astype(BF16)
-    odd = jnp.where(low, got, own).astype(BF16)
-    out_ref[:, size : size + channels, :] = even[:, :channels]
-    out_ref[:, size + channels : size + 2 * channels, :] = odd[:, :channels]
-    out_ref[:, size + 2 * channels : size + 2 * channels + 8, :] = even[:, channels:]
-    out_ref[:, size + 2 * channels + 8 :, :] = odd[:, channels:]
+    even, odd = jnp.where(low, own, got), jnp.where(low, got, own)
+    out_ref[:, size : size + channels, :] = even[:, :channels].astype(BF16)
+    out_ref[:, size + channels : size + 2 * channels, :] = odd[:, :channels].astype(BF16)
+    row = lax.broadcasted_iota(jnp.int32, (1, 8, HD), 1)
+    lines = jnp.where(row < 2, even[:, channels:], pltpu.roll(odd[:, channels:], 2, 1))
+    out_ref[:, size + 2 * channels :, :] = lines.astype(BF16)
     store = pltpu.make_async_copy(out_ref, out_hbm, sems.at[2])
     store.start()
     store.wait()
@@ -221,19 +230,28 @@
     rows, half = mid_ref.shape[2], mid_ref.shape[1]
     channels = out_ref.shape[0] // half
     n_seq = signal_ref.shape[0] // channels
-    count = n_seq * 8
-    edges = mixed_ref[:, start + 2 * channels :, :].astype(F32).reshape(count, rows).T[:channels]
+    count = n_seq * 4
+    edges = mixed_ref[:, start + 2 * channels :, :].astype(F32).reshape(count, rows).T
+    zeroth, first, last_but_one, last = (
+        edges[kind * channels : (kind + 1) * channels] for kind in range(4)
+    )
     lane = lax.broadcasted_iota(jnp.int32, (channels, count), 1)
-    kind = lane % 8
-    before = jnp.where(lane >= 8, 1.0, 0.0)
-    ahead = jnp.where(kind % 4 == 0, pltpu.roll(edges, 5, 1) * before, pltpu.roll(edges, 1, 1))
-    further = pltpu.roll(edges, 6, 1) * before
-    tap = [jnp.where(kind < 4, taps_ref[:, i : i + 1], taps_ref[:, 6 + i : 7 + i]) for i in range(3)]
-    short = tap[0] * edges + tap[1] * ahead + tap[2] * further
-    made = (short * pltpu.roll(short, count - 4, 1)).astype(BF16).astype(F32)
+
+    def before(x):
+        moved = jnp.where(lane % 8 < 2, pltpu.roll(x, 6, 1), pltpu.roll(x, 2, 1))
+        return jnp.where(lane < 2, 0.0, moved)
+
+    is_first = lane % 2 == 0
+    tap = [jnp.where(is_first, taps_ref[:, i : i + 1], taps_ref[:, 6 + i : 7 + i]) for i in range(3)]
+    zero = tap[0] * zeroth + tap[1] * before(last) + tap[2] * before(last_but_one)
+    one = tap[0] * first + tap[1] * zeroth + tap[2] * before(last)
+    zero = zero * pltpu.roll(zero, count - 1, 1)
+    one = one * pltpu.roll(one, count - 1, 1)
+    made = jnp.where(is_first, zero, pltpu.roll(one, 1, 1)).astype(BF16).astype(F32)
     column = lax.broadcasted_iota(jnp.int32, (channels, rows), 1)
     for at in range(n_seq):
-        turned = pltpu.roll(made, count - 8 * at, 1) if at else made
+        lane_at = at // 2 * 8 + at % 2 * 2
+        turned = pltpu.roll(made, count - lane_at, 1) if at else made
         begin = start + at % 2 * channels
         block = mixed_ref[at // 2, begin : begin + channels, :].astype(F32)
         signal_ref[at * channels : (at + 1) * channels, :] = jnp.where(
@@ -490,14 +508,14 @@
     packed, weight = kernel_call(
         repack_kernel,
         (
-            shape((n_z, 3 * part + 2 * channels + 16, HD), BF16),
+            shape((n_z, 3 * part + 2 * channels + 8, HD), BF16),
             shape((n_tp, channels, wide), BF16),
         ),
         (x_scalar,),
         (got_rows, own, got),
         (
             pltpu.VMEM((n_z, channels + 8, rows), BF16),
-            pltpu.VMEM((n_z, 3 * part + 2 * channels + 16, HD), BF16),
+            pltpu.VMEM((n_z, 3 * part + 2 * channels + 8, HD), BF16),
             pltpu.SemaphoreType.DMA((3,)),
         ),
         hbm_in=(1,),

time: 182 us -> 181 us (level)
  waiting for transfers between devices: 59.7 us -> 57 us
where the time goes in v10:
time: 181 us; the launch traced here: 180 us
  starting transfers between devices  78.8 us (44%)
  waiting for transfers between devices  57 us (31%)
  Pallas kernels  24 us (13%)
  between operations  14.3 us (8%)
  local copies, waits for them, and re-layouts  5.42 us (3%)
    pallas_call x13, Pallas kernels, kernel_call(): pl.pallas_call(kernel, out_shape=placed[0] if single else placed, in_spec...  24 us
    all_to_all x1, starting transfers between devices, body(): mixed = lax.all_to_all(packed, 'z', 0, 0)  15.2 us
    all_to_all x1, waiting for transfers between devices, body(): mixed = lax.all_to_all(packed, 'z', 0, 0)  15.2 us
    all_to_all x1, waiting for transfers between devices, body(): back = lax.all_to_all(returned, 'z', 0, 0)  14 us
    all_to_all x1, starting transfers between devices, body(): back = lax.all_to_all(returned, 'z', 0, 0)  13.4 us
    all_to_all x1, waiting for transfers between devices, body(): plane_rows = lax.all_to_all(plane_rows, ('xh', 'tp'), 0, 0)  7.76 us
    all_gather x1, waiting for transfers between devices, body(): weight = lax.all_gather(weight, 'z')  7.45 us
    ppermute x1, starting transfers between devices, body(): lax.ppermute(other_long, ('section', 'xh'), [(2 * s + x, 2 * t + 1 - x) f...  6.49 us
  transfers between devices with their start and end apart: 15, of which 9 were waited for; matrix products, arithmetic and copies ran while one was open for 1% of the time, Pallas kernels for 10%

profile of v10, /device:TPU:32, one launch (start us, length us, event | category | flops | bytes accessed | tf_op | source)
XLA Modules:
  0.0 179.6 jit_solution(7758851082649202665)
XLA Ops:
  7.2 2.6 %shard_map.167 = (bf16[4,128,512]{2,1,0:T(8,128)(2,1)}, bf16[16,40,128]{2,1,0:T(8,128)(2,1)}, bf16[16,40,128]{2,1,0:T(8,128)(2,1)}) custom-call(s32[1]{0:T(128)} %bitcast.x_ref, bf16[128,1024]{1,0:T(8,128)(2,1)} %bitcast.35, bf16[128,1024]{1,0:T(8,128)(2,1)} %bitcast.36, f32[9,1,1024]{2,1,0:T(1,128)} %bitcast.42, bf16[128,512]{1,0:T(8,128)(2,1)} %bitcast.38, ...), custom_call_target="tpu_custom_call" | custom-call | bytes 1937408 | tf_op jit(solution)/shard_map/pallas_call | solution.py:84
  9.8 4.5 %all-to-all-start = ((bf16[4,128,512]{2,1,0:T(8,128)(2,1)}), bf16[4,128,512]{2,1,0:T(8,128)(2,1)S(1)}, u32[]{:S(2)}, u32[]{:S(2)}) async-start(bf16[4,128,512]{2,1,0:T(8,128)(2,1)} %get-tuple-element.28), calls=%async_computation | async-start | bytes 1048576 | tf_op jit(solution)/shard_map/all_to_all | solution.py:507
  14.3 5.1 %collective-permute-start = (bf16[16,40,128]{2,1,0:T(8,128)(2,1)}, bf16[16,40,128]{2,1,0:T(8,128)(2,1)S(1)}, u32[]{:S(2)}, u32[]{:S(2)}) collective-permute-start(bf16[16,40,128]{2,1,0:T(8,128)(2,1)} %get-tuple-element.30), channel_id=1, source_target_pairs={{0,4},{4,0},{1,5},{5,1},{2,6},{6,2},{3,7},{7,3},{8,12},{12,8},{9,1... | collective-permute-start | bytes 491528 | tf_op jit(solution)/shard_map/ppermute | solution.py:506
  19.3 4.3 %collective-permute-done.got_ref = bf16[16,40,128]{2,1,0:T(8,128)(2,1)S(1)} collective-permute-done((bf16[16,40,128]{2,1,0:T(8,128)(2,1)}, bf16[16,40,128]{2,1,0:T(8,128)(2,1)S(1)}, u32[]{:S(2)}, u32[]{:S(2)}) %collective-permute-start) | collective-permute-done | bytes 163872 | tf_op jit(solution)/shard_map/ppermute | solution.py:506
  23.8 1.9 %shard_map.168 = (bf16[16,168,128]{2,1,0:T(8,128)(2,1)}, bf16[4,32,512]{2,1,0:T(8,128)(2,1)}) custom-call(s32[1]{0:T(128)} %bitcast.x_ref, bf16[4,128,512]{2,1,0:T(8,128)(2,1)S(1)} %all-to-all-done.rows_ref, bf16[16,40,128]{2,1,0:T(8,128)(2,1)} %get-tuple-element.29.own_hbm, bf16[16,40,128]{2,1,0:T(8,128)(2,1)S(1)} %collective-permute-done.got_ref), custom_call_target="tpu_custom_call" | custom-call | bytes 1671168 | tf_op jit(solution)/shard_map/pallas_call | solution.py:84
  25.7 15.2 %all-to-all-start.1 = ((bf16[16,168,128]{2,1,0:T(8,128)(2,1)}), bf16[16,168,128]{2,1,0:T(8,128)(2,1)S(1)}, u32[]{:S(2)}, u32[]{:S(2)}) async-start(bf16[16,168,128]{2,1,0:T(8,128)(2,1)} %get-tuple-element.31), calls=%async_computation.1 | async-start | bytes 1376256 | tf_op jit(solution)/shard_map/all_to_all | solution.py:524
  41.6 1.9 %collective-permute-start.1 = (bf16[128,1024]{1,0:T(8,128)(2,1)}, bf16[128,1024]{1,0:T(8,128)(2,1)S(1)}, u32[]{:S(2)}, u32[]{:S(2)}) collective-permute-start(bf16[128,1024]{1,0:T(8,128)(2,1)} %bitcast.10), channel_id=1, source_target_pairs={{0,128},{128,256},{256,384},{384,0},{1,129},{129,257},{257,385},{3... | collective-permute-start | bytes 786440 | tf_op jit(solution)/shard_map/ppermute | solution.py:529
  44.3 3.5 %collective-permute-start.2 = (f32[3,1024]{1,0:T(4,128)S(1)}, f32[3,1024]{1,0:T(4,128)S(1)}, u32[]{:S(2)}, u32[]{:S(2)}) collective-permute-start(f32[3,1024]{1,0:T(4,128)S(1)} %bitcast.43), channel_id=1, source_target_pairs={{0,128},{128,256},{256,384},{384,0},{1,129},{129,257},{257,385},{3... | collective-permute-start | bytes 36872 | tf_op jit(solution)/shard_map/ppermute | solution.py:530
  48.5 4.2 %collective-permute-start.3 = (bf16[2,1024]{1,0:T(2,128)(2,1)S(1)}, bf16[2,1024]{1,0:T(2,128)(2,1)S(1)}, u32[]{:S(2)}, u32[]{:S(2)}) collective-permute-start(bf16[2,1024]{1,0:T(2,128)(2,1)S(1)} %slice_bitcast_fusion), channel_id=1, source_target_pairs={{0,132},{4,136},{8,140},{12,144},{16,148},{20,152},{24,156},{28,16... | collective-permute-start | bytes 12296 | tf_op jit(solution)/shard_map/ppermute | solution.py:531
  53.8 2.0 %shard_map.169.spectrum_ref = f32[1280,256]{1,0:T(8,128)S(1)} custom-call(f32[32,32,128]{2,1,0:T(8,128)S(1)} %bitcast.30, bf16[80,96]{1,0:T(8,128)(2,1)} %constant.41.clone.first_ref, f32[2,40,128]{2,1,0:T(8,128)} %constant.42.clone.mid_ref, bf16[2,256,256]{2,1,0:T(8,128)(2,1)} %constant.43.clone.forward_ref), custom_call_target="tpu_custom_call" | custom-call | bytes 2153472 | tf_op jit(solution)/shard_map/pallas_call | solution.py:84
  55.8 2.6 %collective-permute-done.3.tail_ref = bf16[2,1024]{1,0:T(2,128)(2,1)S(1)} collective-permute-done((bf16[2,1024]{1,0:T(2,128)(2,1)S(1)}, bf16[2,1024]{1,0:T(2,128)(2,1)S(1)}, u32[]{:S(2)}, u32[]{:S(2)}) %collective-permute-start.3) | collective-permute-done | bytes 4128 | tf_op jit(solution)/shard_map/ppermute | solution.py:531
  58.4 15.2 %all-to-all-done.1.mixed_ref = bf16[16,168,128]{2,1,0:T(8,128)(2,1)S(1)} async-done(((bf16[16,168,128]{2,1,0:T(8,128)(2,1)}), bf16[16,168,128]{2,1,0:T(8,128)(2,1)S(1)}, u32[]{:S(2)}, u32[]{:S(2)}) %all-to-all-start.1) | async-done | bytes 688160 | tf_op jit(solution)/shard_map/all_to_all | solution.py:524
  74.7 5.3 %all-to-all-start.2 = ((bf16[4,2,512,128]{3,2,1,0:T(8,128)(2,1)}), bf16[4,2,512,128]{3,2,1,0:T(8,128)(2,1)S(1)}, u32[]{:S(2)}, u32[]{:S(2)}) async-start(bf16[4,2,512,128]{3,2,1,0:T(8,128)(2,1)} %get-tuple-element.34), calls=%async_computation.2 | async-start | bytes 2097152 | tf_op jit(solution)/shard_map/all_to_all | solution.py:566
  79.9 4.9 %collective-permute-start.4 = (bf16[512,128]{1,0:T(8,128)(2,1)S(1)}, bf16[512,128]{1,0:T(8,128)(2,1)}, u32[]{:S(2)}, u32[]{:S(2)}) collective-permute-start(bf16[512,128]{1,0:T(8,128)(2,1)S(1)} %get-tuple-element.38.query_ref), channel_id=1, source_target_pairs={{0,4},{4,0},{1,5},{5,1},{2,6},{6,2},{3,7},{7,3},{8,12},{12,8},{9,1... | collective-permute-start | bytes 393224 | tf_op jit(solution)/shard_map/ppermute | solution.py:565
  84.9 2.7 %shard_map.171 = (f32[1280,256]{1,0:T(8,128)S(1)}, f32[1024,128]{1,0:T(8,128)S(1)}, f32[8,128]{1,0:T(8,128)S(1)}) custom-call(bf16[16,168,128]{2,1,0:T(8,128)(2,1)S(1)} %all-to-all-done.1.mixed_ref, f32[32,9]{1,0:T(8,128)S(1)} %bitcast.32, f32[1280,256]{1,0:T(8,128)S(1)} %shard_map.169.spectrum_ref, bf16[80,64]{1,0:T(8,128)(2,1)} %constant.44.clone.first_ref, ...), custom_call_target="tpu_custom_call" | custom-call | bytes 4152448 | tf_op jit(solution)/shard_map/pallas_call | solution.py:84
  87.6 1.1 copy-done.2
  89.5 1.6 all-to-all-done.2.pairs_ref
  91.1 3.0 %shard_map.172 = bf16[544,128]{1,0:T(8,128)(2,1)S(1)} custom-call(s32[1]{0:T(128)} %bitcast.14.delta_ref, bf16[512,128]{1,0:T(8,128)(2,1)} %collective-permute-done.4.query_ref, bf16[4,2,512,128]{3,2,1,0:T(8,128)(2,1)S(1)} %all-to-all-done.2.pairs_ref, f32[8,128]{1,0:T(8,128)S(1)} %get-tuple-element.37.done_ref), custom_call_target="tpu_custom_call" | custom-call | flops 268435456 | bytes 1323008 | tf_op jit(solution)/shard_map/pallas_call | solution.py:84
  94.1 4.7 %collective-permute-start.5 = (bf16[544,128]{1,0:T(8,128)(2,1)S(1)}, bf16[544,128]{1,0:T(8,128)(2,1)S(1)}, u32[]{:S(2)}, u32[]{:S(2)}) collective-permute-start(bf16[544,128]{1,0:T(8,128)(2,1)S(1)} %shard_map.172), channel_id=1, source_target_pairs={{0,4},{4,0},{1,5},{5,1},{2,6},{6,2},{3,7},{7,3},{8,12},{12,8},{9,1... | collective-permute-start | bytes 417800 | tf_op jit(solution)/shard_map/ppermute | solution.py:599
  100.0 2.7 %shard_map.174 = bf16[32,32,128]{2,1,0:T(8,128)(2,1)S(1)} custom-call(f32[32]{0:T(128)S(1)} %dynamic-slice_bitcast_fusion.gain_ref, f32[1280,256]{1,0:T(8,128)S(1)} %copy-done.3, f32[1024,128]{1,0:T(8,128)S(1)} %copy-done.5, f32[2,40,128]{2,1,0:T(8,128)} %constant.42.clone.mid_ref, bf16[2,256,256]{2,1,0:T(8,128)(2,1)} %constant.45.clone.backward_ref, ...), custom_call_target="tpu_custom_call" | custom-call | bytes 2415616 | tf_op jit(solution)/shard_map/pallas_call | solution.py:84
  102.7 2.2 %shard_map.173 = (f32[512,128]{1,0:T(8,128)S(1)}, f32[512,128]{1,0:T(8,128)S(1)}) custom-call(s32[1]{0:T(128)} %bitcast.1.delta_ref, bf16[512,128]{1,0:T(8,128)(2,1)S(1)} %get-tuple-element.38.query_ref, bf16[4,2,512,128]{3,2,1,0:T(8,128)(2,1)S(1)} %all-to-all-done.2.pairs_ref), custom_call_target="tpu_custom_call" | custom-call | flops 268435456 | bytes 1703936 | tf_op jit(solution)/shard_map/pallas_call | solution.py:84
  105.9 13.4 %all-to-all-start.3 = ((bf16[16,96,128]{2,1,0:T(8,128)(2,1)}), bf16[16,96,128]{2,1,0:T(8,128)(2,1)S(1)}, u32[]{:S(2)}, u32[]{:S(2)}) async-start(bf16[16,96,128]{2,1,0:T(8,128)(2,1)} %shard_map.175), calls=%async_computation.3 | async-start | bytes 786432 | tf_op jit(solution)/shard_map/all_to_all | solution.py:623
  119.2 7.4 %all-gather.3.cloned.1.call-done = bf16[64,32,512]{2,1,0:T(8,128)(2,1)} async-done(((bf16[4,32,512]{2,1,0:T(8,128)(2,1)}), bf16[64,32,512]{2,1,0:T(8,128)(2,1)}) %all-gather.3.cloned.1.call-update) | async-done | bytes 2097168 | tf_op jit(solution)/shard_map/all_gather | solution.py:525
  126.7 14.0 %all-to-all-done.3.back_ref = bf16[16,96,128]{2,1,0:T(8,128)(2,1)S(1)} async-done(((bf16[16,96,128]{2,1,0:T(8,128)(2,1)}), bf16[16,96,128]{2,1,0:T(8,128)(2,1)S(1)}, u32[]{:S(2)}, u32[]{:S(2)}) %all-to-all-start.3) | async-done | bytes 393248 | tf_op jit(solution)/shard_map/all_to_all | solution.py:623
  140.7 1.1 shard_map.176
  141.9 4.6 %all-to-all-start.4 = ((bf16[8,32,2048]{2,1,0:T(8,128)(2,1)}), bf16[8,32,2048]{2,1,0:T(8,128)(2,1)S(1)}, u32[]{:S(2)}, u32[]{:S(2)}) async-start(bf16[8,32,2048]{2,1,0:T(8,128)(2,1)} %get-tuple-element.50), calls=%async_computation.4 | async-start | bytes 2097152 | tf_op jit(solution)/shard_map/all_to_all | solution.py:643
  146.4 1.9 %collective-permute-start.6 = (bf16[16,32,128]{2,1,0:T(8,128)(2,1)}, bf16[16,32,128]{2,1,0:T(8,128)(2,1)S(1)}, u32[]{:S(2)}, u32[]{:S(2)}) collective-permute-start(bf16[16,32,128]{2,1,0:T(8,128)(2,1)} %get-tuple-element.45), channel_id=1, source_target_pairs={{0,128},{128,256},{256,384},{384,0},{1,129},{129,257},{257,385},{3... | collective-permute-start | bytes 393224 | tf_op jit(solution)/shard_map/ppermute | solution.py:644
  148.4 6.5 %collective-permute-start.7 = (bf16[16,32,128]{2,1,0:T(8,128)(2,1)}, bf16[16,32,128]{2,1,0:T(8,128)(2,1)}, u32[]{:S(2)}, u32[]{:S(2)}) collective-permute-start(bf16[16,32,128]{2,1,0:T(8,128)(2,1)} %get-tuple-element.46), channel_id=1, source_target_pairs={{0,132},{4,128},{128,260},{132,256},{256,388},{260,384},{384,4},{3... | collective-permute-start | bytes 393224 | tf_op jit(solution)/shard_map/ppermute | solution.py:645
  154.9 7.8 %all-to-all-done.4.rows_ref = bf16[8,32,2048]{2,1,0:T(8,128)(2,1)S(1)} async-done(((bf16[8,32,2048]{2,1,0:T(8,128)(2,1)}), bf16[8,32,2048]{2,1,0:T(8,128)(2,1)S(1)}, u32[]{:S(2)}, u32[]{:S(2)}) %all-to-all-start.4) | async-done | bytes 1048608 | tf_op jit(solution)/shard_map/all_to_all | solution.py:643
  163.4 3.1 %collective-permute-start.8 = (bf16[128,512]{1,0:T(8,128)(2,1)S(1)}, bf16[128,512]{1,0:T(8,128)(2,1)S(1)}, u32[]{:S(2)}, u32[]{:S(2)}) collective-permute-start(bf16[128,512]{1,0:T(8,128)(2,1)S(1)} %get-tuple-element.53), channel_id=1, source_target_pairs={{0,4},{4,0},{1,5},{5,1},{2,6},{6,2},{3,7},{7,3},{8,12},{12,8},{9,1... | collective-permute-start | bytes 393224 | tf_op jit(solution)/shard_map/ppermute | solution.py:662
  166.6 1.9 %shard_map.177 = bf16[128,1024]{1,0:T(8,128)(2,1)} custom-call(s32[1]{0:T(128)} %bitcast.x_ref, bf16[16,32,128]{2,1,0:T(8,128)(2,1)S(1)} %collective-permute-done.6.own_ref, bf16[16,32,128]{2,1,0:T(8,128)(2,1)} %collective-permute-done.7.got_ref, bf16[128,1024]{1,0:T(8,128)(2,1)S(1)} %collective-permute-done.1.gate_ref, ...), custom_call_target="tpu_custom_call" | custom-call | bytes 802816 | tf_op jit(solution)/shard_map/pallas_call | solution.py:84
  168.5 3.3 %collective-permute-done.8.got_ref = bf16[128,512]{1,0:T(8,128)(2,1)S(1)} collective-permute-done((bf16[128,512]{1,0:T(8,128)(2,1)S(1)}, bf16[128,512]{1,0:T(8,128)(2,1)S(1)}, u32[]{:S(2)}, u32[]{:S(2)}) %collective-permute-start.8) | collective-permute-done | bytes 131104 | tf_op jit(solution)/shard_map/ppermute | solution.py:662
  (38 shorter events, 8.9 us)
Async XLA Ops:
  7.2 91.7 %copy-start = (f32[1,1024]{1,0:T(1,128)S(1)}, f32[1,1024]{1,0:T(1,128)}, u32[]{:S(2)}) copy-start(f32[1,1024]{1,0:T(1,128)} %param.21) | copy-start | bytes 12292
  9.8 13.9 %all-to-all-start = ((bf16[4,128,512]{2,1,0:T(8,128)(2,1)}), bf16[4,128,512]{2,1,0:T(8,128)(2,1)S(1)}, u32[]{:S(2)}, u32[]{:S(2)}) async-start(bf16[4,128,512]{2,1,0:T(8,128)(2,1)} %get-tuple-element.28), calls=%async_computation | async-start | bytes 1048576 | tf_op jit(solution)/shard_map/all_to_all | solution.py:507
  14.3 39.4 %copy-start.8 = (f32[1,1,1,32,4096]{4,3,2,1,0:T(8,128)S(1)}, f32[1,1,1,32,4096]{4,3,2,1,0:T(8,128)}, u32[]{:S(2)}) copy-start(f32[1,1,1,32,4096]{4,3,2,1,0:T(8,128)} %param.20) | copy-start | bytes 1572868
  14.3 9.4 %collective-permute-start = (bf16[16,40,128]{2,1,0:T(8,128)(2,1)}, bf16[16,40,128]{2,1,0:T(8,128)(2,1)S(1)}, u32[]{:S(2)}, u32[]{:S(2)}) collective-permute-start(bf16[16,40,128]{2,1,0:T(8,128)(2,1)} %get-tuple-element.30), channel_id=1, source_target_pairs={{0,4},{4,0},{1,5},{5,1},{2,6},{6,2},{3,7},{7,3},{8,12},{12,8},{9,1... | collective-permute-start | bytes 491528 | tf_op jit(solution)/shard_map/ppermute | solution.py:506
  25.7 47.9 %all-to-all-start.1 = ((bf16[16,168,128]{2,1,0:T(8,128)(2,1)}), bf16[16,168,128]{2,1,0:T(8,128)(2,1)S(1)}, u32[]{:S(2)}, u32[]{:S(2)}) async-start(bf16[16,168,128]{2,1,0:T(8,128)(2,1)} %get-tuple-element.31), calls=%async_computation.1 | async-start | bytes 1376256 | tf_op jit(solution)/shard_map/all_to_all | solution.py:524
  40.9 85.8 %all-gather.3.cloned.1.call-start = ((), (), s32[]{:S(2)}) async-start(), calls=%async_computation.5 | async-start | bytes 2228224 | tf_op jit(solution)/shard_map/all_gather | solution.py:525
  41.6 16.8 %collective-permute-start.1 = (bf16[128,1024]{1,0:T(8,128)(2,1)}, bf16[128,1024]{1,0:T(8,128)(2,1)S(1)}, u32[]{:S(2)}, u32[]{:S(2)}) collective-permute-start(bf16[128,1024]{1,0:T(8,128)(2,1)} %bitcast.10), channel_id=1, source_target_pairs={{0,128},{128,256},{256,384},{384,0},{1,129},{129,257},{257,385},{3... | collective-permute-start | bytes 786440 | tf_op jit(solution)/shard_map/ppermute | solution.py:529
  44.3 14.1 %collective-permute-start.2 = (f32[3,1024]{1,0:T(4,128)S(1)}, f32[3,1024]{1,0:T(4,128)S(1)}, u32[]{:S(2)}, u32[]{:S(2)}) collective-permute-start(f32[3,1024]{1,0:T(4,128)S(1)} %bitcast.43), channel_id=1, source_target_pairs={{0,128},{128,256},{256,384},{384,0},{1,129},{129,257},{257,385},{3... | collective-permute-start | bytes 36872 | tf_op jit(solution)/shard_map/ppermute | solution.py:530
  48.5 9.9 %collective-permute-start.3 = (bf16[2,1024]{1,0:T(2,128)(2,1)S(1)}, bf16[2,1024]{1,0:T(2,128)(2,1)S(1)}, u32[]{:S(2)}, u32[]{:S(2)}) collective-permute-start(bf16[2,1024]{1,0:T(2,128)(2,1)S(1)} %slice_bitcast_fusion), channel_id=1, source_target_pairs={{0,132},{4,136},{8,140},{12,144},{16,148},{20,152},{24,156},{28,16... | collective-permute-start | bytes 12296 | tf_op jit(solution)/shard_map/ppermute | solution.py:531
  58.4 16.2 %copy-start.6 = (f32[3,1024]{1,0:T(4,128)}, f32[3,1024]{1,0:T(4,128)S(1)}, u32[]{:S(2)}) copy-start(f32[3,1024]{1,0:T(4,128)S(1)} %collective-permute-done.2.taps_ref) | copy-start | bytes 36868
  74.7 16.4 %all-to-all-start.2 = ((bf16[4,2,512,128]{3,2,1,0:T(8,128)(2,1)}), bf16[4,2,512,128]{3,2,1,0:T(8,128)(2,1)S(1)}, u32[]{:S(2)}, u32[]{:S(2)}) async-start(bf16[4,2,512,128]{3,2,1,0:T(8,128)(2,1)} %get-tuple-element.34), calls=%async_computation.2 | async-start | bytes 2097152 | tf_op jit(solution)/shard_map/all_to_all | solution.py:566
  79.9 9.5 %collective-permute-start.4 = (bf16[512,128]{1,0:T(8,128)(2,1)S(1)}, bf16[512,128]{1,0:T(8,128)(2,1)}, u32[]{:S(2)}, u32[]{:S(2)}) collective-permute-start(bf16[512,128]{1,0:T(8,128)(2,1)S(1)} %get-tuple-element.38.query_ref), channel_id=1, source_target_pairs={{0,4},{4,0},{1,5},{5,1},{2,6},{6,2},{3,7},{7,3},{8,12},{12,8},{9,1... | collective-permute-start | bytes 393224 | tf_op jit(solution)/shard_map/ppermute | solution.py:565
  87.6 1.1 copy-start.2
  88.7 0.8 copy-start.4
  89.5 9.4 %copy-start.3 = (f32[1280,256]{1,0:T(8,128)S(1)}, f32[1280,256]{1,0:T(8,128)}, u32[]{:S(2)}) copy-start(f32[1280,256]{1,0:T(8,128)} %copy-done.2) | copy-start | bytes 3932164
  94.1 10.8 %collective-permute-start.5 = (bf16[544,128]{1,0:T(8,128)(2,1)S(1)}, bf16[544,128]{1,0:T(8,128)(2,1)S(1)}, u32[]{:S(2)}, u32[]{:S(2)}) collective-permute-start(bf16[544,128]{1,0:T(8,128)(2,1)S(1)} %shard_map.172), channel_id=1, source_target_pairs={{0,4},{4,0},{1,5},{5,1},{2,6},{6,2},{3,7},{7,3},{8,12},{12,8},{9,1... | collective-permute-start | bytes 417800 | tf_op jit(solution)/shard_map/ppermute | solution.py:599
  98.9 1.0 copy-start.5
  105.9 34.9 %all-to-all-start.3 = ((bf16[16,96,128]{2,1,0:T(8,128)(2,1)}), bf16[16,96,128]{2,1,0:T(8,128)(2,1)S(1)}, u32[]{:S(2)}, u32[]{:S(2)}) async-start(bf16[16,96,128]{2,1,0:T(8,128)(2,1)} %shard_map.175), calls=%async_computation.3 | async-start | bytes 786432 | tf_op jit(solution)/shard_map/all_to_all | solution.py:623
  126.7 36.0 %copy-start.1 = (bf16[64,32,512]{2,1,0:T(8,128)(2,1)S(1)}, bf16[64,32,512]{2,1,0:T(8,128)(2,1)}, u32[]{:S(2)}) copy-start(bf16[64,32,512]{2,1,0:T(8,128)(2,1)} %all-gather.3.cloned.1.call-done) | copy-start | bytes 6291460
  141.9 20.7 %all-to-all-start.4 = ((bf16[8,32,2048]{2,1,0:T(8,128)(2,1)}), bf16[8,32,2048]{2,1,0:T(8,128)(2,1)S(1)}, u32[]{:S(2)}, u32[]{:S(2)}) async-start(bf16[8,32,2048]{2,1,0:T(8,128)(2,1)} %get-tuple-element.50), calls=%async_computation.4 | async-start | bytes 2097152 | tf_op jit(solution)/shard_map/all_to_all | solution.py:643
  146.4 20.1 %collective-permute-start.6 = (bf16[16,32,128]{2,1,0:T(8,128)(2,1)}, bf16[16,32,128]{2,1,0:T(8,128)(2,1)S(1)}, u32[]{:S(2)}, u32[]{:S(2)}) collective-permute-start(bf16[16,32,128]{2,1,0:T(8,128)(2,1)} %get-tuple-element.45), channel_id=1, source_target_pairs={{0,128},{128,256},{256,384},{384,0},{1,129},{129,257},{257,385},{3... | collective-permute-start | bytes 393224 | tf_op jit(solution)/shard_map/ppermute | solution.py:644
  148.4 18.2 %collective-permute-start.7 = (bf16[16,32,128]{2,1,0:T(8,128)(2,1)}, bf16[16,32,128]{2,1,0:T(8,128)(2,1)}, u32[]{:S(2)}, u32[]{:S(2)}) collective-permute-start(bf16[16,32,128]{2,1,0:T(8,128)(2,1)} %get-tuple-element.46), channel_id=1, source_target_pairs={{0,132},{4,128},{128,260},{132,256},{256,388},{260,384},{384,4},{3... | collective-permute-start | bytes 393224 | tf_op jit(solution)/shard_map/ppermute | solution.py:645
  162.6 3.9 %copy-start.7 = (f32[3,1024]{1,0:T(4,128)S(1)}, f32[3,1024]{1,0:T(4,128)}, u32[]{:S(2)}) copy-start(f32[3,1024]{1,0:T(4,128)} %copy-done.6) | copy-start | bytes 36868
  163.4 8.4 %collective-permute-start.8 = (bf16[128,512]{1,0:T(8,128)(2,1)S(1)}, bf16[128,512]{1,0:T(8,128)(2,1)S(1)}, u32[]{:S(2)}, u32[]{:S(2)}) collective-permute-start(bf16[128,512]{1,0:T(8,128)(2,1)S(1)} %get-tuple-element.53), channel_id=1, source_target_pairs={{0,4},{4,0},{1,5},{5,1},{2,6},{6,2},{3,7},{7,3},{8,12},{12,8},{9,1... | collective-permute-start | bytes 393224 | tf_op jit(solution)/shard_map/ppermute | solution.py:662
Sparse Core Ops, SparseCore 0:
  44.4 82.2 all-gather.2

commit v11 on v10

--- a/solution.py
+++ b/solution.py
@@ -221,10 +221,13 @@
     first_ref,
     mid_ref,
     forward_ref,
+    out_hbm,
+    signal_hbm,
+    done_ref,
+    turned_ref,
     out_ref,
     signal_ref,
-    done_ref,
-    turned_ref,
+    sems,
 ):
     done_ref[...] = jnp.zeros_like(done_ref)
     rows, half = mid_ref.shape[2], mid_ref.shape[1]
@@ -257,6 +260,8 @@
         signal_ref[at * channels : (at + 1) * channels, :] = jnp.where(
             column < 2, turned[:, :rows], block
         )
+    stores = [pltpu.make_async_copy(signal_ref, signal_hbm, sems.at[0])]
+    stores[0].start()
     cos_mid, sin_mid = mid_ref[0], mid_ref[1]
     for at in range(channels):
         signal = signal_ref[pl.ds(at, n_seq, stride=channels), :].astype(BF16)
@@ -270,6 +275,12 @@
         other_real, other_imag = spectrum_ref[span, :rows], spectrum_ref[span, rows:]
         out_ref[span, :rows] = real * other_real - imag * other_imag
         out_ref[span, rows:] = real * other_imag + imag * other_real
+        begin = pl.ds(group * step, step)
+        store = pltpu.make_async_copy(out_ref.at[begin], out_hbm.at[begin], sems.at[group + 1])
+        store.start()
+        stores.append(store)
+    for store in stores:
+        store.wait()
 
 
 def convolve_kernel(
@@ -582,7 +593,13 @@
             tables["mid"],
             tables["forward"],
         ),
-        (pltpu.VMEM((channels * half, 2 * rows), F32),),
+        (
+            pltpu.VMEM((channels * half, 2 * rows), F32),
+            pltpu.VMEM((channels * half, 2 * rows), F32),
+            pltpu.VMEM((n_seq * channels, rows), F32),
+            pltpu.SemaphoreType.DMA((channels // 4 + 1,)),
+        ),
+        hbm_out=(0, 1),
         from_hbm=(3, 4, 5),
     )
     work = 2 * own_rows * n_tp * own_rows * HD

time: 181 us -> 180 us (level)
  local copies, waits for them, and re-layouts: 5.42 us -> 3.57 us
    all_to_all x1, waiting for transfers between devices: 14 us -> 11.8 us  [body(): back = lax.all_to_all(returned, 'z', 0, 0)]
    all_gather x1, waiting for transfers between devices: 7.45 us -> 9.56 us  [body(): weight = lax.all_gather(weight, 'z')]
    unnamed x20 -> x16, local copies, waits for them, and re-layouts: 3.03 us -> 1.17 us
where the time goes in v11:
time: 180 us; the launch traced here: 179 us
  starting transfers between devices  79.2 us (44%)
  waiting for transfers between devices  57.5 us (32%)
  Pallas kernels  24.8 us (14%)
  between operations  14.3 us (8%)
  local copies, waits for them, and re-layouts  3.57 us (2%)
    pallas_call x13, Pallas kernels, kernel_call(): pl.pallas_call(kernel, out_shape=placed[0] if single else placed, in_spec...  24.8 us
    all_to_all x1, starting transfers between devices, body(): mixed = lax.all_to_all(packed, 'z', 0, 0)  15.2 us
    all_to_all x1, waiting for transfers between devices, body(): mixed = lax.all_to_all(packed, 'z', 0, 0)  15.2 us
    all_to_all x1, starting transfers between devices, body(): back = lax.all_to_all(returned, 'z', 0, 0)  13.4 us
    all_to_all x1, waiting for transfers between devices, body(): back = lax.all_to_all(returned, 'z', 0, 0)  11.8 us
    all_gather x1, waiting for transfers between devices, body(): weight = lax.all_gather(weight, 'z')  9.56 us
    all_to_all x1, waiting for transfers between devices, body(): plane_rows = lax.all_to_all(plane_rows, ('xh', 'tp'), 0, 0)  7.32 us
    ppermute x1, starting transfers between devices, body(): lax.ppermute(other_long, ('section', 'xh'), [(2 * s + x, 2 * t + 1 - x) f...  6.74 us
  transfers between devices with their start and end apart: 15, of which 9 were waited for; matrix products, arithmetic and copies ran while one was open for 1% of the time, Pallas kernels for 10%

profile of v11, /device:TPU:32, one launch (start us, length us, event | category | flops | bytes accessed | tf_op | source)
XLA Modules:
  0.0 179.4 jit_solution(12014417829376303553)
XLA Ops:
  7.2 2.6 %shard_map.167 = (bf16[4,128,512]{2,1,0:T(8,128)(2,1)}, bf16[16,40,128]{2,1,0:T(8,128)(2,1)}, bf16[16,40,128]{2,1,0:T(8,128)(2,1)}) custom-call(s32[1]{0:T(128)} %bitcast.x_ref, bf16[128,1024]{1,0:T(8,128)(2,1)} %bitcast.35, bf16[128,1024]{1,0:T(8,128)(2,1)} %bitcast.36, f32[9,1,1024]{2,1,0:T(1,128)} %bitcast.42, bf16[128,512]{1,0:T(8,128)(2,1)} %bitcast.38, ...), custom_call_target="tpu_custom_call" | custom-call | bytes 1937408 | tf_op jit(solution)/shard_map/pallas_call | solution.py:84
  9.8 4.5 %all-to-all-start = ((bf16[4,128,512]{2,1,0:T(8,128)(2,1)}), bf16[4,128,512]{2,1,0:T(8,128)(2,1)S(1)}, u32[]{:S(2)}, u32[]{:S(2)}) async-start(bf16[4,128,512]{2,1,0:T(8,128)(2,1)} %get-tuple-element.28), calls=%async_computation | async-start | bytes 1048576 | tf_op jit(solution)/shard_map/all_to_all | solution.py:518
  14.3 5.1 %collective-permute-start = (bf16[16,40,128]{2,1,0:T(8,128)(2,1)}, bf16[16,40,128]{2,1,0:T(8,128)(2,1)S(1)}, u32[]{:S(2)}, u32[]{:S(2)}) collective-permute-start(bf16[16,40,128]{2,1,0:T(8,128)(2,1)} %get-tuple-element.30), channel_id=1, source_target_pairs={{0,4},{4,0},{1,5},{5,1},{2,6},{6,2},{3,7},{7,3},{8,12},{12,8},{9,1... | collective-permute-start | bytes 491528 | tf_op jit(solution)/shard_map/ppermute | solution.py:517
  19.3 4.3 %collective-permute-done.got_ref = bf16[16,40,128]{2,1,0:T(8,128)(2,1)S(1)} collective-permute-done((bf16[16,40,128]{2,1,0:T(8,128)(2,1)}, bf16[16,40,128]{2,1,0:T(8,128)(2,1)S(1)}, u32[]{:S(2)}, u32[]{:S(2)}) %collective-permute-start) | collective-permute-done | bytes 163872 | tf_op jit(solution)/shard_map/ppermute | solution.py:517
  23.8 1.9 %shard_map.168 = (bf16[16,168,128]{2,1,0:T(8,128)(2,1)}, bf16[4,32,512]{2,1,0:T(8,128)(2,1)}) custom-call(s32[1]{0:T(128)} %bitcast.x_ref, bf16[4,128,512]{2,1,0:T(8,128)(2,1)S(1)} %all-to-all-done.rows_ref, bf16[16,40,128]{2,1,0:T(8,128)(2,1)} %get-tuple-element.29.own_hbm, bf16[16,40,128]{2,1,0:T(8,128)(2,1)S(1)} %collective-permute-done.got_ref), custom_call_target="tpu_custom_call" | custom-call | bytes 1671168 | tf_op jit(solution)/shard_map/pallas_call | solution.py:84
  25.7 15.2 %all-to-all-start.1 = ((bf16[16,168,128]{2,1,0:T(8,128)(2,1)}), bf16[16,168,128]{2,1,0:T(8,128)(2,1)S(1)}, u32[]{:S(2)}, u32[]{:S(2)}) async-start(bf16[16,168,128]{2,1,0:T(8,128)(2,1)} %get-tuple-element.31), calls=%async_computation.1 | async-start | bytes 1376256 | tf_op jit(solution)/shard_map/all_to_all | solution.py:535
  41.6 1.9 %collective-permute-start.1 = (bf16[128,1024]{1,0:T(8,128)(2,1)}, bf16[128,1024]{1,0:T(8,128)(2,1)S(1)}, u32[]{:S(2)}, u32[]{:S(2)}) collective-permute-start(bf16[128,1024]{1,0:T(8,128)(2,1)} %bitcast.10), channel_id=1, source_target_pairs={{0,128},{128,256},{256,384},{384,0},{1,129},{129,257},{257,385},{3... | collective-permute-start | bytes 786440 | tf_op jit(solution)/shard_map/ppermute | solution.py:540
  44.3 3.5 %collective-permute-start.2 = (f32[3,1024]{1,0:T(4,128)S(1)}, f32[3,1024]{1,0:T(4,128)S(1)}, u32[]{:S(2)}, u32[]{:S(2)}) collective-permute-start(f32[3,1024]{1,0:T(4,128)S(1)} %bitcast.43), channel_id=1, source_target_pairs={{0,128},{128,256},{256,384},{384,0},{1,129},{129,257},{257,385},{3... | collective-permute-start | bytes 36872 | tf_op jit(solution)/shard_map/ppermute | solution.py:541
  48.5 4.2 %collective-permute-start.3 = (bf16[2,1024]{1,0:T(2,128)(2,1)S(1)}, bf16[2,1024]{1,0:T(2,128)(2,1)S(1)}, u32[]{:S(2)}, u32[]{:S(2)}) collective-permute-start(bf16[2,1024]{1,0:T(2,128)(2,1)S(1)} %slice_bitcast_fusion), channel_id=1, source_target_pairs={{0,132},{4,136},{8,140},{12,144},{16,148},{20,152},{24,156},{28,16... | collective-permute-start | bytes 12296 | tf_op jit(solution)/shard_map/ppermute | solution.py:542
  53.8 2.0 %shard_map.169.spectrum_ref = f32[1280,256]{1,0:T(8,128)S(1)} custom-call(f32[32,32,128]{2,1,0:T(8,128)S(1)} %bitcast.30, bf16[80,96]{1,0:T(8,128)(2,1)} %constant.41.clone.first_ref, f32[2,40,128]{2,1,0:T(8,128)} %constant.42.clone.mid_ref, bf16[2,256,256]{2,1,0:T(8,128)(2,1)} %constant.43.clone.forward_ref), custom_call_target="tpu_custom_call" | custom-call | bytes 2153472 | tf_op jit(solution)/shard_map/pallas_call | solution.py:84
  55.8 2.6 %collective-permute-done.3.tail_ref = bf16[2,1024]{1,0:T(2,128)(2,1)S(1)} collective-permute-done((bf16[2,1024]{1,0:T(2,128)(2,1)S(1)}, bf16[2,1024]{1,0:T(2,128)(2,1)S(1)}, u32[]{:S(2)}, u32[]{:S(2)}) %collective-permute-start.3) | collective-permute-done | bytes 4128 | tf_op jit(solution)/shard_map/ppermute | solution.py:542
  58.4 15.2 %all-to-all-done.1.mixed_ref = bf16[16,168,128]{2,1,0:T(8,128)(2,1)S(1)} async-done(((bf16[16,168,128]{2,1,0:T(8,128)(2,1)}), bf16[16,168,128]{2,1,0:T(8,128)(2,1)S(1)}, u32[]{:S(2)}, u32[]{:S(2)}) %all-to-all-start.1) | async-done | bytes 688160 | tf_op jit(solution)/shard_map/all_to_all | solution.py:535
  74.7 5.3 %all-to-all-start.2 = ((bf16[4,2,512,128]{3,2,1,0:T(8,128)(2,1)}), bf16[4,2,512,128]{3,2,1,0:T(8,128)(2,1)S(1)}, u32[]{:S(2)}, u32[]{:S(2)}) async-start(bf16[4,2,512,128]{3,2,1,0:T(8,128)(2,1)} %get-tuple-element.34), calls=%async_computation.2 | async-start | bytes 2097152 | tf_op jit(solution)/shard_map/all_to_all | solution.py:577
  79.9 4.9 %collective-permute-start.4 = (bf16[512,128]{1,0:T(8,128)(2,1)S(1)}, bf16[512,128]{1,0:T(8,128)(2,1)}, u32[]{:S(2)}, u32[]{:S(2)}) collective-permute-start(bf16[512,128]{1,0:T(8,128)(2,1)S(1)} %get-tuple-element.38.query_ref), channel_id=1, source_target_pairs={{0,4},{4,0},{1,5},{5,1},{2,6},{6,2},{3,7},{7,3},{8,12},{12,8},{9,1... | collective-permute-start | bytes 393224 | tf_op jit(solution)/shard_map/ppermute | solution.py:576
  84.9 3.5 %shard_map.171 = (f32[1280,256]{1,0:T(8,128)}, f32[1024,128]{1,0:T(8,128)}, f32[8,128]{1,0:T(8,128)S(1)}) custom-call(bf16[16,168,128]{2,1,0:T(8,128)(2,1)S(1)} %all-to-all-done.1.mixed_ref, f32[32,9]{1,0:T(8,128)S(1)} %bitcast.32, f32[1280,256]{1,0:T(8,128)S(1)} %shard_map.169.spectrum_ref, bf16[80,64]{1,0:T(8,128)(2,1)} %constant.44.clone.first_ref, ...), custom_call_target="tpu_custom_call" | custom-call | bytes 4152448 | tf_op jit(solution)/shard_map/pallas_call | solution.py:84
  88.4 2.6 %all-to-all-done.2.pairs_ref = bf16[4,2,512,128]{3,2,1,0:T(8,128)(2,1)S(1)} async-done(((bf16[4,2,512,128]{3,2,1,0:T(8,128)(2,1)}), bf16[4,2,512,128]{3,2,1,0:T(8,128)(2,1)S(1)}, u32[]{:S(2)}, u32[]{:S(2)}) %all-to-all-start.2) | async-done | bytes 1048608 | tf_op jit(solution)/shard_map/all_to_all | solution.py:577
  91.0 3.0 %shard_map.172 = bf16[544,128]{1,0:T(8,128)(2,1)S(1)} custom-call(s32[1]{0:T(128)} %bitcast.14.delta_ref, bf16[512,128]{1,0:T(8,128)(2,1)} %collective-permute-done.4.query_ref, bf16[4,2,512,128]{3,2,1,0:T(8,128)(2,1)S(1)} %all-to-all-done.2.pairs_ref, f32[8,128]{1,0:T(8,128)S(1)} %get-tuple-element.37.done_ref), custom_call_target="tpu_custom_call" | custom-call | flops 268435456 | bytes 1323008 | tf_op jit(solution)/shard_map/pallas_call | solution.py:84
  94.1 4.7 %collective-permute-start.5 = (bf16[544,128]{1,0:T(8,128)(2,1)S(1)}, bf16[544,128]{1,0:T(8,128)(2,1)S(1)}, u32[]{:S(2)}, u32[]{:S(2)}) collective-permute-start(bf16[544,128]{1,0:T(8,128)(2,1)S(1)} %shard_map.172), channel_id=1, source_target_pairs={{0,4},{4,0},{1,5},{5,1},{2,6},{6,2},{3,7},{7,3},{8,12},{12,8},{9,1... | collective-permute-start | bytes 417800 | tf_op jit(solution)/shard_map/ppermute | solution.py:616
  98.9 1.0 copy-done.3
  99.9 2.7 %shard_map.174 = bf16[32,32,128]{2,1,0:T(8,128)(2,1)S(1)} custom-call(f32[32]{0:T(128)S(1)} %dynamic-slice_bitcast_fusion.gain_ref, f32[1280,256]{1,0:T(8,128)S(1)} %copy-done.2, f32[1024,128]{1,0:T(8,128)S(1)} %copy-done.3, f32[2,40,128]{2,1,0:T(8,128)} %constant.42.clone.mid_ref, bf16[2,256,256]{2,1,0:T(8,128)(2,1)} %constant.45.clone.backward_ref, ...), custom_call_target="tpu_custom_call" | custom-call | bytes 2415616 | tf_op jit(solution)/shard_map/pallas_call | solution.py:84
  102.7 2.2 %shard_map.173 = (f32[512,128]{1,0:T(8,128)S(1)}, f32[512,128]{1,0:T(8,128)S(1)}) custom-call(s32[1]{0:T(128)} %bitcast.1.delta_ref, bf16[512,128]{1,0:T(8,128)(2,1)S(1)} %get-tuple-element.38.query_ref, bf16[4,2,512,128]{3,2,1,0:T(8,128)(2,1)S(1)} %all-to-all-done.2.pairs_ref), custom_call_target="tpu_custom_call" | custom-call | flops 268435456 | bytes 1703936 | tf_op jit(solution)/shard_map/pallas_call | solution.py:84
  105.9 13.4 %all-to-all-start.3 = ((bf16[16,96,128]{2,1,0:T(8,128)(2,1)}), bf16[16,96,128]{2,1,0:T(8,128)(2,1)S(1)}, u32[]{:S(2)}, u32[]{:S(2)}) async-start(bf16[16,96,128]{2,1,0:T(8,128)(2,1)} %shard_map.175), calls=%async_computation.3 | async-start | bytes 786432 | tf_op jit(solution)/shard_map/all_to_all | solution.py:640
  119.2 9.6 %all-gather.3.cloned.1.call-done = bf16[64,32,512]{2,1,0:T(8,128)(2,1)} async-done(((bf16[4,32,512]{2,1,0:T(8,128)(2,1)}), bf16[64,32,512]{2,1,0:T(8,128)(2,1)}) %all-gather.3.cloned.1.call-update) | async-done | bytes 2097168 | tf_op jit(solution)/shard_map/all_gather | solution.py:536
  128.8 11.8 %all-to-all-done.3.back_ref = bf16[16,96,128]{2,1,0:T(8,128)(2,1)S(1)} async-done(((bf16[16,96,128]{2,1,0:T(8,128)(2,1)}), bf16[16,96,128]{2,1,0:T(8,128)(2,1)S(1)}, u32[]{:S(2)}, u32[]{:S(2)}) %all-to-all-start.3) | async-done | bytes 393248 | tf_op jit(solution)/shard_map/all_to_all | solution.py:640
  140.5 1.1 shard_map.176
  141.7 4.7 %all-to-all-start.4 = ((bf16[8,32,2048]{2,1,0:T(8,128)(2,1)}), bf16[8,32,2048]{2,1,0:T(8,128)(2,1)S(1)}, u32[]{:S(2)}, u32[]{:S(2)}) async-start(bf16[8,32,2048]{2,1,0:T(8,128)(2,1)} %get-tuple-element.50), calls=%async_computation.4 | async-start | bytes 2097152 | tf_op jit(solution)/shard_map/all_to_all | solution.py:660
  146.4 1.9 %collective-permute-start.6 = (bf16[16,32,128]{2,1,0:T(8,128)(2,1)}, bf16[16,32,128]{2,1,0:T(8,128)(2,1)S(1)}, u32[]{:S(2)}, u32[]{:S(2)}) collective-permute-start(bf16[16,32,128]{2,1,0:T(8,128)(2,1)} %get-tuple-element.45), channel_id=1, source_target_pairs={{0,128},{128,256},{256,384},{384,0},{1,129},{129,257},{257,385},{3... | collective-permute-start | bytes 393224 | tf_op jit(solution)/shard_map/ppermute | solution.py:661
  148.3 6.7 %collective-permute-start.7 = (bf16[16,32,128]{2,1,0:T(8,128)(2,1)}, bf16[16,32,128]{2,1,0:T(8,128)(2,1)}, u32[]{:S(2)}, u32[]{:S(2)}) collective-permute-start(bf16[16,32,128]{2,1,0:T(8,128)(2,1)} %get-tuple-element.46), channel_id=1, source_target_pairs={{0,132},{4,128},{128,260},{132,256},{256,388},{260,384},{384,4},{3... | collective-permute-start | bytes 393224 | tf_op jit(solution)/shard_map/ppermute | solution.py:662
  155.1 7.3 %all-to-all-done.4.rows_ref = bf16[8,32,2048]{2,1,0:T(8,128)(2,1)S(1)} async-done(((bf16[8,32,2048]{2,1,0:T(8,128)(2,1)}), bf16[8,32,2048]{2,1,0:T(8,128)(2,1)S(1)}, u32[]{:S(2)}, u32[]{:S(2)}) %all-to-all-start.4) | async-done | bytes 1048608 | tf_op jit(solution)/shard_map/all_to_all | solution.py:660
  163.2 3.1 %collective-permute-start.8 = (bf16[128,512]{1,0:T(8,128)(2,1)S(1)}, bf16[128,512]{1,0:T(8,128)(2,1)S(1)}, u32[]{:S(2)}, u32[]{:S(2)}) collective-permute-start(bf16[128,512]{1,0:T(8,128)(2,1)S(1)} %get-tuple-element.53), channel_id=1, source_target_pairs={{0,4},{4,0},{1,5},{5,1},{2,6},{6,2},{3,7},{7,3},{8,12},{12,8},{9,1... | collective-permute-start | bytes 393224 | tf_op jit(solution)/shard_map/ppermute | solution.py:679
  166.3 1.9 %shard_map.177 = bf16[128,1024]{1,0:T(8,128)(2,1)} custom-call(s32[1]{0:T(128)} %bitcast.x_ref, bf16[16,32,128]{2,1,0:T(8,128)(2,1)S(1)} %collective-permute-done.6.own_ref, bf16[16,32,128]{2,1,0:T(8,128)(2,1)} %collective-permute-done.7.got_ref, bf16[128,1024]{1,0:T(8,128)(2,1)S(1)} %collective-permute-done.1.gate_ref, ...), custom_call_target="tpu_custom_call" | custom-call | bytes 802816 | tf_op jit(solution)/shard_map/pallas_call | solution.py:84
  168.2 3.3 %collective-permute-done.8.got_ref = bf16[128,512]{1,0:T(8,128)(2,1)S(1)} collective-permute-done((bf16[128,512]{1,0:T(8,128)(2,1)S(1)}, bf16[128,512]{1,0:T(8,128)(2,1)S(1)}, u32[]{:S(2)}, u32[]{:S(2)}) %collective-permute-start.8) | collective-permute-done | bytes 131104 | tf_op jit(solution)/shard_map/ppermute | solution.py:679
  (34 shorter events, 7.1 us)
Async XLA Ops:
  7.2 91.6 %copy-start = (f32[1,1024]{1,0:T(1,128)S(1)}, f32[1,1024]{1,0:T(1,128)}, u32[]{:S(2)}) copy-start(f32[1,1024]{1,0:T(1,128)} %param.21) | copy-start | bytes 12292
  9.8 13.9 %all-to-all-start = ((bf16[4,128,512]{2,1,0:T(8,128)(2,1)}), bf16[4,128,512]{2,1,0:T(8,128)(2,1)S(1)}, u32[]{:S(2)}, u32[]{:S(2)}) async-start(bf16[4,128,512]{2,1,0:T(8,128)(2,1)} %get-tuple-element.28), calls=%async_computation | async-start | bytes 1048576 | tf_op jit(solution)/shard_map/all_to_all | solution.py:518
  14.3 39.4 %copy-start.6 = (f32[1,1,1,32,4096]{4,3,2,1,0:T(8,128)S(1)}, f32[1,1,1,32,4096]{4,3,2,1,0:T(8,128)}, u32[]{:S(2)}) copy-start(f32[1,1,1,32,4096]{4,3,2,1,0:T(8,128)} %param.20) | copy-start | bytes 1572868
  14.3 9.4 %collective-permute-start = (bf16[16,40,128]{2,1,0:T(8,128)(2,1)}, bf16[16,40,128]{2,1,0:T(8,128)(2,1)S(1)}, u32[]{:S(2)}, u32[]{:S(2)}) collective-permute-start(bf16[16,40,128]{2,1,0:T(8,128)(2,1)} %get-tuple-element.30), channel_id=1, source_target_pairs={{0,4},{4,0},{1,5},{5,1},{2,6},{6,2},{3,7},{7,3},{8,12},{12,8},{9,1... | collective-permute-start | bytes 491528 | tf_op jit(solution)/shard_map/ppermute | solution.py:517
  25.7 47.9 %all-to-all-start.1 = ((bf16[16,168,128]{2,1,0:T(8,128)(2,1)}), bf16[16,168,128]{2,1,0:T(8,128)(2,1)S(1)}, u32[]{:S(2)}, u32[]{:S(2)}) async-start(bf16[16,168,128]{2,1,0:T(8,128)(2,1)} %get-tuple-element.31), calls=%async_computation.1 | async-start | bytes 1376256 | tf_op jit(solution)/shard_map/all_to_all | solution.py:535
  40.9 87.9 %all-gather.3.cloned.1.call-start = ((), (), s32[]{:S(2)}) async-start(), calls=%async_computation.5 | async-start | bytes 2228224 | tf_op jit(solution)/shard_map/all_gather | solution.py:536
  41.6 16.8 %collective-permute-start.1 = (bf16[128,1024]{1,0:T(8,128)(2,1)}, bf16[128,1024]{1,0:T(8,128)(2,1)S(1)}, u32[]{:S(2)}, u32[]{:S(2)}) collective-permute-start(bf16[128,1024]{1,0:T(8,128)(2,1)} %bitcast.10), channel_id=1, source_target_pairs={{0,128},{128,256},{256,384},{384,0},{1,129},{129,257},{257,385},{3... | collective-permute-start | bytes 786440 | tf_op jit(solution)/shard_map/ppermute | solution.py:540
  44.3 14.1 %collective-permute-start.2 = (f32[3,1024]{1,0:T(4,128)S(1)}, f32[3,1024]{1,0:T(4,128)S(1)}, u32[]{:S(2)}, u32[]{:S(2)}) collective-permute-start(f32[3,1024]{1,0:T(4,128)S(1)} %bitcast.43), channel_id=1, source_target_pairs={{0,128},{128,256},{256,384},{384,0},{1,129},{129,257},{257,385},{3... | collective-permute-start | bytes 36872 | tf_op jit(solution)/shard_map/ppermute | solution.py:541
  48.5 9.9 %collective-permute-start.3 = (bf16[2,1024]{1,0:T(2,128)(2,1)S(1)}, bf16[2,1024]{1,0:T(2,128)(2,1)S(1)}, u32[]{:S(2)}, u32[]{:S(2)}) collective-permute-start(bf16[2,1024]{1,0:T(2,128)(2,1)S(1)} %slice_bitcast_fusion), channel_id=1, source_target_pairs={{0,132},{4,136},{8,140},{12,144},{16,148},{20,152},{24,156},{28,16... | collective-permute-start | bytes 12296 | tf_op jit(solution)/shard_map/ppermute | solution.py:542
  58.4 16.2 %copy-start.4 = (f32[3,1024]{1,0:T(4,128)}, f32[3,1024]{1,0:T(4,128)S(1)}, u32[]{:S(2)}) copy-start(f32[3,1024]{1,0:T(4,128)S(1)} %collective-permute-done.2.taps_ref) | copy-start | bytes 36868
  74.7 16.4 %all-to-all-start.2 = ((bf16[4,2,512,128]{3,2,1,0:T(8,128)(2,1)}), bf16[4,2,512,128]{3,2,1,0:T(8,128)(2,1)S(1)}, u32[]{:S(2)}, u32[]{:S(2)}) async-start(bf16[4,2,512,128]{3,2,1,0:T(8,128)(2,1)} %get-tuple-element.34), calls=%async_computation.2 | async-start | bytes 2097152 | tf_op jit(solution)/shard_map/all_to_all | solution.py:577
  79.9 8.5 %collective-permute-start.4 = (bf16[512,128]{1,0:T(8,128)(2,1)S(1)}, bf16[512,128]{1,0:T(8,128)(2,1)}, u32[]{:S(2)}, u32[]{:S(2)}) collective-permute-start(bf16[512,128]{1,0:T(8,128)(2,1)S(1)} %get-tuple-element.38.query_ref), channel_id=1, source_target_pairs={{0,4},{4,0},{1,5},{5,1},{2,6},{6,2},{3,7},{7,3},{8,12},{12,8},{9,1... | collective-permute-start | bytes 393224 | tf_op jit(solution)/shard_map/ppermute | solution.py:576
  88.4 10.5 %copy-start.2 = (f32[1280,256]{1,0:T(8,128)S(1)}, f32[1280,256]{1,0:T(8,128)}, u32[]{:S(2)}) copy-start(f32[1280,256]{1,0:T(8,128)} %get-tuple-element.41.joined_ref) | copy-start | bytes 3932164
  94.1 10.8 %collective-permute-start.5 = (bf16[544,128]{1,0:T(8,128)(2,1)S(1)}, bf16[544,128]{1,0:T(8,128)(2,1)S(1)}, u32[]{:S(2)}, u32[]{:S(2)}) collective-permute-start(bf16[544,128]{1,0:T(8,128)(2,1)S(1)} %shard_map.172), channel_id=1, source_target_pairs={{0,4},{4,0},{1,5},{5,1},{2,6},{6,2},{3,7},{7,3},{8,12},{12,8},{9,1... | collective-permute-start | bytes 417800 | tf_op jit(solution)/shard_map/ppermute | solution.py:616
  98.9 1.0 copy-start.3
  105.9 34.7 %all-to-all-start.3 = ((bf16[16,96,128]{2,1,0:T(8,128)(2,1)}), bf16[16,96,128]{2,1,0:T(8,128)(2,1)S(1)}, u32[]{:S(2)}, u32[]{:S(2)}) async-start(bf16[16,96,128]{2,1,0:T(8,128)(2,1)} %shard_map.175), calls=%async_computation.3 | async-start | bytes 786432 | tf_op jit(solution)/shard_map/all_to_all | solution.py:640
  128.8 33.6 %copy-start.1 = (bf16[64,32,512]{2,1,0:T(8,128)(2,1)S(1)}, bf16[64,32,512]{2,1,0:T(8,128)(2,1)}, u32[]{:S(2)}) copy-start(bf16[64,32,512]{2,1,0:T(8,128)(2,1)} %all-gather.3.cloned.1.call-done) | copy-start | bytes 6291460
  141.7 20.7 %all-to-all-start.4 = ((bf16[8,32,2048]{2,1,0:T(8,128)(2,1)}), bf16[8,32,2048]{2,1,0:T(8,128)(2,1)S(1)}, u32[]{:S(2)}, u32[]{:S(2)}) async-start(bf16[8,32,2048]{2,1,0:T(8,128)(2,1)} %get-tuple-element.50), calls=%async_computation.4 | async-start | bytes 2097152 | tf_op jit(solution)/shard_map/all_to_all | solution.py:660
  146.4 19.9 %collective-permute-start.6 = (bf16[16,32,128]{2,1,0:T(8,128)(2,1)}, bf16[16,32,128]{2,1,0:T(8,128)(2,1)S(1)}, u32[]{:S(2)}, u32[]{:S(2)}) collective-permute-start(bf16[16,32,128]{2,1,0:T(8,128)(2,1)} %get-tuple-element.45), channel_id=1, source_target_pairs={{0,128},{128,256},{256,384},{384,0},{1,129},{129,257},{257,385},{3... | collective-permute-start | bytes 393224 | tf_op jit(solution)/shard_map/ppermute | solution.py:661
  148.3 18.0 %collective-permute-start.7 = (bf16[16,32,128]{2,1,0:T(8,128)(2,1)}, bf16[16,32,128]{2,1,0:T(8,128)(2,1)}, u32[]{:S(2)}, u32[]{:S(2)}) collective-permute-start(bf16[16,32,128]{2,1,0:T(8,128)(2,1)} %get-tuple-element.46), channel_id=1, source_target_pairs={{0,132},{4,128},{128,260},{132,256},{256,388},{260,384},{384,4},{3... | collective-permute-start | bytes 393224 | tf_op jit(solution)/shard_map/ppermute | solution.py:662
  162.4 3.9 %copy-start.5 = (f32[3,1024]{1,0:T(4,128)S(1)}, f32[3,1024]{1,0:T(4,128)}, u32[]{:S(2)}) copy-start(f32[3,1024]{1,0:T(4,128)} %copy-done.4) | copy-start | bytes 36868
  163.2 8.4 %collective-permute-start.8 = (bf16[128,512]{1,0:T(8,128)(2,1)S(1)}, bf16[128,512]{1,0:T(8,128)(2,1)S(1)}, u32[]{:S(2)}, u32[]{:S(2)}) collective-permute-start(bf16[128,512]{1,0:T(8,128)(2,1)S(1)} %get-tuple-element.53), channel_id=1, source_target_pairs={{0,4},{4,0},{1,5},{5,1},{2,6},{6,2},{3,7},{7,3},{8,12},{12,8},{9,1... | collective-permute-start | bytes 393224 | tf_op jit(solution)/shard_map/ppermute | solution.py:679
Sparse Core Ops, SparseCore 0:
  44.4 84.3 all-gather.2

commit v12 on v10

--- a/solution.py
+++ b/solution.py
@@ -153,16 +153,21 @@
             out_ref[at * heads + head, :size, :] = block
     low = x_ref[0] == 0
     fetch.wait()
-    own, got = own_ref[...].astype(F32), got_ref[...].astype(F32)
-    even, odd = jnp.where(low, own, got), jnp.where(low, got, own)
-    out_ref[:, size : size + channels, :] = even[:, :channels].astype(BF16)
-    out_ref[:, size + channels : size + 2 * channels, :] = odd[:, :channels].astype(BF16)
     row = lax.broadcasted_iota(jnp.int32, (1, 8, HD), 1)
-    lines = jnp.where(row < 2, even[:, channels:], pltpu.roll(odd[:, channels:], 2, 1))
-    out_ref[:, size + 2 * channels :, :] = lines.astype(BF16)
-    store = pltpu.make_async_copy(out_ref, out_hbm, sems.at[2])
-    store.start()
-    store.wait()
+    middle = out_ref.shape[0] // 2
+    stores = []
+    for at in range(2):
+        span = pl.ds(at * middle, middle)
+        own, got = own_ref[span].astype(F32), got_ref[span].astype(F32)
+        even, odd = jnp.where(low, own, got), jnp.where(low, got, own)
+        out_ref[span, size : size + channels, :] = even[:, :channels].astype(BF16)
+        out_ref[span, size + channels : size + 2 * channels, :] = odd[:, :channels].astype(BF16)
+        lines = jnp.where(row < 2, even[:, channels:], pltpu.roll(odd[:, channels:], 2, 1))
+        out_ref[span, size + 2 * channels :, :] = lines.astype(BF16)
+        stores.append(pltpu.make_async_copy(out_ref.at[span], out_hbm.at[span], sems.at[2 + at]))
+        stores[at].start()
+    for store in stores:
+        store.wait()
     pass_on.wait()
 
 
@@ -516,7 +521,7 @@
         (
             pltpu.VMEM((n_z, channels + 8, rows), BF16),
             pltpu.VMEM((n_z, 3 * part + 2 * channels + 8, HD), BF16),
-            pltpu.SemaphoreType.DMA((3,)),
+            pltpu.SemaphoreType.DMA((4,)),
         ),
         hbm_in=(1,),
         hbm_out=(0, 1),

time: 181 us -> 181 us (level)
  no operation moved by 1% of the time
where the time goes in v12:
time: 181 us; the launch traced here: 180 us
  starting transfers between devices  78.8 us (44%)
  waiting for transfers between devices  57 us (31%)
  Pallas kernels  24 us (13%)
  between operations  14.3 us (8%)
  local copies, waits for them, and re-layouts  5.42 us (3%)
    pallas_call x13, Pallas kernels, kernel_call(): pl.pallas_call(kernel, out_shape=placed[0] if single else placed, in_spec...  24 us
    all_to_all x1, starting transfers between devices, body(): mixed = lax.all_to_all(packed, 'z', 0, 0)  15.2 us
    all_to_all x1, waiting for transfers between devices, body(): mixed = lax.all_to_all(packed, 'z', 0, 0)  15.2 us
    all_to_all x1, waiting for transfers between devices, body(): back = lax.all_to_all(returned, 'z', 0, 0)  14 us
    all_to_all x1, starting transfers between devices, body(): back = lax.all_to_all(returned, 'z', 0, 0)  13.4 us
    all_to_all x1, waiting for transfers between devices, body(): plane_rows = lax.all_to_all(plane_rows, ('xh', 'tp'), 0, 0)  7.74 us
    all_gather x1, waiting for transfers between devices, body(): weight = lax.all_gather(weight, 'z')  7.46 us
    ppermute x1, starting transfers between devices, body(): lax.ppermute(other_long, ('section', 'xh'), [(2 * s + x, 2 * t + 1 - x) f...  6.47 us
  transfers between devices with their start and end apart: 15, of which 9 were waited for; matrix products, arithmetic and copies ran while one was open for 1% of the time, Pallas kernels for 10%

profile of v12, /device:TPU:32, one launch (start us, length us, event | category | flops | bytes accessed | tf_op | source)
XLA Modules:
  0.0 179.5 jit_solution(6408846154715373557)
XLA Ops:
  7.2 2.6 %shard_map.167 = (bf16[4,128,512]{2,1,0:T(8,128)(2,1)}, bf16[16,40,128]{2,1,0:T(8,128)(2,1)}, bf16[16,40,128]{2,1,0:T(8,128)(2,1)}) custom-call(s32[1]{0:T(128)} %bitcast.x_ref, bf16[128,1024]{1,0:T(8,128)(2,1)} %bitcast.35, bf16[128,1024]{1,0:T(8,128)(2,1)} %bitcast.36, f32[9,1,1024]{2,1,0:T(1,128)} %bitcast.42, bf16[128,512]{1,0:T(8,128)(2,1)} %bitcast.38, ...), custom_call_target="tpu_custom_call" | custom-call | bytes 1937408 | tf_op jit(solution)/shard_map/pallas_call | solution.py:84
  9.8 4.5 %all-to-all-start = ((bf16[4,128,512]{2,1,0:T(8,128)(2,1)}), bf16[4,128,512]{2,1,0:T(8,128)(2,1)S(1)}, u32[]{:S(2)}, u32[]{:S(2)}) async-start(bf16[4,128,512]{2,1,0:T(8,128)(2,1)} %get-tuple-element.28), calls=%async_computation | async-start | bytes 1048576 | tf_op jit(solution)/shard_map/all_to_all | solution.py:512
  14.3 5.1 %collective-permute-start = (bf16[16,40,128]{2,1,0:T(8,128)(2,1)}, bf16[16,40,128]{2,1,0:T(8,128)(2,1)S(1)}, u32[]{:S(2)}, u32[]{:S(2)}) collective-permute-start(bf16[16,40,128]{2,1,0:T(8,128)(2,1)} %get-tuple-element.30), channel_id=1, source_target_pairs={{0,4},{4,0},{1,5},{5,1},{2,6},{6,2},{3,7},{7,3},{8,12},{12,8},{9,1... | collective-permute-start | bytes 491528 | tf_op jit(solution)/shard_map/ppermute | solution.py:511
  19.3 4.3 %collective-permute-done.got_ref = bf16[16,40,128]{2,1,0:T(8,128)(2,1)S(1)} collective-permute-done((bf16[16,40,128]{2,1,0:T(8,128)(2,1)}, bf16[16,40,128]{2,1,0:T(8,128)(2,1)S(1)}, u32[]{:S(2)}, u32[]{:S(2)}) %collective-permute-start) | collective-permute-done | bytes 163872 | tf_op jit(solution)/shard_map/ppermute | solution.py:511
  23.8 1.9 %shard_map.168 = (bf16[16,168,128]{2,1,0:T(8,128)(2,1)}, bf16[4,32,512]{2,1,0:T(8,128)(2,1)}) custom-call(s32[1]{0:T(128)} %bitcast.x_ref, bf16[4,128,512]{2,1,0:T(8,128)(2,1)S(1)} %all-to-all-done.rows_ref, bf16[16,40,128]{2,1,0:T(8,128)(2,1)} %get-tuple-element.29.own_hbm, bf16[16,40,128]{2,1,0:T(8,128)(2,1)S(1)} %collective-permute-done.got_ref), custom_call_target="tpu_custom_call" | custom-call | bytes 1671168 | tf_op jit(solution)/shard_map/pallas_call | solution.py:84
  25.7 15.2 %all-to-all-start.1 = ((bf16[16,168,128]{2,1,0:T(8,128)(2,1)}), bf16[16,168,128]{2,1,0:T(8,128)(2,1)S(1)}, u32[]{:S(2)}, u32[]{:S(2)}) async-start(bf16[16,168,128]{2,1,0:T(8,128)(2,1)} %get-tuple-element.31), calls=%async_computation.1 | async-start | bytes 1376256 | tf_op jit(solution)/shard_map/all_to_all | solution.py:529
  41.6 1.9 %collective-permute-start.1 = (bf16[128,1024]{1,0:T(8,128)(2,1)}, bf16[128,1024]{1,0:T(8,128)(2,1)S(1)}, u32[]{:S(2)}, u32[]{:S(2)}) collective-permute-start(bf16[128,1024]{1,0:T(8,128)(2,1)} %bitcast.10), channel_id=1, source_target_pairs={{0,128},{128,256},{256,384},{384,0},{1,129},{129,257},{257,385},{3... | collective-permute-start | bytes 786440 | tf_op jit(solution)/shard_map/ppermute | solution.py:534
  44.3 3.5 %collective-permute-start.2 = (f32[3,1024]{1,0:T(4,128)S(1)}, f32[3,1024]{1,0:T(4,128)S(1)}, u32[]{:S(2)}, u32[]{:S(2)}) collective-permute-start(f32[3,1024]{1,0:T(4,128)S(1)} %bitcast.43), channel_id=1, source_target_pairs={{0,128},{128,256},{256,384},{384,0},{1,129},{129,257},{257,385},{3... | collective-permute-start | bytes 36872 | tf_op jit(solution)/shard_map/ppermute | solution.py:535
  48.5 4.2 %collective-permute-start.3 = (bf16[2,1024]{1,0:T(2,128)(2,1)S(1)}, bf16[2,1024]{1,0:T(2,128)(2,1)S(1)}, u32[]{:S(2)}, u32[]{:S(2)}) collective-permute-start(bf16[2,1024]{1,0:T(2,128)(2,1)S(1)} %slice_bitcast_fusion), channel_id=1, source_target_pairs={{0,132},{4,136},{8,140},{12,144},{16,148},{20,152},{24,156},{28,16... | collective-permute-start | bytes 12296 | tf_op jit(solution)/shard_map/ppermute | solution.py:536
  53.7 2.0 %shard_map.169.spectrum_ref = f32[1280,256]{1,0:T(8,128)S(1)} custom-call(f32[32,32,128]{2,1,0:T(8,128)S(1)} %bitcast.30, bf16[80,96]{1,0:T(8,128)(2,1)} %constant.41.clone.first_ref, f32[2,40,128]{2,1,0:T(8,128)} %constant.42.clone.mid_ref, bf16[2,256,256]{2,1,0:T(8,128)(2,1)} %constant.43.clone.forward_ref), custom_call_target="tpu_custom_call" | custom-call | bytes 2153472 | tf_op jit(solution)/shard_map/pallas_call | solution.py:84
  55.8 2.6 %collective-permute-done.3.tail_ref = bf16[2,1024]{1,0:T(2,128)(2,1)S(1)} collective-permute-done((bf16[2,1024]{1,0:T(2,128)(2,1)S(1)}, bf16[2,1024]{1,0:T(2,128)(2,1)S(1)}, u32[]{:S(2)}, u32[]{:S(2)}) %collective-permute-start.3) | collective-permute-done | bytes 4128 | tf_op jit(solution)/shard_map/ppermute | solution.py:536
  58.4 15.2 %all-to-all-done.1.mixed_ref = bf16[16,168,128]{2,1,0:T(8,128)(2,1)S(1)} async-done(((bf16[16,168,128]{2,1,0:T(8,128)(2,1)}), bf16[16,168,128]{2,1,0:T(8,128)(2,1)S(1)}, u32[]{:S(2)}, u32[]{:S(2)}) %all-to-all-start.1) | async-done | bytes 688160 | tf_op jit(solution)/shard_map/all_to_all | solution.py:529
  74.6 5.3 %all-to-all-start.2 = ((bf16[4,2,512,128]{3,2,1,0:T(8,128)(2,1)}), bf16[4,2,512,128]{3,2,1,0:T(8,128)(2,1)S(1)}, u32[]{:S(2)}, u32[]{:S(2)}) async-start(bf16[4,2,512,128]{3,2,1,0:T(8,128)(2,1)} %get-tuple-element.34), calls=%async_computation.2 | async-start | bytes 2097152 | tf_op jit(solution)/shard_map/all_to_all | solution.py:571
  79.9 4.9 %collective-permute-start.4 = (bf16[512,128]{1,0:T(8,128)(2,1)S(1)}, bf16[512,128]{1,0:T(8,128)(2,1)}, u32[]{:S(2)}, u32[]{:S(2)}) collective-permute-start(bf16[512,128]{1,0:T(8,128)(2,1)S(1)} %get-tuple-element.38.query_ref), channel_id=1, source_target_pairs={{0,4},{4,0},{1,5},{5,1},{2,6},{6,2},{3,7},{7,3},{8,12},{12,8},{9,1... | collective-permute-start | bytes 393224 | tf_op jit(solution)/shard_map/ppermute | solution.py:570
  84.9 2.7 %shard_map.171 = (f32[1280,256]{1,0:T(8,128)S(1)}, f32[1024,128]{1,0:T(8,128)S(1)}, f32[8,128]{1,0:T(8,128)S(1)}) custom-call(bf16[16,168,128]{2,1,0:T(8,128)(2,1)S(1)} %all-to-all-done.1.mixed_ref, f32[32,9]{1,0:T(8,128)S(1)} %bitcast.32, f32[1280,256]{1,0:T(8,128)S(1)} %shard_map.169.spectrum_ref, bf16[80,64]{1,0:T(8,128)(2,1)} %constant.44.clone.first_ref, ...), custom_call_target="tpu_custom_call" | custom-call | bytes 4152448 | tf_op jit(solution)/shard_map/pallas_call | solution.py:84
  87.6 1.1 copy-done.2
  89.4 1.6 all-to-all-done.2.pairs_ref
  91.0 3.0 %shard_map.172 = bf16[544,128]{1,0:T(8,128)(2,1)S(1)} custom-call(s32[1]{0:T(128)} %bitcast.14.delta_ref, bf16[512,128]{1,0:T(8,128)(2,1)} %collective-permute-done.4.query_ref, bf16[4,2,512,128]{3,2,1,0:T(8,128)(2,1)S(1)} %all-to-all-done.2.pairs_ref, f32[8,128]{1,0:T(8,128)S(1)} %get-tuple-element.37.done_ref), custom_call_target="tpu_custom_call" | custom-call | flops 268435456 | bytes 1323008 | tf_op jit(solution)/shard_map/pallas_call | solution.py:84
  94.1 4.7 %collective-permute-start.5 = (bf16[544,128]{1,0:T(8,128)(2,1)S(1)}, bf16[544,128]{1,0:T(8,128)(2,1)S(1)}, u32[]{:S(2)}, u32[]{:S(2)}) collective-permute-start(bf16[544,128]{1,0:T(8,128)(2,1)S(1)} %shard_map.172), channel_id=1, source_target_pairs={{0,4},{4,0},{1,5},{5,1},{2,6},{6,2},{3,7},{7,3},{8,12},{12,8},{9,1... | collective-permute-start | bytes 417800 | tf_op jit(solution)/shard_map/ppermute | solution.py:604
  99.9 2.7 %shard_map.174 = bf16[32,32,128]{2,1,0:T(8,128)(2,1)S(1)} custom-call(f32[32]{0:T(128)S(1)} %dynamic-slice_bitcast_fusion.gain_ref, f32[1280,256]{1,0:T(8,128)S(1)} %copy-done.3, f32[1024,128]{1,0:T(8,128)S(1)} %copy-done.5, f32[2,40,128]{2,1,0:T(8,128)} %constant.42.clone.mid_ref, bf16[2,256,256]{2,1,0:T(8,128)(2,1)} %constant.45.clone.backward_ref, ...), custom_call_target="tpu_custom_call" | custom-call | bytes 2415616 | tf_op jit(solution)/shard_map/pallas_call | solution.py:84
  102.7 2.2 %shard_map.173 = (f32[512,128]{1,0:T(8,128)S(1)}, f32[512,128]{1,0:T(8,128)S(1)}) custom-call(s32[1]{0:T(128)} %bitcast.1.delta_ref, bf16[512,128]{1,0:T(8,128)(2,1)S(1)} %get-tuple-element.38.query_ref, bf16[4,2,512,128]{3,2,1,0:T(8,128)(2,1)S(1)} %all-to-all-done.2.pairs_ref), custom_call_target="tpu_custom_call" | custom-call | flops 268435456 | bytes 1703936 | tf_op jit(solution)/shard_map/pallas_call | solution.py:84
  105.8 13.4 %all-to-all-start.3 = ((bf16[16,96,128]{2,1,0:T(8,128)(2,1)}), bf16[16,96,128]{2,1,0:T(8,128)(2,1)S(1)}, u32[]{:S(2)}, u32[]{:S(2)}) async-start(bf16[16,96,128]{2,1,0:T(8,128)(2,1)} %shard_map.175), calls=%async_computation.3 | async-start | bytes 786432 | tf_op jit(solution)/shard_map/all_to_all | solution.py:628
  119.2 7.5 %all-gather.3.cloned.1.call-done = bf16[64,32,512]{2,1,0:T(8,128)(2,1)} async-done(((bf16[4,32,512]{2,1,0:T(8,128)(2,1)}), bf16[64,32,512]{2,1,0:T(8,128)(2,1)}) %all-gather.3.cloned.1.call-update) | async-done | bytes 2097168 | tf_op jit(solution)/shard_map/all_gather | solution.py:530
  126.7 14.0 %all-to-all-done.3.back_ref = bf16[16,96,128]{2,1,0:T(8,128)(2,1)S(1)} async-done(((bf16[16,96,128]{2,1,0:T(8,128)(2,1)}), bf16[16,96,128]{2,1,0:T(8,128)(2,1)S(1)}, u32[]{:S(2)}, u32[]{:S(2)}) %all-to-all-start.3) | async-done | bytes 393248 | tf_op jit(solution)/shard_map/all_to_all | solution.py:628
  140.7 1.1 shard_map.176
  141.9 4.6 %all-to-all-start.4 = ((bf16[8,32,2048]{2,1,0:T(8,128)(2,1)}), bf16[8,32,2048]{2,1,0:T(8,128)(2,1)S(1)}, u32[]{:S(2)}, u32[]{:S(2)}) async-start(bf16[8,32,2048]{2,1,0:T(8,128)(2,1)} %get-tuple-element.50), calls=%async_computation.4 | async-start | bytes 2097152 | tf_op jit(solution)/shard_map/all_to_all | solution.py:648
  146.5 1.9 %collective-permute-start.6 = (bf16[16,32,128]{2,1,0:T(8,128)(2,1)}, bf16[16,32,128]{2,1,0:T(8,128)(2,1)S(1)}, u32[]{:S(2)}, u32[]{:S(2)}) collective-permute-start(bf16[16,32,128]{2,1,0:T(8,128)(2,1)} %get-tuple-element.45), channel_id=1, source_target_pairs={{0,128},{128,256},{256,384},{384,0},{1,129},{129,257},{257,385},{3... | collective-permute-start | bytes 393224 | tf_op jit(solution)/shard_map/ppermute | solution.py:649
  148.4 6.5 %collective-permute-start.7 = (bf16[16,32,128]{2,1,0:T(8,128)(2,1)}, bf16[16,32,128]{2,1,0:T(8,128)(2,1)}, u32[]{:S(2)}, u32[]{:S(2)}) collective-permute-start(bf16[16,32,128]{2,1,0:T(8,128)(2,1)} %get-tuple-element.46), channel_id=1, source_target_pairs={{0,132},{4,128},{128,260},{132,256},{256,388},{260,384},{384,4},{3... | collective-permute-start | bytes 393224 | tf_op jit(solution)/shard_map/ppermute | solution.py:650
  154.8 7.7 %all-to-all-done.4.rows_ref = bf16[8,32,2048]{2,1,0:T(8,128)(2,1)S(1)} async-done(((bf16[8,32,2048]{2,1,0:T(8,128)(2,1)}), bf16[8,32,2048]{2,1,0:T(8,128)(2,1)S(1)}, u32[]{:S(2)}, u32[]{:S(2)}) %all-to-all-start.4) | async-done | bytes 1048608 | tf_op jit(solution)/shard_map/all_to_all | solution.py:648
  163.3 3.1 %collective-permute-start.8 = (bf16[128,512]{1,0:T(8,128)(2,1)S(1)}, bf16[128,512]{1,0:T(8,128)(2,1)S(1)}, u32[]{:S(2)}, u32[]{:S(2)}) collective-permute-start(bf16[128,512]{1,0:T(8,128)(2,1)S(1)} %get-tuple-element.53), channel_id=1, source_target_pairs={{0,4},{4,0},{1,5},{5,1},{2,6},{6,2},{3,7},{7,3},{8,12},{12,8},{9,1... | collective-permute-start | bytes 393224 | tf_op jit(solution)/shard_map/ppermute | solution.py:667
  166.5 1.9 %shard_map.177 = bf16[128,1024]{1,0:T(8,128)(2,1)} custom-call(s32[1]{0:T(128)} %bitcast.x_ref, bf16[16,32,128]{2,1,0:T(8,128)(2,1)S(1)} %collective-permute-done.6.own_ref, bf16[16,32,128]{2,1,0:T(8,128)(2,1)} %collective-permute-done.7.got_ref, bf16[128,1024]{1,0:T(8,128)(2,1)S(1)} %collective-permute-done.1.gate_ref, ...), custom_call_target="tpu_custom_call" | custom-call | bytes 802816 | tf_op jit(solution)/shard_map/pallas_call | solution.py:84
  168.4 3.3 %collective-permute-done.8.got_ref = bf16[128,512]{1,0:T(8,128)(2,1)S(1)} collective-permute-done((bf16[128,512]{1,0:T(8,128)(2,1)S(1)}, bf16[128,512]{1,0:T(8,128)(2,1)S(1)}, u32[]{:S(2)}, u32[]{:S(2)}) %collective-permute-start.8) | collective-permute-done | bytes 131104 | tf_op jit(solution)/shard_map/ppermute | solution.py:667
  (38 shorter events, 8.9 us)
Async XLA Ops:
  7.2 91.6 %copy-start = (f32[1,1024]{1,0:T(1,128)S(1)}, f32[1,1024]{1,0:T(1,128)}, u32[]{:S(2)}) copy-start(f32[1,1024]{1,0:T(1,128)} %param.21) | copy-start | bytes 12292
  9.8 13.9 %all-to-all-start = ((bf16[4,128,512]{2,1,0:T(8,128)(2,1)}), bf16[4,128,512]{2,1,0:T(8,128)(2,1)S(1)}, u32[]{:S(2)}, u32[]{:S(2)}) async-start(bf16[4,128,512]{2,1,0:T(8,128)(2,1)} %get-tuple-element.28), calls=%async_computation | async-start | bytes 1048576 | tf_op jit(solution)/shard_map/all_to_all | solution.py:512
  14.3 39.4 %copy-start.8 = (f32[1,1,1,32,4096]{4,3,2,1,0:T(8,128)S(1)}, f32[1,1,1,32,4096]{4,3,2,1,0:T(8,128)}, u32[]{:S(2)}) copy-start(f32[1,1,1,32,4096]{4,3,2,1,0:T(8,128)} %param.20) | copy-start | bytes 1572868
  14.3 9.4 %collective-permute-start = (bf16[16,40,128]{2,1,0:T(8,128)(2,1)}, bf16[16,40,128]{2,1,0:T(8,128)(2,1)S(1)}, u32[]{:S(2)}, u32[]{:S(2)}) collective-permute-start(bf16[16,40,128]{2,1,0:T(8,128)(2,1)} %get-tuple-element.30), channel_id=1, source_target_pairs={{0,4},{4,0},{1,5},{5,1},{2,6},{6,2},{3,7},{7,3},{8,12},{12,8},{9,1... | collective-permute-start | bytes 491528 | tf_op jit(solution)/shard_map/ppermute | solution.py:511
  25.7 47.9 %all-to-all-start.1 = ((bf16[16,168,128]{2,1,0:T(8,128)(2,1)}), bf16[16,168,128]{2,1,0:T(8,128)(2,1)S(1)}, u32[]{:S(2)}, u32[]{:S(2)}) async-start(bf16[16,168,128]{2,1,0:T(8,128)(2,1)} %get-tuple-element.31), calls=%async_computation.1 | async-start | bytes 1376256 | tf_op jit(solution)/shard_map/all_to_all | solution.py:529
  40.9 85.8 %all-gather.3.cloned.1.call-start = ((), (), s32[]{:S(2)}) async-start(), calls=%async_computation.5 | async-start | bytes 2228224 | tf_op jit(solution)/shard_map/all_gather | solution.py:530
  41.6 16.8 %collective-permute-start.1 = (bf16[128,1024]{1,0:T(8,128)(2,1)}, bf16[128,1024]{1,0:T(8,128)(2,1)S(1)}, u32[]{:S(2)}, u32[]{:S(2)}) collective-permute-start(bf16[128,1024]{1,0:T(8,128)(2,1)} %bitcast.10), channel_id=1, source_target_pairs={{0,128},{128,256},{256,384},{384,0},{1,129},{129,257},{257,385},{3... | collective-permute-start | bytes 786440 | tf_op jit(solution)/shard_map/ppermute | solution.py:534
  44.3 14.1 %collective-permute-start.2 = (f32[3,1024]{1,0:T(4,128)S(1)}, f32[3,1024]{1,0:T(4,128)S(1)}, u32[]{:S(2)}, u32[]{:S(2)}) collective-permute-start(f32[3,1024]{1,0:T(4,128)S(1)} %bitcast.43), channel_id=1, source_target_pairs={{0,128},{128,256},{256,384},{384,0},{1,129},{129,257},{257,385},{3... | collective-permute-start | bytes 36872 | tf_op jit(solution)/shard_map/ppermute | solution.py:535
  48.5 9.9 %collective-permute-start.3 = (bf16[2,1024]{1,0:T(2,128)(2,1)S(1)}, bf16[2,1024]{1,0:T(2,128)(2,1)S(1)}, u32[]{:S(2)}, u32[]{:S(2)}) collective-permute-start(bf16[2,1024]{1,0:T(2,128)(2,1)S(1)} %slice_bitcast_fusion), channel_id=1, source_target_pairs={{0,132},{4,136},{8,140},{12,144},{16,148},{20,152},{24,156},{28,16... | collective-permute-start | bytes 12296 | tf_op jit(solution)/shard_map/ppermute | solution.py:536
  58.4 16.2 %copy-start.6 = (f32[3,1024]{1,0:T(4,128)}, f32[3,1024]{1,0:T(4,128)S(1)}, u32[]{:S(2)}) copy-start(f32[3,1024]{1,0:T(4,128)S(1)} %collective-permute-done.2.taps_ref) | copy-start | bytes 36868
  74.6 16.4 %all-to-all-start.2 = ((bf16[4,2,512,128]{3,2,1,0:T(8,128)(2,1)}), bf16[4,2,512,128]{3,2,1,0:T(8,128)(2,1)S(1)}, u32[]{:S(2)}, u32[]{:S(2)}) async-start(bf16[4,2,512,128]{3,2,1,0:T(8,128)(2,1)} %get-tuple-element.34), calls=%async_computation.2 | async-start | bytes 2097152 | tf_op jit(solution)/shard_map/all_to_all | solution.py:571
  79.9 9.5 %collective-permute-start.4 = (bf16[512,128]{1,0:T(8,128)(2,1)S(1)}, bf16[512,128]{1,0:T(8,128)(2,1)}, u32[]{:S(2)}, u32[]{:S(2)}) collective-permute-start(bf16[512,128]{1,0:T(8,128)(2,1)S(1)} %get-tuple-element.38.query_ref), channel_id=1, source_target_pairs={{0,4},{4,0},{1,5},{5,1},{2,6},{6,2},{3,7},{7,3},{8,12},{12,8},{9,1... | collective-permute-start | bytes 393224 | tf_op jit(solution)/shard_map/ppermute | solution.py:570
  87.6 1.1 copy-start.2
  88.6 0.8 copy-start.4
  89.4 9.4 %copy-start.3 = (f32[1280,256]{1,0:T(8,128)S(1)}, f32[1280,256]{1,0:T(8,128)}, u32[]{:S(2)}) copy-start(f32[1280,256]{1,0:T(8,128)} %copy-done.2) | copy-start | bytes 3932164
  94.1 10.8 %collective-permute-start.5 = (bf16[544,128]{1,0:T(8,128)(2,1)S(1)}, bf16[544,128]{1,0:T(8,128)(2,1)S(1)}, u32[]{:S(2)}, u32[]{:S(2)}) collective-permute-start(bf16[544,128]{1,0:T(8,128)(2,1)S(1)} %shard_map.172), channel_id=1, source_target_pairs={{0,4},{4,0},{1,5},{5,1},{2,6},{6,2},{3,7},{7,3},{8,12},{12,8},{9,1... | collective-permute-start | bytes 417800 | tf_op jit(solution)/shard_map/ppermute | solution.py:604
  98.9 1.0 copy-start.5
  105.8 34.9 %all-to-all-start.3 = ((bf16[16,96,128]{2,1,0:T(8,128)(2,1)}), bf16[16,96,128]{2,1,0:T(8,128)(2,1)S(1)}, u32[]{:S(2)}, u32[]{:S(2)}) async-start(bf16[16,96,128]{2,1,0:T(8,128)(2,1)} %shard_map.175), calls=%async_computation.3 | async-start | bytes 786432 | tf_op jit(solution)/shard_map/all_to_all | solution.py:628
  126.7 35.9 %copy-start.1 = (bf16[64,32,512]{2,1,0:T(8,128)(2,1)S(1)}, bf16[64,32,512]{2,1,0:T(8,128)(2,1)}, u32[]{:S(2)}) copy-start(bf16[64,32,512]{2,1,0:T(8,128)(2,1)} %all-gather.3.cloned.1.call-done) | copy-start | bytes 6291460
  141.9 20.7 %all-to-all-start.4 = ((bf16[8,32,2048]{2,1,0:T(8,128)(2,1)}), bf16[8,32,2048]{2,1,0:T(8,128)(2,1)S(1)}, u32[]{:S(2)}, u32[]{:S(2)}) async-start(bf16[8,32,2048]{2,1,0:T(8,128)(2,1)} %get-tuple-element.50), calls=%async_computation.4 | async-start | bytes 2097152 | tf_op jit(solution)/shard_map/all_to_all | solution.py:648
  146.5 20.0 %collective-permute-start.6 = (bf16[16,32,128]{2,1,0:T(8,128)(2,1)}, bf16[16,32,128]{2,1,0:T(8,128)(2,1)S(1)}, u32[]{:S(2)}, u32[]{:S(2)}) collective-permute-start(bf16[16,32,128]{2,1,0:T(8,128)(2,1)} %get-tuple-element.45), channel_id=1, source_target_pairs={{0,128},{128,256},{256,384},{384,0},{1,129},{129,257},{257,385},{3... | collective-permute-start | bytes 393224 | tf_op jit(solution)/shard_map/ppermute | solution.py:649
  148.4 18.1 %collective-permute-start.7 = (bf16[16,32,128]{2,1,0:T(8,128)(2,1)}, bf16[16,32,128]{2,1,0:T(8,128)(2,1)}, u32[]{:S(2)}, u32[]{:S(2)}) collective-permute-start(bf16[16,32,128]{2,1,0:T(8,128)(2,1)} %get-tuple-element.46), channel_id=1, source_target_pairs={{0,132},{4,128},{128,260},{132,256},{256,388},{260,384},{384,4},{3... | collective-permute-start | bytes 393224 | tf_op jit(solution)/shard_map/ppermute | solution.py:650
  162.6 3.9 %copy-start.7 = (f32[3,1024]{1,0:T(4,128)S(1)}, f32[3,1024]{1,0:T(4,128)}, u32[]{:S(2)}) copy-start(f32[3,1024]{1,0:T(4,128)} %copy-done.6) | copy-start | bytes 36868
  163.3 8.4 %collective-permute-start.8 = (bf16[128,512]{1,0:T(8,128)(2,1)S(1)}, bf16[128,512]{1,0:T(8,128)(2,1)S(1)}, u32[]{:S(2)}, u32[]{:S(2)}) collective-permute-start(bf16[128,512]{1,0:T(8,128)(2,1)S(1)} %get-tuple-element.53), channel_id=1, source_target_pairs={{0,4},{4,0},{1,5},{5,1},{2,6},{6,2},{3,7},{7,3},{8,12},{12,8},{9,1... | collective-permute-start | bytes 393224 | tf_op jit(solution)/shard_map/ppermute | solution.py:667
Sparse Core Ops, SparseCore 0:
  44.4 82.2 all-gather.2
